TPU v7x, 32 devices: a whole 2x2x4 slice. The times are simulated.
32 devices in a mesh: blk: 16 (over z, x, core), uly: 2 (over y).
Axes of the slice: x: 2, y: 2, z: 4, core: 2. Of those that a mesh axis runs over, the one named last changes fastest.
Arguments:
- residual: bfloat16 [384, 2048], P(('blk', 'uly')), may hold values from -24 to 24
- query_projection: bfloat16 [384, 4096], P(('blk', 'uly')), may hold values from -51 to 51
- key_projection: bfloat16 [384, 1024], P(('blk', 'uly')), may hold values from -5.1 to 5.1
- value_projection: bfloat16 [384, 1024], P(('blk', 'uly')), may hold values from -6 to 6
- gate_proj: bfloat16 [384, 4096], P(('blk', 'uly')), may hold values from -6 to 6
- positions: int32 [384], replicated, may hold values from 0 to 383, each once
- prefix_len: int32 [1], replicated, may hold values from 48 to 191
- out_weight: bfloat16 [4096, 2048], P('uly', 'blk'), may hold values from -0.375 to 0.375
- norm_gain: float32 [2048], replicated, may hold values from 0.1 to 1.9
- gate_weight: bfloat16 [2048, 6144], P('blk', 'uly'), may hold values from -0.125 to 0.125
- up_weight: bfloat16 [2048, 6144], P('blk', 'uly'), may hold values from -0.125 to 0.125
- down_weight: bfloat16 [6144, 2048], P('uly', 'blk'), may hold values from -0.078125 to 0.078125
Outputs:
- layer_out: bfloat16 [384, 2048], P(('blk', 'uly'))
Inputs may be any that keep to these rules, and one draw needn't show every extreme that they name: `positions`: each of 0 to 383 appears once.
All inputs are finite; a program needn't handle non-finite values.
Results may differ from a plain program's by a relative error of at most 0.014.
Values may be sent and summed in bfloat16 or wider, within the bound.
No kernel may reach another device: no remote copies, remote signals or barrier semaphores. Data moves between devices by JAX's collectives and lax.ppermute only.
A program may use at most 128 MiB of HBM per device.

v0:
```python
import math

import jax
import jax.numpy as jnp
from jax import lax
from jax.sharding import PartitionSpec as P

HEAD_SIZE = 128


def per_device(
    residual,
    query_projection,
    key_projection,
    value_projection,
    gate_proj,
    positions,
    prefix_len,
    out_weight,
    norm_gain,
    gate_weight,
    up_weight,
    down_weight,
):
    q_loc, k_loc, v_loc, g_loc = (
        lax.all_to_all(query_projection, "uly", split_axis=1, concat_axis=0, tiled=True),
        lax.all_to_all(key_projection, "uly", split_axis=1, concat_axis=0, tiled=True),
        lax.all_to_all(value_projection, "uly", split_axis=1, concat_axis=0, tiled=True),
        lax.all_to_all(gate_proj, "uly", split_axis=1, concat_axis=0, tiled=True),
    )
    row_count = q_loc.shape[0]
    kv_heads = k_loc.shape[1] // HEAD_SIZE
    q_heads = q_loc.shape[1] // HEAD_SIZE
    heads_per_group = q_heads // kv_heads
    score_scale = 1.0 / math.sqrt(HEAD_SIZE)
    blk_index = lax.axis_index("blk")
    query_pos = lax.dynamic_slice_in_dim(positions, blk_index * row_count, row_count)
    prefix = prefix_len[0]
    query_heads = q_loc.reshape(row_count, kv_heads, heads_per_group, HEAD_SIZE)
    wo_full, wg_full, wu_full, wd_full = (
        lax.all_gather(out_weight, "blk", axis=1, tiled=True),
        lax.all_gather(gate_weight, "blk", axis=0, tiled=True),
        lax.all_gather(up_weight, "blk", axis=0, tiled=True),
        lax.all_gather(down_weight, "blk", axis=1, tiled=True),
    )
    run_max = jnp.full((row_count, kv_heads, heads_per_group), -jnp.inf, jnp.float32)
    run_sum = jnp.zeros((row_count, kv_heads, heads_per_group), jnp.float32)
    weighted = jnp.zeros((row_count, kv_heads, heads_per_group, HEAD_SIZE), jnp.float32)
    key_part = lax.all_gather(k_loc, "blk", axis=0, tiled=True)
    value_part = lax.all_gather(v_loc, "blk", axis=0, tiled=True)
    key_count = key_part.shape[0]
    scores = (
        jnp.einsum(
            "bkgd,skd->bkgs",
            query_heads,
            key_part.reshape(key_count, kv_heads, HEAD_SIZE),
            preferred_element_type=jnp.float32,
        )
        * score_scale
    )
    visible = (positions[None, :] <= query_pos[:, None]) | (positions[None, :] < prefix)
    scores = jnp.where(visible[:, None, None, :], scores, -jnp.inf)
    new_max = jnp.max(scores, axis=-1)
    safe_max = jnp.where(new_max == -jnp.inf, 0.0, new_max)
    factor = jnp.exp(run_max - safe_max)
    exp_scores = jnp.exp(scores - safe_max[..., None])
    run_sum = run_sum * factor + jnp.sum(exp_scores, axis=-1)
    probs = exp_scores.astype(jnp.bfloat16)
    weighted = weighted * factor[..., None] + jnp.einsum(
        "bkgs,skd->bkgd",
        probs,
        value_part.reshape(key_count, kv_heads, HEAD_SIZE),
        preferred_element_type=jnp.float32,
    )
    _, denom, weighted = (new_max, run_sum, weighted)
    attended = (weighted / denom[..., None]).reshape(row_count, q_heads * HEAD_SIZE)
    gated_out = (attended * jax.nn.sigmoid(g_loc.astype(jnp.float32))).astype(jnp.bfloat16)
    head_partial = jnp.dot(gated_out, wo_full, preferred_element_type=jnp.float32)
    projected = lax.psum_scatter(
        head_partial.astype(jnp.bfloat16), "uly", scatter_dimension=0, tiled=True
    ).astype(jnp.float32)
    hidden_f = (residual.astype(jnp.float32) + projected).astype(jnp.bfloat16).astype(jnp.float32)
    mean_sq = jnp.mean(hidden_f * hidden_f, axis=-1, keepdims=True)
    normed = (hidden_f * lax.rsqrt(mean_sq + 1e-06) * norm_gain).astype(jnp.bfloat16)
    group_rows = lax.all_gather(normed, "uly", axis=0, tiled=True)
    gate_sum = jnp.dot(group_rows, wg_full, preferred_element_type=jnp.float32)
    up_sum = jnp.dot(group_rows, wu_full, preferred_element_type=jnp.float32)
    activated = (jax.nn.silu(gate_sum) * up_sum).astype(jnp.bfloat16)
    ffn_partial = jnp.dot(activated, wd_full, preferred_element_type=jnp.float32)
    ffn_out = lax.psum_scatter(
        ffn_partial.astype(jnp.bfloat16), "uly", scatter_dimension=0, tiled=True
    ).astype(jnp.float32)
    return (hidden_f + ffn_out).astype(jnp.bfloat16)


def solution(mesh):
    return jax.shard_map(
        per_device,
        mesh=mesh,
        in_specs=(
            P(("blk", "uly"), None),
            P(("blk", "uly"), None),
            P(("blk", "uly"), None),
            P(("blk", "uly"), None),
            P(("blk", "uly"), None),
            P(),
            P(),
            P("uly", "blk"),
            P(),
            P("blk", "uly"),
            P("blk", "uly"),
            P("uly", "blk"),
        ),
        out_specs=P(("blk", "uly"), None),
        check_vma=False,
    )
```

profile of v0, /device:TPU:0, one launch (start us, length us, event | category | flops | bytes accessed | tf_op | source)
XLA Modules:
  0.0 432.0 jit_solution(1990123216095584296)
XLA Ops:
  6.5 0.7 all-gather.6.cloned.1.call-update
  7.3 0.7 all-gather.8.cloned.1.call-update
  8.1 0.7 all-gather.10.cloned.1.call-update
  9.3 0.8 all_to_all.50
  10.7 4.2 all-to-all-start
  15.6 0.7 broadcast_compare_fusion
  16.3 0.8 dynamic_slice.3
  17.0 0.8 all_to_all.57
  18.9 3.3 all-to-all-start.2
  22.2 0.8 compare_or_fusion
  22.9 1.0 all_to_all.54
  23.9 0.7 copy.25
  24.6 1.0 all_to_all.61
  25.6 0.7 copy.32
  26.3 3.4 all-to-all-start.1
  29.7 24.4 %all_gather.21 = bf16[384,512]{1,0:T(8,128)(2,1)S(1)} all-gather(bf16[24,512]{1,0:T(8,128)(2,1)S(1)} %all_to_all.53), channel_id=1, replica_groups=mesh['blk'=16,'uly'=2] {'blk'}, dimensions={0}, use_global_device_ids=true | all-gather | bytes 417792 | tf_op jit(solution)/shard_map/all_gather | solution.py:49
  54.0 20.7 %all_gather.22 = bf16[384,512]{1,0:T(8,128)(2,1)S(1)} all-gather(bf16[24,512]{1,0:T(8,128)(2,1)S(1)} %all_to_all.60), channel_id=1, replica_groups=mesh['blk'=16,'uly'=2] {'blk'}, dimensions={0}, use_global_device_ids=true | all-gather | bytes 417792 | tf_op jit(solution)/shard_map/all_gather | solution.py:50
  75.2 3.4 all-to-all-start.3
  79.8 3.4 all-to-all-done.3
  83.3 11.8 %all-gather.6.cloned.1.call-done = bf16[2048,2048]{1,0:T(8,128)(2,1)} async-done(((bf16[2048,128]{1,0:T(8,128)(2,1)}), bf16[2048,2048]{1,0:T(8,128)(2,1)}) %all-gather.6.cloned.1.call-update) | async-done | bytes 8388624 | tf_op jit(solution)/shard_map/all_gather | solution.py:41
  95.1 4.6 %convolution_convert_fusion.1 = bf16[24,2048]{1,0:T(8,128)(2,1)S(1)} fusion(bf16[2048,2048]{1,0:T(8,128)(2,1)} %all-gather.6.cloned.1.call-done, f32[24,2048]{1,0:T(8,128)S(1)} %reshape.92, f32[24,2048]{1,0:T(8,128)S(1)} %reshape.94), kind=kOutput, calls=%fused_computation.3 | convolution fusion | flops 201474048 | bytes 8880128 | tf_op jit(solution)/shard_map/dot_general | solution.py:78
  99.7 7.4 %fusion = bf16[16,2048]{1,0:T(8,128)(2,1)S(1)} fusion(bf16[24,2048]{1,0:T(8,128)(2,1)S(1)} %convolution_convert_fusion.1), kind=kCustom, calls=%all-reduce-scatter | all-reduce-scatter fusion | flops 65537 | bytes 164352
  107.1 2.4 collective-permute-start
  111.4 5.2 %all-gather = bf16[2,12,2048]{2,1,0:T(8,128)(2,1)S(1)} all-gather(bf16[1,12,2048]{2,1,0:T(8,128)(2,1)S(1)} %fusion.22), channel_id=1, replica_groups=mesh['blk'=16,'uly'=2] {'uly'}, dimensions={0}, use_global_device_ids=true | all-gather | bytes 147456 | tf_op jit(solution)/shard_map/all_gather | solution.py:85
  116.7 79.7 %all-gather.8.cloned.1.call-done = bf16[2048,3072]{1,0:T(8,128)(2,1)} async-done(((bf16[128,3072]{1,0:T(8,128)(2,1)}), bf16[2048,3072]{1,0:T(8,128)(2,1)}) %all-gather.8.cloned.1.call-update) | async-done | bytes 12582928 | tf_op jit(solution)/shard_map/all_gather | solution.py:42
  196.3 6.3 %fusion.26 = f32[24,3072]{1,0:T(8,128)S(1)} fusion(bf16[24,2048]{1,0:T(8,128)(2,1)S(1)} %reshape.96, bf16[2048,3072]{1,0:T(8,128)(2,1)} %all-gather.8.cloned.1.call-done), kind=kOutput, calls=%fused_computation.40 | convolution fusion | flops 301989888 | bytes 12976128 | tf_op jit(solution)/shard_map/dot_general | solution.py:86
  202.7 94.9 %all-gather.10.cloned.1.call-done = bf16[2048,3072]{1,0:T(8,128)(2,1)} async-done(((bf16[128,3072]{1,0:T(8,128)(2,1)}), bf16[2048,3072]{1,0:T(8,128)(2,1)}) %all-gather.10.cloned.1.call-update) | async-done | bytes 12582928 | tf_op jit(solution)/shard_map/all_gather | solution.py:43
  297.6 104.2 %all-gather.12.cloned.1.call-done = bf16[3072,2048]{1,0:T(8,128)(2,1)} async-done(((bf16[3072,128]{1,0:T(8,128)(2,1)}), bf16[3072,2048]{1,0:T(8,128)(2,1)}) %all-gather.12.cloned.1.call-update) | async-done | bytes 12582928 | tf_op jit(solution)/shard_map/all_gather | solution.py:44
  401.8 11.5 %convolution_convert_fusion = bf16[24,2048]{1,0:T(8,128)(2,1)S(1)} fusion(bf16[3072,2048]{1,0:T(8,128)(2,1)} %all-gather.12.cloned.1.call-done, bf16[24,2048]{1,0:T(8,128)(2,1)S(1)} %reshape.96, bf16[2048,3072]{1,0:T(8,128)(2,1)} %all-gather.10.cloned.1.call-done, f32[24,3072]{1,0:T(8,128)S(1)} %fusion.26), kind=kOutput, calls=%fused_computation.2 | convolution fusion | flops 604471296 | bytes 25657344 | tf_op jit(solution)/shard_map/dot_general | solution.py:89
  413.3 7.4 %fusion.1 = bf16[16,2048]{1,0:T(8,128)(2,1)S(1)} fusion(bf16[24,2048]{1,0:T(8,128)(2,1)S(1)} %convolution_convert_fusion), kind=kCustom, calls=%all-reduce-scatter.1 | all-reduce-scatter fusion | flops 65537 | bytes 164352
  420.7 2.4 collective-permute-start.1
  423.1 1.4 collective-permute-done.1
  (41 shorter events, 6.2 us)
Async XLA Ops:
  6.5 103.0 %copy-start.2 = (u32[32]{0:T(128)S(1)}, u32[32]{0:T(128)}, u32[]{:S(2)}) copy-start(u32[32]{0:T(128)} %constant.37) | copy-start | bytes 388
  6.5 104.6 %copy-start = (bf16[12,2048]{1,0:T(8,128)(2,1)S(1)}, bf16[12,2048]{1,0:T(8,128)(2,1)}, u32[]{:S(2)}) copy-start(bf16[12,2048]{1,0:T(8,128)(2,1)} %param.12) | copy-start | bytes 147460
  6.5 104.8 %copy-start.1 = (f32[2048]{0:T(1024)S(1)}, f32[2048]{0:T(1024)}, u32[]{:S(2)}) copy-start(f32[2048]{0:T(1024)} %param.20) | copy-start | bytes 24580
  6.5 88.5 %all-gather.6.cloned.1.call-start = ((), (), s32[]{:S(2)}) async-start(), calls=%async_computation.4 | async-start | bytes 8912896 | tf_op jit(solution)/shard_map/all_gather | solution.py:41
  7.3 189.1 %all-gather.8.cloned.1.call-start = ((), (), s32[]{:S(2)}) async-start(), calls=%async_computation.5 | async-start | bytes 13369344 | tf_op jit(solution)/shard_map/all_gather | solution.py:42
  8.0 289.6 %all-gather.10.cloned.1.call-start = ((), (), s32[]{:S(2)}) async-start(), calls=%async_computation.6 | async-start | bytes 13369344 | tf_op jit(solution)/shard_map/all_gather | solution.py:43
  8.7 393.0 %all-gather.12.cloned.1.call-start = ((), (), s32[]{:S(2)}) async-start(), calls=%async_computation.7 | async-start | bytes 13369344 | tf_op jit(solution)/shard_map/all_gather | solution.py:44
  10.7 8.2 %all-to-all-start = ((bf16[12,2,512]{2,0,1:T(8,128)(2,1)}), bf16[12,2,512]{2,0,1:T(8,128)(2,1)S(1)}, u32[]{:S(2)}, u32[]{:S(2)}) async-start(bf16[12,2,512]{2,0,1:T(8,128)(2,1)} %copy.23), calls=%async_computation | async-start | bytes 65536 | tf_op jit(solution)/shard_map/all_to_all | solution.py:27
  18.9 7.4 %all-to-all-start.2 = ((bf16[12,2,512]{2,0,1:T(8,128)(2,1)}), bf16[12,2,512]{2,0,1:T(8,128)(2,1)S(1)}, u32[]{:S(2)}, u32[]{:S(2)}) async-start(bf16[12,2,512]{2,0,1:T(8,128)(2,1)} %copy.28), calls=%async_computation.2 | async-start | bytes 65536 | tf_op jit(solution)/shard_map/all_to_all | solution.py:28
  26.3 48.9 %all-to-all-start.1 = ((bf16[12,2,2048]{2,0,1:T(8,128)(2,1)}), bf16[12,2,2048]{2,0,1:T(8,128)(2,1)S(1)}, u32[]{:S(2)}, u32[]{:S(2)}) async-start(bf16[12,2,2048]{2,0,1:T(8,128)(2,1)} %copy.25), calls=%async_computation.1 | async-start | bytes 262144 | tf_op jit(solution)/shard_map/all_to_all | solution.py:26
  75.2 8.0 %all-to-all-start.3 = ((bf16[12,2,2048]{2,0,1:T(8,128)(2,1)}), bf16[12,2,2048]{2,0,1:T(8,128)(2,1)S(1)}, u32[]{:S(2)}, u32[]{:S(2)}) async-start(bf16[12,2,2048]{2,0,1:T(8,128)(2,1)} %copy.32), calls=%async_computation.3 | async-start | bytes 262144 | tf_op jit(solution)/shard_map/all_to_all | solution.py:29
  107.1 3.9 collective-permute-start
  420.7 3.9 collective-permute-start.1
Sparse Core Ops, SparseCore 0:
  9.5 85.5 all-gather.5
  97.4 98.9 all-gather.7
  198.6 98.9 all-gather.9
  299.6 102.1 all-gather.11
where the time goes:
time: 433 us; the launch traced here: 432 us
  waiting for transfers between devices  299 us (69%)
  blocking collectives  65 us (15%)
  matrix products  23.1 us (5%)
  starting transfers between devices  19.3 us (4%)
  between operations  14.7 us (3%)
  local copies, waits for them, and re-layouts  8.58 us (2%)
    all_gather x1, waiting for transfers between devices, per_device(): lax.all_gather(down_weight, 'blk', axis=1, tiled=True)  104 us
    all_gather x1, waiting for transfers between devices, per_device(): lax.all_gather(up_weight, 'blk', axis=0, tiled=True)  94.9 us
    all_gather x1, waiting for transfers between devices, per_device(): lax.all_gather(gate_weight, 'blk', axis=0, tiled=True)  79.7 us
    all_gather x1, blocking collectives, per_device(): key_part = lax.all_gather(k_loc, 'blk', axis=0, tiled=True)  24.4 us
    all_gather x1, blocking collectives, per_device(): value_part = lax.all_gather(v_loc, 'blk', axis=0, tiled=True)  20.7 us
    unnamed x2, blocking collectives  14.7 us
    all_gather x1, waiting for transfers between devices, per_device(): lax.all_gather(out_weight, 'blk', axis=1, tiled=True)  11.8 us
    dot_general x1, matrix products, per_device(): jnp.dot(activated, wd_full, preferred_element_type=jnp.float32)  11.5 us
  transfers between devices with their start and end apart: 10, of which 8 were waited for; matrix products, arithmetic and copies ran while one was open for 6% of the time, Pallas kernels for 0%

commit v1 on v0

v1 whole, which is shorter than its diff:
```python
import functools
import math

import jax
import jax.numpy as jnp
import numpy as np
from jax import lax
from jax.experimental import pallas as pl
from jax.experimental.pallas import tpu as pltpu
from jax.sharding import PartitionSpec as P

HEAD_SIZE = 128
ROW_TILE = 16
HIDE = -1e30
NO_POSITION = np.iinfo(np.int32).max
F32 = jnp.float32
BF16 = jnp.bfloat16
VMEM = pl.BlockSpec(memory_space=pltpu.VMEM)
SMEM = pl.BlockSpec(memory_space=pltpu.SMEM)
NT = (((1,), (1,)), ((), ()))


def move_weights(
    residual,
    query_projection,
    key_projection,
    value_projection,
    gate_proj,
    positions,
    prefix_len,
    out_weight,
    norm_gain,
    gate_weight,
    up_weight,
    down_weight,
):
    q_loc, k_loc, v_loc, g_loc = (
        lax.all_to_all(query_projection, "uly", split_axis=1, concat_axis=0, tiled=True),
        lax.all_to_all(key_projection, "uly", split_axis=1, concat_axis=0, tiled=True),
        lax.all_to_all(value_projection, "uly", split_axis=1, concat_axis=0, tiled=True),
        lax.all_to_all(gate_proj, "uly", split_axis=1, concat_axis=0, tiled=True),
    )
    row_count = q_loc.shape[0]
    kv_heads = k_loc.shape[1] // HEAD_SIZE
    q_heads = q_loc.shape[1] // HEAD_SIZE
    heads_per_group = q_heads // kv_heads
    score_scale = 1.0 / math.sqrt(HEAD_SIZE)
    blk_index = lax.axis_index("blk")
    query_pos = lax.dynamic_slice_in_dim(positions, blk_index * row_count, row_count)
    prefix = prefix_len[0]
    query_heads = q_loc.reshape(row_count, kv_heads, heads_per_group, HEAD_SIZE)
    wo_full, wg_full, wu_full, wd_full = (
        lax.all_gather(out_weight, "blk", axis=1, tiled=True),
        lax.all_gather(gate_weight, "blk", axis=0, tiled=True),
        lax.all_gather(up_weight, "blk", axis=0, tiled=True),
        lax.all_gather(down_weight, "blk", axis=1, tiled=True),
    )
    key_part = lax.all_gather(k_loc, "blk", axis=0, tiled=True)
    value_part = lax.all_gather(v_loc, "blk", axis=0, tiled=True)
    key_count = key_part.shape[0]
    scores = (
        jnp.einsum(
            "bkgd,skd->bkgs",
            query_heads,
            key_part.reshape(key_count, kv_heads, HEAD_SIZE),
            preferred_element_type=F32,
        )
        * score_scale
    )
    visible = (positions[None, :] <= query_pos[:, None]) | (positions[None, :] < prefix)
    scores = jnp.where(visible[:, None, None, :], scores, -jnp.inf)
    row_max = jnp.max(scores, axis=-1)
    exp_scores = jnp.exp(scores - row_max[..., None])
    denom = jnp.sum(exp_scores, axis=-1)
    probs = exp_scores.astype(BF16)
    weighted = jnp.einsum(
        "bkgs,skd->bkgd",
        probs,
        value_part.reshape(key_count, kv_heads, HEAD_SIZE),
        preferred_element_type=F32,
    )
    attended = (weighted / denom[..., None]).reshape(row_count, q_heads * HEAD_SIZE)
    gated_out = (attended * jax.nn.sigmoid(g_loc.astype(F32))).astype(BF16)
    head_partial = jnp.dot(gated_out, wo_full, preferred_element_type=F32)
    projected = lax.psum_scatter(
        head_partial.astype(BF16), "uly", scatter_dimension=0, tiled=True
    ).astype(F32)
    hidden_f = (residual.astype(F32) + projected).astype(BF16).astype(F32)
    mean_sq = jnp.mean(hidden_f * hidden_f, axis=-1, keepdims=True)
    normed = (hidden_f * lax.rsqrt(mean_sq + 1e-06) * norm_gain).astype(BF16)
    group_rows = lax.all_gather(normed, "uly", axis=0, tiled=True)
    gate_sum = jnp.dot(group_rows, wg_full, preferred_element_type=F32)
    up_sum = jnp.dot(group_rows, wu_full, preferred_element_type=F32)
    activated = (jax.nn.silu(gate_sum) * up_sum).astype(BF16)
    ffn_partial = jnp.dot(activated, wd_full, preferred_element_type=F32)
    ffn_out = lax.psum_scatter(
        ffn_partial.astype(BF16), "uly", scatter_dimension=0, tiled=True
    ).astype(F32)
    return (hidden_f + ffn_out).astype(BF16)


def dot(a, b):
    return jnp.dot(a, b, preferred_element_type=F32)


def attention_kernel(heads, planes, idx, qg, *refs):
    kvs, bias, pick, out = refs[:planes], refs[planes], refs[planes + 1], refs[planes + 2]
    group, rows, _ = qg.shape
    r = idx[1]
    keys = jnp.concatenate([kv[:, :, :HEAD_SIZE].reshape(group * rows, HEAD_SIZE) for kv in kvs])
    values = jnp.concatenate([kv[:, :, HEAD_SIZE:].reshape(group * rows, HEAD_SIZE) for kv in kvs])
    scale = 1.0 / math.sqrt(HEAD_SIZE)
    done = []
    for h in range(heads):
        at = slice(h * HEAD_SIZE, (h + 1) * HEAD_SIZE)
        gate_at = slice((heads + h) * HEAD_SIZE, (heads + h + 1) * HEAD_SIZE)
        q = jnp.concatenate([qg[b ^ r, :, at] for b in range(group)])
        gate = jnp.concatenate([qg[b ^ r, :, gate_at] for b in range(group)]).astype(F32)
        s = lax.dot_general(q, keys, NT, preferred_element_type=F32) * scale + bias[...]
        e = jnp.exp(s - jnp.max(s, axis=-1, keepdims=True))
        denom = jnp.sum(e, axis=-1, keepdims=True)
        attended = dot(e.astype(BF16), values) / denom
        done.append((attended / (1.0 + jnp.exp(-gate))).astype(BF16))
    out[...] = dot(pick[...], jnp.concatenate(done, axis=1)).astype(BF16)


def project_kernel(planes, idx, *refs):
    parts = refs[:planes]
    weight, pick, keep, send, held = refs[planes:]
    z = idx[0]
    for k in range(planes):
        held[z ^ k] = parts[k][...]
    rows, width = parts[0].shape
    x = dot(pick[...], held[...].reshape(planes * rows, width)).astype(BF16)
    w = jnp.concatenate([weight[c] for c in range(weight.shape[0])], axis=1)
    y = dot(x, w).astype(BF16)
    half = y.shape[0] // 2
    keep[...] = y[:half]
    send[...] = y[half:]


def core_sum_kernel(keep, got, *outs):
    rows = outs[0].shape[0]
    for i, out in enumerate(outs):
        at = slice(i * rows, (i + 1) * rows)
        out[...] = (keep[at].astype(F32) + got[at].astype(F32)).astype(out.dtype)


def sum_kernel(*refs):
    *parts, out = refs
    total = parts[0][...].astype(F32)
    for part in parts[1:]:
        total = total + part[...].astype(F32)
    out[...] = total.astype(out.dtype)


def norm_kernel(planes, idx, *refs):
    parts, gain, out = refs[:planes], refs[planes], refs[planes + 1]
    z = idx[0]
    width = parts[0].shape[1]
    held = [p[...].astype(F32) for p in parts]
    square = sum(jnp.sum(h * h, axis=-1, keepdims=True) for h in held)
    factor = lax.rsqrt(square / (width * planes) + 1e-06)
    for k in range(planes):
        out[z ^ k] = (held[k] * factor * gain[z ^ k]).astype(BF16)


def ffn_kernel(blocks, *refs):
    parts, (gate_up, down, keep, send) = refs[:blocks], refs[blocks:]
    planes = parts[0].shape[0]
    sources, both, _ = gate_up.shape
    units = both // 2
    per = sources // planes
    gate = up = 0.0
    for p in range(planes):
        x = jnp.concatenate([part[p] for part in parts])
        w = jnp.concatenate([gate_up[p * per + i] for i in range(per)], axis=1)
        gate = gate + lax.dot_general(x, w[:units], NT, preferred_element_type=F32)
        up = up + lax.dot_general(x, w[units:], NT, preferred_element_type=F32)
    activated = (gate / (1.0 + jnp.exp(-gate)) * up).astype(BF16)
    half = activated.shape[0] // 2
    width = per * down.shape[2]
    for p in range(planes):
        w = jnp.concatenate([down[p * per + i] for i in range(per)], axis=1)
        y = dot(activated, w).astype(BF16)
        keep[:, p * width:(p + 1) * width] = y[:half]
        send[:, p * width:(p + 1) * width] = y[half:]


def row_of(z, k, tokens, rows, total):
    i = lax.broadcasted_iota(jnp.int32, (rows, total), 0)
    j = lax.broadcasted_iota(jnp.int32, (rows, total), 1)
    return jnp.where((j == i + (z ^ k) * tokens) & (i < tokens), 1.0, 0.0).astype(BF16)


def plane_sum_kernel(planes, tokens, idx, *refs):
    parts, outs = refs[:-planes], refs[-planes:]
    total = parts[0][...].astype(F32)
    for part in parts[1:]:
        total = total + part[...].astype(F32)
    total = total.astype(BF16)
    for k, out in enumerate(outs):
        pick = row_of(idx[0], k, tokens, out.shape[0], total.shape[0])
        out[...] = dot(pick, total).astype(BF16)


def last_kernel(planes, tokens, idx, *refs):
    parts, hidden, out = refs[:planes], refs[planes:-1], refs[-1]
    total = parts[0][...].astype(F32)
    for part in parts[1:]:
        total = total + part[...].astype(F32)
    z = idx[0]
    pick = row_of(z, 0, tokens, total.shape[0], hidden[0].shape[0])
    held = jnp.concatenate([dot(pick, h[...]) for h in hidden], axis=1)
    width = hidden[0].shape[1]
    whole = jnp.zeros_like(total)
    for k in range(planes):
        at = pl.ds(pl.multiple_of((z ^ k) * width, width), width)
        out[:, at] = held[:tokens, k * width:(k + 1) * width].astype(BF16)
    out[...] = (out[...].astype(F32) + total[:tokens]).astype(BF16)


def call(kernel, outs, *args, scratch=()):
    single = not isinstance(outs, list)
    shapes = [outs] if single else outs
    got = pl.pallas_call(
        kernel,
        out_shape=shapes,
        in_specs=[SMEM if a.dtype == jnp.int32 else VMEM for a in args],
        out_specs=[VMEM] * len(shapes),
        scratch_shapes=list(scratch),
        compiler_params=pltpu.CompilerParams(vmem_limit_bytes=40 * 2**20),
    )(*args)
    return got[0] if single else got


def like(*shape, dtype=BF16):
    return jax.ShapeDtypeStruct(shape, dtype)


def move_tokens(
    n_blk,
    n_uly,
    residual,
    query_projection,
    key_projection,
    value_projection,
    gate_proj,
    positions,
    prefix_len,
    out_weight,
    norm_gain,
    gate_weight,
    up_weight,
    down_weight,
):
    axes = ("blk", "uly")
    kv_heads = key_projection.shape[1] // HEAD_SIZE
    heads = query_projection.shape[1] // key_projection.shape[1]
    tokens, features = residual.shape
    rows = -(-tokens // ROW_TILE) * ROW_TILE
    group = kv_heads
    per = group // n_uly
    planes = n_blk // per
    devices = n_blk * n_uly
    me = lax.axis_index("blk") * n_uly + lax.axis_index("uly")
    z, r = me // group, me % group
    idx = jnp.stack([z, r]).astype(jnp.int32)
    core = n_uly
    near = [b for b in range(group) if not b & core]
    order = near + [b ^ core for b in near]
    steps = near[1:]

    def swap(x, mask):
        return lax.ppermute(x, axes, [(i, i ^ mask) for i in range(devices)])

    def swap_planes(x):
        return [swap(x, k * group) for k in range(1, planes)]

    def by_head(x):
        x = x.reshape(tokens, n_uly, per, x.shape[1] // group)
        return x.transpose(2, 1, 0, 3).reshape(group, tokens, x.shape[3])

    def packed(*xs):
        x = jnp.concatenate([by_head(x) for x in xs], axis=2)
        return jnp.pad(x, ((0, 0), (0, rows - tokens), (0, 0)))

    plane_groups = [[p * group + i for i in range(group)] for p in range(planes)]

    def plane_exchange(x):
        return lax.all_to_all(x, axes, 0, 0, axis_index_groups=plane_groups, tiled=True)

    kv = plane_exchange(packed(key_projection, value_projection))
    qg = plane_exchange(packed(query_projection, gate_proj))

    wo = lax.all_to_all(
        out_weight.reshape(per, out_weight.shape[0] // per, out_weight.shape[1]),
        "blk", 0, 0,
        axis_index_groups=[[p * per + i for i in range(per)] for p in range(planes)],
        tiled=True,
    )
    units = gate_weight.shape[1] // n_blk

    def by_unit(w):
        return w.reshape(w.shape[0], n_blk, units).transpose(1, 2, 0)

    gate_up = lax.all_to_all(
        jnp.concatenate([by_unit(gate_weight), by_unit(up_weight)], axis=1), "blk", 0, 0, tiled=True
    )
    down = lax.all_to_all(
        down_weight.reshape(n_blk, units, down_weight.shape[1]), "blk", 0, 0, tiled=True
    )
    width = features // planes
    resid = lax.all_to_all(
        residual.reshape(tokens, planes, width).transpose(1, 0, 2),
        "blk", 0, 0,
        axis_index_groups=[[p * per + i for p in range(planes)] for i in range(per)],
        tiled=True,
    ).reshape(planes * tokens, width)

    spots = jnp.pad(
        positions.reshape(planes, group, tokens),
        ((0, 0), (0, 0), (0, rows - tokens)),
        constant_values=NO_POSITION,
    )
    key_spot = spots[z ^ jnp.arange(planes)].reshape(1, -1)
    query_spot = spots[z][r ^ jnp.arange(group)].reshape(-1, 1)
    visible = (key_spot <= query_spot) | (key_spot < prefix_len[0])
    bias = jnp.where(visible, 0.0, HIDE).astype(F32)

    pick = np.zeros((group, tokens, group, rows), np.float32)
    for b in range(group):
        for t in range(tokens):
            pick[b, t, b, t] = 1
    pick = jnp.asarray(pick.reshape(group * tokens, group * rows), BF16)
    gated = call(
        functools.partial(attention_kernel, heads, planes),
        like(group * tokens, heads * HEAD_SIZE),
        idx, qg, kv, *swap_planes(kv), bias, pick,
    )

    turn = np.zeros((group, planes, tokens, planes, group, tokens), np.float32)
    for i, b in enumerate(order):
        for p in range(planes):
            for t in range(tokens):
                turn[i, p, t, p, b, t] = 1
    total = devices * tokens
    turn = jnp.asarray(turn.reshape(total, total), BF16)
    keep, send = call(
        functools.partial(project_kernel, planes),
        [like(total // 2, width)] * 2,
        idx, gated, *swap_planes(gated), wo, turn,
        scratch=[pltpu.VMEM((planes,) + gated.shape, BF16)],
    )
    share = total // group
    own, *rest = call(
        core_sum_kernel,
        [like(share, width, dtype=F32)] + [like(share, width)] * len(steps),
        keep, swap(send, core),
    )
    hidden = call(
        sum_kernel, like(share, width), own, resid, *[swap(x, b) for x, b in zip(rest, steps)]
    )
    hiddens = [hidden] + swap_planes(hidden)
    normed = call(
        functools.partial(norm_kernel, planes),
        like(planes, share, width),
        idx, *hiddens, norm_gain.reshape(planes, 1, width),
    )
    blocks = [normed] + [swap(normed, b) for b in steps]
    blocks = blocks + [swap(x, core) for x in blocks]
    keep, send = call(
        functools.partial(ffn_kernel, group),
        [like(total // 2, features)] * 2,
        *blocks, gate_up, down,
    )
    own, *rest = call(
        core_sum_kernel,
        [like(share, features, dtype=F32)] + [like(share, features)] * len(steps),
        keep, swap(send, core),
    )
    parts = call(
        functools.partial(plane_sum_kernel, planes, tokens),
        [like(rows, features)] * planes,
        idx, own, *[swap(x, b) for x, b in zip(rest, steps)],
    )
    return call(
        functools.partial(last_kernel, planes, tokens),
        like(tokens, features),
        idx, parts[0], *[swap(x, k * group) for k, x in enumerate(parts) if k], *hiddens,
    )


def tokens_can_travel(n_blk, n_uly, kv_heads, token_count, unit_count):
    def power(n):
        return n > 0 and not n & (n - 1)

    per = kv_heads // n_uly
    return (
        power(n_blk)
        and power(n_uly)
        and power(kv_heads)
        and per > 1
        and n_blk % per == 0
        and token_count < unit_count // n_uly
    )


def solution(mesh):
    n_blk, n_uly = mesh.shape["blk"], mesh.shape["uly"]

    def per_device(*args):
        residual, key_projection, gate_weight = args[0], args[2], args[9]
        travel = tokens_can_travel(
            n_blk,
            n_uly,
            key_projection.shape[1] // HEAD_SIZE,
            residual.shape[0] * n_blk * n_uly,
            gate_weight.shape[1] * n_uly,
        )
        if travel:
            return move_tokens(n_blk, n_uly, *args)
        return move_weights(*args)

    return jax.shard_map(
        per_device,
        mesh=mesh,
        in_specs=(
            P(("blk", "uly"), None),
            P(("blk", "uly"), None),
            P(("blk", "uly"), None),
            P(("blk", "uly"), None),
            P(("blk", "uly"), None),
            P(),
            P(),
            P("uly", "blk"),
            P(),
            P("blk", "uly"),
            P("blk", "uly"),
            P("uly", "blk"),
        ),
        out_specs=P(("blk", "uly"), None),
        check_vma=False,
    )
```

time: 433 us -> 189 us (0.44)
  waiting for transfers between devices: 299 us -> 92.2 us
  blocking collectives: 65 us -> 20 us
  starting transfers between devices: 19.3 us -> 48.7 us
  matrix products: 23.1 us -> 0 us
  between operations: 14.7 us -> 0.95 us
  Pallas kernels: 0 us -> 7.64 us
  local copies, waits for them, and re-layouts: 8.58 us -> 15.3 us
    all_gather x4 -> x0, waiting for transfers between devices: 291 us -> none  [the longest x1 104 us: per_device(): lax.all_gather(down_weight, 'blk', axis=1, tiled=True)]
    ppermute x0 -> x27, waiting for transfers between devices: none -> 69.8 us  [swap(): return lax.ppermute(x, axes, [(i, i ^ mask) for i in range(devices)])]
    all_gather x3 -> x0, blocking collectives: 50.3 us -> none  [the longest x1 24.4 us: per_device(): key_part = lax.all_gather(k_loc, 'blk', axis=0, tiled=True)]
    ppermute x0 -> x27, starting transfers between devices: none -> 29.6 us  [swap(): return lax.ppermute(x, axes, [(i, i ^ mask) for i in range(devices)])]
    dot_general x5 -> x0, matrix products: 23.1 us -> none  [the longest x1 11.5 us: per_device(): jnp.dot(activated, wd_full, preferred_element_type=jnp.float32)]
    all_to_all x0 -> x2, blocking collectives: none -> 20 us  [the longest x1 11.2 us: move_tokens(): lax.all_to_all(out_weight.reshape(per, out_weight.shape[0] // per, out_we...]
    all_to_all x4, waiting for transfers between devices: 3.89 us -> 22.4 us  [the longest x1 15.5 us: move_tokens(): lax.all_to_all(down_weight.reshape(n_blk, units, down_weight.shape[1]), '...]
    unnamed x2 -> x0, blocking collectives: 14.7 us -> none
  transfers between devices with their start and end apart: 10 -> 31, of which waited for: 8 -> 24; matrix products, arithmetic and copies ran while one was open for 6% -> 6% of each run, Pallas kernels for 0% -> 2%
where the time goes in v1:
time: 189 us; the launch traced here: 188 us
  waiting for transfers between devices  92.2 us (49%)
  starting transfers between devices  48.7 us (26%)
  blocking collectives  20 us (11%)
  local copies, waits for them, and re-layouts  15.3 us (8%)
  Pallas kernels  7.64 us (4%)
  other arithmetic  3.45 us (2%)
    ppermute x27, waiting for transfers between devices, swap(): return lax.ppermute(x, axes, [(i, i ^ mask) for i in range(devices)])  69.8 us
    ppermute x27, starting transfers between devices, swap(): return lax.ppermute(x, axes, [(i, i ^ mask) for i in range(devices)])  29.6 us
    all_to_all x1, waiting for transfers between devices, move_tokens(): lax.all_to_all(down_weight.reshape(n_blk, units, down_weight.shape[1]), '...  15.5 us
    all_to_all x1, blocking collectives, move_tokens(): lax.all_to_all(out_weight.reshape(per, out_weight.shape[0] // per, out_we...  11.2 us
    all_to_all x1, blocking collectives, plane_exchange(): lax.all_to_all(x, axes, 0, 0, axis_index_groups=plane_groups, tiled=True)  8.8 us
    pallas_call x9, Pallas kernels, call(): pl.pallas_call(kernel, out_shape=shapes, in_specs=[SMEM if a.dtype == jnp...  7.64 us
    unnamed x30, local copies, waits for them, and re-layouts  6.72 us
    all_to_all x1, waiting for transfers between devices, move_tokens(): lax.all_to_all(residual.reshape(tokens, planes, width).transpose(1, 0, 2)...  5.69 us
  transfers between devices with their start and end apart: 31, of which 24 were waited for; matrix products, arithmetic and copies ran while one was open for 6% of the time, Pallas kernels for 2%

profile of v1, /device:TPU:0, one launch (start us, length us, event | category | flops | bytes accessed | tf_op | source)
XLA Modules:
  0.0 188.2 jit_solution(17387348247610022796)
XLA Ops:
  2.3 5.2 %all-to-all-start.1 = ((bf16[8,16,256]{2,1,0:T(8,128)(2,1)}), bf16[8,16,256]{2,1,0:T(8,128)(2,1)S(1)}, u32[]{:S(2)}, u32[]{:S(2)}) async-start(bf16[8,16,256]{2,1,0:T(8,128)(2,1)} %fusion.5), calls=%async_computation.1 | async-start | bytes 131072 | tf_op jit(solution)/shard_map/all_to_all | solution.py:291
  12.2 4.9 %all-to-all-start.3 = ((bf16[4,12,512]{2,1,0:T(8,128)(2,1)}), bf16[4,12,512]{2,1,0:T(8,128)(2,1)S(1)}, u32[]{:S(2)}, u32[]{:S(2)}) async-start(bf16[4,12,512]{2,1,0:T(8,128)(2,1)} %bitcast.32), calls=%async_computation.3 | async-start | bytes 131072 | tf_op jit(solution)/shard_map/all_to_all | solution.py:314
  17.2 5.7 %all-to-all-done.3 = bf16[4,12,512]{2,1,0:T(8,128)(2,1)S(1)} async-done(((bf16[4,12,512]{2,1,0:T(8,128)(2,1)}), bf16[4,12,512]{2,1,0:T(8,128)(2,1)S(1)}, u32[]{:S(2)}, u32[]{:S(2)}) %all-to-all-start.3) | async-done | bytes 49184 | tf_op jit(solution)/shard_map/all_to_all | solution.py:314
  22.8 8.8 %all_to_all.30.qg = bf16[8,16,1024]{2,1,0:T(8,128)(2,1)S(1)} all-to-all(bf16[8,16,1024]{2,1,0:T(8,128)(2,1)S(1)} %fusion.2), channel_id=1, replica_groups={{0,1,2,3,4,5,6,7},{8,9,10,11,12,13,14,15},{16,17,18,19,20,21,22,23},{24..., dimensions={0} | all-to-all | bytes 524288 | tf_op jit(solution)/shard_map/all_to_all | solution.py:291
  31.6 11.2 %all_to_all.31.refs_4_ = bf16[4,512,128]{2,1,0:T(8,128)(2,1)S(1)} all-to-all(bf16[4,512,128]{2,1,0:T(8,128)(2,1)S(1)} %bitcast.37), channel_id=1, replica_groups={{0,2,4,6},{8,10,12,14},{16,18,20,22},{24,26,28,30},{1,3,5,7},{9,11,13,1..., dimensions={0} | all-to-all | bytes 1048576 | tf_op jit(solution)/shard_map/all_to_all | solution.py:296
  42.9 3.6 %all-to-all-start.5 = ((bf16[16,192,128]{2,1,0:T(8,128)(2,1)}), bf16[16,192,128]{2,1,0:T(8,128)(2,1)S(1)}, u32[]{:S(2)}, u32[]{:S(2)}) async-start(bf16[16,192,128]{2,1,0:T(8,128)(2,1)} %bitcast.21), calls=%async_computation.5 | async-start | bytes 1572864 | tf_op jit(solution)/shard_map/all_to_all | solution.py:310
  49.7 15.5 %all-to-all-done.5.refs_9_ = bf16[16,192,128]{2,1,0:T(8,128)(2,1)S(1)} async-done(((bf16[16,192,128]{2,1,0:T(8,128)(2,1)}), bf16[16,192,128]{2,1,0:T(8,128)(2,1)S(1)}, u32[]{:S(2)}, u32[]{:S(2)}) %all-to-all-start.5) | async-done | bytes 786464 | tf_op jit(solution)/shard_map/all_to_all | solution.py:310
  65.2 5.4 %all-to-all-start.4 = ((bf16[16,384,128]{2,1,0:T(8,128)(2,1)}), bf16[16,384,128]{2,1,0:T(8,128)(2,1)S(1)}, u32[]{:S(2)}, u32[]{:S(2)}) async-start(bf16[16,384,128]{2,1,0:T(8,128)(2,1)} %pad_maximum_fusion), calls=%async_computation.4 | async-start | bytes 3145728 | tf_op jit(solution)/shard_map/all_to_all | solution.py:307
  76.2 2.0 %collective-permute-start = (bf16[8,16,256]{2,1,0:T(8,128)(2,1)S(1)}, bf16[8,16,256]{2,1,0:T(8,128)(2,1)S(1)}, u32[]{:S(2)}, u32[]{:S(2)}) collective-permute-start(bf16[8,16,256]{2,1,0:T(8,128)(2,1)S(1)} %all-to-all-done.1.refs_0_), channel_id=1, source_target_pairs={{0,8},{1,9},{2,10},{3,11},{4,12},{5,13},{6,14},{7,15},{8,0},{9,1},... | collective-permute-start | bytes 196616 | tf_op jit(solution)/shard_map/ppermute | solution.py:275
  78.1 2.4 %collective-permute-start.1 = (bf16[8,16,256]{2,1,0:T(8,128)(2,1)S(1)}, bf16[8,16,256]{2,1,0:T(8,128)(2,1)S(1)}, u32[]{:S(2)}, u32[]{:S(2)}) collective-permute-start(bf16[8,16,256]{2,1,0:T(8,128)(2,1)S(1)} %all-to-all-done.1.refs_0_), channel_id=1, source_target_pairs={{0,16},{1,17},{2,18},{3,19},{4,20},{5,21},{6,22},{7,23},{8,24},{9,... | collective-permute-start | bytes 196616 | tf_op jit(solution)/shard_map/ppermute | solution.py:275
  80.7 18.0 %collective-permute-done.refs_1_ = bf16[8,16,256]{2,1,0:T(8,128)(2,1)S(1)} collective-permute-done((bf16[8,16,256]{2,1,0:T(8,128)(2,1)S(1)}, bf16[8,16,256]{2,1,0:T(8,128)(2,1)S(1)}, u32[]{:S(2)}, u32[]{:S(2)}) %collective-permute-start) | collective-permute-done | bytes 65568 | tf_op jit(solution)/shard_map/ppermute | solution.py:275
  98.7 14.5 %collective-permute-done.1.refs_2_ = bf16[8,16,256]{2,1,0:T(8,128)(2,1)S(1)} collective-permute-done((bf16[8,16,256]{2,1,0:T(8,128)(2,1)S(1)}, bf16[8,16,256]{2,1,0:T(8,128)(2,1)S(1)}, u32[]{:S(2)}, u32[]{:S(2)}) %collective-permute-start.1) | collective-permute-done | bytes 65568 | tf_op jit(solution)/shard_map/ppermute | solution.py:275
  113.1 1.9 %shard_map.136.refs_0_ = bf16[96,512]{1,0:T(8,128)(2,1)S(1)} custom-call(s32[2]{0:T(128)S(1)} %pad_add_fusion.idx, bf16[8,16,1024]{2,1,0:T(8,128)(2,1)S(1)} %all_to_all.30.qg, bf16[8,16,256]{2,1,0:T(8,128)(2,1)S(1)} %all-to-all-done.1.refs_0_, bf16[8,16,256]{2,1,0:T(8,128)(2,1)S(1)} %collective-permute-done.refs_1_, ...), custom_call_target="tpu_custom_call" | custom-call | tf_op jit(solution)/shard_map/pallas_call | solution.py:226
  115.0 1.6 collective-permute-start.3
  117.1 2.4 %collective-permute-start.5 = (bf16[96,512]{1,0:T(8,128)(2,1)S(1)}, bf16[96,512]{1,0:T(8,128)(2,1)S(1)}, u32[]{:S(2)}, u32[]{:S(2)}) collective-permute-start(bf16[96,512]{1,0:T(8,128)(2,1)S(1)} %shard_map.136.refs_0_), channel_id=1, source_target_pairs={{0,24},{1,25},{2,26},{3,27},{4,28},{5,29},{6,30},{7,31},{8,16},{9,... | collective-permute-start | bytes 294920 | tf_op jit(solution)/shard_map/ppermute | solution.py:275
  119.8 6.6 %collective-permute-done.4.refs_2_ = bf16[96,512]{1,0:T(8,128)(2,1)S(1)} collective-permute-done((bf16[96,512]{1,0:T(8,128)(2,1)S(1)}, bf16[96,512]{1,0:T(8,128)(2,1)S(1)}, u32[]{:S(2)}, u32[]{:S(2)}) %collective-permute-start.4) | collective-permute-done | bytes 98336 | tf_op jit(solution)/shard_map/ppermute | solution.py:275
  133.3 1.8 collective-permute-done.8.refs_3_
  135.1 2.0 %collective-permute-done.9.refs_4_ = bf16[48,512]{1,0:T(8,128)(2,1)S(1)} collective-permute-done((bf16[48,512]{1,0:T(8,128)(2,1)S(1)}, bf16[48,512]{1,0:T(8,128)(2,1)S(1)}, u32[]{:S(2)}, u32[]{:S(2)}) %collective-permute-start.9) | collective-permute-done | bytes 49184 | tf_op jit(solution)/shard_map/ppermute | solution.py:275
  137.2 1.9 %collective-permute-start.10 = (bf16[48,512]{1,0:T(8,128)(2,1)S(1)}, bf16[48,512]{1,0:T(8,128)(2,1)S(1)}, u32[]{:S(2)}, u32[]{:S(2)}) collective-permute-start(bf16[48,512]{1,0:T(8,128)(2,1)S(1)} %shard_map.139.refs_0_.refs_4_), channel_id=1, source_target_pairs={{0,8},{1,9},{2,10},{3,11},{4,12},{5,13},{6,14},{7,15},{8,0},{9,1},... | collective-permute-start | bytes 147464 | tf_op jit(solution)/shard_map/ppermute | solution.py:275
  139.6 2.0 %collective-permute-start.12 = (bf16[48,512]{1,0:T(8,128)(2,1)S(1)}, bf16[48,512]{1,0:T(8,128)(2,1)S(1)}, u32[]{:S(2)}, u32[]{:S(2)}) collective-permute-start(bf16[48,512]{1,0:T(8,128)(2,1)S(1)} %shard_map.139.refs_0_.refs_4_), channel_id=1, source_target_pairs={{0,24},{1,25},{2,26},{3,27},{4,28},{5,29},{6,30},{7,31},{8,16},{9,... | collective-permute-start | bytes 147464 | tf_op jit(solution)/shard_map/ppermute | solution.py:275
  141.9 2.4 %collective-permute-done.11.refs_2_.refs_6_ = bf16[48,512]{1,0:T(8,128)(2,1)S(1)} collective-permute-done((bf16[48,512]{1,0:T(8,128)(2,1)S(1)}, bf16[48,512]{1,0:T(8,128)(2,1)S(1)}, u32[]{:S(2)}, u32[]{:S(2)}) %collective-permute-start.11) | collective-permute-done | bytes 49184 | tf_op jit(solution)/shard_map/ppermute | solution.py:275
  147.5 2.3 %collective-permute-start.15 = (bf16[4,48,512]{2,1,0:T(8,128)(2,1)S(1)}, bf16[4,48,512]{2,1,0:T(8,128)(2,1)S(1)}, u32[]{:S(2)}, u32[]{:S(2)}) collective-permute-start(bf16[4,48,512]{2,1,0:T(8,128)(2,1)S(1)} %shard_map.140.refs_0_), channel_id=1, source_target_pairs={{0,5},{1,4},{2,7},{3,6},{4,1},{5,0},{6,3},{7,2},{8,13},{9,12},{10,... | collective-permute-start | bytes 589832 | tf_op jit(solution)/shard_map/ppermute | solution.py:275
  149.8 3.5 %collective-permute-done.13.refs_1_ = bf16[4,48,512]{2,1,0:T(8,128)(2,1)S(1)} collective-permute-done((bf16[4,48,512]{2,1,0:T(8,128)(2,1)S(1)}, bf16[4,48,512]{2,1,0:T(8,128)(2,1)S(1)}, u32[]{:S(2)}, u32[]{:S(2)}) %collective-permute-start.13) | collective-permute-done | bytes 196640 | tf_op jit(solution)/shard_map/ppermute | solution.py:275
  153.8 1.7 collective-permute-done.15.refs_3_
  162.4 1.9 %collective-permute-done.20.got = bf16[192,2048]{1,0:T(8,128)(2,1)S(1)} collective-permute-done((bf16[192,2048]{1,0:T(8,128)(2,1)S(1)}, bf16[192,2048]{1,0:T(8,128)(2,1)S(1)}, u32[]{:S(2)}, u32[]{:S(2)}) %collective-permute-start.20) | collective-permute-done | bytes 786464 | tf_op jit(solution)/shard_map/ppermute | solution.py:275
  166.2 1.9 %collective-permute-start.23 = (bf16[48,2048]{1,0:T(8,128)(2,1)S(1)}, bf16[48,2048]{1,0:T(8,128)(2,1)S(1)}, u32[]{:S(2)}, u32[]{:S(2)}) collective-permute-start(bf16[48,2048]{1,0:T(8,128)(2,1)S(1)} %get-tuple-element.32), channel_id=1, source_target_pairs={{0,5},{1,4},{2,7},{3,6},{4,1},{5,0},{6,3},{7,2},{8,13},{9,12},{10,... | collective-permute-start | bytes 589832 | tf_op jit(solution)/shard_map/ppermute | solution.py:275
  168.0 3.7 %collective-permute-done.21.refs_1_ = bf16[48,2048]{1,0:T(8,128)(2,1)S(1)} collective-permute-done((bf16[48,2048]{1,0:T(8,128)(2,1)S(1)}, bf16[48,2048]{1,0:T(8,128)(2,1)S(1)}, u32[]{:S(2)}, u32[]{:S(2)}) %collective-permute-start.21) | collective-permute-done | bytes 196640 | tf_op jit(solution)/shard_map/ppermute | solution.py:275
  171.7 1.8 collective-permute-done.22.refs_2_
  173.5 3.6 %collective-permute-done.23.refs_3_ = bf16[48,2048]{1,0:T(8,128)(2,1)S(1)} collective-permute-done((bf16[48,2048]{1,0:T(8,128)(2,1)S(1)}, bf16[48,2048]{1,0:T(8,128)(2,1)S(1)}, u32[]{:S(2)}, u32[]{:S(2)}) %collective-permute-start.23) | collective-permute-done | bytes 196640 | tf_op jit(solution)/shard_map/ppermute | solution.py:275
  178.8 1.9 collective-permute-start.25
  180.7 1.7 collective-permute-start.26
  182.7 2.8 %collective-permute-done.25.refs_2_ = bf16[16,2048]{1,0:T(8,128)(2,1)S(1)} collective-permute-done((bf16[16,2048]{1,0:T(8,128)(2,1)S(1)}, bf16[16,2048]{1,0:T(8,128)(2,1)S(1)}, u32[]{:S(2)}, u32[]{:S(2)}) %collective-permute-start.25) | collective-permute-done | bytes 65568 | tf_op jit(solution)/shard_map/ppermute | solution.py:275
  (99 shorter events, 40.9 us)
Async XLA Ops:
  2.3 9.9 %all-to-all-start.1 = ((bf16[8,16,256]{2,1,0:T(8,128)(2,1)}), bf16[8,16,256]{2,1,0:T(8,128)(2,1)S(1)}, u32[]{:S(2)}, u32[]{:S(2)}) async-start(bf16[8,16,256]{2,1,0:T(8,128)(2,1)} %fusion.5), calls=%async_computation.1 | async-start | bytes 131072 | tf_op jit(solution)/shard_map/all_to_all | solution.py:291
  12.2 10.6 %all-to-all-start.3 = ((bf16[4,12,512]{2,1,0:T(8,128)(2,1)}), bf16[4,12,512]{2,1,0:T(8,128)(2,1)S(1)}, u32[]{:S(2)}, u32[]{:S(2)}) async-start(bf16[4,12,512]{2,1,0:T(8,128)(2,1)} %bitcast.32), calls=%async_computation.3 | async-start | bytes 131072 | tf_op jit(solution)/shard_map/all_to_all | solution.py:314
  42.9 22.3 %all-to-all-start.5 = ((bf16[16,192,128]{2,1,0:T(8,128)(2,1)}), bf16[16,192,128]{2,1,0:T(8,128)(2,1)S(1)}, u32[]{:S(2)}, u32[]{:S(2)}) async-start(bf16[16,192,128]{2,1,0:T(8,128)(2,1)} %bitcast.21), calls=%async_computation.5 | async-start | bytes 1572864 | tf_op jit(solution)/shard_map/all_to_all | solution.py:310
  49.7 76.7 %copy-start = (bf16[384,384]{1,0:T(8,128)(2,1)S(1)}, bf16[384,384]{1,0:T(8,128)(2,1)}, u32[]{:S(2)}) copy-start(bf16[384,384]{1,0:T(8,128)(2,1)} %constant.56.clone.refs_5_) | copy-start | bytes 884740
  65.2 92.5 %all-to-all-start.4 = ((bf16[16,384,128]{2,1,0:T(8,128)(2,1)}), bf16[16,384,128]{2,1,0:T(8,128)(2,1)S(1)}, u32[]{:S(2)}, u32[]{:S(2)}) async-start(bf16[16,384,128]{2,1,0:T(8,128)(2,1)} %pad_maximum_fusion), calls=%async_computation.4 | async-start | bytes 3145728 | tf_op jit(solution)/shard_map/all_to_all | solution.py:307
  76.2 22.5 %collective-permute-start = (bf16[8,16,256]{2,1,0:T(8,128)(2,1)S(1)}, bf16[8,16,256]{2,1,0:T(8,128)(2,1)S(1)}, u32[]{:S(2)}, u32[]{:S(2)}) collective-permute-start(bf16[8,16,256]{2,1,0:T(8,128)(2,1)S(1)} %all-to-all-done.1.refs_0_), channel_id=1, source_target_pairs={{0,8},{1,9},{2,10},{3,11},{4,12},{5,13},{6,14},{7,15},{8,0},{9,1},... | collective-permute-start | bytes 196616 | tf_op jit(solution)/shard_map/ppermute | solution.py:275
  78.1 35.0 %collective-permute-start.1 = (bf16[8,16,256]{2,1,0:T(8,128)(2,1)S(1)}, bf16[8,16,256]{2,1,0:T(8,128)(2,1)S(1)}, u32[]{:S(2)}, u32[]{:S(2)}) collective-permute-start(bf16[8,16,256]{2,1,0:T(8,128)(2,1)S(1)} %all-to-all-done.1.refs_0_), channel_id=1, source_target_pairs={{0,16},{1,17},{2,18},{3,19},{4,20},{5,21},{6,22},{7,23},{8,24},{9,... | collective-permute-start | bytes 196616 | tf_op jit(solution)/shard_map/ppermute | solution.py:275
  80.5 32.6 %collective-permute-start.2 = (bf16[8,16,256]{2,1,0:T(8,128)(2,1)S(1)}, bf16[8,16,256]{2,1,0:T(8,128)(2,1)S(1)}, u32[]{:S(2)}, u32[]{:S(2)}) collective-permute-start(bf16[8,16,256]{2,1,0:T(8,128)(2,1)S(1)} %all-to-all-done.1.refs_0_), channel_id=1, source_target_pairs={{0,24},{1,25},{2,26},{3,27},{4,28},{5,29},{6,30},{7,31},{8,16},{9,... | collective-permute-start | bytes 196616 | tf_op jit(solution)/shard_map/ppermute | solution.py:275
  115.0 4.8 %collective-permute-start.3 = (bf16[96,512]{1,0:T(8,128)(2,1)S(1)}, bf16[96,512]{1,0:T(8,128)(2,1)S(1)}, u32[]{:S(2)}, u32[]{:S(2)}) collective-permute-start(bf16[96,512]{1,0:T(8,128)(2,1)S(1)} %shard_map.136.refs_0_), channel_id=1, source_target_pairs={{0,8},{1,9},{2,10},{3,11},{4,12},{5,13},{6,14},{7,15},{8,0},{9,1},... | collective-permute-start | bytes 294920 | tf_op jit(solution)/shard_map/ppermute | solution.py:275
  116.6 9.8 %collective-permute-start.4 = (bf16[96,512]{1,0:T(8,128)(2,1)S(1)}, bf16[96,512]{1,0:T(8,128)(2,1)S(1)}, u32[]{:S(2)}, u32[]{:S(2)}) collective-permute-start(bf16[96,512]{1,0:T(8,128)(2,1)S(1)} %shard_map.136.refs_0_), channel_id=1, source_target_pairs={{0,16},{1,17},{2,18},{3,19},{4,20},{5,21},{6,22},{7,23},{8,24},{9,... | collective-permute-start | bytes 294920 | tf_op jit(solution)/shard_map/ppermute | solution.py:275
  117.1 9.3 %collective-permute-start.5 = (bf16[96,512]{1,0:T(8,128)(2,1)S(1)}, bf16[96,512]{1,0:T(8,128)(2,1)S(1)}, u32[]{:S(2)}, u32[]{:S(2)}) collective-permute-start(bf16[96,512]{1,0:T(8,128)(2,1)S(1)} %shard_map.136.refs_0_), channel_id=1, source_target_pairs={{0,24},{1,25},{2,26},{3,27},{4,28},{5,29},{6,30},{7,31},{8,16},{9,... | collective-permute-start | bytes 294920 | tf_op jit(solution)/shard_map/ppermute | solution.py:275
  127.6 1.5 collective-permute-start.6
  129.2 4.2 %collective-permute-start.7 = (bf16[48,512]{1,0:T(8,128)(2,1)S(1)}, bf16[48,512]{1,0:T(8,128)(2,1)S(1)}, u32[]{:S(2)}, u32[]{:S(2)}) collective-permute-start(bf16[48,512]{1,0:T(8,128)(2,1)S(1)} %get-tuple-element.24), channel_id=1, source_target_pairs={{0,1},{1,0},{2,3},{3,2},{4,5},{5,4},{6,7},{7,6},{8,9},{9,8},{10,11... | collective-permute-start | bytes 147464 | tf_op jit(solution)/shard_map/ppermute | solution.py:275
  130.7 4.5 %collective-permute-start.8 = (bf16[48,512]{1,0:T(8,128)(2,1)S(1)}, bf16[48,512]{1,0:T(8,128)(2,1)S(1)}, u32[]{:S(2)}, u32[]{:S(2)}) collective-permute-start(bf16[48,512]{1,0:T(8,128)(2,1)S(1)} %get-tuple-element.25), channel_id=1, source_target_pairs={{0,4},{1,5},{2,6},{3,7},{4,0},{5,1},{6,2},{7,3},{8,12},{9,13},{10,... | collective-permute-start | bytes 147464 | tf_op jit(solution)/shard_map/ppermute | solution.py:275
  132.2 5.0 %collective-permute-start.9 = (bf16[48,512]{1,0:T(8,128)(2,1)S(1)}, bf16[48,512]{1,0:T(8,128)(2,1)S(1)}, u32[]{:S(2)}, u32[]{:S(2)}) collective-permute-start(bf16[48,512]{1,0:T(8,128)(2,1)S(1)} %get-tuple-element.26), channel_id=1, source_target_pairs={{0,5},{1,4},{2,7},{3,6},{4,1},{5,0},{6,3},{7,2},{8,13},{9,12},{10,... | collective-permute-start | bytes 147464 | tf_op jit(solution)/shard_map/ppermute | solution.py:275
  137.2 4.7 %collective-permute-start.10 = (bf16[48,512]{1,0:T(8,128)(2,1)S(1)}, bf16[48,512]{1,0:T(8,128)(2,1)S(1)}, u32[]{:S(2)}, u32[]{:S(2)}) collective-permute-start(bf16[48,512]{1,0:T(8,128)(2,1)S(1)} %shard_map.139.refs_0_.refs_4_), channel_id=1, source_target_pairs={{0,8},{1,9},{2,10},{3,11},{4,12},{5,13},{6,14},{7,15},{8,0},{9,1},... | collective-permute-start | bytes 147464 | tf_op jit(solution)/shard_map/ppermute | solution.py:275
  139.1 5.1 %collective-permute-start.11 = (bf16[48,512]{1,0:T(8,128)(2,1)S(1)}, bf16[48,512]{1,0:T(8,128)(2,1)S(1)}, u32[]{:S(2)}, u32[]{:S(2)}) collective-permute-start(bf16[48,512]{1,0:T(8,128)(2,1)S(1)} %shard_map.139.refs_0_.refs_4_), channel_id=1, source_target_pairs={{0,16},{1,17},{2,18},{3,19},{4,20},{5,21},{6,22},{7,23},{8,24},{9,... | collective-permute-start | bytes 147464 | tf_op jit(solution)/shard_map/ppermute | solution.py:275
  139.6 5.9 %collective-permute-start.12 = (bf16[48,512]{1,0:T(8,128)(2,1)S(1)}, bf16[48,512]{1,0:T(8,128)(2,1)S(1)}, u32[]{:S(2)}, u32[]{:S(2)}) collective-permute-start(bf16[48,512]{1,0:T(8,128)(2,1)S(1)} %shard_map.139.refs_0_.refs_4_), channel_id=1, source_target_pairs={{0,24},{1,25},{2,26},{3,27},{4,28},{5,29},{6,30},{7,31},{8,16},{9,... | collective-permute-start | bytes 147464 | tf_op jit(solution)/shard_map/ppermute | solution.py:275
  146.2 7.1 %collective-permute-start.13 = (bf16[4,48,512]{2,1,0:T(8,128)(2,1)S(1)}, bf16[4,48,512]{2,1,0:T(8,128)(2,1)S(1)}, u32[]{:S(2)}, u32[]{:S(2)}) collective-permute-start(bf16[4,48,512]{2,1,0:T(8,128)(2,1)S(1)} %shard_map.140.refs_0_), channel_id=1, source_target_pairs={{0,1},{1,0},{2,3},{3,2},{4,5},{5,4},{6,7},{7,6},{8,9},{9,8},{10,11... | collective-permute-start | bytes 589832 | tf_op jit(solution)/shard_map/ppermute | solution.py:275
  146.8 6.5 %collective-permute-start.14 = (bf16[4,48,512]{2,1,0:T(8,128)(2,1)S(1)}, bf16[4,48,512]{2,1,0:T(8,128)(2,1)S(1)}, u32[]{:S(2)}, u32[]{:S(2)}) collective-permute-start(bf16[4,48,512]{2,1,0:T(8,128)(2,1)S(1)} %shard_map.140.refs_0_), channel_id=1, source_target_pairs={{0,4},{1,5},{2,6},{3,7},{4,0},{5,1},{6,2},{7,3},{8,12},{9,13},{10,... | collective-permute-start | bytes 589832 | tf_op jit(solution)/shard_map/ppermute | solution.py:275
  147.5 8.1 %collective-permute-start.15 = (bf16[4,48,512]{2,1,0:T(8,128)(2,1)S(1)}, bf16[4,48,512]{2,1,0:T(8,128)(2,1)S(1)}, u32[]{:S(2)}, u32[]{:S(2)}) collective-permute-start(bf16[4,48,512]{2,1,0:T(8,128)(2,1)S(1)} %shard_map.140.refs_0_), channel_id=1, source_target_pairs={{0,5},{1,4},{2,7},{3,6},{4,1},{5,0},{6,3},{7,2},{8,13},{9,12},{10,... | collective-permute-start | bytes 589832 | tf_op jit(solution)/shard_map/ppermute | solution.py:275
  149.8 5.8 %collective-permute-start.16 = (bf16[4,48,512]{2,1,0:T(8,128)(2,1)S(1)}, bf16[4,48,512]{2,1,0:T(8,128)(2,1)S(1)}, u32[]{:S(2)}, u32[]{:S(2)}) collective-permute-start(bf16[4,48,512]{2,1,0:T(8,128)(2,1)S(1)} %shard_map.140.refs_0_), channel_id=1, source_target_pairs={{0,2},{1,3},{2,0},{3,1},{4,6},{5,7},{6,4},{7,5},{8,10},{9,11},{10,... | collective-permute-start | bytes 589832 | tf_op jit(solution)/shard_map/ppermute | solution.py:275
  153.3 2.2 %collective-permute-start.17 = (bf16[4,48,512]{2,1,0:T(8,128)(2,1)S(1)}, bf16[4,48,512]{2,1,0:T(8,128)(2,1)S(1)}, u32[]{:S(2)}, u32[]{:S(2)}) collective-permute-start(bf16[4,48,512]{2,1,0:T(8,128)(2,1)S(1)} %collective-permute-done.13.refs_1_), channel_id=1, source_target_pairs={{0,2},{1,3},{2,0},{3,1},{4,6},{5,7},{6,4},{7,5},{8,10},{9,11},{10,... | collective-permute-start | bytes 589832 | tf_op jit(solution)/shard_map/ppermute | solution.py:275
  153.3 2.9 %collective-permute-start.18 = (bf16[4,48,512]{2,1,0:T(8,128)(2,1)S(1)}, bf16[4,48,512]{2,1,0:T(8,128)(2,1)S(1)}, u32[]{:S(2)}, u32[]{:S(2)}) collective-permute-start(bf16[4,48,512]{2,1,0:T(8,128)(2,1)S(1)} %collective-permute-done.14.refs_2_), channel_id=1, source_target_pairs={{0,2},{1,3},{2,0},{3,1},{4,6},{5,7},{6,4},{7,5},{8,10},{9,11},{10,... | collective-permute-start | bytes 589832 | tf_op jit(solution)/shard_map/ppermute | solution.py:275
  155.5 1.4 collective-permute-start.19
  161.9 2.4 %collective-permute-start.20 = (bf16[192,2048]{1,0:T(8,128)(2,1)S(1)}, bf16[192,2048]{1,0:T(8,128)(2,1)S(1)}, u32[]{:S(2)}, u32[]{:S(2)}) collective-permute-start(bf16[192,2048]{1,0:T(8,128)(2,1)S(1)} %get-tuple-element.28), channel_id=1, source_target_pairs={{0,2},{1,3},{2,0},{3,1},{4,6},{5,7},{6,4},{7,5},{8,10},{9,11},{10,... | collective-permute-start | bytes 2359304 | tf_op jit(solution)/shard_map/ppermute | solution.py:275
  164.5 7.2 %collective-permute-start.21 = (bf16[48,2048]{1,0:T(8,128)(2,1)S(1)}, bf16[48,2048]{1,0:T(8,128)(2,1)S(1)}, u32[]{:S(2)}, u32[]{:S(2)}) collective-permute-start(bf16[48,2048]{1,0:T(8,128)(2,1)S(1)} %get-tuple-element.30), channel_id=1, source_target_pairs={{0,1},{1,0},{2,3},{3,2},{4,5},{5,4},{6,7},{7,6},{8,9},{9,8},{10,11... | collective-permute-start | bytes 589832 | tf_op jit(solution)/shard_map/ppermute | solution.py:275
  165.7 7.8 %collective-permute-start.22 = (bf16[48,2048]{1,0:T(8,128)(2,1)S(1)}, bf16[48,2048]{1,0:T(8,128)(2,1)S(1)}, u32[]{:S(2)}, u32[]{:S(2)}) collective-permute-start(bf16[48,2048]{1,0:T(8,128)(2,1)S(1)} %get-tuple-element.31), channel_id=1, source_target_pairs={{0,4},{1,5},{2,6},{3,7},{4,0},{5,1},{6,2},{7,3},{8,12},{9,13},{10,... | collective-permute-start | bytes 589832 | tf_op jit(solution)/shard_map/ppermute | solution.py:275
  166.2 11.0 %collective-permute-start.23 = (bf16[48,2048]{1,0:T(8,128)(2,1)S(1)}, bf16[48,2048]{1,0:T(8,128)(2,1)S(1)}, u32[]{:S(2)}, u32[]{:S(2)}) collective-permute-start(bf16[48,2048]{1,0:T(8,128)(2,1)S(1)} %get-tuple-element.32), channel_id=1, source_target_pairs={{0,5},{1,4},{2,7},{3,6},{4,1},{5,0},{6,3},{7,2},{8,13},{9,12},{10,... | collective-permute-start | bytes 589832 | tf_op jit(solution)/shard_map/ppermute | solution.py:275
  177.9 4.7 %collective-permute-start.24 = (bf16[16,2048]{1,0:T(8,128)(2,1)S(1)}, bf16[16,2048]{1,0:T(8,128)(2,1)S(1)}, u32[]{:S(2)}, u32[]{:S(2)}) collective-permute-start(bf16[16,2048]{1,0:T(8,128)(2,1)S(1)} %get-tuple-element.34), channel_id=1, source_target_pairs={{0,8},{1,9},{2,10},{3,11},{4,12},{5,13},{6,14},{7,15},{8,0},{9,1},... | collective-permute-start | bytes 196616 | tf_op jit(solution)/shard_map/ppermute | solution.py:275
  178.8 6.7 %collective-permute-start.25 = (bf16[16,2048]{1,0:T(8,128)(2,1)S(1)}, bf16[16,2048]{1,0:T(8,128)(2,1)S(1)}, u32[]{:S(2)}, u32[]{:S(2)}) collective-permute-start(bf16[16,2048]{1,0:T(8,128)(2,1)S(1)} %get-tuple-element.35), channel_id=1, source_target_pairs={{0,16},{1,17},{2,18},{3,19},{4,20},{5,21},{6,22},{7,23},{8,24},{9,... | collective-permute-start | bytes 196616 | tf_op jit(solution)/shard_map/ppermute | solution.py:275
  180.7 6.2 %collective-permute-start.26 = (bf16[16,2048]{1,0:T(8,128)(2,1)S(1)}, bf16[16,2048]{1,0:T(8,128)(2,1)S(1)}, u32[]{:S(2)}, u32[]{:S(2)}) collective-permute-start(bf16[16,2048]{1,0:T(8,128)(2,1)S(1)} %get-tuple-element.36), channel_id=1, source_target_pairs={{0,24},{1,25},{2,26},{3,27},{4,28},{5,29},{6,30},{7,31},{8,16},{9,... | collective-permute-start | bytes 196616 | tf_op jit(solution)/shard_map/ppermute | solution.py:275
  (13 other events, 258.1 us)

commit v2 on v1

--- a/solution.py
+++ b/solution.py
@@ -12,7 +12,7 @@
 HEAD_SIZE = 128
 ROW_TILE = 16
 HIDE = -1e30
-NO_POSITION = np.iinfo(np.int32).max
+NO_POSITION = float(2**30)
 F32 = jnp.float32
 BF16 = jnp.bfloat16
 VMEM = pl.BlockSpec(memory_space=pltpu.VMEM)
@@ -103,12 +103,52 @@
     return jnp.dot(a, b, preferred_element_type=F32)
 
 
-def attention_kernel(heads, planes, idx, qg, *refs):
-    kvs, bias, pick, out = refs[:planes], refs[planes], refs[planes + 1], refs[planes + 2]
+def pack_heads_kernel(head_of, *refs):
+    *parts, out = refs
+    tokens = parts[0].shape[0]
+    out[...] = jnp.zeros_like(out)
+    for r, j in enumerate(head_of):
+        start = 0
+        for part in parts:
+            width = part.shape[1] // len(head_of)
+            out[r, :tokens, start:start + width] = part[:, j * width:(j + 1) * width]
+            start += width
+
+
+def message_kernel(planes, idx, heads, residual, *outs):
+    group, rows, whole = heads.shape
+    tokens, features = residual.shape
+    pair = 2 * HEAD_SIZE
+    lot = group * rows
+    width = features // planes
+    z = idx[0]
+    keys = heads[:, :, whole - pair:].reshape(lot, pair)
+    for k, out in enumerate(outs):
+        out[:lot] = keys
+        out[lot:] = jnp.zeros((out.shape[0] - lot, pair), BF16)
+        for c in range(width // pair):
+            at = pl.ds(pl.multiple_of((z ^ k) * width + c * pair, pair), pair)
+            out[lot + c * rows:lot + c * rows + tokens] = residual[:, at]
+
+
+def attention_kernel(heads, planes, idx, prefix, qg, *refs):
+    messages, (spots, pick, out) = refs[:planes], refs[planes:]
     group, rows, _ = qg.shape
-    r = idx[1]
-    keys = jnp.concatenate([kv[:, :, :HEAD_SIZE].reshape(group * rows, HEAD_SIZE) for kv in kvs])
-    values = jnp.concatenate([kv[:, :, HEAD_SIZE:].reshape(group * rows, HEAD_SIZE) for kv in kvs])
+    z, r = idx[0], idx[1]
+    lot = group * rows
+    keys, values, key_spot = [], [], []
+    for k in range(planes):
+        keys.append(messages[k][:lot, :HEAD_SIZE])
+        values.append(messages[k][:lot, HEAD_SIZE:])
+        key_spot.append(spots[z ^ k])
+    keys, values = jnp.concatenate(keys), jnp.concatenate(values)
+    key_spot = jnp.concatenate(key_spot, axis=1)
+    i = lax.broadcasted_iota(jnp.int32, (lot, lot), 0)
+    j = lax.broadcasted_iota(jnp.int32, (lot, lot), 1)
+    own = jnp.where((i ^ (r * rows)) == j, spots[z], 0.0)
+    query_spot = jnp.sum(own, axis=1, keepdims=True)
+    visible = (key_spot <= query_spot) | (key_spot < prefix[0].astype(F32))
+    bias = jnp.where(visible, 0.0, HIDE)
     scale = 1.0 / math.sqrt(HEAD_SIZE)
     done = []
     for h in range(heads):
@@ -116,7 +156,7 @@
         gate_at = slice((heads + h) * HEAD_SIZE, (heads + h + 1) * HEAD_SIZE)
         q = jnp.concatenate([qg[b ^ r, :, at] for b in range(group)])
         gate = jnp.concatenate([qg[b ^ r, :, gate_at] for b in range(group)]).astype(F32)
-        s = lax.dot_general(q, keys, NT, preferred_element_type=F32) * scale + bias[...]
+        s = lax.dot_general(q, keys, NT, preferred_element_type=F32) * scale + bias
         e = jnp.exp(s - jnp.max(s, axis=-1, keepdims=True))
         denom = jnp.sum(e, axis=-1, keepdims=True)
         attended = dot(e.astype(BF16), values) / denom
@@ -126,14 +166,16 @@
 
 def project_kernel(planes, idx, *refs):
     parts = refs[:planes]
-    weight, pick, keep, send, held = refs[planes:]
-    z = idx[0]
+    weights, (pick, keep, send, held, wide) = refs[planes:-5], refs[-5:]
+    z, q = idx[0], idx[2]
     for k in range(planes):
         held[z ^ k] = parts[k][...]
     rows, width = parts[0].shape
     x = dot(pick[...], held[...].reshape(planes * rows, width)).astype(BF16)
-    w = jnp.concatenate([weight[c] for c in range(weight.shape[0])], axis=1)
-    y = dot(x, w).astype(BF16)
+    lanes = weights[0].shape[1]
+    for c, weight in enumerate(weights):
+        wide[:, pl.ds(pl.multiple_of((q ^ c) * lanes, lanes), lanes)] = weight[...]
+    y = dot(x, wide[...]).astype(BF16)
     half = y.shape[0] // 2
     keep[...] = y[:half]
     send[...] = y[half:]
@@ -146,45 +188,186 @@
         out[...] = (keep[at].astype(F32) + got[at].astype(F32)).astype(out.dtype)
 
 
-def sum_kernel(*refs):
-    *parts, out = refs
-    total = parts[0][...].astype(F32)
+def hidden_kernel(planes, tokens, idx, *refs):
+    parts, messages, out = refs[:-planes - 1], refs[-planes - 1:-1], refs[-1]
+    total = parts[0][...]
     for part in parts[1:]:
         total = total + part[...].astype(F32)
-    out[...] = total.astype(out.dtype)
-
-
-def norm_kernel(planes, idx, *refs):
-    parts, gain, out = refs[:planes], refs[planes], refs[planes + 1]
-    z = idx[0]
-    width = parts[0].shape[1]
-    held = [p[...].astype(F32) for p in parts]
-    square = sum(jnp.sum(h * h, axis=-1, keepdims=True) for h in held)
-    factor = lax.rsqrt(square / (width * planes) + 1e-06)
+    width = out.shape[1]
+    pair = messages[0].shape[1]
+    pieces = width // pair
+    rows = -(-tokens // ROW_TILE) * ROW_TILE
+    for k, message in enumerate(messages):
+        i = lax.broadcasted_iota(jnp.int32, (out.shape[0], rows), 0)
+        j = lax.broadcasted_iota(jnp.int32, (out.shape[0], rows), 1)
+        place = jnp.where((i == j + (idx[0] ^ k) * tokens) & (j < tokens), 1.0, 0.0).astype(BF16)
+        lot = message.shape[0] - pieces * rows
+        held = [message[lot + c * rows:lot + (c + 1) * rows] for c in range(pieces)]
+        total = total + dot(place, jnp.concatenate(held, axis=1))
+    out[...] = total.astype(BF16)
+
+
+def stack_kernel(*refs):
+    *parts, out = refs
+    for k, part in enumerate(parts):
+        out[k] = part[...]
+
+
+def split_gate_up_kernel(planes, sides, idx, gate, up, *outs):
+    half = planes // 2
+    units = outs[0].shape[1] // 4
+    side, near, far = idx[3], idx[0] % half, idx[0] // half
+    for k in range(half):
+        for c in range(sides):
+            chip = (near ^ k) * sides + (side ^ c)
+            for i in range(2):
+                start = pl.multiple_of((chip * 2 + (far ^ i)) * units, units)
+                out = outs[k * sides + c]
+                out[:, 2 * i * units:(2 * i + 1) * units] = gate[:, pl.ds(start, units)]
+                out[:, (2 * i + 1) * units:(2 * i + 2) * units] = up[:, pl.ds(start, units)]
+
+
+def split_down_kernel(planes, idx, weight, *outs):
+    half = planes // 2
+    sides = len(outs)
+    units = outs[0].shape[1]
     for k in range(planes):
-        out[z ^ k] = (held[k] * factor * gain[z ^ k]).astype(BF16)
-
-
-def ffn_kernel(blocks, *refs):
-    parts, (gate_up, down, keep, send) = refs[:blocks], refs[blocks:]
-    planes = parts[0].shape[0]
-    sources, both, _ = gate_up.shape
-    units = both // 2
-    per = sources // planes
+        z = idx[0] ^ k
+        for c, out in enumerate(outs):
+            chip = (z % half) * sides + (idx[3] ^ c)
+            start = pl.multiple_of((chip * 2 + z // half) * units, units)
+            out[k] = weight[pl.ds(start, units), :]
+
+
+def regroup_kernel(*refs):
+    many = refs[-1].shape[0]
+    parts, outs = refs[:many], refs[many:]
+    for k, out in enumerate(outs):
+        for c, part in enumerate(parts):
+            out[c] = part[k]
+
+
+def gate_up_kernel(blocks, per, idx, *refs):
+    parts, pieces = refs[:blocks], refs[blocks:-4]
+    gain, keep, send, held = refs[-4:]
+    half, share, width = parts[0].shape
+    lanes = width // per
+    z, q = idx[0], idx[2]
+    total = square = 0.0
+    for k in range(half):
+        x = jnp.concatenate([part[k] for part in parts]).astype(F32)
+        square = square + jnp.sum(x * x, axis=1, keepdims=True)
+        held[k] = (x * gain[z ^ k]).astype(BF16)
+        x = [held[k, :, pl.ds(pl.multiple_of((q ^ c) * lanes, lanes), lanes)] for c in range(per)]
+        w = jnp.concatenate([pieces[k * per + c][...] for c in range(per)])
+        total = total + dot(jnp.concatenate(x, axis=1), w)
+    columns = total.shape[1] // 2
+    lane = lax.broadcasted_iota(jnp.int32, (blocks * share, HEAD_SIZE), 1)
+    keep[:, :columns] = total[:, :columns]
+    keep[:, columns:] = jnp.where(lane == 0, square, 0.0)
+    send[:, :columns] = total[:, columns:].astype(BF16)
+    high = square.astype(BF16).astype(F32)
+    low = square - high
+    send[:, columns:] = jnp.where(lane == 0, high, jnp.where(lane == 1, low, 0.0)).astype(BF16)
+
+
+def down_kernel(planes, per, features, idx, keep, got, *refs):
+    pieces, own, sends = refs[:planes * 2], refs[planes * 2], refs[planes * 2 + 1:]
+    total = keep[...] + got[...].astype(F32)
+    units = (total.shape[1] - HEAD_SIZE) // 2
+    square = jnp.sum(total[:, 2 * units:], axis=1, keepdims=True)
+    factor = lax.rsqrt(square / features + 1e-06)
+    gate, up = total[:, :units] * factor, total[:, units:2 * units] * factor
+    activated = (gate / (1.0 + jnp.exp(-gate)) * up).astype(BF16)
+    z, q = idx[0], idx[2]
+    rows = own.shape[1]
+    sides = per // 2
+    for k in range(planes):
+        w = [pieces[(c % 2) * planes + k][c // 2] for c in range(per)]
+        y = dot(activated, jnp.concatenate(w, axis=1))
+        lanes = w[0].shape[1]
+        for c in range(per):
+            at = pl.ds(pl.multiple_of((q ^ c) * lanes, lanes), lanes)
+            block = y[:, c * lanes:(c + 1) * lanes]
+            own[z ^ k, :, at] = block[:rows]
+            for i, send in enumerate(sends):
+                send[z ^ k, :, at] = block[(i + 1) * rows:(i + 2) * rows].astype(BF16)
+
+
+def head_rows_kernel(idx, weight, *outs):
+    rows = outs[0].shape[0]
+    for c, out in enumerate(outs):
+        out[...] = weight[pl.ds(pl.multiple_of((idx[2] ^ c) * rows, rows), rows), :]
+
+
+def split_kernel(planes, wide, nearest, idx, weight, *outs):
+    sides = len(outs) if not nearest else outs[0].shape[0]
+    units = outs[0].shape[2 if wide else 1]
+    for k in range(planes):
+        for c in range(sides):
+            chip = (idx[0] ^ k) * sides + (idx[3] ^ c)
+            at = pl.ds(pl.multiple_of(chip * units, units), units)
+            block = weight[:, at] if wide else weight[at, :]
+            if nearest:
+                outs[k][c] = block
+            else:
+                outs[c][k] = block
+
+
+def regroup_kernel(*refs):
+    many = refs[-1].shape[0]
+    parts, outs = refs[:many], refs[many:]
+    for k, out in enumerate(outs):
+        for c, part in enumerate(parts):
+            out[c] = part[k]
+
+
+def ffn_kernel(blocks, planes, idx, *refs):
+    parts, refs = refs[:blocks], refs[blocks:]
+    held = refs[-1]
+    own, *sends = refs[-1 - blocks:-1]
+    per = held.shape[2] // HEAD_SIZE
+    lanes = held.shape[2] // per
+    pieces = refs[:-1 - blocks]
+    near = per // 2 * 2
+    far = planes * 2
+    starts = (0, near, near + far, near + 2 * far)
+    z, q = idx[0], idx[2]
     gate = up = 0.0
-    for p in range(planes):
-        x = jnp.concatenate([part[p] for part in parts])
-        w = jnp.concatenate([gate_up[p * per + i] for i in range(per)], axis=1)
-        gate = gate + lax.dot_general(x, w[:units], NT, preferred_element_type=F32)
-        up = up + lax.dot_general(x, w[units:], NT, preferred_element_type=F32)
+
+    def piece(which, k, c):
+        got = pieces[starts[which]:starts[which + 1]]
+        side, core = c // 2, c % 2
+        sides = per // 2
+        if which:
+            return got[core * planes + k][side]
+        return got[core * sides + side][k]
+
+    for k in range(planes):
+        x = jnp.concatenate([part[z ^ k] for part in parts])
+        held[k] = x
+        x = [held[k, :, pl.ds(pl.multiple_of((q ^ c) * lanes, lanes), lanes)] for c in range(per)]
+        x = jnp.concatenate(x, axis=1)
+        w = jnp.concatenate([piece(0, k, c) for c in range(per)])
+        gate = gate + dot(x, w)
+        w = jnp.concatenate([piece(1, k, c) for c in range(per)])
+        up = up + dot(x, w)
     activated = (gate / (1.0 + jnp.exp(-gate)) * up).astype(BF16)
-    half = activated.shape[0] // 2
-    width = per * down.shape[2]
-    for p in range(planes):
-        w = jnp.concatenate([down[p * per + i] for i in range(per)], axis=1)
-        y = dot(activated, w).astype(BF16)
-        keep[:, p * width:(p + 1) * width] = y[:half]
-        send[:, p * width:(p + 1) * width] = y[half:]
+    rows = own.shape[1]
+    for k in range(planes):
+        y = dot(activated, jnp.concatenate([piece(2, k, c) for c in range(per)], axis=1))
+        for c in range(per):
+            at = pl.ds(pl.multiple_of((q ^ c) * lanes, lanes), lanes)
+            block = y[:, c * lanes:(c + 1) * lanes]
+            own[z ^ k, :, at] = block[:rows]
+            for i, send in enumerate(sends):
+                send[z ^ k, :, at] = block[(i + 1) * rows:(i + 2) * rows].astype(BF16)
+
+
+def head_rows_kernel(idx, weight, *outs):
+    rows = outs[0].shape[0]
+    for c, out in enumerate(outs):
+        out[...] = weight[pl.ds(pl.multiple_of((idx[2] ^ c) * rows, rows), rows), :]
 
 
 def row_of(z, k, tokens, rows, total):
@@ -193,31 +376,30 @@
     return jnp.where((j == i + (z ^ k) * tokens) & (i < tokens), 1.0, 0.0).astype(BF16)
 
 
-def plane_sum_kernel(planes, tokens, idx, *refs):
+def plane_sum_kernel(planes, tokens, idx, hidden, *refs):
     parts, outs = refs[:-planes], refs[-planes:]
-    total = parts[0][...].astype(F32)
+    total = parts[0][...]
     for part in parts[1:]:
         total = total + part[...].astype(F32)
     total = total.astype(BF16)
     for k, out in enumerate(outs):
-        pick = row_of(idx[0], k, tokens, out.shape[0], total.shape[0])
-        out[...] = dot(pick, total).astype(BF16)
+        pick = row_of(idx[0], k, tokens, out.shape[1], total.shape[1])
+        for p in range(planes):
+            out[p] = dot(pick, total[p]).astype(BF16)
+        out[planes] = dot(pick, hidden[...]).astype(BF16)
 
 
 def last_kernel(planes, tokens, idx, *refs):
-    parts, hidden, out = refs[:planes], refs[planes:-1], refs[-1]
-    total = parts[0][...].astype(F32)
+    *parts, out, held = refs
+    width = parts[0].shape[2]
+    total = parts[0][:planes].astype(F32)
     for part in parts[1:]:
-        total = total + part[...].astype(F32)
-    z = idx[0]
-    pick = row_of(z, 0, tokens, total.shape[0], hidden[0].shape[0])
-    held = jnp.concatenate([dot(pick, h[...]) for h in hidden], axis=1)
-    width = hidden[0].shape[1]
-    whole = jnp.zeros_like(total)
-    for k in range(planes):
-        at = pl.ds(pl.multiple_of((z ^ k) * width, width), width)
-        out[:, at] = held[:tokens, k * width:(k + 1) * width].astype(BF16)
-    out[...] = (out[...].astype(F32) + total[:tokens]).astype(BF16)
+        total = total + part[:planes].astype(F32)
+    for k, part in enumerate(parts):
+        held[idx[0] ^ k] = part[planes].astype(F32)
+    for p in range(planes):
+        value = held[p] + total[p]
+        out[:, p * width:(p + 1) * width] = value[:tokens].astype(BF16)
 
 
 def call(kernel, outs, *args, scratch=()):
@@ -229,9 +411,9 @@
         in_specs=[SMEM if a.dtype == jnp.int32 else VMEM for a in args],
         out_specs=[VMEM] * len(shapes),
         scratch_shapes=list(scratch),
-        compiler_params=pltpu.CompilerParams(vmem_limit_bytes=40 * 2**20),
+        compiler_params=pltpu.CompilerParams(vmem_limit_bytes=16 * 2**20),
     )(*args)
-    return got[0] if single else got
+    return got[0] if single else list(got)
 
 
 def like(*shape, dtype=BF16):
@@ -265,7 +447,7 @@
     devices = n_blk * n_uly
     me = lax.axis_index("blk") * n_uly + lax.axis_index("uly")
     z, r = me // group, me % group
-    idx = jnp.stack([z, r]).astype(jnp.int32)
+    idx = jnp.stack([z, r, r // n_uly, r // (2 * n_uly)]).astype(jnp.int32)
     core = n_uly
     near = [b for b in range(group) if not b & core]
     order = near + [b ^ core for b in near]
@@ -277,57 +459,76 @@
     def swap_planes(x):
         return [swap(x, k * group) for k in range(1, planes)]
 
-    def by_head(x):
-        x = x.reshape(tokens, n_uly, per, x.shape[1] // group)
-        return x.transpose(2, 1, 0, 3).reshape(group, tokens, x.shape[3])
-
-    def packed(*xs):
-        x = jnp.concatenate([by_head(x) for x in xs], axis=2)
-        return jnp.pad(x, ((0, 0), (0, rows - tokens), (0, 0)))
-
+    head_of = [(i % n_uly) * per + i // n_uly for i in range(group)]
     plane_groups = [[p * group + i for i in range(group)] for p in range(planes)]
 
     def plane_exchange(x):
         return lax.all_to_all(x, axes, 0, 0, axis_index_groups=plane_groups, tiled=True)
 
-    kv = plane_exchange(packed(key_projection, value_projection))
-    qg = plane_exchange(packed(query_projection, gate_proj))
-
-    wo = lax.all_to_all(
-        out_weight.reshape(per, out_weight.shape[0] // per, out_weight.shape[1]),
-        "blk", 0, 0,
-        axis_index_groups=[[p * per + i for i in range(per)] for p in range(planes)],
-        tiled=True,
-    )
-    units = gate_weight.shape[1] // n_blk
-
-    def by_unit(w):
-        return w.reshape(w.shape[0], n_blk, units).transpose(1, 2, 0)
-
-    gate_up = lax.all_to_all(
-        jnp.concatenate([by_unit(gate_weight), by_unit(up_weight)], axis=1), "blk", 0, 0, tiled=True
-    )
-    down = lax.all_to_all(
-        down_weight.reshape(n_blk, units, down_weight.shape[1]), "blk", 0, 0, tiled=True
-    )
+    def after(xs, later):
+        return lax.optimization_barrier((xs, later))
+
     width = features // planes
-    resid = lax.all_to_all(
-        residual.reshape(tokens, planes, width).transpose(1, 0, 2),
-        "blk", 0, 0,
-        axis_index_groups=[[p * per + i for p in range(planes)] for i in range(per)],
-        tiled=True,
-    ).reshape(planes * tokens, width)
-
+    sides = per // 2
+    units = gate_weight.shape[1] // (planes * sides)
+
+    def within_plane(parts):
+        return [x if not c else swap(x, c * n_uly) for c, x in enumerate(parts)]
+
+    def across_planes(parts):
+        return [x if not k else swap(x, k * group) for k, x in enumerate(parts)]
+
+    def regroup(parts):
+        shape = (len(parts),) + parts[0].shape[1:]
+        return call(regroup_kernel, [like(*shape)] * parts[0].shape[0], *parts)
+
+    half = planes // 2
+    lot = group * rows
+    pair = 2 * HEAD_SIZE
+    head_groups = call(
+        functools.partial(pack_heads_kernel, head_of),
+        like(group, rows, 2 * heads * HEAD_SIZE + pair),
+        query_projection, gate_proj, key_projection, value_projection,
+    )
+    masks = [k * group + c * 2 * n_uly for k in range(half) for c in range(sides)]
+    head_groups, (gate_weight, up_weight, down_weight, out_weight, positions) = after(
+        head_groups, (gate_weight, up_weight, down_weight, out_weight, positions)
+    )
+    gate_up = call(
+        functools.partial(split_gate_up_kernel, planes, sides),
+        [like(gate_weight.shape[0], 4 * units)] * len(masks),
+        idx, gate_weight, up_weight,
+    )
+    head_rows = call(
+        head_rows_kernel,
+        [like(out_weight.shape[0] // per, out_weight.shape[1])] * per,
+        idx, out_weight,
+    )
+    down_parts = call(
+        functools.partial(split_down_kernel, planes),
+        [like(planes, units, down_weight.shape[1])] * sides,
+        idx, down_weight,
+    )
     spots = jnp.pad(
-        positions.reshape(planes, group, tokens),
+        positions.reshape(planes, group, tokens).astype(F32),
         ((0, 0), (0, 0), (0, rows - tokens)),
         constant_values=NO_POSITION,
-    )
-    key_spot = spots[z ^ jnp.arange(planes)].reshape(1, -1)
-    query_spot = spots[z][r ^ jnp.arange(group)].reshape(-1, 1)
-    visible = (key_spot <= query_spot) | (key_spot < prefix_len[0])
-    bias = jnp.where(visible, 0.0, HIDE).astype(F32)
-
+    ).reshape(planes, 1, group * rows)
+    own_heads = plane_exchange(head_groups)
+    gate_up[sides] = swap(gate_up[sides], masks[sides])
+    own_heads, (gate_up, head_rows, down_parts, spots) = after(
+        own_heads, (gate_up, head_rows, down_parts, spots)
+    )
+    messages = across_planes(
+        call(
+            functools.partial(message_kernel, planes),
+            [like(lot + rows * width // pair, pair)] * planes,
+            idx, own_heads, residual,
+        )
+    )
+    wo = within_plane(head_rows)
+    down_parts[1] = swap(down_parts[1], masks[1])
+    gate_up[1] = swap(gate_up[1], masks[1])
     pick = np.zeros((group, tokens, group, rows), np.float32)
     for b in range(group):
         for t in range(tokens):
@@ -336,8 +537,13 @@
     gated = call(
         functools.partial(attention_kernel, heads, planes),
         like(group * tokens, heads * HEAD_SIZE),
-        idx, qg, kv, *swap_planes(kv), bias, pick,
-    )
+        idx, prefix_len, own_heads, *messages, spots, pick,
+    )
+    gated, (wo, down_parts, gate_up[3]) = after(gated, (wo, down_parts, gate_up[3]))
+    gateds = [gated] + swap_planes(gated)
+    gate_up[3] = swap(gate_up[3], masks[3])
+    gateds, (gate_up[1], down_parts) = after(gateds, (gate_up[1], regroup(down_parts)))
+    down_parts = across_planes(down_parts)
 
     turn = np.zeros((group, planes, tokens, planes, group, tokens), np.float32)
     for i, b in enumerate(order):
@@ -349,8 +555,11 @@
     keep, send = call(
         functools.partial(project_kernel, planes),
         [like(total // 2, width)] * 2,
-        idx, gated, *swap_planes(gated), wo, turn,
-        scratch=[pltpu.VMEM((planes,) + gated.shape, BF16)],
+        idx, *gateds, *wo, turn,
+        scratch=[
+            pltpu.VMEM((planes,) + gated.shape, BF16),
+            pltpu.VMEM((wo[0].shape[0], width), BF16),
+        ],
     )
     share = total // group
     own, *rest = call(
@@ -359,35 +568,42 @@
         keep, swap(send, core),
     )
     hidden = call(
-        sum_kernel, like(share, width), own, resid, *[swap(x, b) for x, b in zip(rest, steps)]
-    )
-    hiddens = [hidden] + swap_planes(hidden)
-    normed = call(
-        functools.partial(norm_kernel, planes),
-        like(planes, share, width),
-        idx, *hiddens, norm_gain.reshape(planes, 1, width),
-    )
-    blocks = [normed] + [swap(normed, b) for b in steps]
-    blocks = blocks + [swap(x, core) for x in blocks]
+        functools.partial(hidden_kernel, planes, tokens),
+        like(share, width),
+        idx, own, *[swap(x, b) for x, b in zip(rest, steps)], *messages,
+    )
+    hidden, gate_up[3] = after(hidden, gate_up[3])
+    near_hidden = [hidden] + [swap(hidden, k * group) for k in range(1, half)]
+    gate_up = [x for both in zip(gate_up, [swap(x, core) for x in gate_up]) for x in both]
+    block = call(stack_kernel, like(half, share, width), *near_hidden)
+    blocks = [block] + [swap(block, b) for b in steps]
     keep, send = call(
-        functools.partial(ffn_kernel, group),
-        [like(total // 2, features)] * 2,
-        *blocks, gate_up, down,
-    )
+        functools.partial(gate_up_kernel, len(blocks), per),
+        [
+            like(len(blocks) * share, 2 * units + HEAD_SIZE, dtype=F32),
+            like(len(blocks) * share, 2 * units + HEAD_SIZE),
+        ],
+        idx, *blocks, *gate_up, norm_gain.reshape(planes, 1, width),
+        scratch=[pltpu.VMEM((half, len(blocks) * share, width), BF16)],
+    )
+    send, down_parts = after(send, down_parts)
+    got = swap(send, half * group)
+    down_share = down_parts + [swap(x, core) for x in down_parts]
     own, *rest = call(
-        core_sum_kernel,
-        [like(share, features, dtype=F32)] + [like(share, features)] * len(steps),
-        keep, swap(send, core),
+        functools.partial(down_kernel, planes, per, features),
+        [like(planes, share, width, dtype=F32)] + [like(planes, share, width)] * len(steps),
+        idx, keep, got, *down_share,
     )
     parts = call(
         functools.partial(plane_sum_kernel, planes, tokens),
-        [like(rows, features)] * planes,
-        idx, own, *[swap(x, b) for x, b in zip(rest, steps)],
+        [like(planes + 1, rows, width)] * planes,
+        idx, hidden, own, *[swap(x, b) for x, b in zip(rest, steps)],
     )
     return call(
         functools.partial(last_kernel, planes, tokens),
         like(tokens, features),
-        idx, parts[0], *[swap(x, k * group) for k, x in enumerate(parts) if k], *hiddens,
+        idx, *across_planes(parts),
+        scratch=[pltpu.VMEM((planes, rows, width), F32)],
     )
 
 

time: 189 us -> 141 us (0.75)
  blocking collectives: 20 us -> 0 us
  waiting for transfers between devices: 92.2 us -> 74.6 us
  local copies, waits for them, and re-layouts: 15.3 us -> 7.1 us
  Pallas kernels: 7.64 us -> 12.6 us
  starting transfers between devices: 48.7 us -> 45.2 us
  other arithmetic: 3.45 us -> 0.08 us
    all_to_all x3 -> x0, waiting for transfers between devices: 21.2 us -> none  [the longest x1 15.5 us: move_tokens(): lax.all_to_all(down_weight.reshape(n_blk, units, down_weight.shape[1]), '...]
    all_to_all x2 -> x0, blocking collectives: 20 us -> none  [the longest x1 11.2 us: move_tokens(): lax.all_to_all(out_weight.reshape(per, out_weight.shape[0] // per, out_we...]
    all_to_all x3 -> x0, starting transfers between devices: 13.9 us -> none  [the longest x1 5.43 us: move_tokens(): lax.all_to_all(jnp.concatenate([by_unit(gate_weight), by_unit(up_weight)]...]
    ppermute x27 -> x39, starting transfers between devices: 29.6 us -> 41.4 us  [swap(): return lax.ppermute(x, axes, [(i, i ^ mask) for i in range(devices)])]
    reshape x12 -> x1, local copies, waits for them, and re-layouts: 5.25 us -> 0.08 us  [move_tokens(): spots = jnp.pad(positions.reshape(planes, group, tokens).astype(F32), ((0...]
    pallas_call x9 -> x15, Pallas kernels: 7.64 us -> 12.6 us  [call(): pl.pallas_call(kernel, out_shape=shapes, in_specs=[SMEM if a.dtype == jnp...]
    gather x3 -> x0, local copies, waits for them, and re-layouts: 2.54 us -> none  [the longest x2 1.87 us: move_tokens(): key_spot = spots[z ^ jnp.arange(planes)].reshape(1, -1)]
    all_to_all x1, waiting for transfers between devices: 1.22 us -> 3.27 us  [plane_exchange(): lax.all_to_all(x, axes, 0, 0, axis_index_groups=plane_groups, tiled=True)]
  transfers between devices with their start and end apart: 31 -> 40, of which waited for: 24 -> 25; matrix products, arithmetic and copies ran while one was open for 6% -> 0% of each run, Pallas kernels for 2% -> 5%
where the time goes in v2:
time: 141 us; the launch traced here: 140 us
  waiting for transfers between devices  74.6 us (53%)
  starting transfers between devices  45.2 us (32%)
  Pallas kernels  12.6 us (9%)
  local copies, waits for them, and re-layouts  7.1 us (5%)
    ppermute x39, waiting for transfers between devices, swap(): return lax.ppermute(x, axes, [(i, i ^ mask) for i in range(devices)])  71.4 us
    ppermute x39, starting transfers between devices, swap(): return lax.ppermute(x, axes, [(i, i ^ mask) for i in range(devices)])  41.4 us
    pallas_call x15, Pallas kernels, call(): pl.pallas_call(kernel, out_shape=shapes, in_specs=[SMEM if a.dtype == jnp...  12.6 us
    unnamed x36, local copies, waits for them, and re-layouts  6.91 us
    all_to_all x1, starting transfers between devices, plane_exchange(): lax.all_to_all(x, axes, 0, 0, axis_index_groups=plane_groups, tiled=True)  3.72 us
    all_to_all x1, waiting for transfers between devices, plane_exchange(): lax.all_to_all(x, axes, 0, 0, axis_index_groups=plane_groups, tiled=True)  3.27 us
  transfers between devices with their start and end apart: 40, of which 25 were waited for; matrix products, arithmetic and copies ran while one was open for 0% of the time, Pallas kernels for 5%

profile of v2, /device:TPU:0, one launch (start us, length us, event | category | flops | bytes accessed | tf_op | source)
XLA Modules:
  0.0 140.5 jit_solution(7803714234652234223)
XLA Ops:
  5.7 1.5 %shard_map.137 = (bf16[128,1536]{1,0:T(8,128)(2,1)S(1)}, bf16[128,1536]{1,0:T(8,128)(2,1)S(1)}, bf16[128,1536]{1,0:T(8,128)(2,1)}, bf16[128,1536]{1,0:T(8,128)(2,1)S(1)}) custom-call(s32[4]{0:T(128)S(1)} %pad_add_fusion.idx, bf16[128,3072]{1,0:T(8,128)(2,1)S(1)} %copy-done, bf16[128,3072]{1,0:T(8,128)(2,1)S(1)} %copy-done.1), custom_call_target="tpu_custom_call" | custom-call | tf_op jit(solution)/shard_map/pallas_call | solution.py:408
  7.2 3.0 %collective-permute-start = (bf16[128,1536]{1,0:T(8,128)(2,1)}, bf16[128,1536]{1,0:T(8,128)(2,1)S(1)}, u32[]{:S(2)}, u32[]{:S(2)}) collective-permute-start(bf16[128,1536]{1,0:T(8,128)(2,1)} %get-tuple-element.86), channel_id=1, source_target_pairs={{0,8},{1,9},{2,10},{3,11},{4,12},{5,13},{6,14},{7,15},{8,0},{9,1},... | collective-permute-start | bytes 1179656 | tf_op jit(solution)/shard_map/ppermute | solution.py:457
  10.2 3.7 %all-to-all-start = ((bf16[8,16,1280]{2,1,0:T(8,128)(2,1)}), bf16[8,16,1280]{2,1,0:T(8,128)(2,1)S(1)}, u32[]{:S(2)}, u32[]{:S(2)}) async-start(bf16[8,16,1280]{2,1,0:T(8,128)(2,1)} %shard_map.136), calls=%async_computation | async-start | bytes 655360 | tf_op jit(solution)/shard_map/all_to_all | solution.py:466
  17.4 3.3 %all-to-all-done.heads.qg = bf16[8,16,1280]{2,1,0:T(8,128)(2,1)S(1)} async-done(((bf16[8,16,1280]{2,1,0:T(8,128)(2,1)}), bf16[8,16,1280]{2,1,0:T(8,128)(2,1)S(1)}, u32[]{:S(2)}, u32[]{:S(2)}) %all-to-all-start) | async-done | bytes 327712 | tf_op jit(solution)/shard_map/all_to_all | solution.py:466
  20.7 1.4 %collective-permute-start.7 = (bf16[4,384,128]{2,1,0:T(8,128)(2,1)}, bf16[4,384,128]{2,1,0:T(8,128)(2,1)S(1)}, u32[]{:S(2)}, u32[]{:S(2)}) collective-permute-start(bf16[4,384,128]{2,1,0:T(8,128)(2,1)} %copy-done.12), channel_id=1, source_target_pairs={{0,4},{1,5},{2,6},{3,7},{4,0},{5,1},{6,2},{7,3},{8,12},{9,13},{10,... | collective-permute-start | bytes 1179656 | tf_op jit(solution)/shard_map/ppermute | solution.py:457
  23.9 2.6 %collective-permute-start.2 = (bf16[160,256]{1,0:T(8,128)(2,1)S(1)}, bf16[160,256]{1,0:T(8,128)(2,1)S(1)}, u32[]{:S(2)}, u32[]{:S(2)}) collective-permute-start(bf16[160,256]{1,0:T(8,128)(2,1)S(1)} %get-tuple-element.100), channel_id=1, source_target_pairs={{0,16},{1,17},{2,18},{3,19},{4,20},{5,21},{6,22},{7,23},{8,24},{9,... | collective-permute-start | bytes 245768 | tf_op jit(solution)/shard_map/ppermute | solution.py:457
  28.9 4.5 %collective-permute-done.2.refs_2_.refs_6_ = bf16[160,256]{1,0:T(8,128)(2,1)S(1)} collective-permute-done((bf16[160,256]{1,0:T(8,128)(2,1)S(1)}, bf16[160,256]{1,0:T(8,128)(2,1)S(1)}, u32[]{:S(2)}, u32[]{:S(2)}) %collective-permute-start.2) | collective-permute-done | bytes 81952 | tf_op jit(solution)/shard_map/ppermute | solution.py:457
  33.3 1.7 %collective-permute-start.5 = (bf16[512,128]{1,0:T(8,128)(2,1)S(1)}, bf16[512,128]{1,0:T(8,128)(2,1)S(1)}, u32[]{:S(2)}, u32[]{:S(2)}) collective-permute-start(bf16[512,128]{1,0:T(8,128)(2,1)S(1)} %copy-done.14), channel_id=1, source_target_pairs={{0,4},{1,5},{2,6},{3,7},{4,0},{5,1},{6,2},{7,3},{8,12},{9,13},{10,... | collective-permute-start | bytes 393224 | tf_op jit(solution)/shard_map/ppermute | solution.py:457
  35.7 1.9 %shard_map.141.refs_0_ = bf16[96,512]{1,0:T(8,128)(2,1)S(1)} custom-call(s32[4]{0:T(128)S(1)} %pad_add_fusion.idx, s32[1]{0:T(128)S(6)} %copy.15.prefix, bf16[8,16,1280]{2,1,0:T(8,128)(2,1)S(1)} %all-to-all-done.heads.qg, bf16[160,256]{1,0:T(8,128)(2,1)S(1)} %get-tuple-element.98.refs_0_.refs_4_, ...), custom_call_target="tpu_custom_call" | custom-call | tf_op jit(solution)/shard_map/pallas_call | solution.py:408
  37.6 6.5 %collective-permute-done.5.refs_6_ = bf16[512,128]{1,0:T(8,128)(2,1)S(1)} collective-permute-done((bf16[512,128]{1,0:T(8,128)(2,1)S(1)}, bf16[512,128]{1,0:T(8,128)(2,1)S(1)}, u32[]{:S(2)}, u32[]{:S(2)}) %collective-permute-start.5) | collective-permute-done | bytes 131104 | tf_op jit(solution)/shard_map/ppermute | solution.py:457
  44.1 1.5 %collective-permute-done.6.refs_7_ = bf16[512,128]{1,0:T(8,128)(2,1)S(1)} collective-permute-done((bf16[512,128]{1,0:T(8,128)(2,1)S(1)}, bf16[512,128]{1,0:T(8,128)(2,1)S(1)}, u32[]{:S(2)}, u32[]{:S(2)}) %collective-permute-start.6) | collective-permute-done | bytes 131104 | tf_op jit(solution)/shard_map/ppermute | solution.py:457
  45.6 2.4 %collective-permute-start.10 = (bf16[96,512]{1,0:T(8,128)(2,1)S(1)}, bf16[96,512]{1,0:T(8,128)(2,1)S(1)}, u32[]{:S(2)}, u32[]{:S(2)}) collective-permute-start(bf16[96,512]{1,0:T(8,128)(2,1)S(1)} %shard_map.141.refs_0_), channel_id=1, source_target_pairs={{0,24},{1,25},{2,26},{3,27},{4,28},{5,29},{6,30},{7,31},{8,16},{9,... | collective-permute-start | bytes 294920 | tf_op jit(solution)/shard_map/ppermute | solution.py:457
  48.2 1.8 %collective-permute-start.8 = (bf16[96,512]{1,0:T(8,128)(2,1)S(1)}, bf16[96,512]{1,0:T(8,128)(2,1)S(1)}, u32[]{:S(2)}, u32[]{:S(2)}) collective-permute-start(bf16[96,512]{1,0:T(8,128)(2,1)S(1)} %shard_map.141.refs_0_), channel_id=1, source_target_pairs={{0,8},{1,9},{2,10},{3,11},{4,12},{5,13},{6,14},{7,15},{8,0},{9,1},... | collective-permute-start | bytes 294920 | tf_op jit(solution)/shard_map/ppermute | solution.py:457
  50.8 2.4 %collective-permute-done.10.refs_3_ = bf16[96,512]{1,0:T(8,128)(2,1)S(1)} collective-permute-done((bf16[96,512]{1,0:T(8,128)(2,1)S(1)}, bf16[96,512]{1,0:T(8,128)(2,1)S(1)}, u32[]{:S(2)}, u32[]{:S(2)}) %collective-permute-start.10) | collective-permute-done | bytes 98336 | tf_op jit(solution)/shard_map/ppermute | solution.py:457
  53.1 4.9 %collective-permute-done.9.refs_2_ = bf16[96,512]{1,0:T(8,128)(2,1)S(1)} collective-permute-done((bf16[96,512]{1,0:T(8,128)(2,1)S(1)}, bf16[96,512]{1,0:T(8,128)(2,1)S(1)}, u32[]{:S(2)}, u32[]{:S(2)}) %collective-permute-start.9) | collective-permute-done | bytes 98336 | tf_op jit(solution)/shard_map/ppermute | solution.py:457
  60.9 4.1 %collective-permute-done.13.refs_1_ = bf16[48,512]{1,0:T(8,128)(2,1)S(1)} collective-permute-done((bf16[48,512]{1,0:T(8,128)(2,1)S(1)}, bf16[48,512]{1,0:T(8,128)(2,1)S(1)}, u32[]{:S(2)}, u32[]{:S(2)}) %collective-permute-start.13) | collective-permute-done | bytes 49184 | tf_op jit(solution)/shard_map/ppermute | solution.py:457
  66.2 2.9 %collective-permute-done.14.refs_2_ = bf16[48,512]{1,0:T(8,128)(2,1)S(1)} collective-permute-done((bf16[48,512]{1,0:T(8,128)(2,1)S(1)}, bf16[48,512]{1,0:T(8,128)(2,1)S(1)}, u32[]{:S(2)}, u32[]{:S(2)}) %collective-permute-start.14) | collective-permute-done | bytes 49184 | tf_op jit(solution)/shard_map/ppermute | solution.py:457
  69.7 4.4 %collective-permute-done.15.refs_3_ = bf16[48,512]{1,0:T(8,128)(2,1)S(1)} collective-permute-done((bf16[48,512]{1,0:T(8,128)(2,1)S(1)}, bf16[48,512]{1,0:T(8,128)(2,1)S(1)}, u32[]{:S(2)}, u32[]{:S(2)}) %collective-permute-start.15) | collective-permute-done | bytes 49184 | tf_op jit(solution)/shard_map/ppermute | solution.py:457
  75.0 4.1 %collective-permute-done.17.refs_1_ = bf16[48,512]{1,0:T(8,128)(2,1)S(1)} collective-permute-done((bf16[48,512]{1,0:T(8,128)(2,1)S(1)}, bf16[48,512]{1,0:T(8,128)(2,1)S(1)}, u32[]{:S(2)}, u32[]{:S(2)}) %collective-permute-start.17) | collective-permute-done | bytes 49184 | tf_op jit(solution)/shard_map/ppermute | solution.py:457
  80.9 3.3 %collective-permute-start.26 = (bf16[2,384,128]{2,1,0:T(8,128)(2,1)S(1)}, bf16[2,384,128]{2,1,0:T(8,128)(2,1)S(1)}, u32[]{:S(2)}, u32[]{:S(2)}) collective-permute-start(bf16[2,384,128]{2,1,0:T(8,128)(2,1)S(1)} %get-tuple-element.142), channel_id=1, source_target_pairs={{0,16},{1,17},{2,18},{3,19},{4,20},{5,21},{6,22},{7,23},{8,24},{9,... | collective-permute-start | bytes 589832 | tf_op jit(solution)/shard_map/ppermute | solution.py:457
  85.1 2.6 %collective-permute-start.27 = (bf16[2,384,128]{2,1,0:T(8,128)(2,1)S(1)}, bf16[2,384,128]{2,1,0:T(8,128)(2,1)S(1)}, u32[]{:S(2)}, u32[]{:S(2)}) collective-permute-start(bf16[2,384,128]{2,1,0:T(8,128)(2,1)S(1)} %get-tuple-element.143), channel_id=1, source_target_pairs={{0,24},{1,25},{2,26},{3,27},{4,28},{5,29},{6,30},{7,31},{8,16},{9,... | collective-permute-start | bytes 589832 | tf_op jit(solution)/shard_map/ppermute | solution.py:457
  88.1 4.3 %collective-permute-done.18.refs_1_ = bf16[2,48,512]{2,1,0:T(8,128)(2,1)S(1)} collective-permute-done((bf16[2,48,512]{2,1,0:T(8,128)(2,1)S(1)}, bf16[2,48,512]{2,1,0:T(8,128)(2,1)S(1)}, u32[]{:S(2)}, u32[]{:S(2)}) %collective-permute-start.18) | collective-permute-done | bytes 98336 | tf_op jit(solution)/shard_map/ppermute | solution.py:457
  92.4 1.4 shard_map.147
  93.8 4.5 %collective-permute-done.26.refs_2_ = bf16[2,384,128]{2,1,0:T(8,128)(2,1)S(1)} collective-permute-done((bf16[2,384,128]{2,1,0:T(8,128)(2,1)S(1)}, bf16[2,384,128]{2,1,0:T(8,128)(2,1)S(1)}, u32[]{:S(2)}, u32[]{:S(2)}) %collective-permute-start.26) | collective-permute-done | bytes 196640 | tf_op jit(solution)/shard_map/ppermute | solution.py:457
  98.3 4.9 %collective-permute-start.28 = (bf16[192,896]{1,0:T(8,128)(2,1)S(1)}, bf16[192,896]{1,0:T(8,128)(2,1)S(1)}, u32[]{:S(2)}, u32[]{:S(2)}) collective-permute-start(bf16[192,896]{1,0:T(8,128)(2,1)S(1)} %get-tuple-element.144), channel_id=1, source_target_pairs={{0,16},{1,17},{2,18},{3,19},{4,20},{5,21},{6,22},{7,23},{8,24},{9,... | collective-permute-start | bytes 1032200 | tf_op jit(solution)/shard_map/ppermute | solution.py:457
  105.5 11.1 %collective-permute-done.28.got = bf16[192,896]{1,0:T(8,128)(2,1)S(1)} collective-permute-done((bf16[192,896]{1,0:T(8,128)(2,1)S(1)}, bf16[192,896]{1,0:T(8,128)(2,1)S(1)}, u32[]{:S(2)}, u32[]{:S(2)}) %collective-permute-start.28) | collective-permute-done | bytes 344096 | tf_op jit(solution)/shard_map/ppermute | solution.py:457
  117.8 1.7 %collective-permute-start.33 = (bf16[4,48,512]{2,1,0:T(8,128)(2,1)S(1)}, bf16[4,48,512]{2,1,0:T(8,128)(2,1)S(1)}, u32[]{:S(2)}, u32[]{:S(2)}) collective-permute-start(bf16[4,48,512]{2,1,0:T(8,128)(2,1)S(1)} %get-tuple-element.150), channel_id=1, source_target_pairs={{0,1},{1,0},{2,3},{3,2},{4,5},{5,4},{6,7},{7,6},{8,9},{9,8},{10,11... | collective-permute-start | bytes 589832 | tf_op jit(solution)/shard_map/ppermute | solution.py:457
  121.4 3.4 %collective-permute-done.33.refs_1_ = bf16[4,48,512]{2,1,0:T(8,128)(2,1)S(1)} collective-permute-done((bf16[4,48,512]{2,1,0:T(8,128)(2,1)S(1)}, bf16[4,48,512]{2,1,0:T(8,128)(2,1)S(1)}, u32[]{:S(2)}, u32[]{:S(2)}) %collective-permute-start.33) | collective-permute-done | bytes 196640 | tf_op jit(solution)/shard_map/ppermute | solution.py:457
  124.8 2.6 %collective-permute-done.34.refs_2_ = bf16[4,48,512]{2,1,0:T(8,128)(2,1)S(1)} collective-permute-done((bf16[4,48,512]{2,1,0:T(8,128)(2,1)S(1)}, bf16[4,48,512]{2,1,0:T(8,128)(2,1)S(1)}, u32[]{:S(2)}, u32[]{:S(2)}) %collective-permute-start.34) | collective-permute-done | bytes 196640 | tf_op jit(solution)/shard_map/ppermute | solution.py:457
  127.4 2.6 %collective-permute-done.35.refs_3_ = bf16[4,48,512]{2,1,0:T(8,128)(2,1)S(1)} collective-permute-done((bf16[4,48,512]{2,1,0:T(8,128)(2,1)S(1)}, bf16[4,48,512]{2,1,0:T(8,128)(2,1)S(1)}, u32[]{:S(2)}, u32[]{:S(2)}) %collective-permute-start.35) | collective-permute-done | bytes 196640 | tf_op jit(solution)/shard_map/ppermute | solution.py:457
  131.3 4.0 %collective-permute-start.38 = (bf16[5,16,512]{2,1,0:T(8,128)(2,1)S(1)}, bf16[5,16,512]{2,1,0:T(8,128)(2,1)S(1)}, u32[]{:S(2)}, u32[]{:S(2)}) collective-permute-start(bf16[5,16,512]{2,1,0:T(8,128)(2,1)S(1)} %get-tuple-element.156), channel_id=1, source_target_pairs={{0,24},{1,25},{2,26},{3,27},{4,28},{5,29},{6,30},{7,31},{8,16},{9,... | collective-permute-start | bytes 245768 | tf_op jit(solution)/shard_map/ppermute | solution.py:457
  135.3 3.9 %collective-permute-done.37.refs_2_ = bf16[5,16,512]{2,1,0:T(8,128)(2,1)S(1)} collective-permute-done((bf16[5,16,512]{2,1,0:T(8,128)(2,1)S(1)}, bf16[5,16,512]{2,1,0:T(8,128)(2,1)S(1)}, u32[]{:S(2)}, u32[]{:S(2)}) %collective-permute-start.37) | collective-permute-done | bytes 81952 | tf_op jit(solution)/shard_map/ppermute | solution.py:457
  (104 shorter events, 30.8 us)
Async XLA Ops:
  7.2 13.5 %collective-permute-start = (bf16[128,1536]{1,0:T(8,128)(2,1)}, bf16[128,1536]{1,0:T(8,128)(2,1)S(1)}, u32[]{:S(2)}, u32[]{:S(2)}) collective-permute-start(bf16[128,1536]{1,0:T(8,128)(2,1)} %get-tuple-element.86), channel_id=1, source_target_pairs={{0,8},{1,9},{2,10},{3,11},{4,12},{5,13},{6,14},{7,15},{8,0},{9,1},... | collective-permute-start | bytes 1179656 | tf_op jit(solution)/shard_map/ppermute | solution.py:457
  10.2 10.5 %all-to-all-start = ((bf16[8,16,1280]{2,1,0:T(8,128)(2,1)}), bf16[8,16,1280]{2,1,0:T(8,128)(2,1)S(1)}, u32[]{:S(2)}, u32[]{:S(2)}) async-start(bf16[8,16,1280]{2,1,0:T(8,128)(2,1)} %shard_map.136), calls=%async_computation | async-start | bytes 655360 | tf_op jit(solution)/shard_map/all_to_all | solution.py:466
  20.7 25.0 %collective-permute-start.7 = (bf16[4,384,128]{2,1,0:T(8,128)(2,1)}, bf16[4,384,128]{2,1,0:T(8,128)(2,1)S(1)}, u32[]{:S(2)}, u32[]{:S(2)}) collective-permute-start(bf16[4,384,128]{2,1,0:T(8,128)(2,1)} %copy-done.12), channel_id=1, source_target_pairs={{0,4},{1,5},{2,6},{3,7},{4,0},{5,1},{6,2},{7,3},{8,12},{9,13},{10,... | collective-permute-start | bytes 1179656 | tf_op jit(solution)/shard_map/ppermute | solution.py:457
  22.1 28.7 %collective-permute-start.11 = (bf16[128,1536]{1,0:T(8,128)(2,1)S(1)}, bf16[128,1536]{1,0:T(8,128)(2,1)S(1)}, u32[]{:S(2)}, u32[]{:S(2)}) collective-permute-start(bf16[128,1536]{1,0:T(8,128)(2,1)S(1)} %get-tuple-element.111), channel_id=1, source_target_pairs={{0,4},{1,5},{2,6},{3,7},{4,0},{5,1},{6,2},{7,3},{8,12},{9,13},{10,... | collective-permute-start | bytes 1179656 | tf_op jit(solution)/shard_map/ppermute | solution.py:457
  23.3 5.5 %collective-permute-start.1 = (bf16[160,256]{1,0:T(8,128)(2,1)S(1)}, bf16[160,256]{1,0:T(8,128)(2,1)S(1)}, u32[]{:S(2)}, u32[]{:S(2)}) collective-permute-start(bf16[160,256]{1,0:T(8,128)(2,1)S(1)} %get-tuple-element.99), channel_id=1, source_target_pairs={{0,8},{1,9},{2,10},{3,11},{4,12},{5,13},{6,14},{7,15},{8,0},{9,1},... | collective-permute-start | bytes 245768 | tf_op jit(solution)/shard_map/ppermute | solution.py:457
  23.9 9.4 %collective-permute-start.2 = (bf16[160,256]{1,0:T(8,128)(2,1)S(1)}, bf16[160,256]{1,0:T(8,128)(2,1)S(1)}, u32[]{:S(2)}, u32[]{:S(2)}) collective-permute-start(bf16[160,256]{1,0:T(8,128)(2,1)S(1)} %get-tuple-element.100), channel_id=1, source_target_pairs={{0,16},{1,17},{2,18},{3,19},{4,20},{5,21},{6,22},{7,23},{8,24},{9,... | collective-permute-start | bytes 245768 | tf_op jit(solution)/shard_map/ppermute | solution.py:457
  26.5 8.5 %collective-permute-start.3 = (bf16[160,256]{1,0:T(8,128)(2,1)S(1)}, bf16[160,256]{1,0:T(8,128)(2,1)S(1)}, u32[]{:S(2)}, u32[]{:S(2)}) collective-permute-start(bf16[160,256]{1,0:T(8,128)(2,1)S(1)} %get-tuple-element.101), channel_id=1, source_target_pairs={{0,24},{1,25},{2,26},{3,27},{4,28},{5,29},{6,30},{7,31},{8,16},{9,... | collective-permute-start | bytes 245768 | tf_op jit(solution)/shard_map/ppermute | solution.py:457
  28.9 8.8 %collective-permute-start.4 = (bf16[512,128]{1,0:T(8,128)(2,1)S(1)}, bf16[512,128]{1,0:T(8,128)(2,1)S(1)}, u32[]{:S(2)}, u32[]{:S(2)}) collective-permute-start(bf16[512,128]{1,0:T(8,128)(2,1)S(1)} %copy-done.16), channel_id=1, source_target_pairs={{0,2},{1,3},{2,0},{3,1},{4,6},{5,7},{6,4},{7,5},{8,10},{9,11},{10,... | collective-permute-start | bytes 393224 | tf_op jit(solution)/shard_map/ppermute | solution.py:457
  33.3 10.8 %collective-permute-start.5 = (bf16[512,128]{1,0:T(8,128)(2,1)S(1)}, bf16[512,128]{1,0:T(8,128)(2,1)S(1)}, u32[]{:S(2)}, u32[]{:S(2)}) collective-permute-start(bf16[512,128]{1,0:T(8,128)(2,1)S(1)} %copy-done.14), channel_id=1, source_target_pairs={{0,4},{1,5},{2,6},{3,7},{4,0},{5,1},{6,2},{7,3},{8,12},{9,13},{10,... | collective-permute-start | bytes 393224 | tf_op jit(solution)/shard_map/ppermute | solution.py:457
  35.0 10.6 %collective-permute-start.6 = (bf16[512,128]{1,0:T(8,128)(2,1)S(1)}, bf16[512,128]{1,0:T(8,128)(2,1)S(1)}, u32[]{:S(2)}, u32[]{:S(2)}) collective-permute-start(bf16[512,128]{1,0:T(8,128)(2,1)S(1)} %get-tuple-element.106), channel_id=1, source_target_pairs={{0,6},{1,7},{2,4},{3,5},{4,2},{5,3},{6,0},{7,1},{8,14},{9,15},{10,... | collective-permute-start | bytes 393224 | tf_op jit(solution)/shard_map/ppermute | solution.py:457
  45.6 7.5 %collective-permute-start.10 = (bf16[96,512]{1,0:T(8,128)(2,1)S(1)}, bf16[96,512]{1,0:T(8,128)(2,1)S(1)}, u32[]{:S(2)}, u32[]{:S(2)}) collective-permute-start(bf16[96,512]{1,0:T(8,128)(2,1)S(1)} %shard_map.141.refs_0_), channel_id=1, source_target_pairs={{0,24},{1,25},{2,26},{3,27},{4,28},{5,29},{6,30},{7,31},{8,16},{9,... | collective-permute-start | bytes 294920 | tf_op jit(solution)/shard_map/ppermute | solution.py:457
  48.0 10.1 %collective-permute-start.9 = (bf16[96,512]{1,0:T(8,128)(2,1)S(1)}, bf16[96,512]{1,0:T(8,128)(2,1)S(1)}, u32[]{:S(2)}, u32[]{:S(2)}) collective-permute-start(bf16[96,512]{1,0:T(8,128)(2,1)S(1)} %shard_map.141.refs_0_), channel_id=1, source_target_pairs={{0,16},{1,17},{2,18},{3,19},{4,20},{5,21},{6,22},{7,23},{8,24},{9,... | collective-permute-start | bytes 294920 | tf_op jit(solution)/shard_map/ppermute | solution.py:457
  48.2 9.8 %collective-permute-start.8 = (bf16[96,512]{1,0:T(8,128)(2,1)S(1)}, bf16[96,512]{1,0:T(8,128)(2,1)S(1)}, u32[]{:S(2)}, u32[]{:S(2)}) collective-permute-start(bf16[96,512]{1,0:T(8,128)(2,1)S(1)} %shard_map.141.refs_0_), channel_id=1, source_target_pairs={{0,8},{1,9},{2,10},{3,11},{4,12},{5,13},{6,14},{7,15},{8,0},{9,1},... | collective-permute-start | bytes 294920 | tf_op jit(solution)/shard_map/ppermute | solution.py:457
  50.0 24.8 %collective-permute-start.16 = (bf16[128,1536]{1,0:T(8,128)(2,1)S(1)}, bf16[128,1536]{1,0:T(8,128)(2,1)S(1)}, u32[]{:S(2)}, u32[]{:S(2)}) collective-permute-start(bf16[128,1536]{1,0:T(8,128)(2,1)S(1)} %get-tuple-element.132), channel_id=1, source_target_pairs={{0,12},{1,13},{2,14},{3,15},{4,8},{5,9},{6,10},{7,11},{8,4},{9,5},... | collective-permute-start | bytes 1179656 | tf_op jit(solution)/shard_map/ppermute | solution.py:457
  59.4 20.4 %collective-permute-start.21 = (bf16[128,1536]{1,0:T(8,128)(2,1)S(1)}, bf16[128,1536]{1,0:T(8,128)(2,1)S(1)}, u32[]{:S(2)}, u32[]{:S(2)}) collective-permute-start(bf16[128,1536]{1,0:T(8,128)(2,1)S(1)} %get-tuple-element.134.refs_4_), channel_id=1, source_target_pairs={{0,2},{1,3},{2,0},{3,1},{4,6},{5,7},{6,4},{7,5},{8,10},{9,11},{10,... | collective-permute-start | bytes 1179656 | tf_op jit(solution)/shard_map/ppermute | solution.py:457
  59.9 20.8 %collective-permute-start.23 = (bf16[128,1536]{1,0:T(8,128)(2,1)S(1)}, bf16[128,1536]{1,0:T(8,128)(2,1)S(1)}, u32[]{:S(2)}, u32[]{:S(2)}) collective-permute-start(bf16[128,1536]{1,0:T(8,128)(2,1)S(1)} %collective-permute-done.refs_8_), channel_id=1, source_target_pairs={{0,2},{1,3},{2,0},{3,1},{4,6},{5,7},{6,4},{7,5},{8,10},{9,11},{10,... | collective-permute-start | bytes 1179656 | tf_op jit(solution)/shard_map/ppermute | solution.py:457
  59.9 21.0 %collective-permute-start.22 = (bf16[128,1536]{1,0:T(8,128)(2,1)S(1)}, bf16[128,1536]{1,0:T(8,128)(2,1)S(1)}, u32[]{:S(2)}, u32[]{:S(2)}) collective-permute-start(bf16[128,1536]{1,0:T(8,128)(2,1)S(1)} %collective-permute-done.11.refs_6_), channel_id=1, source_target_pairs={{0,2},{1,3},{2,0},{3,1},{4,6},{5,7},{6,4},{7,5},{8,10},{9,11},{10,... | collective-permute-start | bytes 1179656 | tf_op jit(solution)/shard_map/ppermute | solution.py:457
  69.1 5.0 %collective-permute-start.15 = (bf16[48,512]{1,0:T(8,128)(2,1)S(1)}, bf16[48,512]{1,0:T(8,128)(2,1)S(1)}, u32[]{:S(2)}, u32[]{:S(2)}) collective-permute-start(bf16[48,512]{1,0:T(8,128)(2,1)S(1)} %get-tuple-element.131), channel_id=1, source_target_pairs={{0,5},{1,4},{2,7},{3,6},{4,1},{5,0},{6,3},{7,2},{8,13},{9,12},{10,... | collective-permute-start | bytes 147464 | tf_op jit(solution)/shard_map/ppermute | solution.py:457
  74.8 17.5 %collective-permute-start.24 = (bf16[128,1536]{1,0:T(8,128)(2,1)S(1)}, bf16[128,1536]{1,0:T(8,128)(2,1)S(1)}, u32[]{:S(2)}, u32[]{:S(2)}) collective-permute-start(bf16[128,1536]{1,0:T(8,128)(2,1)S(1)} %collective-permute-done.16.refs_10_), channel_id=1, source_target_pairs={{0,2},{1,3},{2,0},{3,1},{4,6},{5,7},{6,4},{7,5},{8,10},{9,11},{10,... | collective-permute-start | bytes 1179656 | tf_op jit(solution)/shard_map/ppermute | solution.py:457
  79.1 6.0 %collective-permute-start.20 = (bf16[2,48,512]{2,1,0:T(8,128)(2,1)S(1)}, bf16[2,48,512]{2,1,0:T(8,128)(2,1)S(1)}, u32[]{:S(2)}, u32[]{:S(2)}) collective-permute-start(bf16[2,48,512]{2,1,0:T(8,128)(2,1)S(1)} %shard_map.146.refs_0_), channel_id=1, source_target_pairs={{0,5},{1,4},{2,7},{3,6},{4,1},{5,0},{6,3},{7,2},{8,13},{9,12},{10,... | collective-permute-start | bytes 294920 | tf_op jit(solution)/shard_map/ppermute | solution.py:457
  79.8 8.0 %collective-permute-start.19 = (bf16[2,48,512]{2,1,0:T(8,128)(2,1)S(1)}, bf16[2,48,512]{2,1,0:T(8,128)(2,1)S(1)}, u32[]{:S(2)}, u32[]{:S(2)}) collective-permute-start(bf16[2,48,512]{2,1,0:T(8,128)(2,1)S(1)} %shard_map.146.refs_0_), channel_id=1, source_target_pairs={{0,4},{1,5},{2,6},{3,7},{4,0},{5,1},{6,2},{7,3},{8,12},{9,13},{10,... | collective-permute-start | bytes 294920 | tf_op jit(solution)/shard_map/ppermute | solution.py:457
  80.6 13.1 %collective-permute-start.25 = (bf16[2,384,128]{2,1,0:T(8,128)(2,1)S(1)}, bf16[2,384,128]{2,1,0:T(8,128)(2,1)S(1)}, u32[]{:S(2)}, u32[]{:S(2)}) collective-permute-start(bf16[2,384,128]{2,1,0:T(8,128)(2,1)S(1)} %get-tuple-element.141), channel_id=1, source_target_pairs={{0,8},{1,9},{2,10},{3,11},{4,12},{5,13},{6,14},{7,15},{8,0},{9,1},... | collective-permute-start | bytes 589832 | tf_op jit(solution)/shard_map/ppermute | solution.py:457
  80.9 17.4 %collective-permute-start.26 = (bf16[2,384,128]{2,1,0:T(8,128)(2,1)S(1)}, bf16[2,384,128]{2,1,0:T(8,128)(2,1)S(1)}, u32[]{:S(2)}, u32[]{:S(2)}) collective-permute-start(bf16[2,384,128]{2,1,0:T(8,128)(2,1)S(1)} %get-tuple-element.142), channel_id=1, source_target_pairs={{0,16},{1,17},{2,18},{3,19},{4,20},{5,21},{6,22},{7,23},{8,24},{9,... | collective-permute-start | bytes 589832 | tf_op jit(solution)/shard_map/ppermute | solution.py:457
  85.1 13.2 %collective-permute-start.27 = (bf16[2,384,128]{2,1,0:T(8,128)(2,1)S(1)}, bf16[2,384,128]{2,1,0:T(8,128)(2,1)S(1)}, u32[]{:S(2)}, u32[]{:S(2)}) collective-permute-start(bf16[2,384,128]{2,1,0:T(8,128)(2,1)S(1)} %get-tuple-element.143), channel_id=1, source_target_pairs={{0,24},{1,25},{2,26},{3,27},{4,28},{5,29},{6,30},{7,31},{8,16},{9,... | collective-permute-start | bytes 589832 | tf_op jit(solution)/shard_map/ppermute | solution.py:457
  87.7 4.6 %collective-permute-start.18 = (bf16[2,48,512]{2,1,0:T(8,128)(2,1)S(1)}, bf16[2,48,512]{2,1,0:T(8,128)(2,1)S(1)}, u32[]{:S(2)}, u32[]{:S(2)}) collective-permute-start(bf16[2,48,512]{2,1,0:T(8,128)(2,1)S(1)} %shard_map.146.refs_0_), channel_id=1, source_target_pairs={{0,1},{1,0},{2,3},{3,2},{4,5},{5,4},{6,7},{7,6},{8,9},{9,8},{10,11... | collective-permute-start | bytes 294920 | tf_op jit(solution)/shard_map/ppermute | solution.py:457
  98.3 18.3 %collective-permute-start.28 = (bf16[192,896]{1,0:T(8,128)(2,1)S(1)}, bf16[192,896]{1,0:T(8,128)(2,1)S(1)}, u32[]{:S(2)}, u32[]{:S(2)}) collective-permute-start(bf16[192,896]{1,0:T(8,128)(2,1)S(1)} %get-tuple-element.144), channel_id=1, source_target_pairs={{0,16},{1,17},{2,18},{3,19},{4,20},{5,21},{6,22},{7,23},{8,24},{9,... | collective-permute-start | bytes 1032200 | tf_op jit(solution)/shard_map/ppermute | solution.py:457
  117.8 7.0 %collective-permute-start.33 = (bf16[4,48,512]{2,1,0:T(8,128)(2,1)S(1)}, bf16[4,48,512]{2,1,0:T(8,128)(2,1)S(1)}, u32[]{:S(2)}, u32[]{:S(2)}) collective-permute-start(bf16[4,48,512]{2,1,0:T(8,128)(2,1)S(1)} %get-tuple-element.150), channel_id=1, source_target_pairs={{0,1},{1,0},{2,3},{3,2},{4,5},{5,4},{6,7},{7,6},{8,9},{9,8},{10,11... | collective-permute-start | bytes 589832 | tf_op jit(solution)/shard_map/ppermute | solution.py:457
  119.6 7.8 %collective-permute-start.34 = (bf16[4,48,512]{2,1,0:T(8,128)(2,1)S(1)}, bf16[4,48,512]{2,1,0:T(8,128)(2,1)S(1)}, u32[]{:S(2)}, u32[]{:S(2)}) collective-permute-start(bf16[4,48,512]{2,1,0:T(8,128)(2,1)S(1)} %get-tuple-element.151), channel_id=1, source_target_pairs={{0,4},{1,5},{2,6},{3,7},{4,0},{5,1},{6,2},{7,3},{8,12},{9,13},{10,... | collective-permute-start | bytes 589832 | tf_op jit(solution)/shard_map/ppermute | solution.py:457
  120.7 9.2 %collective-permute-start.35 = (bf16[4,48,512]{2,1,0:T(8,128)(2,1)S(1)}, bf16[4,48,512]{2,1,0:T(8,128)(2,1)S(1)}, u32[]{:S(2)}, u32[]{:S(2)}) collective-permute-start(bf16[4,48,512]{2,1,0:T(8,128)(2,1)S(1)} %get-tuple-element.152), channel_id=1, source_target_pairs={{0,5},{1,4},{2,7},{3,6},{4,1},{5,0},{6,3},{7,2},{8,13},{9,12},{10,... | collective-permute-start | bytes 589832 | tf_op jit(solution)/shard_map/ppermute | solution.py:457
  130.8 4.5 %collective-permute-start.36 = (bf16[5,16,512]{2,1,0:T(8,128)(2,1)S(1)}, bf16[5,16,512]{2,1,0:T(8,128)(2,1)S(1)}, u32[]{:S(2)}, u32[]{:S(2)}) collective-permute-start(bf16[5,16,512]{2,1,0:T(8,128)(2,1)S(1)} %get-tuple-element.154), channel_id=1, source_target_pairs={{0,8},{1,9},{2,10},{3,11},{4,12},{5,13},{6,14},{7,15},{8,0},{9,1},... | collective-permute-start | bytes 245768 | tf_op jit(solution)/shard_map/ppermute | solution.py:457
  130.9 8.4 %collective-permute-start.37 = (bf16[5,16,512]{2,1,0:T(8,128)(2,1)S(1)}, bf16[5,16,512]{2,1,0:T(8,128)(2,1)S(1)}, u32[]{:S(2)}, u32[]{:S(2)}) collective-permute-start(bf16[5,16,512]{2,1,0:T(8,128)(2,1)S(1)} %get-tuple-element.155), channel_id=1, source_target_pairs={{0,16},{1,17},{2,18},{3,19},{4,20},{5,21},{6,22},{7,23},{8,24},{9,... | collective-permute-start | bytes 245768 | tf_op jit(solution)/shard_map/ppermute | solution.py:457
  131.3 8.0 %collective-permute-start.38 = (bf16[5,16,512]{2,1,0:T(8,128)(2,1)S(1)}, bf16[5,16,512]{2,1,0:T(8,128)(2,1)S(1)}, u32[]{:S(2)}, u32[]{:S(2)}) collective-permute-start(bf16[5,16,512]{2,1,0:T(8,128)(2,1)S(1)} %get-tuple-element.156), channel_id=1, source_target_pairs={{0,24},{1,25},{2,26},{3,27},{4,28},{5,29},{6,30},{7,31},{8,16},{9,... | collective-permute-start | bytes 245768 | tf_op jit(solution)/shard_map/ppermute | solution.py:457
  (26 other events, 132.0 us)

commit v3 on v2

--- a/solution.py
+++ b/solution.py
@@ -207,81 +207,90 @@
     out[...] = total.astype(BF16)
 
 
-def stack_kernel(*refs):
-    *parts, out = refs
-    for k, part in enumerate(parts):
-        out[k] = part[...]
-
-
 def split_gate_up_kernel(planes, sides, idx, gate, up, *outs):
-    half = planes // 2
-    units = outs[0].shape[1] // 4
-    side, near, far = idx[3], idx[0] % half, idx[0] // half
-    for k in range(half):
+    units = outs[0].shape[1] // (2 * planes)
+    for c, out in enumerate(outs):
+        for k in range(planes):
+            chip = (idx[0] ^ k) * sides + (idx[3] ^ c)
+            at = pl.ds(pl.multiple_of(chip * units, units), units)
+            out[:, 2 * k * units:(2 * k + 1) * units] = gate[:, at]
+            out[:, (2 * k + 1) * units:(2 * k + 2) * units] = up[:, at]
+
+
+def split_rows_kernel(planes, per, idx, down, heads, message, own, own_heads, core_heads):
+    sides = per // 2
+    units, head_rows = own.shape[1], own_heads.shape[0]
+    for k in range(planes):
         for c in range(sides):
-            chip = (near ^ k) * sides + (side ^ c)
-            for i in range(2):
-                start = pl.multiple_of((chip * 2 + (far ^ i)) * units, units)
-                out = outs[k * sides + c]
-                out[:, 2 * i * units:(2 * i + 1) * units] = gate[:, pl.ds(start, units)]
-                out[:, (2 * i + 1) * units:(2 * i + 2) * units] = up[:, pl.ds(start, units)]
-
-
-def split_down_kernel(planes, idx, weight, *outs):
-    half = planes // 2
-    sides = len(outs)
-    units = outs[0].shape[1]
-    for k in range(planes):
-        z = idx[0] ^ k
-        for c, out in enumerate(outs):
-            chip = (z % half) * sides + (idx[3] ^ c)
-            start = pl.multiple_of((chip * 2 + z // half) * units, units)
-            out[k] = weight[pl.ds(start, units), :]
-
-
-def regroup_kernel(*refs):
-    many = refs[-1].shape[0]
-    parts, outs = refs[:many], refs[many:]
+            chip = (idx[0] ^ k) * sides + (idx[3] ^ c)
+            start = pl.multiple_of(chip * units, units)
+            rows = down[pl.ds(start, units), :]
+            if c:
+                message[k * units:(k + 1) * units] = rows
+            else:
+                own[k] = rows
+    for c in range(per):
+        rows = heads[pl.ds(pl.multiple_of((idx[2] ^ c) * head_rows, head_rows), head_rows), :]
+        if c == 0:
+            own_heads[...] = rows
+        elif c == 1:
+            core_heads[...] = rows
+        else:
+            start = planes * units + (c - 2) * head_rows
+            message[start:start + head_rows] = rows
+
+
+def regroup_kernel(own, message, *outs):
+    *downs, near_heads, far_heads = outs
+    units, head_rows = own.shape[1], near_heads.shape[0]
+    for k, out in enumerate(downs):
+        out[0] = own[k]
+        out[1] = message[k * units:(k + 1) * units]
+    start = len(downs) * units
+    near_heads[...] = message[start:start + head_rows]
+    far_heads[...] = message[start + head_rows:start + 2 * head_rows]
+
+
+def gate_up_kernel(blocks, per, planes, idx, *refs):
+    parts, pieces = refs[:blocks], refs[blocks:blocks + per]
+    gain, same, *outs, held = refs[blocks + per:]
+    x = jnp.concatenate([part[...] for part in parts]).astype(F32)
+    rows, width = x.shape
+    lanes = width // per
+    square = jnp.sum(x * x, axis=1, keepdims=True)
+    held[...] = (x * gain[idx[0]]).astype(BF16)
+    x = [held[:, pl.ds(pl.multiple_of((idx[2] ^ c) * lanes, lanes), lanes)] for c in range(per)]
+    x = jnp.concatenate(x, axis=1)
+    columns = pieces[0].shape[1] // planes
+    lane = lax.broadcasted_iota(jnp.int32, (rows, HEAD_SIZE), 1)
+    high = square.astype(BF16).astype(F32)
+    terms = jnp.where(lane == 0, high, jnp.where(lane == 1, square - high, 0.0)).astype(BF16)
+    terms = lax.dot_general(terms, same[...], (((0,), (0,)), ((), ())), preferred_element_type=F32)
     for k, out in enumerate(outs):
-        for c, part in enumerate(parts):
-            out[c] = part[k]
-
-
-def gate_up_kernel(blocks, per, idx, *refs):
-    parts, pieces = refs[:blocks], refs[blocks:-4]
-    gain, keep, send, held = refs[-4:]
-    half, share, width = parts[0].shape
-    lanes = width // per
-    z, q = idx[0], idx[2]
-    total = square = 0.0
-    for k in range(half):
-        x = jnp.concatenate([part[k] for part in parts]).astype(F32)
-        square = square + jnp.sum(x * x, axis=1, keepdims=True)
-        held[k] = (x * gain[z ^ k]).astype(BF16)
-        x = [held[k, :, pl.ds(pl.multiple_of((q ^ c) * lanes, lanes), lanes)] for c in range(per)]
-        w = jnp.concatenate([pieces[k * per + c][...] for c in range(per)])
-        total = total + dot(jnp.concatenate(x, axis=1), w)
-    columns = total.shape[1] // 2
-    lane = lax.broadcasted_iota(jnp.int32, (blocks * share, HEAD_SIZE), 1)
-    keep[:, :columns] = total[:, :columns]
-    keep[:, columns:] = jnp.where(lane == 0, square, 0.0)
-    send[:, :columns] = total[:, columns:].astype(BF16)
-    high = square.astype(BF16).astype(F32)
-    low = square - high
-    send[:, columns:] = jnp.where(lane == 0, high, jnp.where(lane == 1, low, 0.0)).astype(BF16)
-
-
-def down_kernel(planes, per, features, idx, keep, got, *refs):
-    pieces, own, sends = refs[:planes * 2], refs[planes * 2], refs[planes * 2 + 1:]
-    total = keep[...] + got[...].astype(F32)
-    units = (total.shape[1] - HEAD_SIZE) // 2
-    square = jnp.sum(total[:, 2 * units:], axis=1, keepdims=True)
+        at = slice(k * columns, (k + 1) * columns)
+        total = dot(x, jnp.concatenate([piece[:, at] for piece in pieces]))
+        out[:rows] = total.astype(out.dtype)
+        out[rows:] = jnp.zeros((out.shape[0] - rows, columns), out.dtype)
+        out[rows:, :rows] = terms[:out.shape[0] - rows].astype(out.dtype)
+
+
+def down_kernel(planes, per, features, idx, *refs):
+    totals, pieces, same = refs[:planes], refs[planes:3 * planes], refs[3 * planes]
+    own, *sends = refs[3 * planes + 1:]
+    many = same.shape[0]
+    total = totals[0][:many]
+    terms = totals[0][many:, :many]
+    for part in totals[1:]:
+        total = total + part[:many].astype(F32)
+        terms = jnp.concatenate([terms, part[many:, :many].astype(F32)])
+    units = total.shape[1] // 2
+    square = lax.dot_general(same[...], terms.astype(BF16), NT, preferred_element_type=F32)
+    square = jnp.sum(square, axis=1, keepdims=True)
     factor = lax.rsqrt(square / features + 1e-06)
-    gate, up = total[:, :units] * factor, total[:, units:2 * units] * factor
+    gate, up = total[:, :units] * factor, total[:, units:] * factor
     activated = (gate / (1.0 + jnp.exp(-gate)) * up).astype(BF16)
     z, q = idx[0], idx[2]
     rows = own.shape[1]
-    sides = per // 2
     for k in range(planes):
         w = [pieces[(c % 2) * planes + k][c // 2] for c in range(per)]
         y = dot(activated, jnp.concatenate(w, axis=1))
@@ -292,82 +301,6 @@
             own[z ^ k, :, at] = block[:rows]
             for i, send in enumerate(sends):
                 send[z ^ k, :, at] = block[(i + 1) * rows:(i + 2) * rows].astype(BF16)
-
-
-def head_rows_kernel(idx, weight, *outs):
-    rows = outs[0].shape[0]
-    for c, out in enumerate(outs):
-        out[...] = weight[pl.ds(pl.multiple_of((idx[2] ^ c) * rows, rows), rows), :]
-
-
-def split_kernel(planes, wide, nearest, idx, weight, *outs):
-    sides = len(outs) if not nearest else outs[0].shape[0]
-    units = outs[0].shape[2 if wide else 1]
-    for k in range(planes):
-        for c in range(sides):
-            chip = (idx[0] ^ k) * sides + (idx[3] ^ c)
-            at = pl.ds(pl.multiple_of(chip * units, units), units)
-            block = weight[:, at] if wide else weight[at, :]
-            if nearest:
-                outs[k][c] = block
-            else:
-                outs[c][k] = block
-
-
-def regroup_kernel(*refs):
-    many = refs[-1].shape[0]
-    parts, outs = refs[:many], refs[many:]
-    for k, out in enumerate(outs):
-        for c, part in enumerate(parts):
-            out[c] = part[k]
-
-
-def ffn_kernel(blocks, planes, idx, *refs):
-    parts, refs = refs[:blocks], refs[blocks:]
-    held = refs[-1]
-    own, *sends = refs[-1 - blocks:-1]
-    per = held.shape[2] // HEAD_SIZE
-    lanes = held.shape[2] // per
-    pieces = refs[:-1 - blocks]
-    near = per // 2 * 2
-    far = planes * 2
-    starts = (0, near, near + far, near + 2 * far)
-    z, q = idx[0], idx[2]
-    gate = up = 0.0
-
-    def piece(which, k, c):
-        got = pieces[starts[which]:starts[which + 1]]
-        side, core = c // 2, c % 2
-        sides = per // 2
-        if which:
-            return got[core * planes + k][side]
-        return got[core * sides + side][k]
-
-    for k in range(planes):
-        x = jnp.concatenate([part[z ^ k] for part in parts])
-        held[k] = x
-        x = [held[k, :, pl.ds(pl.multiple_of((q ^ c) * lanes, lanes), lanes)] for c in range(per)]
-        x = jnp.concatenate(x, axis=1)
-        w = jnp.concatenate([piece(0, k, c) for c in range(per)])
-        gate = gate + dot(x, w)
-        w = jnp.concatenate([piece(1, k, c) for c in range(per)])
-        up = up + dot(x, w)
-    activated = (gate / (1.0 + jnp.exp(-gate)) * up).astype(BF16)
-    rows = own.shape[1]
-    for k in range(planes):
-        y = dot(activated, jnp.concatenate([piece(2, k, c) for c in range(per)], axis=1))
-        for c in range(per):
-            at = pl.ds(pl.multiple_of((q ^ c) * lanes, lanes), lanes)
-            block = y[:, c * lanes:(c + 1) * lanes]
-            own[z ^ k, :, at] = block[:rows]
-            for i, send in enumerate(sends):
-                send[z ^ k, :, at] = block[(i + 1) * rows:(i + 2) * rows].astype(BF16)
-
-
-def head_rows_kernel(idx, weight, *outs):
-    rows = outs[0].shape[0]
-    for c, out in enumerate(outs):
-        out[...] = weight[pl.ds(pl.multiple_of((idx[2] ^ c) * rows, rows), rows), :]
 
 
 def row_of(z, k, tokens, rows, total):
@@ -465,24 +398,16 @@
     def plane_exchange(x):
         return lax.all_to_all(x, axes, 0, 0, axis_index_groups=plane_groups, tiled=True)
 
-    def after(xs, later):
-        return lax.optimization_barrier((xs, later))
+    def after(*xs):
+        return lax.optimization_barrier(xs)
 
     width = features // planes
     sides = per // 2
     units = gate_weight.shape[1] // (planes * sides)
 
-    def within_plane(parts):
-        return [x if not c else swap(x, c * n_uly) for c, x in enumerate(parts)]
-
     def across_planes(parts):
         return [x if not k else swap(x, k * group) for k, x in enumerate(parts)]
 
-    def regroup(parts):
-        shape = (len(parts),) + parts[0].shape[1:]
-        return call(regroup_kernel, [like(*shape)] * parts[0].shape[0], *parts)
-
-    half = planes // 2
     lot = group * rows
     pair = 2 * HEAD_SIZE
     head_groups = call(
@@ -490,24 +415,26 @@
         like(group, rows, 2 * heads * HEAD_SIZE + pair),
         query_projection, gate_proj, key_projection, value_projection,
     )
-    masks = [k * group + c * 2 * n_uly for k in range(half) for c in range(sides)]
-    head_groups, (gate_weight, up_weight, down_weight, out_weight, positions) = after(
-        head_groups, (gate_weight, up_weight, down_weight, out_weight, positions)
-    )
+    head_groups, gate_weight, up_weight, down_weight, out_weight, positions = after(
+        head_groups, gate_weight, up_weight, down_weight, out_weight, positions
+    )
+    side = 2 * n_uly
     gate_up = call(
         functools.partial(split_gate_up_kernel, planes, sides),
-        [like(gate_weight.shape[0], 4 * units)] * len(masks),
+        [like(gate_weight.shape[0], 2 * planes * units)] * sides,
         idx, gate_weight, up_weight,
     )
-    head_rows = call(
-        head_rows_kernel,
-        [like(out_weight.shape[0] // per, out_weight.shape[1])] * per,
-        idx, out_weight,
-    )
-    down_parts = call(
-        functools.partial(split_down_kernel, planes),
-        [like(planes, units, down_weight.shape[1])] * sides,
-        idx, down_weight,
+    head_rows = out_weight.shape[0] // per
+    lanes = out_weight.shape[1]
+    message, own_down, wo_own, wo_core = call(
+        functools.partial(split_rows_kernel, planes, per),
+        [
+            like(planes * units + 2 * head_rows, lanes),
+            like(planes, units, lanes),
+            like(head_rows, lanes),
+            like(head_rows, lanes),
+        ],
+        idx, down_weight, out_weight,
     )
     spots = jnp.pad(
         positions.reshape(planes, group, tokens).astype(F32),
@@ -515,9 +442,9 @@
         constant_values=NO_POSITION,
     ).reshape(planes, 1, group * rows)
     own_heads = plane_exchange(head_groups)
-    gate_up[sides] = swap(gate_up[sides], masks[sides])
-    own_heads, (gate_up, head_rows, down_parts, spots) = after(
-        own_heads, (gate_up, head_rows, down_parts, spots)
+    wo_core = swap(wo_core, core)
+    own_heads, message, gate_up, wo_core, spots = after(
+        own_heads, message, gate_up, wo_core, spots
     )
     messages = across_planes(
         call(
@@ -526,9 +453,9 @@
             idx, own_heads, residual,
         )
     )
-    wo = within_plane(head_rows)
-    down_parts[1] = swap(down_parts[1], masks[1])
-    gate_up[1] = swap(gate_up[1], masks[1])
+    message = swap(message, side)
+    *messages, gate_up[1] = after(*messages, gate_up[1])
+    gate_up[1] = swap(gate_up[1], side)
     pick = np.zeros((group, tokens, group, rows), np.float32)
     for b in range(group):
         for t in range(tokens):
@@ -539,11 +466,17 @@
         like(group * tokens, heads * HEAD_SIZE),
         idx, prefix_len, own_heads, *messages, spots, pick,
     )
-    gated, (wo, down_parts, gate_up[3]) = after(gated, (wo, down_parts, gate_up[3]))
+    gated, message, own_gate_up = after(gated, message, gate_up[0])
+    *down_parts, wo_near, wo_far = call(
+        regroup_kernel,
+        [like(sides, units, lanes)] * planes + [like(head_rows, lanes)] * 2,
+        own_down, message,
+    )
     gateds = [gated] + swap_planes(gated)
-    gate_up[3] = swap(gate_up[3], masks[3])
-    gateds, (gate_up[1], down_parts) = after(gateds, (gate_up[1], regroup(down_parts)))
-    down_parts = across_planes(down_parts)
+    wo = [wo_own, wo_core, wo_near, swap(wo_far, core)]
+    twin = [swap(own_gate_up, core), None]
+    gateds, wo, down_parts, twin[0] = after(gateds, wo, down_parts, twin[0])
+    down_parts[2] = swap(down_parts[2], 2 * group)
 
     turn = np.zeros((group, planes, tokens, planes, group, tokens), np.float32)
     for i, b in enumerate(order):
@@ -567,32 +500,34 @@
         [like(share, width, dtype=F32)] + [like(share, width)] * len(steps),
         keep, swap(send, core),
     )
+    rest, gate_up[1] = after(rest, gate_up[1])
+    twin[1] = swap(gate_up[1], core)
     hidden = call(
         functools.partial(hidden_kernel, planes, tokens),
         like(share, width),
         idx, own, *[swap(x, b) for x, b in zip(rest, steps)], *messages,
     )
-    hidden, gate_up[3] = after(hidden, gate_up[3])
-    near_hidden = [hidden] + [swap(hidden, k * group) for k in range(1, half)]
-    gate_up = [x for both in zip(gate_up, [swap(x, core) for x in gate_up]) for x in both]
-    block = call(stack_kernel, like(half, share, width), *near_hidden)
-    blocks = [block] + [swap(block, b) for b in steps]
-    keep, send = call(
-        functools.partial(gate_up_kernel, len(blocks), per),
-        [
-            like(len(blocks) * share, 2 * units + HEAD_SIZE, dtype=F32),
-            like(len(blocks) * share, 2 * units + HEAD_SIZE),
-        ],
-        idx, *blocks, *gate_up, norm_gain.reshape(planes, 1, width),
-        scratch=[pltpu.VMEM((half, len(blocks) * share, width), BF16)],
-    )
-    send, down_parts = after(send, down_parts)
-    got = swap(send, half * group)
+    hidden, twin[1], down_parts[3] = after(hidden, twin[1], down_parts[3])
+    blocks = [hidden] + [swap(hidden, b) for b in steps]
+    same = jnp.eye(len(blocks) * share, dtype=BF16)
+    down_parts[3] = swap(down_parts[3], 3 * group)
+    pieces = [x for both in zip(gate_up, twin) for x in both]
+    many = len(blocks) * share
+    keep, *sends = call(
+        functools.partial(gate_up_kernel, len(blocks), per, planes),
+        [like(many + ROW_TILE, 2 * units, dtype=F32)]
+        + [like(many + ROW_TILE, 2 * units)] * (planes - 1),
+        idx, *blocks, *pieces, norm_gain.reshape(planes, 1, width), same,
+        scratch=[pltpu.VMEM((many, width), BF16)],
+    )
+    sends, down_parts[2:3], down_parts[1] = after(sends, down_parts[2:3], down_parts[1])
+    totals = across_planes([keep] + sends)
+    down_parts[1] = swap(down_parts[1], group)
     down_share = down_parts + [swap(x, core) for x in down_parts]
     own, *rest = call(
         functools.partial(down_kernel, planes, per, features),
         [like(planes, share, width, dtype=F32)] + [like(planes, share, width)] * len(steps),
-        idx, keep, got, *down_share,
+        idx, *totals, *down_share, same,
     )
     parts = call(
         functools.partial(plane_sum_kernel, planes, tokens),

time: 141 us -> 131 us (0.929)
  waiting for transfers between devices: 74.6 us -> 59.3 us
  starting transfers between devices: 45.2 us -> 51.9 us
    ppermute x39 -> x35, waiting for transfers between devices: 71.4 us -> 57.6 us  [swap(): return lax.ppermute(x, axes, [(i, i ^ mask) for i in range(devices)])]
    ppermute x39 -> x35, starting transfers between devices: 41.4 us -> 46.6 us  [swap(): return lax.ppermute(x, axes, [(i, i ^ mask) for i in range(devices)])]
    all_to_all x1, starting transfers between devices: 3.72 us -> 5.3 us  [plane_exchange(): lax.all_to_all(x, axes, 0, 0, axis_index_groups=plane_groups, tiled=True)]
    all_to_all x1, waiting for transfers between devices: 3.27 us -> 1.7 us  [plane_exchange(): lax.all_to_all(x, axes, 0, 0, axis_index_groups=plane_groups, tiled=True)]
    pallas_call x15 -> x13, Pallas kernels: 12.6 us -> 11.6 us  [call(): pl.pallas_call(kernel, out_shape=shapes, in_specs=[SMEM if a.dtype == jnp...]
    unnamed x36 -> x32, local copies, waits for them, and re-layouts: 6.91 us -> 6.31 us
  transfers between devices with their start and end apart: 40 -> 36, of which waited for: 25 -> 19; matrix products, arithmetic and copies ran while one was open for 0% -> 0% of each run, Pallas kernels for 5% -> 6%
where the time goes in v3:
time: 131 us; the launch traced here: 130 us
  waiting for transfers between devices  59.3 us (45%)
  starting transfers between devices  51.9 us (40%)
  Pallas kernels  11.6 us (9%)
  local copies, waits for them, and re-layouts  6.5 us (5%)
    ppermute x35, waiting for transfers between devices, swap(): return lax.ppermute(x, axes, [(i, i ^ mask) for i in range(devices)])  57.6 us
    ppermute x35, starting transfers between devices, swap(): return lax.ppermute(x, axes, [(i, i ^ mask) for i in range(devices)])  46.6 us
    pallas_call x13, Pallas kernels, call(): pl.pallas_call(kernel, out_shape=shapes, in_specs=[SMEM if a.dtype == jnp...  11.6 us
    unnamed x32, local copies, waits for them, and re-layouts  6.31 us
    all_to_all x1, starting transfers between devices, plane_exchange(): lax.all_to_all(x, axes, 0, 0, axis_index_groups=plane_groups, tiled=True)  5.3 us
  transfers between devices with their start and end apart: 36, of which 19 were waited for; matrix products, arithmetic and copies ran while one was open for 0% of the time, Pallas kernels for 6%

profile of v3, /device:TPU:0, one launch (start us, length us, event | category | flops | bytes accessed | tf_op | source)
XLA Modules:
  0.0 130.3 jit_solution(13514094311992784340)
XLA Ops:
  4.2 5.3 %all-to-all-start = ((bf16[8,16,1280]{2,1,0:T(8,128)(2,1)}), bf16[8,16,1280]{2,1,0:T(8,128)(2,1)S(1)}, u32[]{:S(2)}, u32[]{:S(2)}) async-start(bf16[8,16,1280]{2,1,0:T(8,128)(2,1)} %shard_map.136), calls=%async_computation | async-start | bytes 655360 | tf_op jit(solution)/shard_map/all_to_all | solution.py:399
  14.5 1.7 %all-to-all-done.heads.qg = bf16[8,16,1280]{2,1,0:T(8,128)(2,1)S(1)} async-done(((bf16[8,16,1280]{2,1,0:T(8,128)(2,1)}), bf16[8,16,1280]{2,1,0:T(8,128)(2,1)S(1)}, u32[]{:S(2)}, u32[]{:S(2)}) %all-to-all-start) | async-done | bytes 327712 | tf_op jit(solution)/shard_map/all_to_all | solution.py:399
  18.1 1.6 %collective-permute-start.1 = (bf16[160,256]{1,0:T(8,128)(2,1)S(1)}, bf16[160,256]{1,0:T(8,128)(2,1)S(1)}, u32[]{:S(2)}, u32[]{:S(2)}) collective-permute-start(bf16[160,256]{1,0:T(8,128)(2,1)S(1)} %get-tuple-element.96), channel_id=1, source_target_pairs={{0,8},{1,9},{2,10},{3,11},{4,12},{5,13},{6,14},{7,15},{8,0},{9,1},... | collective-permute-start | bytes 245768 | tf_op jit(solution)/shard_map/ppermute | solution.py:390
  19.8 2.6 %collective-permute-start.2 = (bf16[160,256]{1,0:T(8,128)(2,1)S(1)}, bf16[160,256]{1,0:T(8,128)(2,1)S(1)}, u32[]{:S(2)}, u32[]{:S(2)}) collective-permute-start(bf16[160,256]{1,0:T(8,128)(2,1)S(1)} %get-tuple-element.97), channel_id=1, source_target_pairs={{0,16},{1,17},{2,18},{3,19},{4,20},{5,21},{6,22},{7,23},{8,24},{9,... | collective-permute-start | bytes 245768 | tf_op jit(solution)/shard_map/ppermute | solution.py:390
  23.3 5.7 %collective-permute-done.2.refs_2_.refs_6_ = bf16[160,256]{1,0:T(8,128)(2,1)S(1)} collective-permute-done((bf16[160,256]{1,0:T(8,128)(2,1)S(1)}, bf16[160,256]{1,0:T(8,128)(2,1)S(1)}, u32[]{:S(2)}, u32[]{:S(2)}) %collective-permute-start.2) | collective-permute-done | bytes 81952 | tf_op jit(solution)/shard_map/ppermute | solution.py:390
  29.0 1.9 %shard_map.140.refs_0_ = bf16[96,512]{1,0:T(8,128)(2,1)S(1)} custom-call(s32[4]{0:T(128)S(1)} %pad_add_fusion.idx, s32[1]{0:T(128)S(6)} %copy.15.prefix, bf16[8,16,1280]{2,1,0:T(8,128)(2,1)S(1)} %all-to-all-done.heads.qg, bf16[160,256]{1,0:T(8,128)(2,1)S(1)} %get-tuple-element.100.refs_0_.refs_4_, ...), custom_call_target="tpu_custom_call" | custom-call | tf_op jit(solution)/shard_map/pallas_call | solution.py:341
  30.9 2.5 %collective-permute-done.4.message = bf16[2560,128]{1,0:T(8,128)(2,1)S(1)} collective-permute-done((bf16[2560,128]{1,0:T(8,128)(2,1)}, bf16[2560,128]{1,0:T(8,128)(2,1)S(1)}, u32[]{:S(2)}, u32[]{:S(2)}) %collective-permute-start.4) | collective-permute-done | bytes 655392 | tf_op jit(solution)/shard_map/ppermute | solution.py:390
  34.5 1.6 %collective-permute-start.5 = (bf16[96,512]{1,0:T(8,128)(2,1)S(1)}, bf16[96,512]{1,0:T(8,128)(2,1)S(1)}, u32[]{:S(2)}, u32[]{:S(2)}) collective-permute-start(bf16[96,512]{1,0:T(8,128)(2,1)S(1)} %shard_map.140.refs_0_), channel_id=1, source_target_pairs={{0,8},{1,9},{2,10},{3,11},{4,12},{5,13},{6,14},{7,15},{8,0},{9,1},... | collective-permute-start | bytes 294920 | tf_op jit(solution)/shard_map/ppermute | solution.py:390
  36.3 2.7 %collective-permute-start.6 = (bf16[96,512]{1,0:T(8,128)(2,1)S(1)}, bf16[96,512]{1,0:T(8,128)(2,1)S(1)}, u32[]{:S(2)}, u32[]{:S(2)}) collective-permute-start(bf16[96,512]{1,0:T(8,128)(2,1)S(1)} %shard_map.140.refs_0_), channel_id=1, source_target_pairs={{0,16},{1,17},{2,18},{3,19},{4,20},{5,21},{6,22},{7,23},{8,24},{9,... | collective-permute-start | bytes 294920 | tf_op jit(solution)/shard_map/ppermute | solution.py:390
  39.5 4.7 %collective-permute-start.7 = (bf16[96,512]{1,0:T(8,128)(2,1)S(1)}, bf16[96,512]{1,0:T(8,128)(2,1)S(1)}, u32[]{:S(2)}, u32[]{:S(2)}) collective-permute-start(bf16[96,512]{1,0:T(8,128)(2,1)S(1)} %shard_map.140.refs_0_), channel_id=1, source_target_pairs={{0,24},{1,25},{2,26},{3,27},{4,28},{5,29},{6,30},{7,31},{8,16},{9,... | collective-permute-start | bytes 294920 | tf_op jit(solution)/shard_map/ppermute | solution.py:390
  44.1 2.9 %collective-permute-done.6.refs_2_ = bf16[96,512]{1,0:T(8,128)(2,1)S(1)} collective-permute-done((bf16[96,512]{1,0:T(8,128)(2,1)S(1)}, bf16[96,512]{1,0:T(8,128)(2,1)S(1)}, u32[]{:S(2)}, u32[]{:S(2)}) %collective-permute-start.6) | collective-permute-done | bytes 98336 | tf_op jit(solution)/shard_map/ppermute | solution.py:390
  48.4 1.4 %collective-permute-done.10.got = bf16[192,512]{1,0:T(8,128)(2,1)S(1)} collective-permute-done((bf16[192,512]{1,0:T(8,128)(2,1)S(1)}, bf16[192,512]{1,0:T(8,128)(2,1)S(1)}, u32[]{:S(2)}, u32[]{:S(2)}) %collective-permute-start.10) | collective-permute-done | bytes 196640 | tf_op jit(solution)/shard_map/ppermute | solution.py:390
  49.8 3.5 %collective-permute-done.11.refs_6_ = bf16[128,3072]{1,0:T(8,128)(2,1)S(1)} collective-permute-done((bf16[128,3072]{1,0:T(8,128)(2,1)S(1)}, bf16[128,3072]{1,0:T(8,128)(2,1)S(1)}, u32[]{:S(2)}, u32[]{:S(2)}) %collective-permute-start.11) | collective-permute-done | bytes 786464 | tf_op jit(solution)/shard_map/ppermute | solution.py:390
  54.9 1.9 %collective-permute-start.14 = (bf16[48,512]{1,0:T(8,128)(2,1)S(1)}, bf16[48,512]{1,0:T(8,128)(2,1)S(1)}, u32[]{:S(2)}, u32[]{:S(2)}) collective-permute-start(bf16[48,512]{1,0:T(8,128)(2,1)S(1)} %get-tuple-element.136), channel_id=1, source_target_pairs={{0,5},{1,4},{2,7},{3,6},{4,1},{5,0},{6,3},{7,2},{8,13},{9,12},{10,... | collective-permute-start | bytes 147464 | tf_op jit(solution)/shard_map/ppermute | solution.py:390
  56.8 2.6 %collective-permute-start.19 = (bf16[2,384,128]{2,1,0:T(8,128)(2,1)S(1)}, bf16[2,384,128]{2,1,0:T(8,128)(2,1)S(1)}, u32[]{:S(2)}, u32[]{:S(2)}) collective-permute-start(bf16[2,384,128]{2,1,0:T(8,128)(2,1)S(1)} %get-tuple-element.146), channel_id=1, source_target_pairs={{0,16},{1,17},{2,18},{3,19},{4,20},{5,21},{6,22},{7,23},{8,24},{9,... | collective-permute-start | bytes 589832 | tf_op jit(solution)/shard_map/ppermute | solution.py:390
  60.6 1.7 %collective-permute-start.16 = (bf16[48,512]{1,0:T(8,128)(2,1)S(1)}, bf16[48,512]{1,0:T(8,128)(2,1)S(1)}, u32[]{:S(2)}, u32[]{:S(2)}) collective-permute-start(bf16[48,512]{1,0:T(8,128)(2,1)S(1)} %shard_map.144.refs_0_.hidden), channel_id=1, source_target_pairs={{0,1},{1,0},{2,3},{3,2},{4,5},{5,4},{6,7},{7,6},{8,9},{9,8},{10,11... | collective-permute-start | bytes 147464 | tf_op jit(solution)/shard_map/ppermute | solution.py:390
  62.3 3.6 %collective-permute-start.24 = (bf16[2,384,128]{2,1,0:T(8,128)(2,1)S(1)}, bf16[2,384,128]{2,1,0:T(8,128)(2,1)S(1)}, u32[]{:S(2)}, u32[]{:S(2)}) collective-permute-start(bf16[2,384,128]{2,1,0:T(8,128)(2,1)S(1)} %get-tuple-element.154), channel_id=1, source_target_pairs={{0,24},{1,25},{2,26},{3,27},{4,28},{5,29},{6,30},{7,31},{8,16},{9,... | collective-permute-start | bytes 589832 | tf_op jit(solution)/shard_map/ppermute | solution.py:390
  67.8 2.6 %collective-permute-done.17.refs_2_ = bf16[48,512]{1,0:T(8,128)(2,1)S(1)} collective-permute-done((bf16[48,512]{1,0:T(8,128)(2,1)S(1)}, bf16[48,512]{1,0:T(8,128)(2,1)S(1)}, u32[]{:S(2)}, u32[]{:S(2)}) %collective-permute-start.17) | collective-permute-done | bytes 49184 | tf_op jit(solution)/shard_map/ppermute | solution.py:390
  71.8 1.5 %shard_map.145 = (f32[208,768]{1,0:T(8,128)S(1)}, bf16[208,768]{1,0:T(8,128)(2,1)S(1)}, bf16[208,768]{1,0:T(8,128)(2,1)S(1)}, bf16[208,768]{1,0:T(8,128)(2,1)S(1)}) custom-call(s32[4]{0:T(128)S(1)} %pad_add_fusion.idx, bf16[48,512]{1,0:T(8,128)(2,1)S(1)} %shard_map.144.refs_0_.hidden, bf16[48,512]{1,0:T(8,128)(2,1)S(1)} %collective-permute-done.16.refs_1_, ...), custom_call_target="tpu_custom_call" | custom-call | tf_op jit(solution)/shard_map/pallas_call | solution.py:341
  73.7 2.0 %collective-permute-start.20 = (bf16[208,768]{1,0:T(8,128)(2,1)S(1)}, bf16[208,768]{1,0:T(8,128)(2,1)S(1)}, u32[]{:S(2)}, u32[]{:S(2)}) collective-permute-start(bf16[208,768]{1,0:T(8,128)(2,1)S(1)} %get-tuple-element.148), channel_id=1, source_target_pairs={{0,8},{1,9},{2,10},{3,11},{4,12},{5,13},{6,14},{7,15},{8,0},{9,1},... | collective-permute-start | bytes 958472 | tf_op jit(solution)/shard_map/ppermute | solution.py:390
  76.8 1.5 %collective-permute-start.22 = (bf16[208,768]{1,0:T(8,128)(2,1)S(1)}, bf16[208,768]{1,0:T(8,128)(2,1)S(1)}, u32[]{:S(2)}, u32[]{:S(2)}) collective-permute-start(bf16[208,768]{1,0:T(8,128)(2,1)S(1)} %get-tuple-element.150), channel_id=1, source_target_pairs={{0,24},{1,25},{2,26},{3,27},{4,28},{5,29},{6,30},{7,31},{8,16},{9,... | collective-permute-start | bytes 958472 | tf_op jit(solution)/shard_map/ppermute | solution.py:390
  78.3 10.1 %collective-permute-done.23.refs_5_ = bf16[2,384,128]{2,1,0:T(8,128)(2,1)S(1)} collective-permute-done((bf16[2,384,128]{2,1,0:T(8,128)(2,1)S(1)}, bf16[2,384,128]{2,1,0:T(8,128)(2,1)S(1)}, u32[]{:S(2)}, u32[]{:S(2)}) %collective-permute-start.23) | collective-permute-done | bytes 196640 | tf_op jit(solution)/shard_map/ppermute | solution.py:390
  88.9 4.0 %collective-permute-done.20.refs_1_ = bf16[208,768]{1,0:T(8,128)(2,1)S(1)} collective-permute-done((bf16[208,768]{1,0:T(8,128)(2,1)S(1)}, bf16[208,768]{1,0:T(8,128)(2,1)S(1)}, u32[]{:S(2)}, u32[]{:S(2)}) %collective-permute-start.20) | collective-permute-done | bytes 319520 | tf_op jit(solution)/shard_map/ppermute | solution.py:390
  92.9 8.9 %collective-permute-done.22.refs_3_ = bf16[208,768]{1,0:T(8,128)(2,1)S(1)} collective-permute-done((bf16[208,768]{1,0:T(8,128)(2,1)S(1)}, bf16[208,768]{1,0:T(8,128)(2,1)S(1)}, u32[]{:S(2)}, u32[]{:S(2)}) %collective-permute-start.22) | collective-permute-done | bytes 319520 | tf_op jit(solution)/shard_map/ppermute | solution.py:390
  101.8 1.4 %shard_map.146 = (f32[4,48,512]{2,1,0:T(8,128)S(1)}, bf16[4,48,512]{2,1,0:T(8,128)(2,1)S(1)}, bf16[4,48,512]{2,1,0:T(8,128)(2,1)S(1)}, bf16[4,48,512]{2,1,0:T(8,128)(2,1)S(1)}) custom-call(s32[4]{0:T(128)S(1)} %pad_add_fusion.idx, f32[208,768]{1,0:T(8,128)S(1)} %get-tuple-element.142.refs_0_, bf16[208,768]{1,0:T(8,128)(2,1)S(1)} %collective-permute-done.20.refs_1_, ...), custom_call_target="tpu_custom_call" | custom-call | tf_op jit(solution)/shard_map/pallas_call | solution.py:341
  104.9 1.9 %collective-permute-start.31 = (bf16[4,48,512]{2,1,0:T(8,128)(2,1)S(1)}, bf16[4,48,512]{2,1,0:T(8,128)(2,1)S(1)}, u32[]{:S(2)}, u32[]{:S(2)}) collective-permute-start(bf16[4,48,512]{2,1,0:T(8,128)(2,1)S(1)} %get-tuple-element.158), channel_id=1, source_target_pairs={{0,5},{1,4},{2,7},{3,6},{4,1},{5,0},{6,3},{7,2},{8,13},{9,12},{10,... | collective-permute-start | bytes 589832 | tf_op jit(solution)/shard_map/ppermute | solution.py:390
  106.8 3.4 %collective-permute-done.29.refs_1_ = bf16[4,48,512]{2,1,0:T(8,128)(2,1)S(1)} collective-permute-done((bf16[4,48,512]{2,1,0:T(8,128)(2,1)S(1)}, bf16[4,48,512]{2,1,0:T(8,128)(2,1)S(1)}, u32[]{:S(2)}, u32[]{:S(2)}) %collective-permute-start.29) | collective-permute-done | bytes 196640 | tf_op jit(solution)/shard_map/ppermute | solution.py:390
  110.2 1.7 %collective-permute-done.30.refs_2_ = bf16[4,48,512]{2,1,0:T(8,128)(2,1)S(1)} collective-permute-done((bf16[4,48,512]{2,1,0:T(8,128)(2,1)S(1)}, bf16[4,48,512]{2,1,0:T(8,128)(2,1)S(1)}, u32[]{:S(2)}, u32[]{:S(2)}) %collective-permute-start.30) | collective-permute-done | bytes 196640 | tf_op jit(solution)/shard_map/ppermute | solution.py:390
  112.0 2.9 %collective-permute-done.31.refs_3_ = bf16[4,48,512]{2,1,0:T(8,128)(2,1)S(1)} collective-permute-done((bf16[4,48,512]{2,1,0:T(8,128)(2,1)S(1)}, bf16[4,48,512]{2,1,0:T(8,128)(2,1)S(1)}, u32[]{:S(2)}, u32[]{:S(2)}) %collective-permute-start.31) | collective-permute-done | bytes 196640 | tf_op jit(solution)/shard_map/ppermute | solution.py:390
  115.7 5.8 %collective-permute-start.32 = (bf16[5,16,512]{2,1,0:T(8,128)(2,1)S(1)}, bf16[5,16,512]{2,1,0:T(8,128)(2,1)S(1)}, u32[]{:S(2)}, u32[]{:S(2)}) collective-permute-start(bf16[5,16,512]{2,1,0:T(8,128)(2,1)S(1)} %get-tuple-element.160), channel_id=1, source_target_pairs={{0,8},{1,9},{2,10},{3,11},{4,12},{5,13},{6,14},{7,15},{8,0},{9,1},... | collective-permute-start | bytes 245768 | tf_op jit(solution)/shard_map/ppermute | solution.py:390
  122.6 1.4 %collective-permute-start.34 = (bf16[5,16,512]{2,1,0:T(8,128)(2,1)S(1)}, bf16[5,16,512]{2,1,0:T(8,128)(2,1)S(1)}, u32[]{:S(2)}, u32[]{:S(2)}) collective-permute-start(bf16[5,16,512]{2,1,0:T(8,128)(2,1)S(1)} %get-tuple-element.162), channel_id=1, source_target_pairs={{0,24},{1,25},{2,26},{3,27},{4,28},{5,29},{6,30},{7,31},{8,16},{9,... | collective-permute-start | bytes 245768 | tf_op jit(solution)/shard_map/ppermute | solution.py:390
  124.6 4.5 %collective-permute-done.33.refs_2_ = bf16[5,16,512]{2,1,0:T(8,128)(2,1)S(1)} collective-permute-done((bf16[5,16,512]{2,1,0:T(8,128)(2,1)S(1)}, bf16[5,16,512]{2,1,0:T(8,128)(2,1)S(1)}, u32[]{:S(2)}, u32[]{:S(2)}) %collective-permute-start.33) | collective-permute-done | bytes 81952 | tf_op jit(solution)/shard_map/ppermute | solution.py:390
  (91 shorter events, 28.0 us)
Async XLA Ops:
  4.2 12.0 %all-to-all-start = ((bf16[8,16,1280]{2,1,0:T(8,128)(2,1)}), bf16[8,16,1280]{2,1,0:T(8,128)(2,1)S(1)}, u32[]{:S(2)}, u32[]{:S(2)}) async-start(bf16[8,16,1280]{2,1,0:T(8,128)(2,1)} %shard_map.136), calls=%async_computation | async-start | bytes 655360 | tf_op jit(solution)/shard_map/all_to_all | solution.py:399
  16.2 17.1 %collective-permute-start.4 = (bf16[2560,128]{1,0:T(8,128)(2,1)}, bf16[2560,128]{1,0:T(8,128)(2,1)S(1)}, u32[]{:S(2)}, u32[]{:S(2)}) collective-permute-start(bf16[2560,128]{1,0:T(8,128)(2,1)} %copy-done.14), channel_id=1, source_target_pairs={{0,4},{1,5},{2,6},{3,7},{4,0},{5,1},{6,2},{7,3},{8,12},{9,13},{10,... | collective-permute-start | bytes 1966088 | tf_op jit(solution)/shard_map/ppermute | solution.py:390
  18.1 5.1 %collective-permute-start.1 = (bf16[160,256]{1,0:T(8,128)(2,1)S(1)}, bf16[160,256]{1,0:T(8,128)(2,1)S(1)}, u32[]{:S(2)}, u32[]{:S(2)}) collective-permute-start(bf16[160,256]{1,0:T(8,128)(2,1)S(1)} %get-tuple-element.96), channel_id=1, source_target_pairs={{0,8},{1,9},{2,10},{3,11},{4,12},{5,13},{6,14},{7,15},{8,0},{9,1},... | collective-permute-start | bytes 245768 | tf_op jit(solution)/shard_map/ppermute | solution.py:390
  19.8 9.2 %collective-permute-start.2 = (bf16[160,256]{1,0:T(8,128)(2,1)S(1)}, bf16[160,256]{1,0:T(8,128)(2,1)S(1)}, u32[]{:S(2)}, u32[]{:S(2)}) collective-permute-start(bf16[160,256]{1,0:T(8,128)(2,1)S(1)} %get-tuple-element.97), channel_id=1, source_target_pairs={{0,16},{1,17},{2,18},{3,19},{4,20},{5,21},{6,22},{7,23},{8,24},{9,... | collective-permute-start | bytes 245768 | tf_op jit(solution)/shard_map/ppermute | solution.py:390
  22.4 6.6 %collective-permute-start.3 = (bf16[160,256]{1,0:T(8,128)(2,1)S(1)}, bf16[160,256]{1,0:T(8,128)(2,1)S(1)}, u32[]{:S(2)}, u32[]{:S(2)}) collective-permute-start(bf16[160,256]{1,0:T(8,128)(2,1)S(1)} %get-tuple-element.98), channel_id=1, source_target_pairs={{0,24},{1,25},{2,26},{3,27},{4,28},{5,29},{6,30},{7,31},{8,16},{9,... | collective-permute-start | bytes 245768 | tf_op jit(solution)/shard_map/ppermute | solution.py:390
  33.3 13.7 %collective-permute-start.9 = (bf16[128,3072]{1,0:T(8,128)(2,1)S(1)}, bf16[128,3072]{1,0:T(8,128)(2,1)S(1)}, u32[]{:S(2)}, u32[]{:S(2)}) collective-permute-start(bf16[128,3072]{1,0:T(8,128)(2,1)S(1)} %get-tuple-element.118.refs_4_), channel_id=1, source_target_pairs={{0,2},{1,3},{2,0},{3,1},{4,6},{5,7},{6,4},{7,5},{8,10},{9,11},{10,... | collective-permute-start | bytes 2359304 | tf_op jit(solution)/shard_map/ppermute | solution.py:390
  33.3 20.0 %collective-permute-start.11 = (bf16[128,3072]{1,0:T(8,128)(2,1)S(1)}, bf16[128,3072]{1,0:T(8,128)(2,1)S(1)}, u32[]{:S(2)}, u32[]{:S(2)}) collective-permute-start(bf16[128,3072]{1,0:T(8,128)(2,1)S(1)} %copy-done.13), channel_id=1, source_target_pairs={{0,4},{1,5},{2,6},{3,7},{4,0},{5,1},{6,2},{7,3},{8,12},{9,13},{10,... | collective-permute-start | bytes 2359304 | tf_op jit(solution)/shard_map/ppermute | solution.py:390
  36.2 10.9 %collective-permute-start.8 = (bf16[512,128]{1,0:T(8,128)(2,1)S(1)}, bf16[512,128]{1,0:T(8,128)(2,1)S(1)}, u32[]{:S(2)}, u32[]{:S(2)}) collective-permute-start(bf16[512,128]{1,0:T(8,128)(2,1)S(1)} %get-tuple-element.113), channel_id=1, source_target_pairs={{0,2},{1,3},{2,0},{3,1},{4,6},{5,7},{6,4},{7,5},{8,10},{9,11},{10,... | collective-permute-start | bytes 393224 | tf_op jit(solution)/shard_map/ppermute | solution.py:390
  36.3 10.8 %collective-permute-start.6 = (bf16[96,512]{1,0:T(8,128)(2,1)S(1)}, bf16[96,512]{1,0:T(8,128)(2,1)S(1)}, u32[]{:S(2)}, u32[]{:S(2)}) collective-permute-start(bf16[96,512]{1,0:T(8,128)(2,1)S(1)} %shard_map.140.refs_0_), channel_id=1, source_target_pairs={{0,16},{1,17},{2,18},{3,19},{4,20},{5,21},{6,22},{7,23},{8,24},{9,... | collective-permute-start | bytes 294920 | tf_op jit(solution)/shard_map/ppermute | solution.py:390
  39.5 7.6 %collective-permute-start.7 = (bf16[96,512]{1,0:T(8,128)(2,1)S(1)}, bf16[96,512]{1,0:T(8,128)(2,1)S(1)}, u32[]{:S(2)}, u32[]{:S(2)}) collective-permute-start(bf16[96,512]{1,0:T(8,128)(2,1)S(1)} %shard_map.140.refs_0_), channel_id=1, source_target_pairs={{0,24},{1,25},{2,26},{3,27},{4,28},{5,29},{6,30},{7,31},{8,16},{9,... | collective-permute-start | bytes 294920 | tf_op jit(solution)/shard_map/ppermute | solution.py:390
  53.3 7.4 %collective-permute-start.15 = (bf16[128,3072]{1,0:T(8,128)(2,1)S(1)}, bf16[128,3072]{1,0:T(8,128)(2,1)S(1)}, u32[]{:S(2)}, u32[]{:S(2)}) collective-permute-start(bf16[128,3072]{1,0:T(8,128)(2,1)S(1)} %collective-permute-done.11.refs_6_), channel_id=1, source_target_pairs={{0,2},{1,3},{2,0},{3,1},{4,6},{5,7},{6,4},{7,5},{8,10},{9,11},{10,... | collective-permute-start | bytes 2359304 | tf_op jit(solution)/shard_map/ppermute | solution.py:390
  53.3 6.1 %collective-permute-start.12 = (bf16[48,512]{1,0:T(8,128)(2,1)S(1)}, bf16[48,512]{1,0:T(8,128)(2,1)S(1)}, u32[]{:S(2)}, u32[]{:S(2)}) collective-permute-start(bf16[48,512]{1,0:T(8,128)(2,1)S(1)} %get-tuple-element.134), channel_id=1, source_target_pairs={{0,1},{1,0},{2,3},{3,2},{4,5},{5,4},{6,7},{7,6},{8,9},{9,8},{10,11... | collective-permute-start | bytes 147464 | tf_op jit(solution)/shard_map/ppermute | solution.py:390
  54.1 5.3 %collective-permute-start.13 = (bf16[48,512]{1,0:T(8,128)(2,1)S(1)}, bf16[48,512]{1,0:T(8,128)(2,1)S(1)}, u32[]{:S(2)}, u32[]{:S(2)}) collective-permute-start(bf16[48,512]{1,0:T(8,128)(2,1)S(1)} %get-tuple-element.135), channel_id=1, source_target_pairs={{0,4},{1,5},{2,6},{3,7},{4,0},{5,1},{6,2},{7,3},{8,12},{9,13},{10,... | collective-permute-start | bytes 147464 | tf_op jit(solution)/shard_map/ppermute | solution.py:390
  54.9 5.0 %collective-permute-start.14 = (bf16[48,512]{1,0:T(8,128)(2,1)S(1)}, bf16[48,512]{1,0:T(8,128)(2,1)S(1)}, u32[]{:S(2)}, u32[]{:S(2)}) collective-permute-start(bf16[48,512]{1,0:T(8,128)(2,1)S(1)} %get-tuple-element.136), channel_id=1, source_target_pairs={{0,5},{1,4},{2,7},{3,6},{4,1},{5,0},{6,3},{7,2},{8,13},{9,12},{10,... | collective-permute-start | bytes 147464 | tf_op jit(solution)/shard_map/ppermute | solution.py:390
  56.8 16.9 %collective-permute-start.19 = (bf16[2,384,128]{2,1,0:T(8,128)(2,1)S(1)}, bf16[2,384,128]{2,1,0:T(8,128)(2,1)S(1)}, u32[]{:S(2)}, u32[]{:S(2)}) collective-permute-start(bf16[2,384,128]{2,1,0:T(8,128)(2,1)S(1)} %get-tuple-element.146), channel_id=1, source_target_pairs={{0,16},{1,17},{2,18},{3,19},{4,20},{5,21},{6,22},{7,23},{8,24},{9,... | collective-permute-start | bytes 589832 | tf_op jit(solution)/shard_map/ppermute | solution.py:390
  60.6 6.1 %collective-permute-start.16 = (bf16[48,512]{1,0:T(8,128)(2,1)S(1)}, bf16[48,512]{1,0:T(8,128)(2,1)S(1)}, u32[]{:S(2)}, u32[]{:S(2)}) collective-permute-start(bf16[48,512]{1,0:T(8,128)(2,1)S(1)} %shard_map.144.refs_0_.hidden), channel_id=1, source_target_pairs={{0,1},{1,0},{2,3},{3,2},{4,5},{5,4},{6,7},{7,6},{8,9},{9,8},{10,11... | collective-permute-start | bytes 147464 | tf_op jit(solution)/shard_map/ppermute | solution.py:390
  62.3 13.4 %collective-permute-start.25 = (bf16[2,384,128]{2,1,0:T(8,128)(2,1)S(1)}, bf16[2,384,128]{2,1,0:T(8,128)(2,1)S(1)}, u32[]{:S(2)}, u32[]{:S(2)}) collective-permute-start(bf16[2,384,128]{2,1,0:T(8,128)(2,1)S(1)} %get-tuple-element.151.refs_4_), channel_id=1, source_target_pairs={{0,2},{1,3},{2,0},{3,1},{4,6},{5,7},{6,4},{7,5},{8,10},{9,11},{10,... | collective-permute-start | bytes 589832 | tf_op jit(solution)/shard_map/ppermute | solution.py:390
  62.3 14.5 %collective-permute-start.24 = (bf16[2,384,128]{2,1,0:T(8,128)(2,1)S(1)}, bf16[2,384,128]{2,1,0:T(8,128)(2,1)S(1)}, u32[]{:S(2)}, u32[]{:S(2)}) collective-permute-start(bf16[2,384,128]{2,1,0:T(8,128)(2,1)S(1)} %get-tuple-element.154), channel_id=1, source_target_pairs={{0,24},{1,25},{2,26},{3,27},{4,28},{5,29},{6,30},{7,31},{8,16},{9,... | collective-permute-start | bytes 589832 | tf_op jit(solution)/shard_map/ppermute | solution.py:390
  66.8 5.0 %collective-permute-start.18 = (bf16[48,512]{1,0:T(8,128)(2,1)S(1)}, bf16[48,512]{1,0:T(8,128)(2,1)S(1)}, u32[]{:S(2)}, u32[]{:S(2)}) collective-permute-start(bf16[48,512]{1,0:T(8,128)(2,1)S(1)} %shard_map.144.refs_0_.hidden), channel_id=1, source_target_pairs={{0,5},{1,4},{2,7},{3,6},{4,1},{5,0},{6,3},{7,2},{8,13},{9,12},{10,... | collective-permute-start | bytes 147464 | tf_op jit(solution)/shard_map/ppermute | solution.py:390
  73.7 14.7 %collective-permute-start.23 = (bf16[2,384,128]{2,1,0:T(8,128)(2,1)S(1)}, bf16[2,384,128]{2,1,0:T(8,128)(2,1)S(1)}, u32[]{:S(2)}, u32[]{:S(2)}) collective-permute-start(bf16[2,384,128]{2,1,0:T(8,128)(2,1)S(1)} %get-tuple-element.152), channel_id=1, source_target_pairs={{0,8},{1,9},{2,10},{3,11},{4,12},{5,13},{6,14},{7,15},{8,0},{9,1},... | collective-permute-start | bytes 589832 | tf_op jit(solution)/shard_map/ppermute | solution.py:390
  73.7 14.7 %collective-permute-start.27 = (bf16[2,384,128]{2,1,0:T(8,128)(2,1)S(1)}, bf16[2,384,128]{2,1,0:T(8,128)(2,1)S(1)}, u32[]{:S(2)}, u32[]{:S(2)}) collective-permute-start(bf16[2,384,128]{2,1,0:T(8,128)(2,1)S(1)} %collective-permute-done.19.refs_6_), channel_id=1, source_target_pairs={{0,2},{1,3},{2,0},{3,1},{4,6},{5,7},{6,4},{7,5},{8,10},{9,11},{10,... | collective-permute-start | bytes 589832 | tf_op jit(solution)/shard_map/ppermute | solution.py:390
  73.7 19.2 %collective-permute-start.20 = (bf16[208,768]{1,0:T(8,128)(2,1)S(1)}, bf16[208,768]{1,0:T(8,128)(2,1)S(1)}, u32[]{:S(2)}, u32[]{:S(2)}) collective-permute-start(bf16[208,768]{1,0:T(8,128)(2,1)S(1)} %get-tuple-element.148), channel_id=1, source_target_pairs={{0,8},{1,9},{2,10},{3,11},{4,12},{5,13},{6,14},{7,15},{8,0},{9,1},... | collective-permute-start | bytes 958472 | tf_op jit(solution)/shard_map/ppermute | solution.py:390
  75.8 17.2 %collective-permute-start.21 = (bf16[208,768]{1,0:T(8,128)(2,1)S(1)}, bf16[208,768]{1,0:T(8,128)(2,1)S(1)}, u32[]{:S(2)}, u32[]{:S(2)}) collective-permute-start(bf16[208,768]{1,0:T(8,128)(2,1)S(1)} %get-tuple-element.149), channel_id=1, source_target_pairs={{0,16},{1,17},{2,18},{3,19},{4,20},{5,21},{6,22},{7,23},{8,24},{9,... | collective-permute-start | bytes 958472 | tf_op jit(solution)/shard_map/ppermute | solution.py:390
  76.8 25.0 %collective-permute-start.22 = (bf16[208,768]{1,0:T(8,128)(2,1)S(1)}, bf16[208,768]{1,0:T(8,128)(2,1)S(1)}, u32[]{:S(2)}, u32[]{:S(2)}) collective-permute-start(bf16[208,768]{1,0:T(8,128)(2,1)S(1)} %get-tuple-element.150), channel_id=1, source_target_pairs={{0,24},{1,25},{2,26},{3,27},{4,28},{5,29},{6,30},{7,31},{8,16},{9,... | collective-permute-start | bytes 958472 | tf_op jit(solution)/shard_map/ppermute | solution.py:390
  88.4 13.4 %collective-permute-start.28 = (bf16[2,384,128]{2,1,0:T(8,128)(2,1)S(1)}, bf16[2,384,128]{2,1,0:T(8,128)(2,1)S(1)}, u32[]{:S(2)}, u32[]{:S(2)}) collective-permute-start(bf16[2,384,128]{2,1,0:T(8,128)(2,1)S(1)} %collective-permute-done.24.refs_7_), channel_id=1, source_target_pairs={{0,2},{1,3},{2,0},{3,1},{4,6},{5,7},{6,4},{7,5},{8,10},{9,11},{10,... | collective-permute-start | bytes 589832 | tf_op jit(solution)/shard_map/ppermute | solution.py:390
  88.4 13.4 %collective-permute-start.26 = (bf16[2,384,128]{2,1,0:T(8,128)(2,1)S(1)}, bf16[2,384,128]{2,1,0:T(8,128)(2,1)S(1)}, u32[]{:S(2)}, u32[]{:S(2)}) collective-permute-start(bf16[2,384,128]{2,1,0:T(8,128)(2,1)S(1)} %collective-permute-done.23.refs_5_), channel_id=1, source_target_pairs={{0,2},{1,3},{2,0},{3,1},{4,6},{5,7},{6,4},{7,5},{8,10},{9,11},{10,... | collective-permute-start | bytes 589832 | tf_op jit(solution)/shard_map/ppermute | solution.py:390
  103.2 7.0 %collective-permute-start.29 = (bf16[4,48,512]{2,1,0:T(8,128)(2,1)S(1)}, bf16[4,48,512]{2,1,0:T(8,128)(2,1)S(1)}, u32[]{:S(2)}, u32[]{:S(2)}) collective-permute-start(bf16[4,48,512]{2,1,0:T(8,128)(2,1)S(1)} %get-tuple-element.156), channel_id=1, source_target_pairs={{0,1},{1,0},{2,3},{3,2},{4,5},{5,4},{6,7},{7,6},{8,9},{9,8},{10,11... | collective-permute-start | bytes 589832 | tf_op jit(solution)/shard_map/ppermute | solution.py:390
  104.1 7.8 %collective-permute-start.30 = (bf16[4,48,512]{2,1,0:T(8,128)(2,1)S(1)}, bf16[4,48,512]{2,1,0:T(8,128)(2,1)S(1)}, u32[]{:S(2)}, u32[]{:S(2)}) collective-permute-start(bf16[4,48,512]{2,1,0:T(8,128)(2,1)S(1)} %get-tuple-element.157), channel_id=1, source_target_pairs={{0,4},{1,5},{2,6},{3,7},{4,0},{5,1},{6,2},{7,3},{8,12},{9,13},{10,... | collective-permute-start | bytes 589832 | tf_op jit(solution)/shard_map/ppermute | solution.py:390
  104.9 9.9 %collective-permute-start.31 = (bf16[4,48,512]{2,1,0:T(8,128)(2,1)S(1)}, bf16[4,48,512]{2,1,0:T(8,128)(2,1)S(1)}, u32[]{:S(2)}, u32[]{:S(2)}) collective-permute-start(bf16[4,48,512]{2,1,0:T(8,128)(2,1)S(1)} %get-tuple-element.158), channel_id=1, source_target_pairs={{0,5},{1,4},{2,7},{3,6},{4,1},{5,0},{6,3},{7,2},{8,13},{9,12},{10,... | collective-permute-start | bytes 589832 | tf_op jit(solution)/shard_map/ppermute | solution.py:390
  115.7 8.9 %collective-permute-start.32 = (bf16[5,16,512]{2,1,0:T(8,128)(2,1)S(1)}, bf16[5,16,512]{2,1,0:T(8,128)(2,1)S(1)}, u32[]{:S(2)}, u32[]{:S(2)}) collective-permute-start(bf16[5,16,512]{2,1,0:T(8,128)(2,1)S(1)} %get-tuple-element.160), channel_id=1, source_target_pairs={{0,8},{1,9},{2,10},{3,11},{4,12},{5,13},{6,14},{7,15},{8,0},{9,1},... | collective-permute-start | bytes 245768 | tf_op jit(solution)/shard_map/ppermute | solution.py:390
  121.5 7.6 %collective-permute-start.33 = (bf16[5,16,512]{2,1,0:T(8,128)(2,1)S(1)}, bf16[5,16,512]{2,1,0:T(8,128)(2,1)S(1)}, u32[]{:S(2)}, u32[]{:S(2)}) collective-permute-start(bf16[5,16,512]{2,1,0:T(8,128)(2,1)S(1)} %get-tuple-element.161), channel_id=1, source_target_pairs={{0,16},{1,17},{2,18},{3,19},{4,20},{5,21},{6,22},{7,23},{8,24},{9,... | collective-permute-start | bytes 245768 | tf_op jit(solution)/shard_map/ppermute | solution.py:390
  122.6 6.5 %collective-permute-start.34 = (bf16[5,16,512]{2,1,0:T(8,128)(2,1)S(1)}, bf16[5,16,512]{2,1,0:T(8,128)(2,1)S(1)}, u32[]{:S(2)}, u32[]{:S(2)}) collective-permute-start(bf16[5,16,512]{2,1,0:T(8,128)(2,1)S(1)} %get-tuple-element.162), channel_id=1, source_target_pairs={{0,24},{1,25},{2,26},{3,27},{4,28},{5,29},{6,30},{7,31},{8,16},{9,... | collective-permute-start | bytes 245768 | tf_op jit(solution)/shard_map/ppermute | solution.py:390
  (20 other events, 97.1 us)

commit v4 on v3

--- a/solution.py
+++ b/solution.py
@@ -12,7 +12,6 @@
 HEAD_SIZE = 128
 ROW_TILE = 16
 HIDE = -1e30
-NO_POSITION = float(2**30)
 F32 = jnp.float32
 BF16 = jnp.bfloat16
 VMEM = pl.BlockSpec(memory_space=pltpu.VMEM)
@@ -104,25 +103,33 @@
 
 
 def pack_heads_kernel(head_of, *refs):
-    *parts, out = refs
+    many = (len(refs) - 2) // 2
+    parts, out, held, sems = refs[:many], refs[many], refs[many + 1:-1], refs[-1]
+    copies = [
+        pltpu.make_async_copy(part, spot, sems.at[i])
+        for i, (part, spot) in enumerate(zip(parts, held))
+    ]
+    for copy in copies:
+        copy.start()
+    out[...] = jnp.zeros_like(out)
     tokens = parts[0].shape[0]
-    out[...] = jnp.zeros_like(out)
-    for r, j in enumerate(head_of):
-        start = 0
-        for part in parts:
-            width = part.shape[1] // len(head_of)
-            out[r, :tokens, start:start + width] = part[:, j * width:(j + 1) * width]
-            start += width
-
-
-def message_kernel(planes, idx, heads, residual, *outs):
-    group, rows, whole = heads.shape
+    start = 0
+    for copy, spot in zip(copies, held):
+        copy.wait()
+        width = spot.shape[1] // len(head_of)
+        for r, j in enumerate(head_of):
+            out[r, :tokens, start:start + width] = spot[:, j * width:(j + 1) * width]
+        start += width
+
+
+def message_kernel(planes, idx, heads, residual, pick, *outs):
+    group, rows, _ = heads.shape
     tokens, features = residual.shape
     pair = 2 * HEAD_SIZE
-    lot = group * rows
     width = features // planes
     z = idx[0]
-    keys = heads[:, :, whole - pair:].reshape(lot, pair)
+    keys = dot(pick[...], heads[:, :, :pair].reshape(group * rows, pair)).astype(BF16)
+    lot = keys.shape[0]
     for k, out in enumerate(outs):
         out[:lot] = keys
         out[lot:] = jnp.zeros((out.shape[0] - lot, pair), BF16)
@@ -135,25 +142,26 @@
     messages, (spots, pick, out) = refs[:planes], refs[planes:]
     group, rows, _ = qg.shape
     z, r = idx[0], idx[1]
-    lot = group * rows
+    lot, held = group * rows, pick.shape[0]
+    tokens = held // group
     keys, values, key_spot = [], [], []
     for k in range(planes):
-        keys.append(messages[k][:lot, :HEAD_SIZE])
-        values.append(messages[k][:lot, HEAD_SIZE:])
+        keys.append(messages[k][:held, :HEAD_SIZE])
+        values.append(messages[k][:held, HEAD_SIZE:])
         key_spot.append(spots[z ^ k])
     keys, values = jnp.concatenate(keys), jnp.concatenate(values)
     key_spot = jnp.concatenate(key_spot, axis=1)
-    i = lax.broadcasted_iota(jnp.int32, (lot, lot), 0)
-    j = lax.broadcasted_iota(jnp.int32, (lot, lot), 1)
-    own = jnp.where((i ^ (r * rows)) == j, spots[z], 0.0)
-    query_spot = jnp.sum(own, axis=1, keepdims=True)
+    i = lax.broadcasted_iota(jnp.int32, (lot, held), 0) ^ (r * rows)
+    j = lax.broadcasted_iota(jnp.int32, (lot, held), 1)
+    source = i // rows * tokens + jnp.minimum(i % rows, tokens - 1)
+    query_spot = jnp.sum(jnp.where(source == j, spots[z], 0.0), axis=1, keepdims=True)
     visible = (key_spot <= query_spot) | (key_spot < prefix[0].astype(F32))
     bias = jnp.where(visible, 0.0, HIDE)
     scale = 1.0 / math.sqrt(HEAD_SIZE)
     done = []
     for h in range(heads):
-        at = slice(h * HEAD_SIZE, (h + 1) * HEAD_SIZE)
-        gate_at = slice((heads + h) * HEAD_SIZE, (heads + h + 1) * HEAD_SIZE)
+        at = slice((h + 2) * HEAD_SIZE, (h + 3) * HEAD_SIZE)
+        gate_at = slice((heads + h + 2) * HEAD_SIZE, (heads + h + 3) * HEAD_SIZE)
         q = jnp.concatenate([qg[b ^ r, :, at] for b in range(group)])
         gate = jnp.concatenate([qg[b ^ r, :, gate_at] for b in range(group)]).astype(F32)
         s = lax.dot_general(q, keys, NT, preferred_element_type=F32) * scale + bias
@@ -205,6 +213,12 @@
         held = [message[lot + c * rows:lot + (c + 1) * rows] for c in range(pieces)]
         total = total + dot(place, jnp.concatenate(held, axis=1))
     out[...] = total.astype(BF16)
+
+
+def stack_kernel(*refs):
+    *parts, out = refs
+    for k, part in enumerate(parts):
+        out[k] = part[...]
 
 
 def split_gate_up_kernel(planes, sides, idx, gate, up, *outs):
@@ -275,8 +289,7 @@
 
 
 def down_kernel(planes, per, features, idx, *refs):
-    totals, pieces, same = refs[:planes], refs[planes:3 * planes], refs[3 * planes]
-    own, *sends = refs[3 * planes + 1:]
+    totals, (near, far, same, own, *sends) = refs[:planes], refs[planes:]
     many = same.shape[0]
     total = totals[0][:many]
     terms = totals[0][many:, :many]
@@ -292,7 +305,7 @@
     z, q = idx[0], idx[2]
     rows = own.shape[1]
     for k in range(planes):
-        w = [pieces[(c % 2) * planes + k][c // 2] for c in range(per)]
+        w = [(far if c % 2 else near)[k, c // 2] for c in range(per)]
         y = dot(activated, jnp.concatenate(w, axis=1))
         lanes = w[0].shape[1]
         for c in range(per):
@@ -335,16 +348,16 @@
         out[:, p * width:(p + 1) * width] = value[:tokens].astype(BF16)
 
 
-def call(kernel, outs, *args, scratch=()):
+def call(kernel, outs, *args, scratch=(), place=VMEM, limit=16):
     single = not isinstance(outs, list)
     shapes = [outs] if single else outs
     got = pl.pallas_call(
         kernel,
         out_shape=shapes,
-        in_specs=[SMEM if a.dtype == jnp.int32 else VMEM for a in args],
+        in_specs=[SMEM if a.dtype == jnp.int32 else place for a in args],
         out_specs=[VMEM] * len(shapes),
         scratch_shapes=list(scratch),
-        compiler_params=pltpu.CompilerParams(vmem_limit_bytes=16 * 2**20),
+        compiler_params=pltpu.CompilerParams(vmem_limit_bytes=limit * 2**20),
     )(*args)
     return got[0] if single else list(got)
 
@@ -408,12 +421,16 @@
     def across_planes(parts):
         return [x if not k else swap(x, k * group) for k, x in enumerate(parts)]
 
-    lot = group * rows
     pair = 2 * HEAD_SIZE
+    tokens_in = (key_projection, value_projection, query_projection, gate_proj)
     head_groups = call(
         functools.partial(pack_heads_kernel, head_of),
         like(group, rows, 2 * heads * HEAD_SIZE + pair),
-        query_projection, gate_proj, key_projection, value_projection,
+        *tokens_in,
+        scratch=[pltpu.VMEM(x.shape, x.dtype) for x in tokens_in]
+        + [pltpu.SemaphoreType.DMA((len(tokens_in),))],
+        place=pl.BlockSpec(memory_space=pl.ANY),
+        limit=60,
     )
     head_groups, gate_weight, up_weight, down_weight, out_weight, positions = after(
         head_groups, gate_weight, up_weight, down_weight, out_weight, positions
@@ -436,37 +453,34 @@
         ],
         idx, down_weight, out_weight,
     )
-    spots = jnp.pad(
-        positions.reshape(planes, group, tokens).astype(F32),
-        ((0, 0), (0, 0), (0, rows - tokens)),
-        constant_values=NO_POSITION,
-    ).reshape(planes, 1, group * rows)
+    spots = positions.astype(F32).reshape(planes, 1, group * tokens)
     own_heads = plane_exchange(head_groups)
     wo_core = swap(wo_core, core)
     own_heads, message, gate_up, wo_core, spots = after(
         own_heads, message, gate_up, wo_core, spots
     )
-    messages = across_planes(
-        call(
-            functools.partial(message_kernel, planes),
-            [like(lot + rows * width // pair, pair)] * planes,
-            idx, own_heads, residual,
-        )
-    )
-    message = swap(message, side)
-    *messages, gate_up[1] = after(*messages, gate_up[1])
-    gate_up[1] = swap(gate_up[1], side)
     pick = np.zeros((group, tokens, group, rows), np.float32)
     for b in range(group):
         for t in range(tokens):
             pick[b, t, b, t] = 1
     pick = jnp.asarray(pick.reshape(group * tokens, group * rows), BF16)
+    messages = across_planes(
+        call(
+            functools.partial(message_kernel, planes),
+            [like(group * tokens + rows * width // pair, pair)] * planes,
+            idx, own_heads, residual, pick,
+        )
+    )
+    message = swap(message, side)
+    twin = [swap(gate_up[0], core), None]
+    *messages, gate_up[1], twin[0] = after(*messages, gate_up[1], twin[0])
+    gate_up[1] = swap(gate_up[1], side)
     gated = call(
         functools.partial(attention_kernel, heads, planes),
         like(group * tokens, heads * HEAD_SIZE),
         idx, prefix_len, own_heads, *messages, spots, pick,
     )
-    gated, message, own_gate_up = after(gated, message, gate_up[0])
+    gated, message = after(gated, message)
     *down_parts, wo_near, wo_far = call(
         regroup_kernel,
         [like(sides, units, lanes)] * planes + [like(head_rows, lanes)] * 2,
@@ -474,9 +488,10 @@
     )
     gateds = [gated] + swap_planes(gated)
     wo = [wo_own, wo_core, wo_near, swap(wo_far, core)]
-    twin = [swap(own_gate_up, core), None]
-    gateds, wo, down_parts, twin[0] = after(gateds, wo, down_parts, twin[0])
-    down_parts[2] = swap(down_parts[2], 2 * group)
+    down_parts[1] = swap(down_parts[1], group)
+    gateds, wo, down_parts = after(gateds, wo, down_parts)
+    for k in (2, 3):
+        down_parts[k] = swap(down_parts[k], k * group)
 
     turn = np.zeros((group, planes, tokens, planes, group, tokens), np.float32)
     for i, b in enumerate(order):
@@ -501,16 +516,15 @@
         keep, swap(send, core),
     )
     rest, gate_up[1] = after(rest, gate_up[1])
-    twin[1] = swap(gate_up[1], core)
     hidden = call(
         functools.partial(hidden_kernel, planes, tokens),
         like(share, width),
         idx, own, *[swap(x, b) for x, b in zip(rest, steps)], *messages,
     )
-    hidden, twin[1], down_parts[3] = after(hidden, twin[1], down_parts[3])
+    hidden, gate_up[1], down_parts[2] = after(hidden, gate_up[1], down_parts[2])
+    twin[1] = swap(gate_up[1], core)
     blocks = [hidden] + [swap(hidden, b) for b in steps]
     same = jnp.eye(len(blocks) * share, dtype=BF16)
-    down_parts[3] = swap(down_parts[3], 3 * group)
     pieces = [x for both in zip(gate_up, twin) for x in both]
     many = len(blocks) * share
     keep, *sends = call(
@@ -520,14 +534,13 @@
         idx, *blocks, *pieces, norm_gain.reshape(planes, 1, width), same,
         scratch=[pltpu.VMEM((many, width), BF16)],
     )
-    sends, down_parts[2:3], down_parts[1] = after(sends, down_parts[2:3], down_parts[1])
+    sends, down_parts = after(sends, down_parts)
     totals = across_planes([keep] + sends)
-    down_parts[1] = swap(down_parts[1], group)
-    down_share = down_parts + [swap(x, core) for x in down_parts]
+    downs = call(stack_kernel, like(planes, *down_parts[0].shape), *down_parts)
     own, *rest = call(
         functools.partial(down_kernel, planes, per, features),
         [like(planes, share, width, dtype=F32)] + [like(planes, share, width)] * len(steps),
-        idx, *totals, *down_share, same,
+        idx, *totals, downs, swap(downs, core), same,
     )
     parts = call(
         functools.partial(plane_sum_kernel, planes, tokens),

time: 131 us -> 126 us (0.962)
  starting transfers between devices: 51.9 us -> 44.8 us
  waiting for transfers between devices: 59.3 us -> 63.5 us
  local copies, waits for them, and re-layouts: 6.5 us -> 2.97 us
  Pallas kernels: 11.6 us -> 13.4 us
    ppermute x35 -> x32, starting transfers between devices: 46.6 us -> 39.5 us  [swap(): return lax.ppermute(x, axes, [(i, i ^ mask) for i in range(devices)])]
    ppermute x35 -> x32, waiting for transfers between devices: 57.6 us -> 62.3 us  [swap(): return lax.ppermute(x, axes, [(i, i ^ mask) for i in range(devices)])]
    unnamed x32 -> x22, local copies, waits for them, and re-layouts: 6.31 us -> 2.89 us
    pallas_call x13 -> x14, Pallas kernels: 11.6 us -> 13.4 us  [call(): pl.pallas_call(kernel, out_shape=shapes, in_specs=[SMEM if a.dtype == jnp...]
  transfers between devices with their start and end apart: 36 -> 33, of which waited for: 19 -> 22; matrix products, arithmetic and copies ran while one was open for 0% -> 0% of each run, Pallas kernels for 6% -> 6%
where the time goes in v4:
time: 126 us
  waiting for transfers between devices  63.5 us (50%)
  starting transfers between devices  44.8 us (36%)
  Pallas kernels  13.4 us (11%)
  local copies, waits for them, and re-layouts  2.97 us (2%)
    ppermute x32, waiting for transfers between devices, swap(): return lax.ppermute(x, axes, [(i, i ^ mask) for i in range(devices)])  62.3 us
    ppermute x32, starting transfers between devices, swap(): return lax.ppermute(x, axes, [(i, i ^ mask) for i in range(devices)])  39.5 us
    pallas_call x14, Pallas kernels, call(): pl.pallas_call(kernel, out_shape=shapes, in_specs=[SMEM if a.dtype == jnp...  13.4 us
    all_to_all x1, starting transfers between devices, plane_exchange(): lax.all_to_all(x, axes, 0, 0, axis_index_groups=plane_groups, tiled=True)  5.31 us
    unnamed x22, local copies, waits for them, and re-layouts  2.89 us
  transfers between devices with their start and end apart: 33, of which 22 were waited for; matrix products, arithmetic and copies ran while one was open for 0% of the time, Pallas kernels for 6%

profile of v4, /device:TPU:0, one launch (start us, length us, event | category | flops | bytes accessed | tf_op | source)
XLA Modules:
  0.0 125.7 jit_solution(68851015074478631)
XLA Ops:
  0.0 1.9 %shard_map.136 = bf16[8,16,1280]{2,1,0:T(8,128)(2,1)} custom-call(bf16[12,1024]{1,0:T(8,128)(2,1)} %refs_0_.1, bf16[12,1024]{1,0:T(8,128)(2,1)} %refs_1_.1, bf16[12,4096]{1,0:T(8,128)(2,1)} %refs_2_.1, bf16[12,4096]{1,0:T(8,128)(2,1)} %refs_3_.1), custom_call_target="tpu_custom_call" | custom-call | tf_op jit(solution)/shard_map/pallas_call | solution.py:354
  1.9 5.3 %all-to-all-start = ((bf16[8,16,1280]{2,1,0:T(8,128)(2,1)}), bf16[8,16,1280]{2,1,0:T(8,128)(2,1)S(1)}, u32[]{:S(2)}, u32[]{:S(2)}) async-start(bf16[8,16,1280]{2,1,0:T(8,128)(2,1)} %shard_map.136), calls=%async_computation | async-start | bytes 655360 | tf_op jit(solution)/shard_map/all_to_all | solution.py:412
  16.1 1.6 %collective-permute-start.1 = (bf16[128,256]{1,0:T(8,128)(2,1)S(1)}, bf16[128,256]{1,0:T(8,128)(2,1)S(1)}, u32[]{:S(2)}, u32[]{:S(2)}) collective-permute-start(bf16[128,256]{1,0:T(8,128)(2,1)S(1)} %get-tuple-element.97), channel_id=1, source_target_pairs={{0,8},{1,9},{2,10},{3,11},{4,12},{5,13},{6,14},{7,15},{8,0},{9,1},... | collective-permute-start | bytes 196616 | tf_op jit(solution)/shard_map/ppermute | solution.py:403
  17.8 2.6 %collective-permute-start.2 = (bf16[128,256]{1,0:T(8,128)(2,1)S(1)}, bf16[128,256]{1,0:T(8,128)(2,1)S(1)}, u32[]{:S(2)}, u32[]{:S(2)}) collective-permute-start(bf16[128,256]{1,0:T(8,128)(2,1)S(1)} %get-tuple-element.98), channel_id=1, source_target_pairs={{0,16},{1,17},{2,18},{3,19},{4,20},{5,21},{6,22},{7,23},{8,24},{9,... | collective-permute-start | bytes 196616 | tf_op jit(solution)/shard_map/ppermute | solution.py:403
  20.6 4.7 %collective-permute-done.2.refs_2_.refs_6_ = bf16[128,256]{1,0:T(8,128)(2,1)S(1)} collective-permute-done((bf16[128,256]{1,0:T(8,128)(2,1)S(1)}, bf16[128,256]{1,0:T(8,128)(2,1)S(1)}, u32[]{:S(2)}, u32[]{:S(2)}) %collective-permute-start.2) | collective-permute-done | bytes 65568 | tf_op jit(solution)/shard_map/ppermute | solution.py:403
  28.0 1.9 %shard_map.140.refs_0_ = bf16[96,512]{1,0:T(8,128)(2,1)S(1)} custom-call(s32[4]{0:T(128)S(1)} %pad_add_fusion.idx, s32[1]{0:T(128)S(6)} %copy.15.prefix, bf16[8,16,1280]{2,1,0:T(8,128)(2,1)S(1)} %all-to-all-done.heads.qg, bf16[128,256]{1,0:T(8,128)(2,1)S(1)} %get-tuple-element.102.refs_0_.refs_4_, ...), custom_call_target="tpu_custom_call" | custom-call | tf_op jit(solution)/shard_map/pallas_call | solution.py:354
  29.8 2.1 %collective-permute-done.5.message = bf16[2560,128]{1,0:T(8,128)(2,1)S(1)} collective-permute-done((bf16[2560,128]{1,0:T(8,128)(2,1)}, bf16[2560,128]{1,0:T(8,128)(2,1)S(1)}, u32[]{:S(2)}, u32[]{:S(2)}) %collective-permute-start.5) | collective-permute-done | bytes 655392 | tf_op jit(solution)/shard_map/ppermute | solution.py:403
  32.0 3.6 %collective-permute-start.8 = (bf16[96,512]{1,0:T(8,128)(2,1)S(1)}, bf16[96,512]{1,0:T(8,128)(2,1)S(1)}, u32[]{:S(2)}, u32[]{:S(2)}) collective-permute-start(bf16[96,512]{1,0:T(8,128)(2,1)S(1)} %shard_map.140.refs_0_), channel_id=1, source_target_pairs={{0,24},{1,25},{2,26},{3,27},{4,28},{5,29},{6,30},{7,31},{8,16},{9,... | collective-permute-start | bytes 294920 | tf_op jit(solution)/shard_map/ppermute | solution.py:403
  36.5 2.9 %collective-permute-done.8.refs_3_ = bf16[96,512]{1,0:T(8,128)(2,1)S(1)} collective-permute-done((bf16[96,512]{1,0:T(8,128)(2,1)S(1)}, bf16[96,512]{1,0:T(8,128)(2,1)S(1)}, u32[]{:S(2)}, u32[]{:S(2)}) %collective-permute-start.8) | collective-permute-done | bytes 98336 | tf_op jit(solution)/shard_map/ppermute | solution.py:403
  39.4 4.7 %collective-permute-done.7.refs_2_ = bf16[96,512]{1,0:T(8,128)(2,1)S(1)} collective-permute-done((bf16[96,512]{1,0:T(8,128)(2,1)S(1)}, bf16[96,512]{1,0:T(8,128)(2,1)S(1)}, u32[]{:S(2)}, u32[]{:S(2)}) %collective-permute-start.7) | collective-permute-done | bytes 98336 | tf_op jit(solution)/shard_map/ppermute | solution.py:403
  44.1 2.1 %collective-permute-done.6.refs_1_ = bf16[96,512]{1,0:T(8,128)(2,1)S(1)} collective-permute-done((bf16[96,512]{1,0:T(8,128)(2,1)S(1)}, bf16[96,512]{1,0:T(8,128)(2,1)S(1)}, u32[]{:S(2)}, u32[]{:S(2)}) %collective-permute-start.6) | collective-permute-done | bytes 98336 | tf_op jit(solution)/shard_map/ppermute | solution.py:403
  49.0 1.9 %collective-permute-start.13 = (bf16[48,512]{1,0:T(8,128)(2,1)S(1)}, bf16[48,512]{1,0:T(8,128)(2,1)S(1)}, u32[]{:S(2)}, u32[]{:S(2)}) collective-permute-start(bf16[48,512]{1,0:T(8,128)(2,1)S(1)} %get-tuple-element.134), channel_id=1, source_target_pairs={{0,1},{1,0},{2,3},{3,2},{4,5},{5,4},{6,7},{7,6},{8,9},{9,8},{10,11... | collective-permute-start | bytes 147464 | tf_op jit(solution)/shard_map/ppermute | solution.py:403
  51.1 1.4 %collective-permute-start.15 = (bf16[48,512]{1,0:T(8,128)(2,1)S(1)}, bf16[48,512]{1,0:T(8,128)(2,1)S(1)}, u32[]{:S(2)}, u32[]{:S(2)}) collective-permute-start(bf16[48,512]{1,0:T(8,128)(2,1)S(1)} %get-tuple-element.136), channel_id=1, source_target_pairs={{0,5},{1,4},{2,7},{3,6},{4,1},{5,0},{6,3},{7,2},{8,13},{9,12},{10,... | collective-permute-start | bytes 147464 | tf_op jit(solution)/shard_map/ppermute | solution.py:403
  53.2 2.1 %collective-permute-done.14.refs_2_ = bf16[48,512]{1,0:T(8,128)(2,1)S(1)} collective-permute-done((bf16[48,512]{1,0:T(8,128)(2,1)S(1)}, bf16[48,512]{1,0:T(8,128)(2,1)S(1)}, u32[]{:S(2)}, u32[]{:S(2)}) %collective-permute-start.14) | collective-permute-done | bytes 49184 | tf_op jit(solution)/shard_map/ppermute | solution.py:403
  56.9 3.1 %collective-permute-done.16.refs_2_ = bf16[2,384,128]{2,1,0:T(8,128)(2,1)S(1)} collective-permute-done((bf16[2,384,128]{2,1,0:T(8,128)(2,1)S(1)}, bf16[2,384,128]{2,1,0:T(8,128)(2,1)S(1)}, u32[]{:S(2)}, u32[]{:S(2)}) %collective-permute-start.16) | collective-permute-done | bytes 196640 | tf_op jit(solution)/shard_map/ppermute | solution.py:403
  59.9 1.5 %collective-permute-start.21 = (bf16[2,384,128]{2,1,0:T(8,128)(2,1)S(1)}, bf16[2,384,128]{2,1,0:T(8,128)(2,1)S(1)}, u32[]{:S(2)}, u32[]{:S(2)}) collective-permute-start(bf16[2,384,128]{2,1,0:T(8,128)(2,1)S(1)} %get-tuple-element.149), channel_id=1, source_target_pairs={{0,24},{1,25},{2,26},{3,27},{4,28},{5,29},{6,30},{7,31},{8,16},{9,... | collective-permute-start | bytes 589832 | tf_op jit(solution)/shard_map/ppermute | solution.py:403
  61.5 1.4 %collective-permute-start.19 = (bf16[48,512]{1,0:T(8,128)(2,1)S(1)}, bf16[48,512]{1,0:T(8,128)(2,1)S(1)}, u32[]{:S(2)}, u32[]{:S(2)}) collective-permute-start(bf16[48,512]{1,0:T(8,128)(2,1)S(1)} %shard_map.144.refs_0_.hidden), channel_id=1, source_target_pairs={{0,5},{1,4},{2,7},{3,6},{4,1},{5,0},{6,3},{7,2},{8,13},{9,12},{10,... | collective-permute-start | bytes 147464 | tf_op jit(solution)/shard_map/ppermute | solution.py:403
  62.9 1.7 %collective-permute-start.18 = (bf16[48,512]{1,0:T(8,128)(2,1)S(1)}, bf16[48,512]{1,0:T(8,128)(2,1)S(1)}, u32[]{:S(2)}, u32[]{:S(2)}) collective-permute-start(bf16[48,512]{1,0:T(8,128)(2,1)S(1)} %shard_map.144.refs_0_.hidden), channel_id=1, source_target_pairs={{0,4},{1,5},{2,6},{3,7},{4,0},{5,1},{6,2},{7,3},{8,12},{9,13},{10,... | collective-permute-start | bytes 147464 | tf_op jit(solution)/shard_map/ppermute | solution.py:403
  65.0 1.7 %collective-permute-done.19.refs_3_ = bf16[48,512]{1,0:T(8,128)(2,1)S(1)} collective-permute-done((bf16[48,512]{1,0:T(8,128)(2,1)S(1)}, bf16[48,512]{1,0:T(8,128)(2,1)S(1)}, u32[]{:S(2)}, u32[]{:S(2)}) %collective-permute-start.19) | collective-permute-done | bytes 49184 | tf_op jit(solution)/shard_map/ppermute | solution.py:403
  68.6 1.5 %shard_map.145 = (f32[208,768]{1,0:T(8,128)S(1)}, bf16[208,768]{1,0:T(8,128)(2,1)S(1)}, bf16[208,768]{1,0:T(8,128)(2,1)S(1)}, bf16[208,768]{1,0:T(8,128)(2,1)S(1)}) custom-call(s32[4]{0:T(128)S(1)} %pad_add_fusion.idx, bf16[48,512]{1,0:T(8,128)(2,1)S(1)} %shard_map.144.refs_0_.hidden, bf16[48,512]{1,0:T(8,128)(2,1)S(1)} %collective-permute-done.17.refs_1_, ...), custom_call_target="tpu_custom_call" | custom-call | tf_op jit(solution)/shard_map/pallas_call | solution.py:354
  70.4 3.0 %collective-permute-start.23 = (bf16[208,768]{1,0:T(8,128)(2,1)S(1)}, bf16[208,768]{1,0:T(8,128)(2,1)S(1)}, u32[]{:S(2)}, u32[]{:S(2)}) collective-permute-start(bf16[208,768]{1,0:T(8,128)(2,1)S(1)} %get-tuple-element.151), channel_id=1, source_target_pairs={{0,16},{1,17},{2,18},{3,19},{4,20},{5,21},{6,22},{7,23},{8,24},{9,... | collective-permute-start | bytes 958472 | tf_op jit(solution)/shard_map/ppermute | solution.py:403
  74.8 12.0 %collective-permute-done.22.refs_1_ = bf16[208,768]{1,0:T(8,128)(2,1)S(1)} collective-permute-done((bf16[208,768]{1,0:T(8,128)(2,1)S(1)}, bf16[208,768]{1,0:T(8,128)(2,1)S(1)}, u32[]{:S(2)}, u32[]{:S(2)}) %collective-permute-start.22) | collective-permute-done | bytes 319520 | tf_op jit(solution)/shard_map/ppermute | solution.py:403
  86.8 8.7 %collective-permute-done.23.refs_2_ = bf16[208,768]{1,0:T(8,128)(2,1)S(1)} collective-permute-done((bf16[208,768]{1,0:T(8,128)(2,1)S(1)}, bf16[208,768]{1,0:T(8,128)(2,1)S(1)}, u32[]{:S(2)}, u32[]{:S(2)}) %collective-permute-start.23) | collective-permute-done | bytes 319520 | tf_op jit(solution)/shard_map/ppermute | solution.py:403
  95.5 1.4 %shard_map.147 = (f32[4,48,512]{2,1,0:T(8,128)S(1)}, bf16[4,48,512]{2,1,0:T(8,128)(2,1)S(1)}, bf16[4,48,512]{2,1,0:T(8,128)(2,1)S(1)}, bf16[4,48,512]{2,1,0:T(8,128)(2,1)S(1)}) custom-call(s32[4]{0:T(128)S(1)} %pad_add_fusion.idx, f32[208,768]{1,0:T(8,128)S(1)} %get-tuple-element.142.refs_0_, bf16[208,768]{1,0:T(8,128)(2,1)S(1)} %collective-permute-done.22.refs_1_, ...), custom_call_target="tpu_custom_call" | custom-call | tf_op jit(solution)/shard_map/pallas_call | solution.py:354
  96.9 1.6 %collective-permute-start.26 = (bf16[4,48,512]{2,1,0:T(8,128)(2,1)S(1)}, bf16[4,48,512]{2,1,0:T(8,128)(2,1)S(1)}, u32[]{:S(2)}, u32[]{:S(2)}) collective-permute-start(bf16[4,48,512]{2,1,0:T(8,128)(2,1)S(1)} %get-tuple-element.158), channel_id=1, source_target_pairs={{0,1},{1,0},{2,3},{3,2},{4,5},{5,4},{6,7},{7,6},{8,9},{9,8},{10,11... | collective-permute-start | bytes 589832 | tf_op jit(solution)/shard_map/ppermute | solution.py:403
  98.8 1.6 %collective-permute-start.28 = (bf16[4,48,512]{2,1,0:T(8,128)(2,1)S(1)}, bf16[4,48,512]{2,1,0:T(8,128)(2,1)S(1)}, u32[]{:S(2)}, u32[]{:S(2)}) collective-permute-start(bf16[4,48,512]{2,1,0:T(8,128)(2,1)S(1)} %get-tuple-element.160), channel_id=1, source_target_pairs={{0,5},{1,4},{2,7},{3,6},{4,1},{5,0},{6,3},{7,2},{8,13},{9,12},{10,... | collective-permute-start | bytes 589832 | tf_op jit(solution)/shard_map/ppermute | solution.py:403
  100.4 3.4 %collective-permute-done.26.refs_1_ = bf16[4,48,512]{2,1,0:T(8,128)(2,1)S(1)} collective-permute-done((bf16[4,48,512]{2,1,0:T(8,128)(2,1)S(1)}, bf16[4,48,512]{2,1,0:T(8,128)(2,1)S(1)}, u32[]{:S(2)}, u32[]{:S(2)}) %collective-permute-start.26) | collective-permute-done | bytes 196640 | tf_op jit(solution)/shard_map/ppermute | solution.py:403
  103.9 2.0 %collective-permute-done.27.refs_2_ = bf16[4,48,512]{2,1,0:T(8,128)(2,1)S(1)} collective-permute-done((bf16[4,48,512]{2,1,0:T(8,128)(2,1)S(1)}, bf16[4,48,512]{2,1,0:T(8,128)(2,1)S(1)}, u32[]{:S(2)}, u32[]{:S(2)}) %collective-permute-start.27) | collective-permute-done | bytes 196640 | tf_op jit(solution)/shard_map/ppermute | solution.py:403
  105.9 2.4 %collective-permute-done.28.refs_3_ = bf16[4,48,512]{2,1,0:T(8,128)(2,1)S(1)} collective-permute-done((bf16[4,48,512]{2,1,0:T(8,128)(2,1)S(1)}, bf16[4,48,512]{2,1,0:T(8,128)(2,1)S(1)}, u32[]{:S(2)}, u32[]{:S(2)}) %collective-permute-start.28) | collective-permute-done | bytes 196640 | tf_op jit(solution)/shard_map/ppermute | solution.py:403
  109.1 7.6 %collective-permute-start.29 = (bf16[5,16,512]{2,1,0:T(8,128)(2,1)S(1)}, bf16[5,16,512]{2,1,0:T(8,128)(2,1)S(1)}, u32[]{:S(2)}, u32[]{:S(2)}) collective-permute-start(bf16[5,16,512]{2,1,0:T(8,128)(2,1)S(1)} %get-tuple-element.162), channel_id=1, source_target_pairs={{0,8},{1,9},{2,10},{3,11},{4,12},{5,13},{6,14},{7,15},{8,0},{9,1},... | collective-permute-start | bytes 245768 | tf_op jit(solution)/shard_map/ppermute | solution.py:403
  117.5 1.6 %collective-permute-start.31 = (bf16[5,16,512]{2,1,0:T(8,128)(2,1)S(1)}, bf16[5,16,512]{2,1,0:T(8,128)(2,1)S(1)}, u32[]{:S(2)}, u32[]{:S(2)}) collective-permute-start(bf16[5,16,512]{2,1,0:T(8,128)(2,1)S(1)} %get-tuple-element.164), channel_id=1, source_target_pairs={{0,24},{1,25},{2,26},{3,27},{4,28},{5,29},{6,30},{7,31},{8,16},{9,... | collective-permute-start | bytes 245768 | tf_op jit(solution)/shard_map/ppermute | solution.py:403
  119.6 4.9 %collective-permute-done.30.refs_2_ = bf16[5,16,512]{2,1,0:T(8,128)(2,1)S(1)} collective-permute-done((bf16[5,16,512]{2,1,0:T(8,128)(2,1)S(1)}, bf16[5,16,512]{2,1,0:T(8,128)(2,1)S(1)}, u32[]{:S(2)}, u32[]{:S(2)}) %collective-permute-start.30) | collective-permute-done | bytes 81952 | tf_op jit(solution)/shard_map/ppermute | solution.py:403
  (74 shorter events, 24.9 us)
Async XLA Ops:
  1.9 12.1 %all-to-all-start = ((bf16[8,16,1280]{2,1,0:T(8,128)(2,1)}), bf16[8,16,1280]{2,1,0:T(8,128)(2,1)S(1)}, u32[]{:S(2)}, u32[]{:S(2)}) async-start(bf16[8,16,1280]{2,1,0:T(8,128)(2,1)} %shard_map.136), calls=%async_computation | async-start | bytes 655360 | tf_op jit(solution)/shard_map/all_to_all | solution.py:412
  10.6 2.1 %collective-permute-start = (bf16[512,128]{1,0:T(8,128)(2,1)}, bf16[512,128]{1,0:T(8,128)(2,1)S(1)}, u32[]{:S(2)}, u32[]{:S(2)}) collective-permute-start(bf16[512,128]{1,0:T(8,128)(2,1)} %get-tuple-element.93), channel_id=1, source_target_pairs={{0,2},{1,3},{2,0},{3,1},{4,6},{5,7},{6,4},{7,5},{8,10},{9,11},{10,... | collective-permute-start | bytes 393224 | tf_op jit(solution)/shard_map/ppermute | solution.py:403
  13.9 12.6 %collective-permute-start.4 = (bf16[128,3072]{1,0:T(8,128)(2,1)S(1)}, bf16[128,3072]{1,0:T(8,128)(2,1)S(1)}, u32[]{:S(2)}, u32[]{:S(2)}) collective-permute-start(bf16[128,3072]{1,0:T(8,128)(2,1)S(1)} %get-tuple-element.101.refs_4_), channel_id=1, source_target_pairs={{0,2},{1,3},{2,0},{3,1},{4,6},{5,7},{6,4},{7,5},{8,10},{9,11},{10,... | collective-permute-start | bytes 2359304 | tf_op jit(solution)/shard_map/ppermute | solution.py:403
  14.2 17.8 %collective-permute-start.5 = (bf16[2560,128]{1,0:T(8,128)(2,1)}, bf16[2560,128]{1,0:T(8,128)(2,1)S(1)}, u32[]{:S(2)}, u32[]{:S(2)}) collective-permute-start(bf16[2560,128]{1,0:T(8,128)(2,1)} %copy-done.9), channel_id=1, source_target_pairs={{0,4},{1,5},{2,6},{3,7},{4,0},{5,1},{6,2},{7,3},{8,12},{9,13},{10,... | collective-permute-start | bytes 1966088 | tf_op jit(solution)/shard_map/ppermute | solution.py:403
  16.1 4.5 %collective-permute-start.1 = (bf16[128,256]{1,0:T(8,128)(2,1)S(1)}, bf16[128,256]{1,0:T(8,128)(2,1)S(1)}, u32[]{:S(2)}, u32[]{:S(2)}) collective-permute-start(bf16[128,256]{1,0:T(8,128)(2,1)S(1)} %get-tuple-element.97), channel_id=1, source_target_pairs={{0,8},{1,9},{2,10},{3,11},{4,12},{5,13},{6,14},{7,15},{8,0},{9,1},... | collective-permute-start | bytes 196616 | tf_op jit(solution)/shard_map/ppermute | solution.py:403
  17.8 7.5 %collective-permute-start.2 = (bf16[128,256]{1,0:T(8,128)(2,1)S(1)}, bf16[128,256]{1,0:T(8,128)(2,1)S(1)}, u32[]{:S(2)}, u32[]{:S(2)}) collective-permute-start(bf16[128,256]{1,0:T(8,128)(2,1)S(1)} %get-tuple-element.98), channel_id=1, source_target_pairs={{0,16},{1,17},{2,18},{3,19},{4,20},{5,21},{6,22},{7,23},{8,24},{9,... | collective-permute-start | bytes 196616 | tf_op jit(solution)/shard_map/ppermute | solution.py:403
  20.4 6.2 %collective-permute-start.3 = (bf16[128,256]{1,0:T(8,128)(2,1)S(1)}, bf16[128,256]{1,0:T(8,128)(2,1)S(1)}, u32[]{:S(2)}, u32[]{:S(2)}) collective-permute-start(bf16[128,256]{1,0:T(8,128)(2,1)S(1)} %get-tuple-element.99), channel_id=1, source_target_pairs={{0,24},{1,25},{2,26},{3,27},{4,28},{5,29},{6,30},{7,31},{8,16},{9,... | collective-permute-start | bytes 196616 | tf_op jit(solution)/shard_map/ppermute | solution.py:403
  26.5 22.5 %collective-permute-start.12 = (bf16[128,3072]{1,0:T(8,128)(2,1)}, bf16[128,3072]{1,0:T(8,128)(2,1)S(1)}, u32[]{:S(2)}, u32[]{:S(2)}) collective-permute-start(bf16[128,3072]{1,0:T(8,128)(2,1)} %copy-done.8), channel_id=1, source_target_pairs={{0,4},{1,5},{2,6},{3,7},{4,0},{5,1},{6,2},{7,3},{8,12},{9,13},{10,... | collective-permute-start | bytes 2359304 | tf_op jit(solution)/shard_map/ppermute | solution.py:403
  32.0 7.4 %collective-permute-start.8 = (bf16[96,512]{1,0:T(8,128)(2,1)S(1)}, bf16[96,512]{1,0:T(8,128)(2,1)S(1)}, u32[]{:S(2)}, u32[]{:S(2)}) collective-permute-start(bf16[96,512]{1,0:T(8,128)(2,1)S(1)} %shard_map.140.refs_0_), channel_id=1, source_target_pairs={{0,24},{1,25},{2,26},{3,27},{4,28},{5,29},{6,30},{7,31},{8,16},{9,... | collective-permute-start | bytes 294920 | tf_op jit(solution)/shard_map/ppermute | solution.py:403
  35.7 10.6 %collective-permute-start.10 = (bf16[2,384,128]{2,1,0:T(8,128)(2,1)S(1)}, bf16[2,384,128]{2,1,0:T(8,128)(2,1)S(1)}, u32[]{:S(2)}, u32[]{:S(2)}) collective-permute-start(bf16[2,384,128]{2,1,0:T(8,128)(2,1)S(1)} %get-tuple-element.116), channel_id=1, source_target_pairs={{0,8},{1,9},{2,10},{3,11},{4,12},{5,13},{6,14},{7,15},{8,0},{9,1},... | collective-permute-start | bytes 589832 | tf_op jit(solution)/shard_map/ppermute | solution.py:403
  35.7 10.5 %collective-permute-start.9 = (bf16[512,128]{1,0:T(8,128)(2,1)S(1)}, bf16[512,128]{1,0:T(8,128)(2,1)S(1)}, u32[]{:S(2)}, u32[]{:S(2)}) collective-permute-start(bf16[512,128]{1,0:T(8,128)(2,1)S(1)} %get-tuple-element.114), channel_id=1, source_target_pairs={{0,2},{1,3},{2,0},{3,1},{4,6},{5,7},{6,4},{7,5},{8,10},{9,11},{10,... | collective-permute-start | bytes 393224 | tf_op jit(solution)/shard_map/ppermute | solution.py:403
  35.8 8.3 %collective-permute-start.7 = (bf16[96,512]{1,0:T(8,128)(2,1)S(1)}, bf16[96,512]{1,0:T(8,128)(2,1)S(1)}, u32[]{:S(2)}, u32[]{:S(2)}) collective-permute-start(bf16[96,512]{1,0:T(8,128)(2,1)S(1)} %shard_map.140.refs_0_), channel_id=1, source_target_pairs={{0,16},{1,17},{2,18},{3,19},{4,20},{5,21},{6,22},{7,23},{8,24},{9,... | collective-permute-start | bytes 294920 | tf_op jit(solution)/shard_map/ppermute | solution.py:403
  39.4 6.8 %collective-permute-start.6 = (bf16[96,512]{1,0:T(8,128)(2,1)S(1)}, bf16[96,512]{1,0:T(8,128)(2,1)S(1)}, u32[]{:S(2)}, u32[]{:S(2)}) collective-permute-start(bf16[96,512]{1,0:T(8,128)(2,1)S(1)} %shard_map.140.refs_0_), channel_id=1, source_target_pairs={{0,8},{1,9},{2,10},{3,11},{4,12},{5,13},{6,14},{7,15},{8,0},{9,1},... | collective-permute-start | bytes 294920 | tf_op jit(solution)/shard_map/ppermute | solution.py:403
  47.5 12.4 %collective-permute-start.16 = (bf16[2,384,128]{2,1,0:T(8,128)(2,1)S(1)}, bf16[2,384,128]{2,1,0:T(8,128)(2,1)S(1)}, u32[]{:S(2)}, u32[]{:S(2)}) collective-permute-start(bf16[2,384,128]{2,1,0:T(8,128)(2,1)S(1)} %get-tuple-element.138), channel_id=1, source_target_pairs={{0,16},{1,17},{2,18},{3,19},{4,20},{5,21},{6,22},{7,23},{8,24},{9,... | collective-permute-start | bytes 589832 | tf_op jit(solution)/shard_map/ppermute | solution.py:403
  49.0 4.2 %collective-permute-start.13 = (bf16[48,512]{1,0:T(8,128)(2,1)S(1)}, bf16[48,512]{1,0:T(8,128)(2,1)S(1)}, u32[]{:S(2)}, u32[]{:S(2)}) collective-permute-start(bf16[48,512]{1,0:T(8,128)(2,1)S(1)} %get-tuple-element.134), channel_id=1, source_target_pairs={{0,1},{1,0},{2,3},{3,2},{4,5},{5,4},{6,7},{7,6},{8,9},{9,8},{10,11... | collective-permute-start | bytes 147464 | tf_op jit(solution)/shard_map/ppermute | solution.py:403
  50.9 4.4 %collective-permute-start.14 = (bf16[48,512]{1,0:T(8,128)(2,1)S(1)}, bf16[48,512]{1,0:T(8,128)(2,1)S(1)}, u32[]{:S(2)}, u32[]{:S(2)}) collective-permute-start(bf16[48,512]{1,0:T(8,128)(2,1)S(1)} %get-tuple-element.135), channel_id=1, source_target_pairs={{0,4},{1,5},{2,6},{3,7},{4,0},{5,1},{6,2},{7,3},{8,12},{9,13},{10,... | collective-permute-start | bytes 147464 | tf_op jit(solution)/shard_map/ppermute | solution.py:403
  51.1 5.0 %collective-permute-start.15 = (bf16[48,512]{1,0:T(8,128)(2,1)S(1)}, bf16[48,512]{1,0:T(8,128)(2,1)S(1)}, u32[]{:S(2)}, u32[]{:S(2)}) collective-permute-start(bf16[48,512]{1,0:T(8,128)(2,1)S(1)} %get-tuple-element.136), channel_id=1, source_target_pairs={{0,5},{1,4},{2,7},{3,6},{4,1},{5,0},{6,3},{7,2},{8,13},{9,12},{10,... | collective-permute-start | bytes 147464 | tf_op jit(solution)/shard_map/ppermute | solution.py:403
  59.9 8.7 %collective-permute-start.20 = (bf16[128,3072]{1,0:T(8,128)(2,1)S(1)}, bf16[128,3072]{1,0:T(8,128)(2,1)S(1)}, u32[]{:S(2)}, u32[]{:S(2)}) collective-permute-start(bf16[128,3072]{1,0:T(8,128)(2,1)S(1)} %collective-permute-done.12.refs_6_), channel_id=1, source_target_pairs={{0,2},{1,3},{2,0},{3,1},{4,6},{5,7},{6,4},{7,5},{8,10},{9,11},{10,... | collective-permute-start | bytes 2359304 | tf_op jit(solution)/shard_map/ppermute | solution.py:403
  59.9 10.2 %collective-permute-start.21 = (bf16[2,384,128]{2,1,0:T(8,128)(2,1)S(1)}, bf16[2,384,128]{2,1,0:T(8,128)(2,1)S(1)}, u32[]{:S(2)}, u32[]{:S(2)}) collective-permute-start(bf16[2,384,128]{2,1,0:T(8,128)(2,1)S(1)} %get-tuple-element.149), channel_id=1, source_target_pairs={{0,24},{1,25},{2,26},{3,27},{4,28},{5,29},{6,30},{7,31},{8,16},{9,... | collective-permute-start | bytes 589832 | tf_op jit(solution)/shard_map/ppermute | solution.py:403
  61.5 5.2 %collective-permute-start.19 = (bf16[48,512]{1,0:T(8,128)(2,1)S(1)}, bf16[48,512]{1,0:T(8,128)(2,1)S(1)}, u32[]{:S(2)}, u32[]{:S(2)}) collective-permute-start(bf16[48,512]{1,0:T(8,128)(2,1)S(1)} %shard_map.144.refs_0_.hidden), channel_id=1, source_target_pairs={{0,5},{1,4},{2,7},{3,6},{4,1},{5,0},{6,3},{7,2},{8,13},{9,12},{10,... | collective-permute-start | bytes 147464 | tf_op jit(solution)/shard_map/ppermute | solution.py:403
  62.9 4.6 %collective-permute-start.18 = (bf16[48,512]{1,0:T(8,128)(2,1)S(1)}, bf16[48,512]{1,0:T(8,128)(2,1)S(1)}, u32[]{:S(2)}, u32[]{:S(2)}) collective-permute-start(bf16[48,512]{1,0:T(8,128)(2,1)S(1)} %shard_map.144.refs_0_.hidden), channel_id=1, source_target_pairs={{0,4},{1,5},{2,6},{3,7},{4,0},{5,1},{6,2},{7,3},{8,12},{9,13},{10,... | collective-permute-start | bytes 147464 | tf_op jit(solution)/shard_map/ppermute | solution.py:403
  64.6 4.1 %collective-permute-start.17 = (bf16[48,512]{1,0:T(8,128)(2,1)S(1)}, bf16[48,512]{1,0:T(8,128)(2,1)S(1)}, u32[]{:S(2)}, u32[]{:S(2)}) collective-permute-start(bf16[48,512]{1,0:T(8,128)(2,1)S(1)} %shard_map.144.refs_0_.hidden), channel_id=1, source_target_pairs={{0,1},{1,0},{2,3},{3,2},{4,5},{5,4},{6,7},{7,6},{8,9},{9,8},{10,11... | collective-permute-start | bytes 147464 | tf_op jit(solution)/shard_map/ppermute | solution.py:403
  70.2 25.2 %collective-permute-start.25 = (bf16[4,2,384,128]{3,2,1,0:T(8,128)(2,1)S(1)}, bf16[4,2,384,128]{3,2,1,0:T(8,128)(2,1)S(1)}, u32[]{:S(2)}, u32[]{:S(2)}) collective-permute-start(bf16[4,2,384,128]{3,2,1,0:T(8,128)(2,1)S(1)} %shard_map.146.refs_4_), channel_id=1, source_target_pairs={{0,2},{1,3},{2,0},{3,1},{4,6},{5,7},{6,4},{7,5},{8,10},{9,11},{10,... | collective-permute-start | bytes 2359304 | tf_op jit(solution)/shard_map/ppermute | solution.py:403
  70.3 16.5 %collective-permute-start.22 = (bf16[208,768]{1,0:T(8,128)(2,1)S(1)}, bf16[208,768]{1,0:T(8,128)(2,1)S(1)}, u32[]{:S(2)}, u32[]{:S(2)}) collective-permute-start(bf16[208,768]{1,0:T(8,128)(2,1)S(1)} %get-tuple-element.150), channel_id=1, source_target_pairs={{0,8},{1,9},{2,10},{3,11},{4,12},{5,13},{6,14},{7,15},{8,0},{9,1},... | collective-permute-start | bytes 958472 | tf_op jit(solution)/shard_map/ppermute | solution.py:403
  70.4 25.1 %collective-permute-start.23 = (bf16[208,768]{1,0:T(8,128)(2,1)S(1)}, bf16[208,768]{1,0:T(8,128)(2,1)S(1)}, u32[]{:S(2)}, u32[]{:S(2)}) collective-permute-start(bf16[208,768]{1,0:T(8,128)(2,1)S(1)} %get-tuple-element.151), channel_id=1, source_target_pairs={{0,16},{1,17},{2,18},{3,19},{4,20},{5,21},{6,22},{7,23},{8,24},{9,... | collective-permute-start | bytes 958472 | tf_op jit(solution)/shard_map/ppermute | solution.py:403
  73.4 22.1 %collective-permute-start.24 = (bf16[208,768]{1,0:T(8,128)(2,1)S(1)}, bf16[208,768]{1,0:T(8,128)(2,1)S(1)}, u32[]{:S(2)}, u32[]{:S(2)}) collective-permute-start(bf16[208,768]{1,0:T(8,128)(2,1)S(1)} %get-tuple-element.152), channel_id=1, source_target_pairs={{0,24},{1,25},{2,26},{3,27},{4,28},{5,29},{6,30},{7,31},{8,16},{9,... | collective-permute-start | bytes 958472 | tf_op jit(solution)/shard_map/ppermute | solution.py:403
  96.9 7.0 %collective-permute-start.26 = (bf16[4,48,512]{2,1,0:T(8,128)(2,1)S(1)}, bf16[4,48,512]{2,1,0:T(8,128)(2,1)S(1)}, u32[]{:S(2)}, u32[]{:S(2)}) collective-permute-start(bf16[4,48,512]{2,1,0:T(8,128)(2,1)S(1)} %get-tuple-element.158), channel_id=1, source_target_pairs={{0,1},{1,0},{2,3},{3,2},{4,5},{5,4},{6,7},{7,6},{8,9},{9,8},{10,11... | collective-permute-start | bytes 589832 | tf_op jit(solution)/shard_map/ppermute | solution.py:403
  98.5 7.4 %collective-permute-start.27 = (bf16[4,48,512]{2,1,0:T(8,128)(2,1)S(1)}, bf16[4,48,512]{2,1,0:T(8,128)(2,1)S(1)}, u32[]{:S(2)}, u32[]{:S(2)}) collective-permute-start(bf16[4,48,512]{2,1,0:T(8,128)(2,1)S(1)} %get-tuple-element.159), channel_id=1, source_target_pairs={{0,4},{1,5},{2,6},{3,7},{4,0},{5,1},{6,2},{7,3},{8,12},{9,13},{10,... | collective-permute-start | bytes 589832 | tf_op jit(solution)/shard_map/ppermute | solution.py:403
  98.8 9.4 %collective-permute-start.28 = (bf16[4,48,512]{2,1,0:T(8,128)(2,1)S(1)}, bf16[4,48,512]{2,1,0:T(8,128)(2,1)S(1)}, u32[]{:S(2)}, u32[]{:S(2)}) collective-permute-start(bf16[4,48,512]{2,1,0:T(8,128)(2,1)S(1)} %get-tuple-element.160), channel_id=1, source_target_pairs={{0,5},{1,4},{2,7},{3,6},{4,1},{5,0},{6,3},{7,2},{8,13},{9,12},{10,... | collective-permute-start | bytes 589832 | tf_op jit(solution)/shard_map/ppermute | solution.py:403
  109.1 10.5 %collective-permute-start.29 = (bf16[5,16,512]{2,1,0:T(8,128)(2,1)S(1)}, bf16[5,16,512]{2,1,0:T(8,128)(2,1)S(1)}, u32[]{:S(2)}, u32[]{:S(2)}) collective-permute-start(bf16[5,16,512]{2,1,0:T(8,128)(2,1)S(1)} %get-tuple-element.162), channel_id=1, source_target_pairs={{0,8},{1,9},{2,10},{3,11},{4,12},{5,13},{6,14},{7,15},{8,0},{9,1},... | collective-permute-start | bytes 245768 | tf_op jit(solution)/shard_map/ppermute | solution.py:403
  116.7 7.8 %collective-permute-start.30 = (bf16[5,16,512]{2,1,0:T(8,128)(2,1)S(1)}, bf16[5,16,512]{2,1,0:T(8,128)(2,1)S(1)}, u32[]{:S(2)}, u32[]{:S(2)}) collective-permute-start(bf16[5,16,512]{2,1,0:T(8,128)(2,1)S(1)} %get-tuple-element.163), channel_id=1, source_target_pairs={{0,16},{1,17},{2,18},{3,19},{4,20},{5,21},{6,22},{7,23},{8,24},{9,... | collective-permute-start | bytes 245768 | tf_op jit(solution)/shard_map/ppermute | solution.py:403
  117.5 7.0 %collective-permute-start.31 = (bf16[5,16,512]{2,1,0:T(8,128)(2,1)S(1)}, bf16[5,16,512]{2,1,0:T(8,128)(2,1)S(1)}, u32[]{:S(2)}, u32[]{:S(2)}) collective-permute-start(bf16[5,16,512]{2,1,0:T(8,128)(2,1)S(1)} %get-tuple-element.164), channel_id=1, source_target_pairs={{0,24},{1,25},{2,26},{3,27},{4,28},{5,29},{6,30},{7,31},{8,16},{9,... | collective-permute-start | bytes 245768 | tf_op jit(solution)/shard_map/ppermute | solution.py:403
  (12 other events, 58.5 us)

commit v5 on v4

--- a/solution.py
+++ b/solution.py
@@ -280,30 +280,50 @@
     high = square.astype(BF16).astype(F32)
     terms = jnp.where(lane == 0, high, jnp.where(lane == 1, square - high, 0.0)).astype(BF16)
     terms = lax.dot_general(terms, same[...], (((0,), (0,)), ((), ())), preferred_element_type=F32)
-    for k, out in enumerate(outs):
+    keep, near, *fars = outs
+    terms = terms[:ROW_TILE]
+    split = rows // 2
+    for k in range(planes):
         at = slice(k * columns, (k + 1) * columns)
         total = dot(x, jnp.concatenate([piece[:, at] for piece in pieces]))
-        out[:rows] = total.astype(out.dtype)
-        out[rows:] = jnp.zeros((out.shape[0] - rows, columns), out.dtype)
-        out[rows:, :rows] = terms[:out.shape[0] - rows].astype(out.dtype)
-
-
-def down_kernel(planes, per, features, idx, *refs):
-    totals, (near, far, same, own, *sends) = refs[:planes], refs[planes:]
+        if k < 2:
+            places = [(outs[k], 0, rows)]
+        else:
+            places = [(fars[2 * k - 4], split, rows), (fars[2 * k - 3], 0, split)]
+        for out, start, end in places:
+            many = end - start
+            out[:many] = total[start:end].astype(out.dtype)
+            if out.shape[0] > many:
+                out[many:] = jnp.zeros((ROW_TILE, columns), out.dtype)
+                out[many:, :rows] = terms.astype(out.dtype)
+
+
+def far_sum_kernel(rows, kept, got, out):
+    total = kept[...] + got[...].astype(F32)
+    out[:rows] = total[:rows].astype(BF16)
+    if out.shape[0] > rows:
+        square = jnp.sum(total[rows:], axis=0, keepdims=True)
+        high = square.astype(BF16).astype(F32)
+        row = lax.broadcasted_iota(jnp.int32, (out.shape[0] - rows, total.shape[1]), 0)
+        terms = jnp.where(row == 0, high, jnp.where(row == 1, square - high, 0.0))
+        out[rows:] = terms.astype(BF16)
+
+
+def down_kernel(start, planes, per, features, idx, keep, got, far_head, far_part, near, far, same, *outs):
     many = same.shape[0]
-    total = totals[0][:many]
-    terms = totals[0][many:, :many]
-    for part in totals[1:]:
-        total = total + part[:many].astype(F32)
-        terms = jnp.concatenate([terms, part[many:, :many].astype(F32)])
+    half = many // 2
+    at = slice(start, start + half)
+    total = keep[at] + got[at].astype(F32) + far_part[:half].astype(F32)
+    terms = [keep[many:, :many], got[many:, :many].astype(F32), far_head[half:, :many].astype(F32)]
     units = total.shape[1] // 2
-    square = lax.dot_general(same[...], terms.astype(BF16), NT, preferred_element_type=F32)
+    square = jnp.concatenate(terms).astype(BF16)
+    square = lax.dot_general(same[at], square, NT, preferred_element_type=F32)
     square = jnp.sum(square, axis=1, keepdims=True)
     factor = lax.rsqrt(square / features + 1e-06)
     gate, up = total[:, :units] * factor, total[:, units:] * factor
     activated = (gate / (1.0 + jnp.exp(-gate)) * up).astype(BF16)
     z, q = idx[0], idx[2]
-    rows = own.shape[1]
+    rows = outs[0].shape[1]
     for k in range(planes):
         w = [(far if c % 2 else near)[k, c // 2] for c in range(per)]
         y = dot(activated, jnp.concatenate(w, axis=1))
@@ -311,9 +331,8 @@
         for c in range(per):
             at = pl.ds(pl.multiple_of((q ^ c) * lanes, lanes), lanes)
             block = y[:, c * lanes:(c + 1) * lanes]
-            own[z ^ k, :, at] = block[:rows]
-            for i, send in enumerate(sends):
-                send[z ^ k, :, at] = block[(i + 1) * rows:(i + 2) * rows].astype(BF16)
+            for i, out in enumerate(outs):
+                out[z ^ k, :, at] = block[i * rows:(i + 1) * rows].astype(out.dtype)
 
 
 def row_of(z, k, tokens, rows, total):
@@ -527,21 +546,44 @@
     same = jnp.eye(len(blocks) * share, dtype=BF16)
     pieces = [x for both in zip(gate_up, twin) for x in both]
     many = len(blocks) * share
-    keep, *sends = call(
+    group_far = planes // 2 * group
+    split = many // 2
+    ends = (split + ROW_TILE, split)
+    keep, near_send, *fars = call(
         functools.partial(gate_up_kernel, len(blocks), per, planes),
-        [like(many + ROW_TILE, 2 * units, dtype=F32)]
-        + [like(many + ROW_TILE, 2 * units)] * (planes - 1),
+        [like(many + ROW_TILE, 2 * units, dtype=F32), like(many + ROW_TILE, 2 * units)]
+        + [like(rows_, 2 * units, dtype=F32) for rows_ in ends]
+        + [like(rows_, 2 * units) for rows_ in ends],
         idx, *blocks, *pieces, norm_gain.reshape(planes, 1, width), same,
         scratch=[pltpu.VMEM((many, width), BF16)],
     )
-    sends, down_parts = after(sends, down_parts)
-    totals = across_planes([keep] + sends)
+    far_keeps, far_sends = fars[:2], fars[2:]
+    far_sends[0], down_parts = after(far_sends[0], down_parts)
+
+    def far_sum(i, got):
+        return call(
+            functools.partial(far_sum_kernel, split), like(ends[i], 2 * units), far_keeps[i], got
+        )
+
+    got = swap(far_sends[0], group)
+    got, far_sends[1] = after(got, far_sends[1])
+    far_head = swap(far_sum(0, got), group_far)
+    got, near_send = after(swap(far_sends[1], group), near_send)
+    far_rest = swap(far_sum(1, got), group_far)
+    near_got = swap(near_send, group)
     downs = call(stack_kernel, like(planes, *down_parts[0].shape), *down_parts)
-    own, *rest = call(
-        functools.partial(down_kernel, planes, per, features),
-        [like(planes, share, width, dtype=F32)] + [like(planes, share, width)] * len(steps),
-        idx, *totals, downs, swap(downs, core), same,
-    )
+    weights = [downs, swap(downs, core), same]
+
+    def ffn_out(start, part, dtypes):
+        return call(
+            functools.partial(down_kernel, start, planes, per, features),
+            [like(planes, share, width, dtype=dtype) for dtype in dtypes],
+            idx, keep, near_got, far_head, part, *weights,
+        )
+
+    late = ffn_out(split, far_head, [BF16, BF16])
+    own, early = ffn_out(0, far_rest, [F32, BF16])
+    rest = [early] + late
     parts = call(
         functools.partial(plane_sum_kernel, planes, tokens),
         [like(planes + 1, rows, width)] * planes,
@@ -565,7 +607,7 @@
         and power(n_uly)
         and power(kv_heads)
         and per > 1
-        and n_blk % per == 0
+        and n_blk == 4 * per
         and token_count < unit_count // n_uly
     )
 

time: 126 us -> 121 us (0.960)
  starting transfers between devices: 44.8 us -> 38.7 us
    ppermute x32 -> x34, starting transfers between devices: 39.5 us -> 33.4 us  [swap(): return lax.ppermute(x, axes, [(i, i ^ mask) for i in range(devices)])]
    pallas_call x14 -> x17, Pallas kernels: 13.4 us -> 14.5 us  [call(): pl.pallas_call(kernel, out_shape=shapes, in_specs=[SMEM if a.dtype == jnp...]
    ppermute x32 -> x34, waiting for transfers between devices: 62.3 us -> 62.2 us  [swap(): return lax.ppermute(x, axes, [(i, i ^ mask) for i in range(devices)])]
  transfers between devices with their start and end apart: 33 -> 35, of which waited for: 22 -> 24; matrix products, arithmetic and copies ran while one was open for 0% -> 0% of each run, Pallas kernels for 6% -> 9%
where the time goes in v5:
time: 121 us
  waiting for transfers between devices  63.4 us (52%)
  starting transfers between devices  38.7 us (32%)
  Pallas kernels  14.5 us (12%)
  local copies, waits for them, and re-layouts  3 us (2%)
    ppermute x34, waiting for transfers between devices, swap(): return lax.ppermute(x, axes, [(i, i ^ mask) for i in range(devices)])  62.2 us
    ppermute x34, starting transfers between devices, swap(): return lax.ppermute(x, axes, [(i, i ^ mask) for i in range(devices)])  33.4 us
    pallas_call x17, Pallas kernels, call(): pl.pallas_call(kernel, out_shape=shapes, in_specs=[SMEM if a.dtype == jnp...  14.5 us
    all_to_all x1, starting transfers between devices, plane_exchange(): lax.all_to_all(x, axes, 0, 0, axis_index_groups=plane_groups, tiled=True)  5.31 us
    unnamed x22, local copies, waits for them, and re-layouts  2.92 us
  transfers between devices with their start and end apart: 35, of which 24 were waited for; matrix products, arithmetic and copies ran while one was open for 0% of the time, Pallas kernels for 9%

profile of v5, /device:TPU:0, one launch (start us, length us, event | category | flops | bytes accessed | tf_op | source)
XLA Modules:
  0.0 120.6 jit_solution(1229440947930627657)
XLA Ops:
  0.0 1.8 %shard_map.136 = bf16[8,16,1280]{2,1,0:T(8,128)(2,1)} custom-call(bf16[12,1024]{1,0:T(8,128)(2,1)} %refs_0_.1, bf16[12,1024]{1,0:T(8,128)(2,1)} %refs_1_.1, bf16[12,4096]{1,0:T(8,128)(2,1)} %refs_2_.1, bf16[12,4096]{1,0:T(8,128)(2,1)} %refs_3_.1), custom_call_target="tpu_custom_call" | custom-call | tf_op jit(solution)/shard_map/pallas_call | solution.py:373
  1.9 5.3 %all-to-all-start = ((bf16[8,16,1280]{2,1,0:T(8,128)(2,1)}), bf16[8,16,1280]{2,1,0:T(8,128)(2,1)S(1)}, u32[]{:S(2)}, u32[]{:S(2)}) async-start(bf16[8,16,1280]{2,1,0:T(8,128)(2,1)} %shard_map.136), calls=%async_computation | async-start | bytes 655360 | tf_op jit(solution)/shard_map/all_to_all | solution.py:431
  8.4 1.3 %shard_map.137 = (bf16[2560,128]{1,0:T(8,128)(2,1)S(1)}, bf16[4,384,128]{2,1,0:T(8,128)(2,1)S(1)}, bf16[512,128]{1,0:T(8,128)(2,1)S(1)}, bf16[512,128]{1,0:T(8,128)(2,1)}) custom-call(s32[4]{0:T(128)S(1)} %pad_add_fusion.idx, bf16[3072,128]{1,0:T(8,128)(2,1)S(1)} %copy-done, bf16[2048,128]{1,0:T(8,128)(2,1)S(1)} %copy-done.3), custom_call_target="tpu_custom_call" | custom-call | tf_op jit(solution)/shard_map/pallas_call | solution.py:373
  16.1 1.6 %collective-permute-start.1 = (bf16[128,256]{1,0:T(8,128)(2,1)S(1)}, bf16[128,256]{1,0:T(8,128)(2,1)S(1)}, u32[]{:S(2)}, u32[]{:S(2)}) collective-permute-start(bf16[128,256]{1,0:T(8,128)(2,1)S(1)} %get-tuple-element.101), channel_id=1, source_target_pairs={{0,8},{1,9},{2,10},{3,11},{4,12},{5,13},{6,14},{7,15},{8,0},{9,1},... | collective-permute-start | bytes 196616 | tf_op jit(solution)/shard_map/ppermute | solution.py:422
  17.8 2.6 %collective-permute-start.2 = (bf16[128,256]{1,0:T(8,128)(2,1)S(1)}, bf16[128,256]{1,0:T(8,128)(2,1)S(1)}, u32[]{:S(2)}, u32[]{:S(2)}) collective-permute-start(bf16[128,256]{1,0:T(8,128)(2,1)S(1)} %get-tuple-element.102), channel_id=1, source_target_pairs={{0,16},{1,17},{2,18},{3,19},{4,20},{5,21},{6,22},{7,23},{8,24},{9,... | collective-permute-start | bytes 196616 | tf_op jit(solution)/shard_map/ppermute | solution.py:422
  20.6 4.7 %collective-permute-done.2.refs_2_.refs_6_ = bf16[128,256]{1,0:T(8,128)(2,1)S(1)} collective-permute-done((bf16[128,256]{1,0:T(8,128)(2,1)S(1)}, bf16[128,256]{1,0:T(8,128)(2,1)S(1)}, u32[]{:S(2)}, u32[]{:S(2)}) %collective-permute-start.2) | collective-permute-done | bytes 65568 | tf_op jit(solution)/shard_map/ppermute | solution.py:422
  28.0 1.9 %shard_map.140.refs_0_ = bf16[96,512]{1,0:T(8,128)(2,1)S(1)} custom-call(s32[4]{0:T(128)S(1)} %pad_add_fusion.idx, s32[1]{0:T(128)S(6)} %copy.15.prefix, bf16[8,16,1280]{2,1,0:T(8,128)(2,1)S(1)} %all-to-all-done.heads.qg, bf16[128,256]{1,0:T(8,128)(2,1)S(1)} %get-tuple-element.106.refs_0_.refs_4_, ...), custom_call_target="tpu_custom_call" | custom-call | tf_op jit(solution)/shard_map/pallas_call | solution.py:373
  29.8 2.1 %collective-permute-done.5.message = bf16[2560,128]{1,0:T(8,128)(2,1)S(1)} collective-permute-done((bf16[2560,128]{1,0:T(8,128)(2,1)}, bf16[2560,128]{1,0:T(8,128)(2,1)S(1)}, u32[]{:S(2)}, u32[]{:S(2)}) %collective-permute-start.5) | collective-permute-done | bytes 655392 | tf_op jit(solution)/shard_map/ppermute | solution.py:422
  32.0 3.6 %collective-permute-start.8 = (bf16[96,512]{1,0:T(8,128)(2,1)S(1)}, bf16[96,512]{1,0:T(8,128)(2,1)S(1)}, u32[]{:S(2)}, u32[]{:S(2)}) collective-permute-start(bf16[96,512]{1,0:T(8,128)(2,1)S(1)} %shard_map.140.refs_0_), channel_id=1, source_target_pairs={{0,24},{1,25},{2,26},{3,27},{4,28},{5,29},{6,30},{7,31},{8,16},{9,... | collective-permute-start | bytes 294920 | tf_op jit(solution)/shard_map/ppermute | solution.py:422
  36.5 2.9 %collective-permute-done.8.refs_3_ = bf16[96,512]{1,0:T(8,128)(2,1)S(1)} collective-permute-done((bf16[96,512]{1,0:T(8,128)(2,1)S(1)}, bf16[96,512]{1,0:T(8,128)(2,1)S(1)}, u32[]{:S(2)}, u32[]{:S(2)}) %collective-permute-start.8) | collective-permute-done | bytes 98336 | tf_op jit(solution)/shard_map/ppermute | solution.py:422
  39.4 4.7 %collective-permute-done.7.refs_2_ = bf16[96,512]{1,0:T(8,128)(2,1)S(1)} collective-permute-done((bf16[96,512]{1,0:T(8,128)(2,1)S(1)}, bf16[96,512]{1,0:T(8,128)(2,1)S(1)}, u32[]{:S(2)}, u32[]{:S(2)}) %collective-permute-start.7) | collective-permute-done | bytes 98336 | tf_op jit(solution)/shard_map/ppermute | solution.py:422
  44.1 2.1 %collective-permute-done.6.refs_1_ = bf16[96,512]{1,0:T(8,128)(2,1)S(1)} collective-permute-done((bf16[96,512]{1,0:T(8,128)(2,1)S(1)}, bf16[96,512]{1,0:T(8,128)(2,1)S(1)}, u32[]{:S(2)}, u32[]{:S(2)}) %collective-permute-start.6) | collective-permute-done | bytes 98336 | tf_op jit(solution)/shard_map/ppermute | solution.py:422
  49.0 1.8 %collective-permute-start.13 = (bf16[48,512]{1,0:T(8,128)(2,1)S(1)}, bf16[48,512]{1,0:T(8,128)(2,1)S(1)}, u32[]{:S(2)}, u32[]{:S(2)}) collective-permute-start(bf16[48,512]{1,0:T(8,128)(2,1)S(1)} %get-tuple-element.138), channel_id=1, source_target_pairs={{0,1},{1,0},{2,3},{3,2},{4,5},{5,4},{6,7},{7,6},{8,9},{9,8},{10,11... | collective-permute-start | bytes 147464 | tf_op jit(solution)/shard_map/ppermute | solution.py:422
  51.1 1.5 %collective-permute-start.15 = (bf16[48,512]{1,0:T(8,128)(2,1)S(1)}, bf16[48,512]{1,0:T(8,128)(2,1)S(1)}, u32[]{:S(2)}, u32[]{:S(2)}) collective-permute-start(bf16[48,512]{1,0:T(8,128)(2,1)S(1)} %get-tuple-element.140), channel_id=1, source_target_pairs={{0,5},{1,4},{2,7},{3,6},{4,1},{5,0},{6,3},{7,2},{8,13},{9,12},{10,... | collective-permute-start | bytes 147464 | tf_op jit(solution)/shard_map/ppermute | solution.py:422
  53.2 2.1 %collective-permute-done.14.refs_2_ = bf16[48,512]{1,0:T(8,128)(2,1)S(1)} collective-permute-done((bf16[48,512]{1,0:T(8,128)(2,1)S(1)}, bf16[48,512]{1,0:T(8,128)(2,1)S(1)}, u32[]{:S(2)}, u32[]{:S(2)}) %collective-permute-start.14) | collective-permute-done | bytes 49184 | tf_op jit(solution)/shard_map/ppermute | solution.py:422
  56.8 3.1 %collective-permute-done.16.refs_2_ = bf16[2,384,128]{2,1,0:T(8,128)(2,1)S(1)} collective-permute-done((bf16[2,384,128]{2,1,0:T(8,128)(2,1)S(1)}, bf16[2,384,128]{2,1,0:T(8,128)(2,1)S(1)}, u32[]{:S(2)}, u32[]{:S(2)}) %collective-permute-start.16) | collective-permute-done | bytes 196640 | tf_op jit(solution)/shard_map/ppermute | solution.py:422
  60.0 1.5 %collective-permute-start.21 = (bf16[2,384,128]{2,1,0:T(8,128)(2,1)S(1)}, bf16[2,384,128]{2,1,0:T(8,128)(2,1)S(1)}, u32[]{:S(2)}, u32[]{:S(2)}) collective-permute-start(bf16[2,384,128]{2,1,0:T(8,128)(2,1)S(1)} %get-tuple-element.151), channel_id=1, source_target_pairs={{0,24},{1,25},{2,26},{3,27},{4,28},{5,29},{6,30},{7,31},{8,16},{9,... | collective-permute-start | bytes 589832 | tf_op jit(solution)/shard_map/ppermute | solution.py:422
  61.5 1.5 %collective-permute-start.19 = (bf16[48,512]{1,0:T(8,128)(2,1)S(1)}, bf16[48,512]{1,0:T(8,128)(2,1)S(1)}, u32[]{:S(2)}, u32[]{:S(2)}) collective-permute-start(bf16[48,512]{1,0:T(8,128)(2,1)S(1)} %shard_map.144.refs_0_.hidden), channel_id=1, source_target_pairs={{0,5},{1,4},{2,7},{3,6},{4,1},{5,0},{6,3},{7,2},{8,13},{9,12},{10,... | collective-permute-start | bytes 147464 | tf_op jit(solution)/shard_map/ppermute | solution.py:422
  63.0 1.5 %collective-permute-start.18 = (bf16[48,512]{1,0:T(8,128)(2,1)S(1)}, bf16[48,512]{1,0:T(8,128)(2,1)S(1)}, u32[]{:S(2)}, u32[]{:S(2)}) collective-permute-start(bf16[48,512]{1,0:T(8,128)(2,1)S(1)} %shard_map.144.refs_0_.hidden), channel_id=1, source_target_pairs={{0,4},{1,5},{2,6},{3,7},{4,0},{5,1},{6,2},{7,3},{8,12},{9,13},{10,... | collective-permute-start | bytes 147464 | tf_op jit(solution)/shard_map/ppermute | solution.py:422
  65.0 1.7 %collective-permute-done.19.refs_3_ = bf16[48,512]{1,0:T(8,128)(2,1)S(1)} collective-permute-done((bf16[48,512]{1,0:T(8,128)(2,1)S(1)}, bf16[48,512]{1,0:T(8,128)(2,1)S(1)}, u32[]{:S(2)}, u32[]{:S(2)}) %collective-permute-start.19) | collective-permute-done | bytes 49184 | tf_op jit(solution)/shard_map/ppermute | solution.py:422
  68.6 1.5 %shard_map.145 = (f32[208,768]{1,0:T(8,128)S(1)}, bf16[208,768]{1,0:T(8,128)(2,1)S(1)}, f32[112,768]{1,0:T(8,128)S(1)}, f32[96,768]{1,0:T(8,128)S(1)}, bf16[112,...) custom-call(s32[4]{0:T(128)S(1)} %pad_add_fusion.idx, bf16[48,512]{1,0:T(8,128)(2,1)S(1)} %shard_map.144.refs_0_.hidden, ...), custom_call_target="tpu_custom_call" | custom-call | tf_op jit(solution)/shard_map/pallas_call | solution.py:373
  70.4 6.7 %collective-permute-done.22.got = bf16[112,768]{1,0:T(8,128)(2,1)S(1)} collective-permute-done((bf16[112,768]{1,0:T(8,128)(2,1)S(1)}, bf16[112,768]{1,0:T(8,128)(2,1)S(1)}, u32[]{:S(2)}, u32[]{:S(2)}) %collective-permute-start.22) | collective-permute-done | bytes 172064 | tf_op jit(solution)/shard_map/ppermute | solution.py:422
  77.3 5.1 %collective-permute-done.23.got = bf16[96,768]{1,0:T(8,128)(2,1)S(1)} collective-permute-done((bf16[96,768]{1,0:T(8,128)(2,1)S(1)}, bf16[96,768]{1,0:T(8,128)(2,1)S(1)}, u32[]{:S(2)}, u32[]{:S(2)}) %collective-permute-start.23) | collective-permute-done | bytes 147488 | tf_op jit(solution)/shard_map/ppermute | solution.py:422
  83.0 2.7 %collective-permute-start.25 = (bf16[112,768]{1,0:T(8,128)(2,1)S(1)}, bf16[112,768]{1,0:T(8,128)(2,1)S(1)}, u32[]{:S(2)}, u32[]{:S(2)}) collective-permute-start(bf16[112,768]{1,0:T(8,128)(2,1)S(1)} %shard_map.146), channel_id=1, source_target_pairs={{0,16},{1,17},{2,18},{3,19},{4,20},{5,21},{6,22},{7,23},{8,24},{9,... | collective-permute-start | bytes 516104 | tf_op jit(solution)/shard_map/ppermute | solution.py:422
  86.1 8.1 %collective-permute-done.25.far_head.far_part = bf16[112,768]{1,0:T(8,128)(2,1)S(1)} collective-permute-done((bf16[112,768]{1,0:T(8,128)(2,1)S(1)}, bf16[112,768]{1,0:T(8,128)(2,1)S(1)}, u32[]{:S(2)}, u32[]{:S(2)}) %collective-permute-start.25) | collective-permute-done | bytes 172064 | tf_op jit(solution)/shard_map/ppermute | solution.py:422
  94.1 2.9 %collective-permute-done.24.got = bf16[208,768]{1,0:T(8,128)(2,1)S(1)} collective-permute-done((bf16[208,768]{1,0:T(8,128)(2,1)S(1)}, bf16[208,768]{1,0:T(8,128)(2,1)S(1)}, u32[]{:S(2)}, u32[]{:S(2)}) %collective-permute-start.24) | collective-permute-done | bytes 319520 | tf_op jit(solution)/shard_map/ppermute | solution.py:422
  99.1 1.7 %collective-permute-start.30 = (bf16[4,48,512]{2,1,0:T(8,128)(2,1)S(1)}, bf16[4,48,512]{2,1,0:T(8,128)(2,1)S(1)}, u32[]{:S(2)}, u32[]{:S(2)}) collective-permute-start(bf16[4,48,512]{2,1,0:T(8,128)(2,1)S(1)} %get-tuple-element.168), channel_id=1, source_target_pairs={{0,5},{1,4},{2,7},{3,6},{4,1},{5,0},{6,3},{7,2},{8,13},{9,12},{10,... | collective-permute-start | bytes 589832 | tf_op jit(solution)/shard_map/ppermute | solution.py:422
  103.0 2.7 %collective-permute-done.29.refs_2_ = bf16[4,48,512]{2,1,0:T(8,128)(2,1)S(1)} collective-permute-done((bf16[4,48,512]{2,1,0:T(8,128)(2,1)S(1)}, bf16[4,48,512]{2,1,0:T(8,128)(2,1)S(1)}, u32[]{:S(2)}, u32[]{:S(2)}) %collective-permute-start.29) | collective-permute-done | bytes 196640 | tf_op jit(solution)/shard_map/ppermute | solution.py:422
  105.8 2.5 %collective-permute-done.30.refs_3_ = bf16[4,48,512]{2,1,0:T(8,128)(2,1)S(1)} collective-permute-done((bf16[4,48,512]{2,1,0:T(8,128)(2,1)S(1)}, bf16[4,48,512]{2,1,0:T(8,128)(2,1)S(1)}, u32[]{:S(2)}, u32[]{:S(2)}) %collective-permute-start.30) | collective-permute-done | bytes 196640 | tf_op jit(solution)/shard_map/ppermute | solution.py:422
  108.3 2.0 %collective-permute-done.28.refs_1_ = bf16[4,48,512]{2,1,0:T(8,128)(2,1)S(1)} collective-permute-done((bf16[4,48,512]{2,1,0:T(8,128)(2,1)S(1)}, bf16[4,48,512]{2,1,0:T(8,128)(2,1)S(1)}, u32[]{:S(2)}, u32[]{:S(2)}) %collective-permute-start.28) | collective-permute-done | bytes 196640 | tf_op jit(solution)/shard_map/ppermute | solution.py:422
  112.3 3.3 %collective-permute-start.33 = (bf16[5,16,512]{2,1,0:T(8,128)(2,1)S(1)}, bf16[5,16,512]{2,1,0:T(8,128)(2,1)S(1)}, u32[]{:S(2)}, u32[]{:S(2)}) collective-permute-start(bf16[5,16,512]{2,1,0:T(8,128)(2,1)S(1)} %get-tuple-element.172), channel_id=1, source_target_pairs={{0,24},{1,25},{2,26},{3,27},{4,28},{5,29},{6,30},{7,31},{8,16},{9,... | collective-permute-start | bytes 245768 | tf_op jit(solution)/shard_map/ppermute | solution.py:422
  116.9 2.5 %collective-permute-done.32.refs_2_ = bf16[5,16,512]{2,1,0:T(8,128)(2,1)S(1)} collective-permute-done((bf16[5,16,512]{2,1,0:T(8,128)(2,1)S(1)}, bf16[5,16,512]{2,1,0:T(8,128)(2,1)S(1)}, u32[]{:S(2)}, u32[]{:S(2)}) %collective-permute-start.32) | collective-permute-done | bytes 81952 | tf_op jit(solution)/shard_map/ppermute | solution.py:422
  (81 shorter events, 28.3 us)
Async XLA Ops:
  1.9 12.1 %all-to-all-start = ((bf16[8,16,1280]{2,1,0:T(8,128)(2,1)}), bf16[8,16,1280]{2,1,0:T(8,128)(2,1)S(1)}, u32[]{:S(2)}, u32[]{:S(2)}) async-start(bf16[8,16,1280]{2,1,0:T(8,128)(2,1)} %shard_map.136), calls=%async_computation | async-start | bytes 655360 | tf_op jit(solution)/shard_map/all_to_all | solution.py:431
  13.9 12.6 %collective-permute-start.4 = (bf16[128,3072]{1,0:T(8,128)(2,1)S(1)}, bf16[128,3072]{1,0:T(8,128)(2,1)S(1)}, u32[]{:S(2)}, u32[]{:S(2)}) collective-permute-start(bf16[128,3072]{1,0:T(8,128)(2,1)S(1)} %get-tuple-element.105.refs_4_), channel_id=1, source_target_pairs={{0,2},{1,3},{2,0},{3,1},{4,6},{5,7},{6,4},{7,5},{8,10},{9,11},{10,... | collective-permute-start | bytes 2359304 | tf_op jit(solution)/shard_map/ppermute | solution.py:422
  14.2 17.8 %collective-permute-start.5 = (bf16[2560,128]{1,0:T(8,128)(2,1)}, bf16[2560,128]{1,0:T(8,128)(2,1)S(1)}, u32[]{:S(2)}, u32[]{:S(2)}) collective-permute-start(bf16[2560,128]{1,0:T(8,128)(2,1)} %copy-done.9), channel_id=1, source_target_pairs={{0,4},{1,5},{2,6},{3,7},{4,0},{5,1},{6,2},{7,3},{8,12},{9,13},{10,... | collective-permute-start | bytes 1966088 | tf_op jit(solution)/shard_map/ppermute | solution.py:422
  16.1 4.5 %collective-permute-start.1 = (bf16[128,256]{1,0:T(8,128)(2,1)S(1)}, bf16[128,256]{1,0:T(8,128)(2,1)S(1)}, u32[]{:S(2)}, u32[]{:S(2)}) collective-permute-start(bf16[128,256]{1,0:T(8,128)(2,1)S(1)} %get-tuple-element.101), channel_id=1, source_target_pairs={{0,8},{1,9},{2,10},{3,11},{4,12},{5,13},{6,14},{7,15},{8,0},{9,1},... | collective-permute-start | bytes 196616 | tf_op jit(solution)/shard_map/ppermute | solution.py:422
  17.8 7.5 %collective-permute-start.2 = (bf16[128,256]{1,0:T(8,128)(2,1)S(1)}, bf16[128,256]{1,0:T(8,128)(2,1)S(1)}, u32[]{:S(2)}, u32[]{:S(2)}) collective-permute-start(bf16[128,256]{1,0:T(8,128)(2,1)S(1)} %get-tuple-element.102), channel_id=1, source_target_pairs={{0,16},{1,17},{2,18},{3,19},{4,20},{5,21},{6,22},{7,23},{8,24},{9,... | collective-permute-start | bytes 196616 | tf_op jit(solution)/shard_map/ppermute | solution.py:422
  20.3 6.2 %collective-permute-start.3 = (bf16[128,256]{1,0:T(8,128)(2,1)S(1)}, bf16[128,256]{1,0:T(8,128)(2,1)S(1)}, u32[]{:S(2)}, u32[]{:S(2)}) collective-permute-start(bf16[128,256]{1,0:T(8,128)(2,1)S(1)} %get-tuple-element.103), channel_id=1, source_target_pairs={{0,24},{1,25},{2,26},{3,27},{4,28},{5,29},{6,30},{7,31},{8,16},{9,... | collective-permute-start | bytes 196616 | tf_op jit(solution)/shard_map/ppermute | solution.py:422
  26.5 22.5 %collective-permute-start.12 = (bf16[128,3072]{1,0:T(8,128)(2,1)}, bf16[128,3072]{1,0:T(8,128)(2,1)S(1)}, u32[]{:S(2)}, u32[]{:S(2)}) collective-permute-start(bf16[128,3072]{1,0:T(8,128)(2,1)} %copy-done.8), channel_id=1, source_target_pairs={{0,4},{1,5},{2,6},{3,7},{4,0},{5,1},{6,2},{7,3},{8,12},{9,13},{10,... | collective-permute-start | bytes 2359304 | tf_op jit(solution)/shard_map/ppermute | solution.py:422
  32.0 7.4 %collective-permute-start.8 = (bf16[96,512]{1,0:T(8,128)(2,1)S(1)}, bf16[96,512]{1,0:T(8,128)(2,1)S(1)}, u32[]{:S(2)}, u32[]{:S(2)}) collective-permute-start(bf16[96,512]{1,0:T(8,128)(2,1)S(1)} %shard_map.140.refs_0_), channel_id=1, source_target_pairs={{0,24},{1,25},{2,26},{3,27},{4,28},{5,29},{6,30},{7,31},{8,16},{9,... | collective-permute-start | bytes 294920 | tf_op jit(solution)/shard_map/ppermute | solution.py:422
  35.6 10.6 %collective-permute-start.10 = (bf16[2,384,128]{2,1,0:T(8,128)(2,1)S(1)}, bf16[2,384,128]{2,1,0:T(8,128)(2,1)S(1)}, u32[]{:S(2)}, u32[]{:S(2)}) collective-permute-start(bf16[2,384,128]{2,1,0:T(8,128)(2,1)S(1)} %get-tuple-element.120), channel_id=1, source_target_pairs={{0,8},{1,9},{2,10},{3,11},{4,12},{5,13},{6,14},{7,15},{8,0},{9,1},... | collective-permute-start | bytes 589832 | tf_op jit(solution)/shard_map/ppermute | solution.py:422
  35.7 10.5 %collective-permute-start.9 = (bf16[512,128]{1,0:T(8,128)(2,1)S(1)}, bf16[512,128]{1,0:T(8,128)(2,1)S(1)}, u32[]{:S(2)}, u32[]{:S(2)}) collective-permute-start(bf16[512,128]{1,0:T(8,128)(2,1)S(1)} %get-tuple-element.118), channel_id=1, source_target_pairs={{0,2},{1,3},{2,0},{3,1},{4,6},{5,7},{6,4},{7,5},{8,10},{9,11},{10,... | collective-permute-start | bytes 393224 | tf_op jit(solution)/shard_map/ppermute | solution.py:422
  35.8 8.3 %collective-permute-start.7 = (bf16[96,512]{1,0:T(8,128)(2,1)S(1)}, bf16[96,512]{1,0:T(8,128)(2,1)S(1)}, u32[]{:S(2)}, u32[]{:S(2)}) collective-permute-start(bf16[96,512]{1,0:T(8,128)(2,1)S(1)} %shard_map.140.refs_0_), channel_id=1, source_target_pairs={{0,16},{1,17},{2,18},{3,19},{4,20},{5,21},{6,22},{7,23},{8,24},{9,... | collective-permute-start | bytes 294920 | tf_op jit(solution)/shard_map/ppermute | solution.py:422
  39.4 6.8 %collective-permute-start.6 = (bf16[96,512]{1,0:T(8,128)(2,1)S(1)}, bf16[96,512]{1,0:T(8,128)(2,1)S(1)}, u32[]{:S(2)}, u32[]{:S(2)}) collective-permute-start(bf16[96,512]{1,0:T(8,128)(2,1)S(1)} %shard_map.140.refs_0_), channel_id=1, source_target_pairs={{0,8},{1,9},{2,10},{3,11},{4,12},{5,13},{6,14},{7,15},{8,0},{9,1},... | collective-permute-start | bytes 294920 | tf_op jit(solution)/shard_map/ppermute | solution.py:422
  47.5 12.4 %collective-permute-start.16 = (bf16[2,384,128]{2,1,0:T(8,128)(2,1)S(1)}, bf16[2,384,128]{2,1,0:T(8,128)(2,1)S(1)}, u32[]{:S(2)}, u32[]{:S(2)}) collective-permute-start(bf16[2,384,128]{2,1,0:T(8,128)(2,1)S(1)} %get-tuple-element.142), channel_id=1, source_target_pairs={{0,16},{1,17},{2,18},{3,19},{4,20},{5,21},{6,22},{7,23},{8,24},{9,... | collective-permute-start | bytes 589832 | tf_op jit(solution)/shard_map/ppermute | solution.py:422
  49.0 4.2 %collective-permute-start.13 = (bf16[48,512]{1,0:T(8,128)(2,1)S(1)}, bf16[48,512]{1,0:T(8,128)(2,1)S(1)}, u32[]{:S(2)}, u32[]{:S(2)}) collective-permute-start(bf16[48,512]{1,0:T(8,128)(2,1)S(1)} %get-tuple-element.138), channel_id=1, source_target_pairs={{0,1},{1,0},{2,3},{3,2},{4,5},{5,4},{6,7},{7,6},{8,9},{9,8},{10,11... | collective-permute-start | bytes 147464 | tf_op jit(solution)/shard_map/ppermute | solution.py:422
  50.8 4.4 %collective-permute-start.14 = (bf16[48,512]{1,0:T(8,128)(2,1)S(1)}, bf16[48,512]{1,0:T(8,128)(2,1)S(1)}, u32[]{:S(2)}, u32[]{:S(2)}) collective-permute-start(bf16[48,512]{1,0:T(8,128)(2,1)S(1)} %get-tuple-element.139), channel_id=1, source_target_pairs={{0,4},{1,5},{2,6},{3,7},{4,0},{5,1},{6,2},{7,3},{8,12},{9,13},{10,... | collective-permute-start | bytes 147464 | tf_op jit(solution)/shard_map/ppermute | solution.py:422
  51.1 5.0 %collective-permute-start.15 = (bf16[48,512]{1,0:T(8,128)(2,1)S(1)}, bf16[48,512]{1,0:T(8,128)(2,1)S(1)}, u32[]{:S(2)}, u32[]{:S(2)}) collective-permute-start(bf16[48,512]{1,0:T(8,128)(2,1)S(1)} %get-tuple-element.140), channel_id=1, source_target_pairs={{0,5},{1,4},{2,7},{3,6},{4,1},{5,0},{6,3},{7,2},{8,13},{9,12},{10,... | collective-permute-start | bytes 147464 | tf_op jit(solution)/shard_map/ppermute | solution.py:422
  60.0 8.7 %collective-permute-start.20 = (bf16[128,3072]{1,0:T(8,128)(2,1)S(1)}, bf16[128,3072]{1,0:T(8,128)(2,1)S(1)}, u32[]{:S(2)}, u32[]{:S(2)}) collective-permute-start(bf16[128,3072]{1,0:T(8,128)(2,1)S(1)} %collective-permute-done.12.refs_6_), channel_id=1, source_target_pairs={{0,2},{1,3},{2,0},{3,1},{4,6},{5,7},{6,4},{7,5},{8,10},{9,11},{10,... | collective-permute-start | bytes 2359304 | tf_op jit(solution)/shard_map/ppermute | solution.py:422
  60.0 10.2 %collective-permute-start.21 = (bf16[2,384,128]{2,1,0:T(8,128)(2,1)S(1)}, bf16[2,384,128]{2,1,0:T(8,128)(2,1)S(1)}, u32[]{:S(2)}, u32[]{:S(2)}) collective-permute-start(bf16[2,384,128]{2,1,0:T(8,128)(2,1)S(1)} %get-tuple-element.151), channel_id=1, source_target_pairs={{0,24},{1,25},{2,26},{3,27},{4,28},{5,29},{6,30},{7,31},{8,16},{9,... | collective-permute-start | bytes 589832 | tf_op jit(solution)/shard_map/ppermute | solution.py:422
  61.5 5.2 %collective-permute-start.19 = (bf16[48,512]{1,0:T(8,128)(2,1)S(1)}, bf16[48,512]{1,0:T(8,128)(2,1)S(1)}, u32[]{:S(2)}, u32[]{:S(2)}) collective-permute-start(bf16[48,512]{1,0:T(8,128)(2,1)S(1)} %shard_map.144.refs_0_.hidden), channel_id=1, source_target_pairs={{0,5},{1,4},{2,7},{3,6},{4,1},{5,0},{6,3},{7,2},{8,13},{9,12},{10,... | collective-permute-start | bytes 147464 | tf_op jit(solution)/shard_map/ppermute | solution.py:422
  63.0 4.4 %collective-permute-start.18 = (bf16[48,512]{1,0:T(8,128)(2,1)S(1)}, bf16[48,512]{1,0:T(8,128)(2,1)S(1)}, u32[]{:S(2)}, u32[]{:S(2)}) collective-permute-start(bf16[48,512]{1,0:T(8,128)(2,1)S(1)} %shard_map.144.refs_0_.hidden), channel_id=1, source_target_pairs={{0,4},{1,5},{2,6},{3,7},{4,0},{5,1},{6,2},{7,3},{8,12},{9,13},{10,... | collective-permute-start | bytes 147464 | tf_op jit(solution)/shard_map/ppermute | solution.py:422
  70.2 26.8 %collective-permute-start.27 = (bf16[4,2,384,128]{3,2,1,0:T(8,128)(2,1)S(1)}, bf16[4,2,384,128]{3,2,1,0:T(8,128)(2,1)S(1)}, u32[]{:S(2)}, u32[]{:S(2)}) collective-permute-start(bf16[4,2,384,128]{3,2,1,0:T(8,128)(2,1)S(1)} %shard_map.148.near), channel_id=1, source_target_pairs={{0,2},{1,3},{2,0},{3,1},{4,6},{5,7},{6,4},{7,5},{8,10},{9,11},{10,... | collective-permute-start | bytes 2359304 | tf_op jit(solution)/shard_map/ppermute | solution.py:422
  70.3 6.8 %collective-permute-start.22 = (bf16[112,768]{1,0:T(8,128)(2,1)S(1)}, bf16[112,768]{1,0:T(8,128)(2,1)S(1)}, u32[]{:S(2)}, u32[]{:S(2)}) collective-permute-start(bf16[112,768]{1,0:T(8,128)(2,1)S(1)} %get-tuple-element.152), channel_id=1, source_target_pairs={{0,8},{1,9},{2,10},{3,11},{4,12},{5,13},{6,14},{7,15},{8,0},{9,1},... | collective-permute-start | bytes 516104 | tf_op jit(solution)/shard_map/ppermute | solution.py:422
  77.1 5.4 %collective-permute-start.23 = (bf16[96,768]{1,0:T(8,128)(2,1)S(1)}, bf16[96,768]{1,0:T(8,128)(2,1)S(1)}, u32[]{:S(2)}, u32[]{:S(2)}) collective-permute-start(bf16[96,768]{1,0:T(8,128)(2,1)S(1)} %get-tuple-element.154), channel_id=1, source_target_pairs={{0,8},{1,9},{2,10},{3,11},{4,12},{5,13},{6,14},{7,15},{8,0},{9,1},... | collective-permute-start | bytes 442376 | tf_op jit(solution)/shard_map/ppermute | solution.py:422
  82.5 14.5 %collective-permute-start.24 = (bf16[208,768]{1,0:T(8,128)(2,1)S(1)}, bf16[208,768]{1,0:T(8,128)(2,1)S(1)}, u32[]{:S(2)}, u32[]{:S(2)}) collective-permute-start(bf16[208,768]{1,0:T(8,128)(2,1)S(1)} %get-tuple-element.156), channel_id=1, source_target_pairs={{0,8},{1,9},{2,10},{3,11},{4,12},{5,13},{6,14},{7,15},{8,0},{9,1},... | collective-permute-start | bytes 958472 | tf_op jit(solution)/shard_map/ppermute | solution.py:422
  83.0 11.2 %collective-permute-start.25 = (bf16[112,768]{1,0:T(8,128)(2,1)S(1)}, bf16[112,768]{1,0:T(8,128)(2,1)S(1)}, u32[]{:S(2)}, u32[]{:S(2)}) collective-permute-start(bf16[112,768]{1,0:T(8,128)(2,1)S(1)} %shard_map.146), channel_id=1, source_target_pairs={{0,16},{1,17},{2,18},{3,19},{4,20},{5,21},{6,22},{7,23},{8,24},{9,... | collective-permute-start | bytes 516104 | tf_op jit(solution)/shard_map/ppermute | solution.py:422
  85.7 15.1 %collective-permute-start.26 = (bf16[96,768]{1,0:T(8,128)(2,1)S(1)}, bf16[96,768]{1,0:T(8,128)(2,1)S(1)}, u32[]{:S(2)}, u32[]{:S(2)}) collective-permute-start(bf16[96,768]{1,0:T(8,128)(2,1)S(1)} %shard_map.147), channel_id=1, source_target_pairs={{0,16},{1,17},{2,18},{3,19},{4,20},{5,21},{6,22},{7,23},{8,24},{9,... | collective-permute-start | bytes 442376 | tf_op jit(solution)/shard_map/ppermute | solution.py:422
  98.2 7.6 %collective-permute-start.29 = (bf16[4,48,512]{2,1,0:T(8,128)(2,1)S(1)}, bf16[4,48,512]{2,1,0:T(8,128)(2,1)S(1)}, u32[]{:S(2)}, u32[]{:S(2)}) collective-permute-start(bf16[4,48,512]{2,1,0:T(8,128)(2,1)S(1)} %get-tuple-element.167), channel_id=1, source_target_pairs={{0,4},{1,5},{2,6},{3,7},{4,0},{5,1},{6,2},{7,3},{8,12},{9,13},{10,... | collective-permute-start | bytes 589832 | tf_op jit(solution)/shard_map/ppermute | solution.py:422
  99.1 9.2 %collective-permute-start.30 = (bf16[4,48,512]{2,1,0:T(8,128)(2,1)S(1)}, bf16[4,48,512]{2,1,0:T(8,128)(2,1)S(1)}, u32[]{:S(2)}, u32[]{:S(2)}) collective-permute-start(bf16[4,48,512]{2,1,0:T(8,128)(2,1)S(1)} %get-tuple-element.168), channel_id=1, source_target_pairs={{0,5},{1,4},{2,7},{3,6},{4,1},{5,0},{6,3},{7,2},{8,13},{9,12},{10,... | collective-permute-start | bytes 589832 | tf_op jit(solution)/shard_map/ppermute | solution.py:422
  102.0 8.3 %collective-permute-start.28 = (bf16[4,48,512]{2,1,0:T(8,128)(2,1)S(1)}, bf16[4,48,512]{2,1,0:T(8,128)(2,1)S(1)}, u32[]{:S(2)}, u32[]{:S(2)}) collective-permute-start(bf16[4,48,512]{2,1,0:T(8,128)(2,1)S(1)} %get-tuple-element.166), channel_id=1, source_target_pairs={{0,1},{1,0},{2,3},{3,2},{4,5},{5,4},{6,7},{7,6},{8,9},{9,8},{10,11... | collective-permute-start | bytes 589832 | tf_op jit(solution)/shard_map/ppermute | solution.py:422
  111.2 5.7 %collective-permute-start.31 = (bf16[5,16,512]{2,1,0:T(8,128)(2,1)S(1)}, bf16[5,16,512]{2,1,0:T(8,128)(2,1)S(1)}, u32[]{:S(2)}, u32[]{:S(2)}) collective-permute-start(bf16[5,16,512]{2,1,0:T(8,128)(2,1)S(1)} %get-tuple-element.170), channel_id=1, source_target_pairs={{0,8},{1,9},{2,10},{3,11},{4,12},{5,13},{6,14},{7,15},{8,0},{9,1},... | collective-permute-start | bytes 245768 | tf_op jit(solution)/shard_map/ppermute | solution.py:422
  111.3 8.1 %collective-permute-start.32 = (bf16[5,16,512]{2,1,0:T(8,128)(2,1)S(1)}, bf16[5,16,512]{2,1,0:T(8,128)(2,1)S(1)}, u32[]{:S(2)}, u32[]{:S(2)}) collective-permute-start(bf16[5,16,512]{2,1,0:T(8,128)(2,1)S(1)} %get-tuple-element.171), channel_id=1, source_target_pairs={{0,16},{1,17},{2,18},{3,19},{4,20},{5,21},{6,22},{7,23},{8,24},{9,... | collective-permute-start | bytes 245768 | tf_op jit(solution)/shard_map/ppermute | solution.py:422
  112.3 7.1 %collective-permute-start.33 = (bf16[5,16,512]{2,1,0:T(8,128)(2,1)S(1)}, bf16[5,16,512]{2,1,0:T(8,128)(2,1)S(1)}, u32[]{:S(2)}, u32[]{:S(2)}) collective-permute-start(bf16[5,16,512]{2,1,0:T(8,128)(2,1)S(1)} %get-tuple-element.172), channel_id=1, source_target_pairs={{0,24},{1,25},{2,26},{3,27},{4,28},{5,29},{6,30},{7,31},{8,16},{9,... | collective-permute-start | bytes 245768 | tf_op jit(solution)/shard_map/ppermute | solution.py:422
  (14 other events, 64.8 us)

commit v6 on v5

--- a/solution.py
+++ b/solution.py
@@ -335,36 +335,34 @@
                 out[z ^ k, :, at] = block[i * rows:(i + 1) * rows].astype(out.dtype)
 
 
-def row_of(z, k, tokens, rows, total):
-    i = lax.broadcasted_iota(jnp.int32, (rows, total), 0)
-    j = lax.broadcasted_iota(jnp.int32, (rows, total), 1)
-    return jnp.where((j == i + (z ^ k) * tokens) & (i < tokens), 1.0, 0.0).astype(BF16)
-
-
 def plane_sum_kernel(planes, tokens, idx, hidden, *refs):
     parts, outs = refs[:-planes], refs[-planes:]
     total = parts[0][...]
     for part in parts[1:]:
         total = total + part[...].astype(F32)
     total = total.astype(BF16)
+    share = hidden.shape[0]
+    source = jnp.concatenate([total[p] for p in range(planes)] + [hidden[...]])
     for k, out in enumerate(outs):
-        pick = row_of(idx[0], k, tokens, out.shape[1], total.shape[1])
-        for p in range(planes):
-            out[p] = dot(pick, total[p]).astype(BF16)
-        out[planes] = dot(pick, hidden[...]).astype(BF16)
+        i = lax.broadcasted_iota(jnp.int32, (out.shape[0], source.shape[0]), 0)
+        j = lax.broadcasted_iota(jnp.int32, (out.shape[0], source.shape[0]), 1)
+        spot = i // tokens * share + (idx[0] ^ k) * tokens + i % tokens
+        pick = jnp.where((spot == j) & (i < (planes + 1) * tokens), 1.0, 0.0).astype(BF16)
+        out[...] = dot(pick, source).astype(BF16)
 
 
 def last_kernel(planes, tokens, idx, *refs):
     *parts, out, held = refs
-    width = parts[0].shape[2]
-    total = parts[0][:planes].astype(F32)
+    width = parts[0].shape[1]
+    total = parts[0][...].astype(F32)
     for part in parts[1:]:
-        total = total + part[:planes].astype(F32)
+        total = total + part[...].astype(F32)
+    end = planes * tokens
     for k, part in enumerate(parts):
-        held[idx[0] ^ k] = part[planes].astype(F32)
+        held[idx[0] ^ k, :tokens] = part[...].astype(F32)[end:end + tokens]
     for p in range(planes):
-        value = held[p] + total[p]
-        out[:, p * width:(p + 1) * width] = value[:tokens].astype(BF16)
+        value = held[p, :tokens] + total[p * tokens:(p + 1) * tokens]
+        out[:, p * width:(p + 1) * width] = value.astype(BF16)
 
 
 def call(kernel, outs, *args, scratch=(), place=VMEM, limit=16):
@@ -566,7 +564,6 @@
         )
 
     got = swap(far_sends[0], group)
-    got, far_sends[1] = after(got, far_sends[1])
     far_head = swap(far_sum(0, got), group_far)
     got, near_send = after(swap(far_sends[1], group), near_send)
     far_rest = swap(far_sum(1, got), group_far)
@@ -586,7 +583,7 @@
     rest = [early] + late
     parts = call(
         functools.partial(plane_sum_kernel, planes, tokens),
-        [like(planes + 1, rows, width)] * planes,
+        [like(-(-(planes + 1) * tokens // ROW_TILE) * ROW_TILE, width)] * planes,
         idx, hidden, own, *[swap(x, b) for x, b in zip(rest, steps)],
     )
     return call(

time: 121 us -> 118 us (0.975)
  waiting for transfers between devices: 63.4 us -> 59.1 us
  starting transfers between devices: 38.7 us -> 40.1 us
    ppermute x34, waiting for transfers between devices: 62.2 us -> 58 us  [swap(): return lax.ppermute(x, axes, [(i, i ^ mask) for i in range(devices)])]
    ppermute x34, starting transfers between devices: 33.4 us -> 34.8 us  [swap(): return lax.ppermute(x, axes, [(i, i ^ mask) for i in range(devices)])]
  transfers between devices with their start and end apart: 35 -> 35, of which waited for: 24 -> 23; matrix products, arithmetic and copies ran while one was open for 0% -> 0% of each run, Pallas kernels for 9% -> 9%
where the time goes in v6:
time: 118 us
  waiting for transfers between devices  59.1 us (50%)
  starting transfers between devices  40.1 us (34%)
  Pallas kernels  14.5 us (12%)
  local copies, waits for them, and re-layouts  3 us (3%)
    ppermute x34, waiting for transfers between devices, swap(): return lax.ppermute(x, axes, [(i, i ^ mask) for i in range(devices)])  58 us
    ppermute x34, starting transfers between devices, swap(): return lax.ppermute(x, axes, [(i, i ^ mask) for i in range(devices)])  34.8 us
    pallas_call x17, Pallas kernels, call(): pl.pallas_call(kernel, out_shape=shapes, in_specs=[SMEM if a.dtype == jnp...  14.5 us
    all_to_all x1, starting transfers between devices, plane_exchange(): lax.all_to_all(x, axes, 0, 0, axis_index_groups=plane_groups, tiled=True)  5.31 us
    unnamed x22, local copies, waits for them, and re-layouts  2.92 us
  transfers between devices with their start and end apart: 35, of which 23 were waited for; matrix products, arithmetic and copies ran while one was open for 0% of the time, Pallas kernels for 9%

profile of v6, /device:TPU:0, one launch (start us, length us, event | category | flops | bytes accessed | tf_op | source)
XLA Modules:
  0.0 117.8 jit_solution(15692731495048814946)
XLA Ops:
  0.0 1.8 %shard_map.136 = bf16[8,16,1280]{2,1,0:T(8,128)(2,1)} custom-call(bf16[12,1024]{1,0:T(8,128)(2,1)} %refs_0_.1, bf16[12,1024]{1,0:T(8,128)(2,1)} %refs_1_.1, bf16[12,4096]{1,0:T(8,128)(2,1)} %refs_2_.1, bf16[12,4096]{1,0:T(8,128)(2,1)} %refs_3_.1), custom_call_target="tpu_custom_call" | custom-call | tf_op jit(solution)/shard_map/pallas_call | solution.py:371
  1.9 5.3 %all-to-all-start = ((bf16[8,16,1280]{2,1,0:T(8,128)(2,1)}), bf16[8,16,1280]{2,1,0:T(8,128)(2,1)S(1)}, u32[]{:S(2)}, u32[]{:S(2)}) async-start(bf16[8,16,1280]{2,1,0:T(8,128)(2,1)} %shard_map.136), calls=%async_computation | async-start | bytes 655360 | tf_op jit(solution)/shard_map/all_to_all | solution.py:429
  16.1 1.6 %collective-permute-start.1 = (bf16[128,256]{1,0:T(8,128)(2,1)S(1)}, bf16[128,256]{1,0:T(8,128)(2,1)S(1)}, u32[]{:S(2)}, u32[]{:S(2)}) collective-permute-start(bf16[128,256]{1,0:T(8,128)(2,1)S(1)} %get-tuple-element.99), channel_id=1, source_target_pairs={{0,8},{1,9},{2,10},{3,11},{4,12},{5,13},{6,14},{7,15},{8,0},{9,1},... | collective-permute-start | bytes 196616 | tf_op jit(solution)/shard_map/ppermute | solution.py:420
  17.8 2.6 %collective-permute-start.2 = (bf16[128,256]{1,0:T(8,128)(2,1)S(1)}, bf16[128,256]{1,0:T(8,128)(2,1)S(1)}, u32[]{:S(2)}, u32[]{:S(2)}) collective-permute-start(bf16[128,256]{1,0:T(8,128)(2,1)S(1)} %get-tuple-element.100), channel_id=1, source_target_pairs={{0,16},{1,17},{2,18},{3,19},{4,20},{5,21},{6,22},{7,23},{8,24},{9,... | collective-permute-start | bytes 196616 | tf_op jit(solution)/shard_map/ppermute | solution.py:420
  20.6 4.7 %collective-permute-done.2.refs_2_.refs_6_ = bf16[128,256]{1,0:T(8,128)(2,1)S(1)} collective-permute-done((bf16[128,256]{1,0:T(8,128)(2,1)S(1)}, bf16[128,256]{1,0:T(8,128)(2,1)S(1)}, u32[]{:S(2)}, u32[]{:S(2)}) %collective-permute-start.2) | collective-permute-done | bytes 65568 | tf_op jit(solution)/shard_map/ppermute | solution.py:420
  28.0 1.9 %shard_map.140.refs_0_ = bf16[96,512]{1,0:T(8,128)(2,1)S(1)} custom-call(s32[4]{0:T(128)S(1)} %pad_add_fusion.idx, s32[1]{0:T(128)S(6)} %copy.15.prefix, bf16[8,16,1280]{2,1,0:T(8,128)(2,1)S(1)} %all-to-all-done.heads.qg, bf16[128,256]{1,0:T(8,128)(2,1)S(1)} %get-tuple-element.104.refs_0_.refs_4_, ...), custom_call_target="tpu_custom_call" | custom-call | tf_op jit(solution)/shard_map/pallas_call | solution.py:371
  29.8 2.1 %collective-permute-done.5.message = bf16[2560,128]{1,0:T(8,128)(2,1)S(1)} collective-permute-done((bf16[2560,128]{1,0:T(8,128)(2,1)}, bf16[2560,128]{1,0:T(8,128)(2,1)S(1)}, u32[]{:S(2)}, u32[]{:S(2)}) %collective-permute-start.5) | collective-permute-done | bytes 655392 | tf_op jit(solution)/shard_map/ppermute | solution.py:420
  32.0 3.6 %collective-permute-start.8 = (bf16[96,512]{1,0:T(8,128)(2,1)S(1)}, bf16[96,512]{1,0:T(8,128)(2,1)S(1)}, u32[]{:S(2)}, u32[]{:S(2)}) collective-permute-start(bf16[96,512]{1,0:T(8,128)(2,1)S(1)} %shard_map.140.refs_0_), channel_id=1, source_target_pairs={{0,24},{1,25},{2,26},{3,27},{4,28},{5,29},{6,30},{7,31},{8,16},{9,... | collective-permute-start | bytes 294920 | tf_op jit(solution)/shard_map/ppermute | solution.py:420
  36.5 2.9 %collective-permute-done.8.refs_3_ = bf16[96,512]{1,0:T(8,128)(2,1)S(1)} collective-permute-done((bf16[96,512]{1,0:T(8,128)(2,1)S(1)}, bf16[96,512]{1,0:T(8,128)(2,1)S(1)}, u32[]{:S(2)}, u32[]{:S(2)}) %collective-permute-start.8) | collective-permute-done | bytes 98336 | tf_op jit(solution)/shard_map/ppermute | solution.py:420
  39.4 4.7 %collective-permute-done.7.refs_2_ = bf16[96,512]{1,0:T(8,128)(2,1)S(1)} collective-permute-done((bf16[96,512]{1,0:T(8,128)(2,1)S(1)}, bf16[96,512]{1,0:T(8,128)(2,1)S(1)}, u32[]{:S(2)}, u32[]{:S(2)}) %collective-permute-start.7) | collective-permute-done | bytes 98336 | tf_op jit(solution)/shard_map/ppermute | solution.py:420
  44.1 2.1 %collective-permute-done.6.refs_1_ = bf16[96,512]{1,0:T(8,128)(2,1)S(1)} collective-permute-done((bf16[96,512]{1,0:T(8,128)(2,1)S(1)}, bf16[96,512]{1,0:T(8,128)(2,1)S(1)}, u32[]{:S(2)}, u32[]{:S(2)}) %collective-permute-start.6) | collective-permute-done | bytes 98336 | tf_op jit(solution)/shard_map/ppermute | solution.py:420
  49.0 1.8 %collective-permute-start.13 = (bf16[48,512]{1,0:T(8,128)(2,1)S(1)}, bf16[48,512]{1,0:T(8,128)(2,1)S(1)}, u32[]{:S(2)}, u32[]{:S(2)}) collective-permute-start(bf16[48,512]{1,0:T(8,128)(2,1)S(1)} %get-tuple-element.136), channel_id=1, source_target_pairs={{0,1},{1,0},{2,3},{3,2},{4,5},{5,4},{6,7},{7,6},{8,9},{9,8},{10,11... | collective-permute-start | bytes 147464 | tf_op jit(solution)/shard_map/ppermute | solution.py:420
  51.1 1.5 %collective-permute-start.15 = (bf16[48,512]{1,0:T(8,128)(2,1)S(1)}, bf16[48,512]{1,0:T(8,128)(2,1)S(1)}, u32[]{:S(2)}, u32[]{:S(2)}) collective-permute-start(bf16[48,512]{1,0:T(8,128)(2,1)S(1)} %get-tuple-element.138), channel_id=1, source_target_pairs={{0,5},{1,4},{2,7},{3,6},{4,1},{5,0},{6,3},{7,2},{8,13},{9,12},{10,... | collective-permute-start | bytes 147464 | tf_op jit(solution)/shard_map/ppermute | solution.py:420
  53.2 2.1 %collective-permute-done.14.refs_2_ = bf16[48,512]{1,0:T(8,128)(2,1)S(1)} collective-permute-done((bf16[48,512]{1,0:T(8,128)(2,1)S(1)}, bf16[48,512]{1,0:T(8,128)(2,1)S(1)}, u32[]{:S(2)}, u32[]{:S(2)}) %collective-permute-start.14) | collective-permute-done | bytes 49184 | tf_op jit(solution)/shard_map/ppermute | solution.py:420
  56.8 3.1 %collective-permute-done.16.refs_2_ = bf16[2,384,128]{2,1,0:T(8,128)(2,1)S(1)} collective-permute-done((bf16[2,384,128]{2,1,0:T(8,128)(2,1)S(1)}, bf16[2,384,128]{2,1,0:T(8,128)(2,1)S(1)}, u32[]{:S(2)}, u32[]{:S(2)}) %collective-permute-start.16) | collective-permute-done | bytes 196640 | tf_op jit(solution)/shard_map/ppermute | solution.py:420
  60.0 1.5 %collective-permute-start.23 = (bf16[2,384,128]{2,1,0:T(8,128)(2,1)S(1)}, bf16[2,384,128]{2,1,0:T(8,128)(2,1)S(1)}, u32[]{:S(2)}, u32[]{:S(2)}) collective-permute-start(bf16[2,384,128]{2,1,0:T(8,128)(2,1)S(1)} %get-tuple-element.153), channel_id=1, source_target_pairs={{0,24},{1,25},{2,26},{3,27},{4,28},{5,29},{6,30},{7,31},{8,16},{9,... | collective-permute-start | bytes 589832 | tf_op jit(solution)/shard_map/ppermute | solution.py:420
  61.5 1.5 %collective-permute-start.19 = (bf16[48,512]{1,0:T(8,128)(2,1)S(1)}, bf16[48,512]{1,0:T(8,128)(2,1)S(1)}, u32[]{:S(2)}, u32[]{:S(2)}) collective-permute-start(bf16[48,512]{1,0:T(8,128)(2,1)S(1)} %shard_map.144.refs_0_.hidden), channel_id=1, source_target_pairs={{0,5},{1,4},{2,7},{3,6},{4,1},{5,0},{6,3},{7,2},{8,13},{9,12},{10,... | collective-permute-start | bytes 147464 | tf_op jit(solution)/shard_map/ppermute | solution.py:420
  63.0 1.5 %collective-permute-start.18 = (bf16[48,512]{1,0:T(8,128)(2,1)S(1)}, bf16[48,512]{1,0:T(8,128)(2,1)S(1)}, u32[]{:S(2)}, u32[]{:S(2)}) collective-permute-start(bf16[48,512]{1,0:T(8,128)(2,1)S(1)} %shard_map.144.refs_0_.hidden), channel_id=1, source_target_pairs={{0,4},{1,5},{2,6},{3,7},{4,0},{5,1},{6,2},{7,3},{8,12},{9,13},{10,... | collective-permute-start | bytes 147464 | tf_op jit(solution)/shard_map/ppermute | solution.py:420
  65.0 1.7 %collective-permute-done.19.refs_3_ = bf16[48,512]{1,0:T(8,128)(2,1)S(1)} collective-permute-done((bf16[48,512]{1,0:T(8,128)(2,1)S(1)}, bf16[48,512]{1,0:T(8,128)(2,1)S(1)}, u32[]{:S(2)}, u32[]{:S(2)}) %collective-permute-start.19) | collective-permute-done | bytes 49184 | tf_op jit(solution)/shard_map/ppermute | solution.py:420
  68.6 1.5 %shard_map.145 = (f32[208,768]{1,0:T(8,128)S(1)}, bf16[208,768]{1,0:T(8,128)(2,1)S(1)}, f32[112,768]{1,0:T(8,128)S(1)}, f32[96,768]{1,0:T(8,128)S(1)}, bf16[112,...) custom-call(s32[4]{0:T(128)S(1)} %pad_add_fusion.idx, bf16[48,512]{1,0:T(8,128)(2,1)S(1)} %shard_map.144.refs_0_.hidden, ...), custom_call_target="tpu_custom_call" | custom-call | tf_op jit(solution)/shard_map/pallas_call | solution.py:371
  70.4 2.0 %collective-permute-start.24 = (bf16[112,768]{1,0:T(8,128)(2,1)S(1)}, bf16[112,768]{1,0:T(8,128)(2,1)S(1)}, u32[]{:S(2)}, u32[]{:S(2)}) collective-permute-start(bf16[112,768]{1,0:T(8,128)(2,1)S(1)} %get-tuple-element.154), channel_id=1, source_target_pairs={{0,8},{1,9},{2,10},{3,11},{4,12},{5,13},{6,14},{7,15},{8,0},{9,1},... | collective-permute-start | bytes 516104 | tf_op jit(solution)/shard_map/ppermute | solution.py:420
  72.4 4.6 %collective-permute-done.21.got = bf16[96,768]{1,0:T(8,128)(2,1)S(1)} collective-permute-done((bf16[96,768]{1,0:T(8,128)(2,1)S(1)}, bf16[96,768]{1,0:T(8,128)(2,1)S(1)}, u32[]{:S(2)}, u32[]{:S(2)}) %collective-permute-start.21) | collective-permute-done | bytes 147488 | tf_op jit(solution)/shard_map/ppermute | solution.py:420
  77.1 3.6 %collective-permute-done.24.got = bf16[112,768]{1,0:T(8,128)(2,1)S(1)} collective-permute-done((bf16[112,768]{1,0:T(8,128)(2,1)S(1)}, bf16[112,768]{1,0:T(8,128)(2,1)S(1)}, u32[]{:S(2)}, u32[]{:S(2)}) %collective-permute-start.24) | collective-permute-done | bytes 172064 | tf_op jit(solution)/shard_map/ppermute | solution.py:420
  81.9 1.9 %collective-permute-start.26 = (bf16[96,768]{1,0:T(8,128)(2,1)S(1)}, bf16[96,768]{1,0:T(8,128)(2,1)S(1)}, u32[]{:S(2)}, u32[]{:S(2)}) collective-permute-start(bf16[96,768]{1,0:T(8,128)(2,1)S(1)} %shard_map.147), channel_id=1, source_target_pairs={{0,16},{1,17},{2,18},{3,19},{4,20},{5,21},{6,22},{7,23},{8,24},{9,... | collective-permute-start | bytes 442376 | tf_op jit(solution)/shard_map/ppermute | solution.py:420
  83.8 11.8 %collective-permute-done.25.far_head.far_part = bf16[112,768]{1,0:T(8,128)(2,1)S(1)} collective-permute-done((bf16[112,768]{1,0:T(8,128)(2,1)S(1)}, bf16[112,768]{1,0:T(8,128)(2,1)S(1)}, u32[]{:S(2)}, u32[]{:S(2)}) %collective-permute-start.25) | collective-permute-done | bytes 172064 | tf_op jit(solution)/shard_map/ppermute | solution.py:420
  97.5 1.7 %collective-permute-start.30 = (bf16[4,48,512]{2,1,0:T(8,128)(2,1)S(1)}, bf16[4,48,512]{2,1,0:T(8,128)(2,1)S(1)}, u32[]{:S(2)}, u32[]{:S(2)}) collective-permute-start(bf16[4,48,512]{2,1,0:T(8,128)(2,1)S(1)} %get-tuple-element.164), channel_id=1, source_target_pairs={{0,5},{1,4},{2,7},{3,6},{4,1},{5,0},{6,3},{7,2},{8,13},{9,12},{10,... | collective-permute-start | bytes 589832 | tf_op jit(solution)/shard_map/ppermute | solution.py:420
  100.4 1.3 %collective-permute-start.28 = (bf16[4,48,512]{2,1,0:T(8,128)(2,1)S(1)}, bf16[4,48,512]{2,1,0:T(8,128)(2,1)S(1)}, u32[]{:S(2)}, u32[]{:S(2)}) collective-permute-start(bf16[4,48,512]{2,1,0:T(8,128)(2,1)S(1)} %get-tuple-element.162), channel_id=1, source_target_pairs={{0,1},{1,0},{2,3},{3,2},{4,5},{5,4},{6,7},{7,6},{8,9},{9,8},{10,11... | collective-permute-start | bytes 589832 | tf_op jit(solution)/shard_map/ppermute | solution.py:420
  102.6 2.4 %collective-permute-done.30.refs_3_ = bf16[4,48,512]{2,1,0:T(8,128)(2,1)S(1)} collective-permute-done((bf16[4,48,512]{2,1,0:T(8,128)(2,1)S(1)}, bf16[4,48,512]{2,1,0:T(8,128)(2,1)S(1)}, u32[]{:S(2)}, u32[]{:S(2)}) %collective-permute-start.30) | collective-permute-done | bytes 196640 | tf_op jit(solution)/shard_map/ppermute | solution.py:420
  105.1 2.0 %collective-permute-done.28.refs_1_ = bf16[4,48,512]{2,1,0:T(8,128)(2,1)S(1)} collective-permute-done((bf16[4,48,512]{2,1,0:T(8,128)(2,1)S(1)}, bf16[4,48,512]{2,1,0:T(8,128)(2,1)S(1)}, u32[]{:S(2)}, u32[]{:S(2)}) %collective-permute-start.28) | collective-permute-done | bytes 196640 | tf_op jit(solution)/shard_map/ppermute | solution.py:420
  108.0 2.5 %collective-permute-start.32 = (bf16[64,512]{1,0:T(8,128)(2,1)S(1)}, bf16[64,512]{1,0:T(8,128)(2,1)S(1)}, u32[]{:S(2)}, u32[]{:S(2)}) collective-permute-start(bf16[64,512]{1,0:T(8,128)(2,1)S(1)} %get-tuple-element.167), channel_id=1, source_target_pairs={{0,16},{1,17},{2,18},{3,19},{4,20},{5,21},{6,22},{7,23},{8,24},{9,... | collective-permute-start | bytes 196616 | tf_op jit(solution)/shard_map/ppermute | solution.py:420
  110.6 1.9 %collective-permute-start.33 = (bf16[64,512]{1,0:T(8,128)(2,1)S(1)}, bf16[64,512]{1,0:T(8,128)(2,1)S(1)}, u32[]{:S(2)}, u32[]{:S(2)}) collective-permute-start(bf16[64,512]{1,0:T(8,128)(2,1)S(1)} %get-tuple-element.168), channel_id=1, source_target_pairs={{0,24},{1,25},{2,26},{3,27},{4,28},{5,29},{6,30},{7,31},{8,16},{9,... | collective-permute-start | bytes 196616 | tf_op jit(solution)/shard_map/ppermute | solution.py:420
  113.3 3.4 %collective-permute-done.33.refs_3_ = bf16[64,512]{1,0:T(8,128)(2,1)S(1)} collective-permute-done((bf16[64,512]{1,0:T(8,128)(2,1)S(1)}, bf16[64,512]{1,0:T(8,128)(2,1)S(1)}, u32[]{:S(2)}, u32[]{:S(2)}) %collective-permute-start.33) | collective-permute-done | bytes 65568 | tf_op jit(solution)/shard_map/ppermute | solution.py:420
  (81 shorter events, 28.0 us)
Async XLA Ops:
  1.9 12.1 %all-to-all-start = ((bf16[8,16,1280]{2,1,0:T(8,128)(2,1)}), bf16[8,16,1280]{2,1,0:T(8,128)(2,1)S(1)}, u32[]{:S(2)}, u32[]{:S(2)}) async-start(bf16[8,16,1280]{2,1,0:T(8,128)(2,1)} %shard_map.136), calls=%async_computation | async-start | bytes 655360 | tf_op jit(solution)/shard_map/all_to_all | solution.py:429
  13.9 12.6 %collective-permute-start.4 = (bf16[128,3072]{1,0:T(8,128)(2,1)S(1)}, bf16[128,3072]{1,0:T(8,128)(2,1)S(1)}, u32[]{:S(2)}, u32[]{:S(2)}) collective-permute-start(bf16[128,3072]{1,0:T(8,128)(2,1)S(1)} %get-tuple-element.103.refs_4_), channel_id=1, source_target_pairs={{0,2},{1,3},{2,0},{3,1},{4,6},{5,7},{6,4},{7,5},{8,10},{9,11},{10,... | collective-permute-start | bytes 2359304 | tf_op jit(solution)/shard_map/ppermute | solution.py:420
  14.2 17.8 %collective-permute-start.5 = (bf16[2560,128]{1,0:T(8,128)(2,1)}, bf16[2560,128]{1,0:T(8,128)(2,1)S(1)}, u32[]{:S(2)}, u32[]{:S(2)}) collective-permute-start(bf16[2560,128]{1,0:T(8,128)(2,1)} %copy-done.9), channel_id=1, source_target_pairs={{0,4},{1,5},{2,6},{3,7},{4,0},{5,1},{6,2},{7,3},{8,12},{9,13},{10,... | collective-permute-start | bytes 1966088 | tf_op jit(solution)/shard_map/ppermute | solution.py:420
  16.1 4.5 %collective-permute-start.1 = (bf16[128,256]{1,0:T(8,128)(2,1)S(1)}, bf16[128,256]{1,0:T(8,128)(2,1)S(1)}, u32[]{:S(2)}, u32[]{:S(2)}) collective-permute-start(bf16[128,256]{1,0:T(8,128)(2,1)S(1)} %get-tuple-element.99), channel_id=1, source_target_pairs={{0,8},{1,9},{2,10},{3,11},{4,12},{5,13},{6,14},{7,15},{8,0},{9,1},... | collective-permute-start | bytes 196616 | tf_op jit(solution)/shard_map/ppermute | solution.py:420
  17.8 7.5 %collective-permute-start.2 = (bf16[128,256]{1,0:T(8,128)(2,1)S(1)}, bf16[128,256]{1,0:T(8,128)(2,1)S(1)}, u32[]{:S(2)}, u32[]{:S(2)}) collective-permute-start(bf16[128,256]{1,0:T(8,128)(2,1)S(1)} %get-tuple-element.100), channel_id=1, source_target_pairs={{0,16},{1,17},{2,18},{3,19},{4,20},{5,21},{6,22},{7,23},{8,24},{9,... | collective-permute-start | bytes 196616 | tf_op jit(solution)/shard_map/ppermute | solution.py:420
  20.3 6.2 %collective-permute-start.3 = (bf16[128,256]{1,0:T(8,128)(2,1)S(1)}, bf16[128,256]{1,0:T(8,128)(2,1)S(1)}, u32[]{:S(2)}, u32[]{:S(2)}) collective-permute-start(bf16[128,256]{1,0:T(8,128)(2,1)S(1)} %get-tuple-element.101), channel_id=1, source_target_pairs={{0,24},{1,25},{2,26},{3,27},{4,28},{5,29},{6,30},{7,31},{8,16},{9,... | collective-permute-start | bytes 196616 | tf_op jit(solution)/shard_map/ppermute | solution.py:420
  26.5 22.5 %collective-permute-start.12 = (bf16[128,3072]{1,0:T(8,128)(2,1)}, bf16[128,3072]{1,0:T(8,128)(2,1)S(1)}, u32[]{:S(2)}, u32[]{:S(2)}) collective-permute-start(bf16[128,3072]{1,0:T(8,128)(2,1)} %copy-done.8), channel_id=1, source_target_pairs={{0,4},{1,5},{2,6},{3,7},{4,0},{5,1},{6,2},{7,3},{8,12},{9,13},{10,... | collective-permute-start | bytes 2359304 | tf_op jit(solution)/shard_map/ppermute | solution.py:420
  32.0 7.4 %collective-permute-start.8 = (bf16[96,512]{1,0:T(8,128)(2,1)S(1)}, bf16[96,512]{1,0:T(8,128)(2,1)S(1)}, u32[]{:S(2)}, u32[]{:S(2)}) collective-permute-start(bf16[96,512]{1,0:T(8,128)(2,1)S(1)} %shard_map.140.refs_0_), channel_id=1, source_target_pairs={{0,24},{1,25},{2,26},{3,27},{4,28},{5,29},{6,30},{7,31},{8,16},{9,... | collective-permute-start | bytes 294920 | tf_op jit(solution)/shard_map/ppermute | solution.py:420
  35.6 10.6 %collective-permute-start.10 = (bf16[2,384,128]{2,1,0:T(8,128)(2,1)S(1)}, bf16[2,384,128]{2,1,0:T(8,128)(2,1)S(1)}, u32[]{:S(2)}, u32[]{:S(2)}) collective-permute-start(bf16[2,384,128]{2,1,0:T(8,128)(2,1)S(1)} %get-tuple-element.118), channel_id=1, source_target_pairs={{0,8},{1,9},{2,10},{3,11},{4,12},{5,13},{6,14},{7,15},{8,0},{9,1},... | collective-permute-start | bytes 589832 | tf_op jit(solution)/shard_map/ppermute | solution.py:420
  35.7 10.5 %collective-permute-start.9 = (bf16[512,128]{1,0:T(8,128)(2,1)S(1)}, bf16[512,128]{1,0:T(8,128)(2,1)S(1)}, u32[]{:S(2)}, u32[]{:S(2)}) collective-permute-start(bf16[512,128]{1,0:T(8,128)(2,1)S(1)} %get-tuple-element.116), channel_id=1, source_target_pairs={{0,2},{1,3},{2,0},{3,1},{4,6},{5,7},{6,4},{7,5},{8,10},{9,11},{10,... | collective-permute-start | bytes 393224 | tf_op jit(solution)/shard_map/ppermute | solution.py:420
  35.8 8.3 %collective-permute-start.7 = (bf16[96,512]{1,0:T(8,128)(2,1)S(1)}, bf16[96,512]{1,0:T(8,128)(2,1)S(1)}, u32[]{:S(2)}, u32[]{:S(2)}) collective-permute-start(bf16[96,512]{1,0:T(8,128)(2,1)S(1)} %shard_map.140.refs_0_), channel_id=1, source_target_pairs={{0,16},{1,17},{2,18},{3,19},{4,20},{5,21},{6,22},{7,23},{8,24},{9,... | collective-permute-start | bytes 294920 | tf_op jit(solution)/shard_map/ppermute | solution.py:420
  39.4 6.8 %collective-permute-start.6 = (bf16[96,512]{1,0:T(8,128)(2,1)S(1)}, bf16[96,512]{1,0:T(8,128)(2,1)S(1)}, u32[]{:S(2)}, u32[]{:S(2)}) collective-permute-start(bf16[96,512]{1,0:T(8,128)(2,1)S(1)} %shard_map.140.refs_0_), channel_id=1, source_target_pairs={{0,8},{1,9},{2,10},{3,11},{4,12},{5,13},{6,14},{7,15},{8,0},{9,1},... | collective-permute-start | bytes 294920 | tf_op jit(solution)/shard_map/ppermute | solution.py:420
  47.5 12.4 %collective-permute-start.16 = (bf16[2,384,128]{2,1,0:T(8,128)(2,1)S(1)}, bf16[2,384,128]{2,1,0:T(8,128)(2,1)S(1)}, u32[]{:S(2)}, u32[]{:S(2)}) collective-permute-start(bf16[2,384,128]{2,1,0:T(8,128)(2,1)S(1)} %get-tuple-element.140), channel_id=1, source_target_pairs={{0,16},{1,17},{2,18},{3,19},{4,20},{5,21},{6,22},{7,23},{8,24},{9,... | collective-permute-start | bytes 589832 | tf_op jit(solution)/shard_map/ppermute | solution.py:420
  49.0 4.2 %collective-permute-start.13 = (bf16[48,512]{1,0:T(8,128)(2,1)S(1)}, bf16[48,512]{1,0:T(8,128)(2,1)S(1)}, u32[]{:S(2)}, u32[]{:S(2)}) collective-permute-start(bf16[48,512]{1,0:T(8,128)(2,1)S(1)} %get-tuple-element.136), channel_id=1, source_target_pairs={{0,1},{1,0},{2,3},{3,2},{4,5},{5,4},{6,7},{7,6},{8,9},{9,8},{10,11... | collective-permute-start | bytes 147464 | tf_op jit(solution)/shard_map/ppermute | solution.py:420
  50.8 4.4 %collective-permute-start.14 = (bf16[48,512]{1,0:T(8,128)(2,1)S(1)}, bf16[48,512]{1,0:T(8,128)(2,1)S(1)}, u32[]{:S(2)}, u32[]{:S(2)}) collective-permute-start(bf16[48,512]{1,0:T(8,128)(2,1)S(1)} %get-tuple-element.137), channel_id=1, source_target_pairs={{0,4},{1,5},{2,6},{3,7},{4,0},{5,1},{6,2},{7,3},{8,12},{9,13},{10,... | collective-permute-start | bytes 147464 | tf_op jit(solution)/shard_map/ppermute | solution.py:420
  51.1 5.0 %collective-permute-start.15 = (bf16[48,512]{1,0:T(8,128)(2,1)S(1)}, bf16[48,512]{1,0:T(8,128)(2,1)S(1)}, u32[]{:S(2)}, u32[]{:S(2)}) collective-permute-start(bf16[48,512]{1,0:T(8,128)(2,1)S(1)} %get-tuple-element.138), channel_id=1, source_target_pairs={{0,5},{1,4},{2,7},{3,6},{4,1},{5,0},{6,3},{7,2},{8,13},{9,12},{10,... | collective-permute-start | bytes 147464 | tf_op jit(solution)/shard_map/ppermute | solution.py:420
  60.0 8.7 %collective-permute-start.20 = (bf16[128,3072]{1,0:T(8,128)(2,1)S(1)}, bf16[128,3072]{1,0:T(8,128)(2,1)S(1)}, u32[]{:S(2)}, u32[]{:S(2)}) collective-permute-start(bf16[128,3072]{1,0:T(8,128)(2,1)S(1)} %collective-permute-done.12.refs_6_), channel_id=1, source_target_pairs={{0,2},{1,3},{2,0},{3,1},{4,6},{5,7},{6,4},{7,5},{8,10},{9,11},{10,... | collective-permute-start | bytes 2359304 | tf_op jit(solution)/shard_map/ppermute | solution.py:420
  60.0 10.2 %collective-permute-start.23 = (bf16[2,384,128]{2,1,0:T(8,128)(2,1)S(1)}, bf16[2,384,128]{2,1,0:T(8,128)(2,1)S(1)}, u32[]{:S(2)}, u32[]{:S(2)}) collective-permute-start(bf16[2,384,128]{2,1,0:T(8,128)(2,1)S(1)} %get-tuple-element.153), channel_id=1, source_target_pairs={{0,24},{1,25},{2,26},{3,27},{4,28},{5,29},{6,30},{7,31},{8,16},{9,... | collective-permute-start | bytes 589832 | tf_op jit(solution)/shard_map/ppermute | solution.py:420
  61.5 5.2 %collective-permute-start.19 = (bf16[48,512]{1,0:T(8,128)(2,1)S(1)}, bf16[48,512]{1,0:T(8,128)(2,1)S(1)}, u32[]{:S(2)}, u32[]{:S(2)}) collective-permute-start(bf16[48,512]{1,0:T(8,128)(2,1)S(1)} %shard_map.144.refs_0_.hidden), channel_id=1, source_target_pairs={{0,5},{1,4},{2,7},{3,6},{4,1},{5,0},{6,3},{7,2},{8,13},{9,12},{10,... | collective-permute-start | bytes 147464 | tf_op jit(solution)/shard_map/ppermute | solution.py:420
  63.0 4.4 %collective-permute-start.18 = (bf16[48,512]{1,0:T(8,128)(2,1)S(1)}, bf16[48,512]{1,0:T(8,128)(2,1)S(1)}, u32[]{:S(2)}, u32[]{:S(2)}) collective-permute-start(bf16[48,512]{1,0:T(8,128)(2,1)S(1)} %shard_map.144.refs_0_.hidden), channel_id=1, source_target_pairs={{0,4},{1,5},{2,6},{3,7},{4,0},{5,1},{6,2},{7,3},{8,12},{9,13},{10,... | collective-permute-start | bytes 147464 | tf_op jit(solution)/shard_map/ppermute | solution.py:420
  70.2 25.5 %collective-permute-start.27 = (bf16[4,2,384,128]{3,2,1,0:T(8,128)(2,1)S(1)}, bf16[4,2,384,128]{3,2,1,0:T(8,128)(2,1)S(1)}, u32[]{:S(2)}, u32[]{:S(2)}) collective-permute-start(bf16[4,2,384,128]{3,2,1,0:T(8,128)(2,1)S(1)} %shard_map.148.near), channel_id=1, source_target_pairs={{0,2},{1,3},{2,0},{3,1},{4,6},{5,7},{6,4},{7,5},{8,10},{9,11},{10,... | collective-permute-start | bytes 2359304 | tf_op jit(solution)/shard_map/ppermute | solution.py:420
  70.3 6.7 %collective-permute-start.21 = (bf16[96,768]{1,0:T(8,128)(2,1)S(1)}, bf16[96,768]{1,0:T(8,128)(2,1)S(1)}, u32[]{:S(2)}, u32[]{:S(2)}) collective-permute-start(bf16[96,768]{1,0:T(8,128)(2,1)S(1)} %get-tuple-element.145), channel_id=1, source_target_pairs={{0,8},{1,9},{2,10},{3,11},{4,12},{5,13},{6,14},{7,15},{8,0},{9,1},... | collective-permute-start | bytes 442376 | tf_op jit(solution)/shard_map/ppermute | solution.py:420
  70.4 10.3 %collective-permute-start.24 = (bf16[112,768]{1,0:T(8,128)(2,1)S(1)}, bf16[112,768]{1,0:T(8,128)(2,1)S(1)}, u32[]{:S(2)}, u32[]{:S(2)}) collective-permute-start(bf16[112,768]{1,0:T(8,128)(2,1)S(1)} %get-tuple-element.154), channel_id=1, source_target_pairs={{0,8},{1,9},{2,10},{3,11},{4,12},{5,13},{6,14},{7,15},{8,0},{9,1},... | collective-permute-start | bytes 516104 | tf_op jit(solution)/shard_map/ppermute | solution.py:420
  77.0 18.7 %collective-permute-start.22 = (bf16[208,768]{1,0:T(8,128)(2,1)S(1)}, bf16[208,768]{1,0:T(8,128)(2,1)S(1)}, u32[]{:S(2)}, u32[]{:S(2)}) collective-permute-start(bf16[208,768]{1,0:T(8,128)(2,1)S(1)} %get-tuple-element.147), channel_id=1, source_target_pairs={{0,8},{1,9},{2,10},{3,11},{4,12},{5,13},{6,14},{7,15},{8,0},{9,1},... | collective-permute-start | bytes 958472 | tf_op jit(solution)/shard_map/ppermute | solution.py:420
  80.7 14.9 %collective-permute-start.25 = (bf16[112,768]{1,0:T(8,128)(2,1)S(1)}, bf16[112,768]{1,0:T(8,128)(2,1)S(1)}, u32[]{:S(2)}, u32[]{:S(2)}) collective-permute-start(bf16[112,768]{1,0:T(8,128)(2,1)S(1)} %shard_map.146), channel_id=1, source_target_pairs={{0,16},{1,17},{2,18},{3,19},{4,20},{5,21},{6,22},{7,23},{8,24},{9,... | collective-permute-start | bytes 516104 | tf_op jit(solution)/shard_map/ppermute | solution.py:420
  81.9 17.3 %collective-permute-start.26 = (bf16[96,768]{1,0:T(8,128)(2,1)S(1)}, bf16[96,768]{1,0:T(8,128)(2,1)S(1)}, u32[]{:S(2)}, u32[]{:S(2)}) collective-permute-start(bf16[96,768]{1,0:T(8,128)(2,1)S(1)} %shard_map.147), channel_id=1, source_target_pairs={{0,16},{1,17},{2,18},{3,19},{4,20},{5,21},{6,22},{7,23},{8,24},{9,... | collective-permute-start | bytes 442376 | tf_op jit(solution)/shard_map/ppermute | solution.py:420
  96.9 5.7 %collective-permute-start.29 = (bf16[4,48,512]{2,1,0:T(8,128)(2,1)S(1)}, bf16[4,48,512]{2,1,0:T(8,128)(2,1)S(1)}, u32[]{:S(2)}, u32[]{:S(2)}) collective-permute-start(bf16[4,48,512]{2,1,0:T(8,128)(2,1)S(1)} %get-tuple-element.163), channel_id=1, source_target_pairs={{0,4},{1,5},{2,6},{3,7},{4,0},{5,1},{6,2},{7,3},{8,12},{9,13},{10,... | collective-permute-start | bytes 589832 | tf_op jit(solution)/shard_map/ppermute | solution.py:420
  97.5 7.6 %collective-permute-start.30 = (bf16[4,48,512]{2,1,0:T(8,128)(2,1)S(1)}, bf16[4,48,512]{2,1,0:T(8,128)(2,1)S(1)}, u32[]{:S(2)}, u32[]{:S(2)}) collective-permute-start(bf16[4,48,512]{2,1,0:T(8,128)(2,1)S(1)} %get-tuple-element.164), channel_id=1, source_target_pairs={{0,5},{1,4},{2,7},{3,6},{4,1},{5,0},{6,3},{7,2},{8,13},{9,12},{10,... | collective-permute-start | bytes 589832 | tf_op jit(solution)/shard_map/ppermute | solution.py:420
  100.4 6.7 %collective-permute-start.28 = (bf16[4,48,512]{2,1,0:T(8,128)(2,1)S(1)}, bf16[4,48,512]{2,1,0:T(8,128)(2,1)S(1)}, u32[]{:S(2)}, u32[]{:S(2)}) collective-permute-start(bf16[4,48,512]{2,1,0:T(8,128)(2,1)S(1)} %get-tuple-element.162), channel_id=1, source_target_pairs={{0,1},{1,0},{2,3},{3,2},{4,5},{5,4},{6,7},{7,6},{8,9},{9,8},{10,11... | collective-permute-start | bytes 589832 | tf_op jit(solution)/shard_map/ppermute | solution.py:420
  108.0 4.5 %collective-permute-start.31 = (bf16[64,512]{1,0:T(8,128)(2,1)S(1)}, bf16[64,512]{1,0:T(8,128)(2,1)S(1)}, u32[]{:S(2)}, u32[]{:S(2)}) collective-permute-start(bf16[64,512]{1,0:T(8,128)(2,1)S(1)} %get-tuple-element.166), channel_id=1, source_target_pairs={{0,8},{1,9},{2,10},{3,11},{4,12},{5,13},{6,14},{7,15},{8,0},{9,1},... | collective-permute-start | bytes 196616 | tf_op jit(solution)/shard_map/ppermute | solution.py:420
  108.0 5.2 %collective-permute-start.32 = (bf16[64,512]{1,0:T(8,128)(2,1)S(1)}, bf16[64,512]{1,0:T(8,128)(2,1)S(1)}, u32[]{:S(2)}, u32[]{:S(2)}) collective-permute-start(bf16[64,512]{1,0:T(8,128)(2,1)S(1)} %get-tuple-element.167), channel_id=1, source_target_pairs={{0,16},{1,17},{2,18},{3,19},{4,20},{5,21},{6,22},{7,23},{8,24},{9,... | collective-permute-start | bytes 196616 | tf_op jit(solution)/shard_map/ppermute | solution.py:420
  110.6 6.1 %collective-permute-start.33 = (bf16[64,512]{1,0:T(8,128)(2,1)S(1)}, bf16[64,512]{1,0:T(8,128)(2,1)S(1)}, u32[]{:S(2)}, u32[]{:S(2)}) collective-permute-start(bf16[64,512]{1,0:T(8,128)(2,1)S(1)} %get-tuple-element.168), channel_id=1, source_target_pairs={{0,24},{1,25},{2,26},{3,27},{4,28},{5,29},{6,30},{7,31},{8,16},{9,... | collective-permute-start | bytes 196616 | tf_op jit(solution)/shard_map/ppermute | solution.py:420
  (14 other events, 64.8 us)

commit v7 on v6

--- a/solution.py
+++ b/solution.py
@@ -505,9 +505,8 @@
     )
     gateds = [gated] + swap_planes(gated)
     wo = [wo_own, wo_core, wo_near, swap(wo_far, core)]
-    down_parts[1] = swap(down_parts[1], group)
     gateds, wo, down_parts = after(gateds, wo, down_parts)
-    for k in (2, 3):
+    for k in (1, 2):
         down_parts[k] = swap(down_parts[k], k * group)
 
     turn = np.zeros((group, planes, tokens, planes, group, tokens), np.float32)
@@ -538,7 +537,8 @@
         like(share, width),
         idx, own, *[swap(x, b) for x, b in zip(rest, steps)], *messages,
     )
-    hidden, gate_up[1], down_parts[2] = after(hidden, gate_up[1], down_parts[2])
+    hidden, gate_up[1], down_parts = after(hidden, gate_up[1], down_parts)
+    down_parts[3] = swap(down_parts[3], 3 * group)
     twin[1] = swap(gate_up[1], core)
     blocks = [hidden] + [swap(hidden, b) for b in steps]
     same = jnp.eye(len(blocks) * share, dtype=BF16)

time: 118 us -> 116 us (0.983)
  waiting for transfers between devices: 59.1 us -> 53.6 us
  starting transfers between devices: 40.1 us -> 44.1 us
    ppermute x34, waiting for transfers between devices: 58 us -> 52.4 us  [swap(): return lax.ppermute(x, axes, [(i, i ^ mask) for i in range(devices)])]
    ppermute x34, starting transfers between devices: 34.8 us -> 38.7 us  [swap(): return lax.ppermute(x, axes, [(i, i ^ mask) for i in range(devices)])]
  transfers between devices with their start and end apart: 35 -> 35, of which waited for: 23 -> 22; matrix products, arithmetic and copies ran while one was open for 0% -> 0% of each run, Pallas kernels for 9% -> 9%
where the time goes in v7:
time: 116 us
  waiting for transfers between devices  53.6 us (46%)
  starting transfers between devices  44.1 us (38%)
  Pallas kernels  14.5 us (12%)
  local copies, waits for them, and re-layouts  3 us (3%)
    ppermute x34, waiting for transfers between devices, swap(): return lax.ppermute(x, axes, [(i, i ^ mask) for i in range(devices)])  52.4 us
    ppermute x34, starting transfers between devices, swap(): return lax.ppermute(x, axes, [(i, i ^ mask) for i in range(devices)])  38.7 us
    pallas_call x17, Pallas kernels, call(): pl.pallas_call(kernel, out_shape=shapes, in_specs=[SMEM if a.dtype == jnp...  14.5 us
    all_to_all x1, starting transfers between devices, plane_exchange(): lax.all_to_all(x, axes, 0, 0, axis_index_groups=plane_groups, tiled=True)  5.31 us
    unnamed x22, local copies, waits for them, and re-layouts  2.92 us
  transfers between devices with their start and end apart: 35, of which 22 were waited for; matrix products, arithmetic and copies ran while one was open for 0% of the time, Pallas kernels for 9%

profile of v7, /device:TPU:0, one launch (start us, length us, event | category | flops | bytes accessed | tf_op | source)
XLA Modules:
  0.0 116.2 jit_solution(5450026164765382141)
XLA Ops:
  0.0 1.8 %shard_map.136 = bf16[8,16,1280]{2,1,0:T(8,128)(2,1)} custom-call(bf16[12,1024]{1,0:T(8,128)(2,1)} %refs_0_.1, bf16[12,1024]{1,0:T(8,128)(2,1)} %refs_1_.1, bf16[12,4096]{1,0:T(8,128)(2,1)} %refs_2_.1, bf16[12,4096]{1,0:T(8,128)(2,1)} %refs_3_.1), custom_call_target="tpu_custom_call" | custom-call | tf_op jit(solution)/shard_map/pallas_call | solution.py:371
  1.9 5.3 %all-to-all-start = ((bf16[8,16,1280]{2,1,0:T(8,128)(2,1)}), bf16[8,16,1280]{2,1,0:T(8,128)(2,1)S(1)}, u32[]{:S(2)}, u32[]{:S(2)}) async-start(bf16[8,16,1280]{2,1,0:T(8,128)(2,1)} %shard_map.136), calls=%async_computation | async-start | bytes 655360 | tf_op jit(solution)/shard_map/all_to_all | solution.py:429
  8.4 1.3 %shard_map.137 = (bf16[2560,128]{1,0:T(8,128)(2,1)S(1)}, bf16[4,384,128]{2,1,0:T(8,128)(2,1)S(1)}, bf16[512,128]{1,0:T(8,128)(2,1)S(1)}, bf16[512,128]{1,0:T(8,128)(2,1)}) custom-call(s32[4]{0:T(128)S(1)} %pad_add_fusion.idx, bf16[3072,128]{1,0:T(8,128)(2,1)S(1)} %copy-done, bf16[2048,128]{1,0:T(8,128)(2,1)S(1)} %copy-done.3), custom_call_target="tpu_custom_call" | custom-call | tf_op jit(solution)/shard_map/pallas_call | solution.py:371
  16.1 1.6 %collective-permute-start.1 = (bf16[128,256]{1,0:T(8,128)(2,1)S(1)}, bf16[128,256]{1,0:T(8,128)(2,1)S(1)}, u32[]{:S(2)}, u32[]{:S(2)}) collective-permute-start(bf16[128,256]{1,0:T(8,128)(2,1)S(1)} %get-tuple-element.102), channel_id=1, source_target_pairs={{0,8},{1,9},{2,10},{3,11},{4,12},{5,13},{6,14},{7,15},{8,0},{9,1},... | collective-permute-start | bytes 196616 | tf_op jit(solution)/shard_map/ppermute | solution.py:420
  17.8 2.6 %collective-permute-start.2 = (bf16[128,256]{1,0:T(8,128)(2,1)S(1)}, bf16[128,256]{1,0:T(8,128)(2,1)S(1)}, u32[]{:S(2)}, u32[]{:S(2)}) collective-permute-start(bf16[128,256]{1,0:T(8,128)(2,1)S(1)} %get-tuple-element.103), channel_id=1, source_target_pairs={{0,16},{1,17},{2,18},{3,19},{4,20},{5,21},{6,22},{7,23},{8,24},{9,... | collective-permute-start | bytes 196616 | tf_op jit(solution)/shard_map/ppermute | solution.py:420
  20.6 4.7 %collective-permute-done.2.refs_2_.refs_6_ = bf16[128,256]{1,0:T(8,128)(2,1)S(1)} collective-permute-done((bf16[128,256]{1,0:T(8,128)(2,1)S(1)}, bf16[128,256]{1,0:T(8,128)(2,1)S(1)}, u32[]{:S(2)}, u32[]{:S(2)}) %collective-permute-start.2) | collective-permute-done | bytes 65568 | tf_op jit(solution)/shard_map/ppermute | solution.py:420
  28.0 1.9 %shard_map.140.refs_0_ = bf16[96,512]{1,0:T(8,128)(2,1)S(1)} custom-call(s32[4]{0:T(128)S(1)} %pad_add_fusion.idx, s32[1]{0:T(128)S(6)} %copy.15.prefix, bf16[8,16,1280]{2,1,0:T(8,128)(2,1)S(1)} %all-to-all-done.heads.qg, bf16[128,256]{1,0:T(8,128)(2,1)S(1)} %get-tuple-element.107.refs_0_.refs_4_, ...), custom_call_target="tpu_custom_call" | custom-call | tf_op jit(solution)/shard_map/pallas_call | solution.py:371
  29.8 2.1 %collective-permute-done.5.message = bf16[2560,128]{1,0:T(8,128)(2,1)S(1)} collective-permute-done((bf16[2560,128]{1,0:T(8,128)(2,1)}, bf16[2560,128]{1,0:T(8,128)(2,1)S(1)}, u32[]{:S(2)}, u32[]{:S(2)}) %collective-permute-start.5) | collective-permute-done | bytes 655392 | tf_op jit(solution)/shard_map/ppermute | solution.py:420
  32.1 3.7 %collective-permute-start.8 = (bf16[96,512]{1,0:T(8,128)(2,1)S(1)}, bf16[96,512]{1,0:T(8,128)(2,1)S(1)}, u32[]{:S(2)}, u32[]{:S(2)}) collective-permute-start(bf16[96,512]{1,0:T(8,128)(2,1)S(1)} %shard_map.140.refs_0_), channel_id=1, source_target_pairs={{0,24},{1,25},{2,26},{3,27},{4,28},{5,29},{6,30},{7,31},{8,16},{9,... | collective-permute-start | bytes 294920 | tf_op jit(solution)/shard_map/ppermute | solution.py:420
  36.6 3.1 %collective-permute-done.8.refs_3_ = bf16[96,512]{1,0:T(8,128)(2,1)S(1)} collective-permute-done((bf16[96,512]{1,0:T(8,128)(2,1)S(1)}, bf16[96,512]{1,0:T(8,128)(2,1)S(1)}, u32[]{:S(2)}, u32[]{:S(2)}) %collective-permute-start.8) | collective-permute-done | bytes 98336 | tf_op jit(solution)/shard_map/ppermute | solution.py:420
  39.7 5.0 %collective-permute-done.7.refs_2_ = bf16[96,512]{1,0:T(8,128)(2,1)S(1)} collective-permute-done((bf16[96,512]{1,0:T(8,128)(2,1)S(1)}, bf16[96,512]{1,0:T(8,128)(2,1)S(1)}, u32[]{:S(2)}, u32[]{:S(2)}) %collective-permute-start.7) | collective-permute-done | bytes 98336 | tf_op jit(solution)/shard_map/ppermute | solution.py:420
  46.5 2.5 %collective-permute-start.16 = (bf16[2,384,128]{2,1,0:T(8,128)(2,1)S(1)}, bf16[2,384,128]{2,1,0:T(8,128)(2,1)S(1)}, u32[]{:S(2)}, u32[]{:S(2)}) collective-permute-start(bf16[2,384,128]{2,1,0:T(8,128)(2,1)S(1)} %get-tuple-element.145), channel_id=1, source_target_pairs={{0,16},{1,17},{2,18},{3,19},{4,20},{5,21},{6,22},{7,23},{8,24},{9,... | collective-permute-start | bytes 589832 | tf_op jit(solution)/shard_map/ppermute | solution.py:420
  51.2 1.4 %collective-permute-start.14 = (bf16[48,512]{1,0:T(8,128)(2,1)S(1)}, bf16[48,512]{1,0:T(8,128)(2,1)S(1)}, u32[]{:S(2)}, u32[]{:S(2)}) collective-permute-start(bf16[48,512]{1,0:T(8,128)(2,1)S(1)} %get-tuple-element.141), channel_id=1, source_target_pairs={{0,5},{1,4},{2,7},{3,6},{4,1},{5,0},{6,3},{7,2},{8,13},{9,12},{10,... | collective-permute-start | bytes 147464 | tf_op jit(solution)/shard_map/ppermute | solution.py:420
  53.3 1.5 %collective-permute-done.13.refs_2_ = bf16[48,512]{1,0:T(8,128)(2,1)S(1)} collective-permute-done((bf16[48,512]{1,0:T(8,128)(2,1)S(1)}, bf16[48,512]{1,0:T(8,128)(2,1)S(1)}, u32[]{:S(2)}, u32[]{:S(2)}) %collective-permute-start.13) | collective-permute-done | bytes 49184 | tf_op jit(solution)/shard_map/ppermute | solution.py:420
  54.8 1.4 %collective-permute-done.14.refs_3_ = bf16[48,512]{1,0:T(8,128)(2,1)S(1)} collective-permute-done((bf16[48,512]{1,0:T(8,128)(2,1)S(1)}, bf16[48,512]{1,0:T(8,128)(2,1)S(1)}, u32[]{:S(2)}, u32[]{:S(2)}) %collective-permute-start.14) | collective-permute-done | bytes 49184 | tf_op jit(solution)/shard_map/ppermute | solution.py:420
  57.1 1.5 %collective-permute-done.16.refs_2_ = bf16[2,384,128]{2,1,0:T(8,128)(2,1)S(1)} collective-permute-done((bf16[2,384,128]{2,1,0:T(8,128)(2,1)S(1)}, bf16[2,384,128]{2,1,0:T(8,128)(2,1)S(1)}, u32[]{:S(2)}, u32[]{:S(2)}) %collective-permute-start.16) | collective-permute-done | bytes 196640 | tf_op jit(solution)/shard_map/ppermute | solution.py:420
  58.7 2.2 %collective-permute-start.23 = (bf16[2,384,128]{2,1,0:T(8,128)(2,1)S(1)}, bf16[2,384,128]{2,1,0:T(8,128)(2,1)S(1)}, u32[]{:S(2)}, u32[]{:S(2)}) collective-permute-start(bf16[2,384,128]{2,1,0:T(8,128)(2,1)S(1)} %get-tuple-element.159), channel_id=1, source_target_pairs={{0,24},{1,25},{2,26},{3,27},{4,28},{5,29},{6,30},{7,31},{8,16},{9,... | collective-permute-start | bytes 589832 | tf_op jit(solution)/shard_map/ppermute | solution.py:420
  60.9 1.5 %collective-permute-start.19 = (bf16[48,512]{1,0:T(8,128)(2,1)S(1)}, bf16[48,512]{1,0:T(8,128)(2,1)S(1)}, u32[]{:S(2)}, u32[]{:S(2)}) collective-permute-start(bf16[48,512]{1,0:T(8,128)(2,1)S(1)} %shard_map.144.refs_0_.hidden), channel_id=1, source_target_pairs={{0,5},{1,4},{2,7},{3,6},{4,1},{5,0},{6,3},{7,2},{8,13},{9,12},{10,... | collective-permute-start | bytes 147464 | tf_op jit(solution)/shard_map/ppermute | solution.py:420
  64.4 1.8 %collective-permute-done.19.refs_3_ = bf16[48,512]{1,0:T(8,128)(2,1)S(1)} collective-permute-done((bf16[48,512]{1,0:T(8,128)(2,1)S(1)}, bf16[48,512]{1,0:T(8,128)(2,1)S(1)}, u32[]{:S(2)}, u32[]{:S(2)}) %collective-permute-start.19) | collective-permute-done | bytes 49184 | tf_op jit(solution)/shard_map/ppermute | solution.py:420
  67.6 1.5 %shard_map.145 = (f32[208,768]{1,0:T(8,128)S(1)}, bf16[208,768]{1,0:T(8,128)(2,1)S(1)}, f32[112,768]{1,0:T(8,128)S(1)}, f32[96,768]{1,0:T(8,128)S(1)}, bf16[112,...) custom-call(s32[4]{0:T(128)S(1)} %pad_add_fusion.idx, bf16[48,512]{1,0:T(8,128)(2,1)S(1)} %shard_map.144.refs_0_.hidden, ...), custom_call_target="tpu_custom_call" | custom-call | tf_op jit(solution)/shard_map/pallas_call | solution.py:371
  69.3 1.3 %collective-permute-start.21 = (bf16[96,768]{1,0:T(8,128)(2,1)S(1)}, bf16[96,768]{1,0:T(8,128)(2,1)S(1)}, u32[]{:S(2)}, u32[]{:S(2)}) collective-permute-start(bf16[96,768]{1,0:T(8,128)(2,1)S(1)} %get-tuple-element.151), channel_id=1, source_target_pairs={{0,8},{1,9},{2,10},{3,11},{4,12},{5,13},{6,14},{7,15},{8,0},{9,1},... | collective-permute-start | bytes 442376 | tf_op jit(solution)/shard_map/ppermute | solution.py:420
  71.4 4.6 %collective-permute-done.21.got = bf16[96,768]{1,0:T(8,128)(2,1)S(1)} collective-permute-done((bf16[96,768]{1,0:T(8,128)(2,1)S(1)}, bf16[96,768]{1,0:T(8,128)(2,1)S(1)}, u32[]{:S(2)}, u32[]{:S(2)}) %collective-permute-start.21) | collective-permute-done | bytes 147488 | tf_op jit(solution)/shard_map/ppermute | solution.py:420
  77.3 2.4 %collective-permute-done.24.got = bf16[112,768]{1,0:T(8,128)(2,1)S(1)} collective-permute-done((bf16[112,768]{1,0:T(8,128)(2,1)S(1)}, bf16[112,768]{1,0:T(8,128)(2,1)S(1)}, u32[]{:S(2)}, u32[]{:S(2)}) %collective-permute-start.24) | collective-permute-done | bytes 172064 | tf_op jit(solution)/shard_map/ppermute | solution.py:420
  79.7 1.5 %collective-permute-start.25 = (bf16[112,768]{1,0:T(8,128)(2,1)S(1)}, bf16[112,768]{1,0:T(8,128)(2,1)S(1)}, u32[]{:S(2)}, u32[]{:S(2)}) collective-permute-start(bf16[112,768]{1,0:T(8,128)(2,1)S(1)} %shard_map.146), channel_id=1, source_target_pairs={{0,16},{1,17},{2,18},{3,19},{4,20},{5,21},{6,22},{7,23},{8,24},{9,... | collective-permute-start | bytes 516104 | tf_op jit(solution)/shard_map/ppermute | solution.py:420
  81.2 1.6 %collective-permute-start.26 = (bf16[96,768]{1,0:T(8,128)(2,1)S(1)}, bf16[96,768]{1,0:T(8,128)(2,1)S(1)}, u32[]{:S(2)}, u32[]{:S(2)}) collective-permute-start(bf16[96,768]{1,0:T(8,128)(2,1)S(1)} %shard_map.147), channel_id=1, source_target_pairs={{0,16},{1,17},{2,18},{3,19},{4,20},{5,21},{6,22},{7,23},{8,24},{9,... | collective-permute-start | bytes 442376 | tf_op jit(solution)/shard_map/ppermute | solution.py:420
  82.8 11.8 %collective-permute-done.25.far_head.far_part = bf16[112,768]{1,0:T(8,128)(2,1)S(1)} collective-permute-done((bf16[112,768]{1,0:T(8,128)(2,1)S(1)}, bf16[112,768]{1,0:T(8,128)(2,1)S(1)}, u32[]{:S(2)}, u32[]{:S(2)}) %collective-permute-start.25) | collective-permute-done | bytes 172064 | tf_op jit(solution)/shard_map/ppermute | solution.py:420
  96.8 1.5 %collective-permute-start.30 = (bf16[4,48,512]{2,1,0:T(8,128)(2,1)S(1)}, bf16[4,48,512]{2,1,0:T(8,128)(2,1)S(1)}, u32[]{:S(2)}, u32[]{:S(2)}) collective-permute-start(bf16[4,48,512]{2,1,0:T(8,128)(2,1)S(1)} %get-tuple-element.170), channel_id=1, source_target_pairs={{0,5},{1,4},{2,7},{3,6},{4,1},{5,0},{6,3},{7,2},{8,13},{9,12},{10,... | collective-permute-start | bytes 589832 | tf_op jit(solution)/shard_map/ppermute | solution.py:420
  101.6 2.5 %collective-permute-done.30.refs_3_ = bf16[4,48,512]{2,1,0:T(8,128)(2,1)S(1)} collective-permute-done((bf16[4,48,512]{2,1,0:T(8,128)(2,1)S(1)}, bf16[4,48,512]{2,1,0:T(8,128)(2,1)S(1)}, u32[]{:S(2)}, u32[]{:S(2)}) %collective-permute-start.30) | collective-permute-done | bytes 196640 | tf_op jit(solution)/shard_map/ppermute | solution.py:420
  104.1 2.0 %collective-permute-done.28.refs_1_ = bf16[4,48,512]{2,1,0:T(8,128)(2,1)S(1)} collective-permute-done((bf16[4,48,512]{2,1,0:T(8,128)(2,1)S(1)}, bf16[4,48,512]{2,1,0:T(8,128)(2,1)S(1)}, u32[]{:S(2)}, u32[]{:S(2)}) %collective-permute-start.28) | collective-permute-done | bytes 196640 | tf_op jit(solution)/shard_map/ppermute | solution.py:420
  107.1 1.8 %collective-permute-start.32 = (bf16[64,512]{1,0:T(8,128)(2,1)S(1)}, bf16[64,512]{1,0:T(8,128)(2,1)S(1)}, u32[]{:S(2)}, u32[]{:S(2)}) collective-permute-start(bf16[64,512]{1,0:T(8,128)(2,1)S(1)} %get-tuple-element.173), channel_id=1, source_target_pairs={{0,16},{1,17},{2,18},{3,19},{4,20},{5,21},{6,22},{7,23},{8,24},{9,... | collective-permute-start | bytes 196616 | tf_op jit(solution)/shard_map/ppermute | solution.py:420
  108.9 2.6 %collective-permute-start.33 = (bf16[64,512]{1,0:T(8,128)(2,1)S(1)}, bf16[64,512]{1,0:T(8,128)(2,1)S(1)}, u32[]{:S(2)}, u32[]{:S(2)}) collective-permute-start(bf16[64,512]{1,0:T(8,128)(2,1)S(1)} %get-tuple-element.174), channel_id=1, source_target_pairs={{0,24},{1,25},{2,26},{3,27},{4,28},{5,29},{6,30},{7,31},{8,16},{9,... | collective-permute-start | bytes 196616 | tf_op jit(solution)/shard_map/ppermute | solution.py:420
  112.4 2.6 %collective-permute-done.33.refs_3_ = bf16[64,512]{1,0:T(8,128)(2,1)S(1)} collective-permute-done((bf16[64,512]{1,0:T(8,128)(2,1)S(1)}, bf16[64,512]{1,0:T(8,128)(2,1)S(1)}, u32[]{:S(2)}, u32[]{:S(2)}) %collective-permute-start.33) | collective-permute-done | bytes 65568 | tf_op jit(solution)/shard_map/ppermute | solution.py:420
  (81 shorter events, 30.4 us)
Async XLA Ops:
  1.9 12.1 %all-to-all-start = ((bf16[8,16,1280]{2,1,0:T(8,128)(2,1)}), bf16[8,16,1280]{2,1,0:T(8,128)(2,1)S(1)}, u32[]{:S(2)}, u32[]{:S(2)}) async-start(bf16[8,16,1280]{2,1,0:T(8,128)(2,1)} %shard_map.136), calls=%async_computation | async-start | bytes 655360 | tf_op jit(solution)/shard_map/all_to_all | solution.py:429
  13.9 12.6 %collective-permute-start.4 = (bf16[128,3072]{1,0:T(8,128)(2,1)S(1)}, bf16[128,3072]{1,0:T(8,128)(2,1)S(1)}, u32[]{:S(2)}, u32[]{:S(2)}) collective-permute-start(bf16[128,3072]{1,0:T(8,128)(2,1)S(1)} %get-tuple-element.106.refs_4_), channel_id=1, source_target_pairs={{0,2},{1,3},{2,0},{3,1},{4,6},{5,7},{6,4},{7,5},{8,10},{9,11},{10,... | collective-permute-start | bytes 2359304 | tf_op jit(solution)/shard_map/ppermute | solution.py:420
  14.2 17.8 %collective-permute-start.5 = (bf16[2560,128]{1,0:T(8,128)(2,1)}, bf16[2560,128]{1,0:T(8,128)(2,1)S(1)}, u32[]{:S(2)}, u32[]{:S(2)}) collective-permute-start(bf16[2560,128]{1,0:T(8,128)(2,1)} %copy-done.9), channel_id=1, source_target_pairs={{0,4},{1,5},{2,6},{3,7},{4,0},{5,1},{6,2},{7,3},{8,12},{9,13},{10,... | collective-permute-start | bytes 1966088 | tf_op jit(solution)/shard_map/ppermute | solution.py:420
  16.1 4.5 %collective-permute-start.1 = (bf16[128,256]{1,0:T(8,128)(2,1)S(1)}, bf16[128,256]{1,0:T(8,128)(2,1)S(1)}, u32[]{:S(2)}, u32[]{:S(2)}) collective-permute-start(bf16[128,256]{1,0:T(8,128)(2,1)S(1)} %get-tuple-element.102), channel_id=1, source_target_pairs={{0,8},{1,9},{2,10},{3,11},{4,12},{5,13},{6,14},{7,15},{8,0},{9,1},... | collective-permute-start | bytes 196616 | tf_op jit(solution)/shard_map/ppermute | solution.py:420
  17.8 7.5 %collective-permute-start.2 = (bf16[128,256]{1,0:T(8,128)(2,1)S(1)}, bf16[128,256]{1,0:T(8,128)(2,1)S(1)}, u32[]{:S(2)}, u32[]{:S(2)}) collective-permute-start(bf16[128,256]{1,0:T(8,128)(2,1)S(1)} %get-tuple-element.103), channel_id=1, source_target_pairs={{0,16},{1,17},{2,18},{3,19},{4,20},{5,21},{6,22},{7,23},{8,24},{9,... | collective-permute-start | bytes 196616 | tf_op jit(solution)/shard_map/ppermute | solution.py:420
  20.3 6.2 %collective-permute-start.3 = (bf16[128,256]{1,0:T(8,128)(2,1)S(1)}, bf16[128,256]{1,0:T(8,128)(2,1)S(1)}, u32[]{:S(2)}, u32[]{:S(2)}) collective-permute-start(bf16[128,256]{1,0:T(8,128)(2,1)S(1)} %get-tuple-element.104), channel_id=1, source_target_pairs={{0,24},{1,25},{2,26},{3,27},{4,28},{5,29},{6,30},{7,31},{8,16},{9,... | collective-permute-start | bytes 196616 | tf_op jit(solution)/shard_map/ppermute | solution.py:420
  26.5 22.6 %collective-permute-start.11 = (bf16[128,3072]{1,0:T(8,128)(2,1)}, bf16[128,3072]{1,0:T(8,128)(2,1)S(1)}, u32[]{:S(2)}, u32[]{:S(2)}) collective-permute-start(bf16[128,3072]{1,0:T(8,128)(2,1)} %copy-done.8), channel_id=1, source_target_pairs={{0,4},{1,5},{2,6},{3,7},{4,0},{5,1},{6,2},{7,3},{8,12},{9,13},{10,... | collective-permute-start | bytes 2359304 | tf_op jit(solution)/shard_map/ppermute | solution.py:420
  32.0 12.6 %collective-permute-start.9 = (bf16[512,128]{1,0:T(8,128)(2,1)S(1)}, bf16[512,128]{1,0:T(8,128)(2,1)S(1)}, u32[]{:S(2)}, u32[]{:S(2)}) collective-permute-start(bf16[512,128]{1,0:T(8,128)(2,1)S(1)} %get-tuple-element.119), channel_id=1, source_target_pairs={{0,2},{1,3},{2,0},{3,1},{4,6},{5,7},{6,4},{7,5},{8,10},{9,11},{10,... | collective-permute-start | bytes 393224 | tf_op jit(solution)/shard_map/ppermute | solution.py:420
  32.1 7.6 %collective-permute-start.8 = (bf16[96,512]{1,0:T(8,128)(2,1)S(1)}, bf16[96,512]{1,0:T(8,128)(2,1)S(1)}, u32[]{:S(2)}, u32[]{:S(2)}) collective-permute-start(bf16[96,512]{1,0:T(8,128)(2,1)S(1)} %shard_map.140.refs_0_), channel_id=1, source_target_pairs={{0,24},{1,25},{2,26},{3,27},{4,28},{5,29},{6,30},{7,31},{8,16},{9,... | collective-permute-start | bytes 294920 | tf_op jit(solution)/shard_map/ppermute | solution.py:420
  35.8 8.9 %collective-permute-start.7 = (bf16[96,512]{1,0:T(8,128)(2,1)S(1)}, bf16[96,512]{1,0:T(8,128)(2,1)S(1)}, u32[]{:S(2)}, u32[]{:S(2)}) collective-permute-start(bf16[96,512]{1,0:T(8,128)(2,1)S(1)} %shard_map.140.refs_0_), channel_id=1, source_target_pairs={{0,16},{1,17},{2,18},{3,19},{4,20},{5,21},{6,22},{7,23},{8,24},{9,... | collective-permute-start | bytes 294920 | tf_op jit(solution)/shard_map/ppermute | solution.py:420
  35.8 8.9 %collective-permute-start.6 = (bf16[96,512]{1,0:T(8,128)(2,1)S(1)}, bf16[96,512]{1,0:T(8,128)(2,1)S(1)}, u32[]{:S(2)}, u32[]{:S(2)}) collective-permute-start(bf16[96,512]{1,0:T(8,128)(2,1)S(1)} %shard_map.140.refs_0_), channel_id=1, source_target_pairs={{0,8},{1,9},{2,10},{3,11},{4,12},{5,13},{6,14},{7,15},{8,0},{9,1},... | collective-permute-start | bytes 294920 | tf_op jit(solution)/shard_map/ppermute | solution.py:420
  46.0 11.2 %collective-permute-start.15 = (bf16[2,384,128]{2,1,0:T(8,128)(2,1)S(1)}, bf16[2,384,128]{2,1,0:T(8,128)(2,1)S(1)}, u32[]{:S(2)}, u32[]{:S(2)}) collective-permute-start(bf16[2,384,128]{2,1,0:T(8,128)(2,1)S(1)} %get-tuple-element.144), channel_id=1, source_target_pairs={{0,8},{1,9},{2,10},{3,11},{4,12},{5,13},{6,14},{7,15},{8,0},{9,1},... | collective-permute-start | bytes 589832 | tf_op jit(solution)/shard_map/ppermute | solution.py:420
  46.5 12.1 %collective-permute-start.16 = (bf16[2,384,128]{2,1,0:T(8,128)(2,1)S(1)}, bf16[2,384,128]{2,1,0:T(8,128)(2,1)S(1)}, u32[]{:S(2)}, u32[]{:S(2)}) collective-permute-start(bf16[2,384,128]{2,1,0:T(8,128)(2,1)S(1)} %get-tuple-element.145), channel_id=1, source_target_pairs={{0,16},{1,17},{2,18},{3,19},{4,20},{5,21},{6,22},{7,23},{8,24},{9,... | collective-permute-start | bytes 589832 | tf_op jit(solution)/shard_map/ppermute | solution.py:420
  49.1 4.2 %collective-permute-start.12 = (bf16[48,512]{1,0:T(8,128)(2,1)S(1)}, bf16[48,512]{1,0:T(8,128)(2,1)S(1)}, u32[]{:S(2)}, u32[]{:S(2)}) collective-permute-start(bf16[48,512]{1,0:T(8,128)(2,1)S(1)} %get-tuple-element.139), channel_id=1, source_target_pairs={{0,1},{1,0},{2,3},{3,2},{4,5},{5,4},{6,7},{7,6},{8,9},{9,8},{10,11... | collective-permute-start | bytes 147464 | tf_op jit(solution)/shard_map/ppermute | solution.py:420
  50.3 4.5 %collective-permute-start.13 = (bf16[48,512]{1,0:T(8,128)(2,1)S(1)}, bf16[48,512]{1,0:T(8,128)(2,1)S(1)}, u32[]{:S(2)}, u32[]{:S(2)}) collective-permute-start(bf16[48,512]{1,0:T(8,128)(2,1)S(1)} %get-tuple-element.140), channel_id=1, source_target_pairs={{0,4},{1,5},{2,6},{3,7},{4,0},{5,1},{6,2},{7,3},{8,12},{9,13},{10,... | collective-permute-start | bytes 147464 | tf_op jit(solution)/shard_map/ppermute | solution.py:420
  51.2 5.0 %collective-permute-start.14 = (bf16[48,512]{1,0:T(8,128)(2,1)S(1)}, bf16[48,512]{1,0:T(8,128)(2,1)S(1)}, u32[]{:S(2)}, u32[]{:S(2)}) collective-permute-start(bf16[48,512]{1,0:T(8,128)(2,1)S(1)} %get-tuple-element.141), channel_id=1, source_target_pairs={{0,5},{1,4},{2,7},{3,6},{4,1},{5,0},{6,3},{7,2},{8,13},{9,12},{10,... | collective-permute-start | bytes 147464 | tf_op jit(solution)/shard_map/ppermute | solution.py:420
  58.7 8.9 %collective-permute-start.20 = (bf16[128,3072]{1,0:T(8,128)(2,1)S(1)}, bf16[128,3072]{1,0:T(8,128)(2,1)S(1)}, u32[]{:S(2)}, u32[]{:S(2)}) collective-permute-start(bf16[128,3072]{1,0:T(8,128)(2,1)S(1)} %collective-permute-done.11.refs_6_), channel_id=1, source_target_pairs={{0,2},{1,3},{2,0},{3,1},{4,6},{5,7},{6,4},{7,5},{8,10},{9,11},{10,... | collective-permute-start | bytes 2359304 | tf_op jit(solution)/shard_map/ppermute | solution.py:420
  58.7 10.4 %collective-permute-start.23 = (bf16[2,384,128]{2,1,0:T(8,128)(2,1)S(1)}, bf16[2,384,128]{2,1,0:T(8,128)(2,1)S(1)}, u32[]{:S(2)}, u32[]{:S(2)}) collective-permute-start(bf16[2,384,128]{2,1,0:T(8,128)(2,1)S(1)} %get-tuple-element.159), channel_id=1, source_target_pairs={{0,24},{1,25},{2,26},{3,27},{4,28},{5,29},{6,30},{7,31},{8,16},{9,... | collective-permute-start | bytes 589832 | tf_op jit(solution)/shard_map/ppermute | solution.py:420
  60.9 5.3 %collective-permute-start.19 = (bf16[48,512]{1,0:T(8,128)(2,1)S(1)}, bf16[48,512]{1,0:T(8,128)(2,1)S(1)}, u32[]{:S(2)}, u32[]{:S(2)}) collective-permute-start(bf16[48,512]{1,0:T(8,128)(2,1)S(1)} %shard_map.144.refs_0_.hidden), channel_id=1, source_target_pairs={{0,5},{1,4},{2,7},{3,6},{4,1},{5,0},{6,3},{7,2},{8,13},{9,12},{10,... | collective-permute-start | bytes 147464 | tf_op jit(solution)/shard_map/ppermute | solution.py:420
  62.4 4.1 %collective-permute-start.18 = (bf16[48,512]{1,0:T(8,128)(2,1)S(1)}, bf16[48,512]{1,0:T(8,128)(2,1)S(1)}, u32[]{:S(2)}, u32[]{:S(2)}) collective-permute-start(bf16[48,512]{1,0:T(8,128)(2,1)S(1)} %shard_map.144.refs_0_.hidden), channel_id=1, source_target_pairs={{0,4},{1,5},{2,6},{3,7},{4,0},{5,1},{6,2},{7,3},{8,12},{9,13},{10,... | collective-permute-start | bytes 147464 | tf_op jit(solution)/shard_map/ppermute | solution.py:420
  69.2 25.5 %collective-permute-start.27 = (bf16[4,2,384,128]{3,2,1,0:T(8,128)(2,1)S(1)}, bf16[4,2,384,128]{3,2,1,0:T(8,128)(2,1)S(1)}, u32[]{:S(2)}, u32[]{:S(2)}) collective-permute-start(bf16[4,2,384,128]{3,2,1,0:T(8,128)(2,1)S(1)} %shard_map.148.near), channel_id=1, source_target_pairs={{0,2},{1,3},{2,0},{3,1},{4,6},{5,7},{6,4},{7,5},{8,10},{9,11},{10,... | collective-permute-start | bytes 2359304 | tf_op jit(solution)/shard_map/ppermute | solution.py:420
  69.3 6.7 %collective-permute-start.21 = (bf16[96,768]{1,0:T(8,128)(2,1)S(1)}, bf16[96,768]{1,0:T(8,128)(2,1)S(1)}, u32[]{:S(2)}, u32[]{:S(2)}) collective-permute-start(bf16[96,768]{1,0:T(8,128)(2,1)S(1)} %get-tuple-element.151), channel_id=1, source_target_pairs={{0,8},{1,9},{2,10},{3,11},{4,12},{5,13},{6,14},{7,15},{8,0},{9,1},... | collective-permute-start | bytes 442376 | tf_op jit(solution)/shard_map/ppermute | solution.py:420
  70.6 9.1 %collective-permute-start.24 = (bf16[112,768]{1,0:T(8,128)(2,1)S(1)}, bf16[112,768]{1,0:T(8,128)(2,1)S(1)}, u32[]{:S(2)}, u32[]{:S(2)}) collective-permute-start(bf16[112,768]{1,0:T(8,128)(2,1)S(1)} %get-tuple-element.160), channel_id=1, source_target_pairs={{0,8},{1,9},{2,10},{3,11},{4,12},{5,13},{6,14},{7,15},{8,0},{9,1},... | collective-permute-start | bytes 516104 | tf_op jit(solution)/shard_map/ppermute | solution.py:420
  76.0 18.7 %collective-permute-start.22 = (bf16[208,768]{1,0:T(8,128)(2,1)S(1)}, bf16[208,768]{1,0:T(8,128)(2,1)S(1)}, u32[]{:S(2)}, u32[]{:S(2)}) collective-permute-start(bf16[208,768]{1,0:T(8,128)(2,1)S(1)} %get-tuple-element.153), channel_id=1, source_target_pairs={{0,8},{1,9},{2,10},{3,11},{4,12},{5,13},{6,14},{7,15},{8,0},{9,1},... | collective-permute-start | bytes 958472 | tf_op jit(solution)/shard_map/ppermute | solution.py:420
  79.7 14.9 %collective-permute-start.25 = (bf16[112,768]{1,0:T(8,128)(2,1)S(1)}, bf16[112,768]{1,0:T(8,128)(2,1)S(1)}, u32[]{:S(2)}, u32[]{:S(2)}) collective-permute-start(bf16[112,768]{1,0:T(8,128)(2,1)S(1)} %shard_map.146), channel_id=1, source_target_pairs={{0,16},{1,17},{2,18},{3,19},{4,20},{5,21},{6,22},{7,23},{8,24},{9,... | collective-permute-start | bytes 516104 | tf_op jit(solution)/shard_map/ppermute | solution.py:420
  81.2 17.1 %collective-permute-start.26 = (bf16[96,768]{1,0:T(8,128)(2,1)S(1)}, bf16[96,768]{1,0:T(8,128)(2,1)S(1)}, u32[]{:S(2)}, u32[]{:S(2)}) collective-permute-start(bf16[96,768]{1,0:T(8,128)(2,1)S(1)} %shard_map.147), channel_id=1, source_target_pairs={{0,16},{1,17},{2,18},{3,19},{4,20},{5,21},{6,22},{7,23},{8,24},{9,... | collective-permute-start | bytes 442376 | tf_op jit(solution)/shard_map/ppermute | solution.py:420
  95.9 5.7 %collective-permute-start.29 = (bf16[4,48,512]{2,1,0:T(8,128)(2,1)S(1)}, bf16[4,48,512]{2,1,0:T(8,128)(2,1)S(1)}, u32[]{:S(2)}, u32[]{:S(2)}) collective-permute-start(bf16[4,48,512]{2,1,0:T(8,128)(2,1)S(1)} %get-tuple-element.169), channel_id=1, source_target_pairs={{0,4},{1,5},{2,6},{3,7},{4,0},{5,1},{6,2},{7,3},{8,12},{9,13},{10,... | collective-permute-start | bytes 589832 | tf_op jit(solution)/shard_map/ppermute | solution.py:420
  96.8 7.3 %collective-permute-start.30 = (bf16[4,48,512]{2,1,0:T(8,128)(2,1)S(1)}, bf16[4,48,512]{2,1,0:T(8,128)(2,1)S(1)}, u32[]{:S(2)}, u32[]{:S(2)}) collective-permute-start(bf16[4,48,512]{2,1,0:T(8,128)(2,1)S(1)} %get-tuple-element.170), channel_id=1, source_target_pairs={{0,5},{1,4},{2,7},{3,6},{4,1},{5,0},{6,3},{7,2},{8,13},{9,12},{10,... | collective-permute-start | bytes 589832 | tf_op jit(solution)/shard_map/ppermute | solution.py:420
  99.5 6.6 %collective-permute-start.28 = (bf16[4,48,512]{2,1,0:T(8,128)(2,1)S(1)}, bf16[4,48,512]{2,1,0:T(8,128)(2,1)S(1)}, u32[]{:S(2)}, u32[]{:S(2)}) collective-permute-start(bf16[4,48,512]{2,1,0:T(8,128)(2,1)S(1)} %get-tuple-element.168), channel_id=1, source_target_pairs={{0,1},{1,0},{2,3},{3,2},{4,5},{5,4},{6,7},{7,6},{8,9},{9,8},{10,11... | collective-permute-start | bytes 589832 | tf_op jit(solution)/shard_map/ppermute | solution.py:420
  107.1 4.5 %collective-permute-start.31 = (bf16[64,512]{1,0:T(8,128)(2,1)S(1)}, bf16[64,512]{1,0:T(8,128)(2,1)S(1)}, u32[]{:S(2)}, u32[]{:S(2)}) collective-permute-start(bf16[64,512]{1,0:T(8,128)(2,1)S(1)} %get-tuple-element.172), channel_id=1, source_target_pairs={{0,8},{1,9},{2,10},{3,11},{4,12},{5,13},{6,14},{7,15},{8,0},{9,1},... | collective-permute-start | bytes 196616 | tf_op jit(solution)/shard_map/ppermute | solution.py:420
  107.1 5.2 %collective-permute-start.32 = (bf16[64,512]{1,0:T(8,128)(2,1)S(1)}, bf16[64,512]{1,0:T(8,128)(2,1)S(1)}, u32[]{:S(2)}, u32[]{:S(2)}) collective-permute-start(bf16[64,512]{1,0:T(8,128)(2,1)S(1)} %get-tuple-element.173), channel_id=1, source_target_pairs={{0,16},{1,17},{2,18},{3,19},{4,20},{5,21},{6,22},{7,23},{8,24},{9,... | collective-permute-start | bytes 196616 | tf_op jit(solution)/shard_map/ppermute | solution.py:420
  108.9 6.1 %collective-permute-start.33 = (bf16[64,512]{1,0:T(8,128)(2,1)S(1)}, bf16[64,512]{1,0:T(8,128)(2,1)S(1)}, u32[]{:S(2)}, u32[]{:S(2)}) collective-permute-start(bf16[64,512]{1,0:T(8,128)(2,1)S(1)} %get-tuple-element.174), channel_id=1, source_target_pairs={{0,24},{1,25},{2,26},{3,27},{4,28},{5,29},{6,30},{7,31},{8,16},{9,... | collective-permute-start | bytes 196616 | tf_op jit(solution)/shard_map/ppermute | solution.py:420
  (14 other events, 67.4 us)

commit v8 on v7

--- a/solution.py
+++ b/solution.py
@@ -103,22 +103,14 @@
 
 
 def pack_heads_kernel(head_of, *refs):
-    many = (len(refs) - 2) // 2
-    parts, out, held, sems = refs[:many], refs[many], refs[many + 1:-1], refs[-1]
-    copies = [
-        pltpu.make_async_copy(part, spot, sems.at[i])
-        for i, (part, spot) in enumerate(zip(parts, held))
-    ]
-    for copy in copies:
-        copy.start()
+    *parts, out = refs
     out[...] = jnp.zeros_like(out)
     tokens = parts[0].shape[0]
     start = 0
-    for copy, spot in zip(copies, held):
-        copy.wait()
-        width = spot.shape[1] // len(head_of)
+    for part in parts:
+        width = part.shape[1] // len(head_of)
         for r, j in enumerate(head_of):
-            out[r, :tokens, start:start + width] = spot[:, j * width:(j + 1) * width]
+            out[r, :tokens, start:start + width] = part[:, j * width:(j + 1) * width]
         start += width
 
 
@@ -158,17 +150,21 @@
     visible = (key_spot <= query_spot) | (key_spot < prefix[0].astype(F32))
     bias = jnp.where(visible, 0.0, HIDE)
     scale = 1.0 / math.sqrt(HEAD_SIZE)
-    done = []
-    for h in range(heads):
-        at = slice((h + 2) * HEAD_SIZE, (h + 3) * HEAD_SIZE)
-        gate_at = slice((heads + h + 2) * HEAD_SIZE, (heads + h + 3) * HEAD_SIZE)
-        q = jnp.concatenate([qg[b ^ r, :, at] for b in range(group)])
-        gate = jnp.concatenate([qg[b ^ r, :, gate_at] for b in range(group)]).astype(F32)
-        s = lax.dot_general(q, keys, NT, preferred_element_type=F32) * scale + bias
-        e = jnp.exp(s - jnp.max(s, axis=-1, keepdims=True))
-        denom = jnp.sum(e, axis=-1, keepdims=True)
-        attended = dot(e.astype(BF16), values) / denom
-        done.append((attended / (1.0 + jnp.exp(-gate))).astype(BF16))
+    wide = jnp.concatenate([qg[b ^ r, :, 2 * HEAD_SIZE:] for b in range(group)])
+
+    def by_head(start):
+        return jnp.concatenate(
+            [wide[:, (start + h) * HEAD_SIZE:(start + h + 1) * HEAD_SIZE] for h in range(heads)]
+        )
+
+    gate = by_head(heads).astype(F32)
+    s = lax.dot_general(by_head(0), keys, NT, preferred_element_type=F32) * scale
+    s = s + jnp.concatenate([bias] * heads)
+    e = jnp.exp(s - jnp.max(s, axis=-1, keepdims=True))
+    denom = jnp.sum(e, axis=-1, keepdims=True)
+    attended = dot(e.astype(BF16), values) / denom
+    gated = (attended / (1.0 + jnp.exp(-gate))).astype(BF16)
+    done = [gated[h * lot:(h + 1) * lot] for h in range(heads)]
     out[...] = dot(pick[...], jnp.concatenate(done, axis=1)).astype(BF16)
 
 
@@ -365,13 +361,13 @@
         out[:, p * width:(p + 1) * width] = value.astype(BF16)
 
 
-def call(kernel, outs, *args, scratch=(), place=VMEM, limit=16):
+def call(kernel, outs, *args, scratch=(), limit=16):
     single = not isinstance(outs, list)
     shapes = [outs] if single else outs
     got = pl.pallas_call(
         kernel,
         out_shape=shapes,
-        in_specs=[SMEM if a.dtype == jnp.int32 else place for a in args],
+        in_specs=[SMEM if a.dtype == jnp.int32 else VMEM for a in args],
         out_specs=[VMEM] * len(shapes),
         scratch_shapes=list(scratch),
         compiler_params=pltpu.CompilerParams(vmem_limit_bytes=limit * 2**20),
@@ -444,9 +440,6 @@
         functools.partial(pack_heads_kernel, head_of),
         like(group, rows, 2 * heads * HEAD_SIZE + pair),
         *tokens_in,
-        scratch=[pltpu.VMEM(x.shape, x.dtype) for x in tokens_in]
-        + [pltpu.SemaphoreType.DMA((len(tokens_in),))],
-        place=pl.BlockSpec(memory_space=pl.ANY),
         limit=60,
     )
     head_groups, gate_weight, up_weight, down_weight, out_weight, positions = after(
@@ -603,7 +596,7 @@
         power(n_blk)
         and power(n_uly)
         and power(kv_heads)
-        and per > 1
+        and per == 4
         and n_blk == 4 * per
         and token_count < unit_count // n_uly
     )

time: 116 us -> 116 us (level)
  no operation moved by 1% of the time
where the time goes in v8:
time: 116 us
  waiting for transfers between devices  54.2 us (47%)
  starting transfers between devices  44 us (38%)
  Pallas kernels  13.9 us (12%)
  local copies, waits for them, and re-layouts  3 us (3%)
    ppermute x34, waiting for transfers between devices, swap(): return lax.ppermute(x, axes, [(i, i ^ mask) for i in range(devices)])  53.1 us
    ppermute x34, starting transfers between devices, swap(): return lax.ppermute(x, axes, [(i, i ^ mask) for i in range(devices)])  38.7 us
    pallas_call x17, Pallas kernels, call(): pl.pallas_call(kernel, out_shape=shapes, in_specs=[SMEM if a.dtype == jnp...  13.9 us
    all_to_all x1, starting transfers between devices, plane_exchange(): lax.all_to_all(x, axes, 0, 0, axis_index_groups=plane_groups, tiled=True)  5.3 us
    unnamed x22, local copies, waits for them, and re-layouts  2.91 us
  transfers between devices with their start and end apart: 35, of which 22 were waited for; matrix products, arithmetic and copies ran while one was open for 0% of the time, Pallas kernels for 9%

profile of v8, /device:TPU:0, one launch (start us, length us, event | category | flops | bytes accessed | tf_op | source)
XLA Modules:
  0.0 116.2 jit_solution(16556210094208855966)
XLA Ops:
  0.0 1.8 %shard_map.136 = bf16[8,16,1280]{2,1,0:T(8,128)(2,1)} custom-call(bf16[12,1024]{1,0:T(8,128)(2,1)} %refs_0_.1, bf16[12,1024]{1,0:T(8,128)(2,1)} %refs_1_.1, bf16[12,4096]{1,0:T(8,128)(2,1)} %refs_2_.1, bf16[12,4096]{1,0:T(8,128)(2,1)} %refs_3_.1), custom_call_target="tpu_custom_call" | custom-call | tf_op jit(solution)/shard_map/pallas_call | solution.py:367
  1.8 5.3 %all-to-all-start = ((bf16[8,16,1280]{2,1,0:T(8,128)(2,1)}), bf16[8,16,1280]{2,1,0:T(8,128)(2,1)S(1)}, u32[]{:S(2)}, u32[]{:S(2)}) async-start(bf16[8,16,1280]{2,1,0:T(8,128)(2,1)} %shard_map.136), calls=%async_computation | async-start | bytes 655360 | tf_op jit(solution)/shard_map/all_to_all | solution.py:425
  8.4 1.3 %shard_map.137 = (bf16[2560,128]{1,0:T(8,128)(2,1)S(1)}, bf16[4,384,128]{2,1,0:T(8,128)(2,1)S(1)}, bf16[512,128]{1,0:T(8,128)(2,1)S(1)}, bf16[512,128]{1,0:T(8,128)(2,1)}) custom-call(s32[4]{0:T(128)S(1)} %pad_add_fusion.idx, bf16[3072,128]{1,0:T(8,128)(2,1)S(1)} %copy-done, bf16[2048,128]{1,0:T(8,128)(2,1)S(1)} %copy-done.3), custom_call_target="tpu_custom_call" | custom-call | tf_op jit(solution)/shard_map/pallas_call | solution.py:367
  16.1 1.6 %collective-permute-start.1 = (bf16[128,256]{1,0:T(8,128)(2,1)S(1)}, bf16[128,256]{1,0:T(8,128)(2,1)S(1)}, u32[]{:S(2)}, u32[]{:S(2)}) collective-permute-start(bf16[128,256]{1,0:T(8,128)(2,1)S(1)} %get-tuple-element.102), channel_id=1, source_target_pairs={{0,8},{1,9},{2,10},{3,11},{4,12},{5,13},{6,14},{7,15},{8,0},{9,1},... | collective-permute-start | bytes 196616 | tf_op jit(solution)/shard_map/ppermute | solution.py:416
  17.7 2.6 %collective-permute-start.2 = (bf16[128,256]{1,0:T(8,128)(2,1)S(1)}, bf16[128,256]{1,0:T(8,128)(2,1)S(1)}, u32[]{:S(2)}, u32[]{:S(2)}) collective-permute-start(bf16[128,256]{1,0:T(8,128)(2,1)S(1)} %get-tuple-element.103), channel_id=1, source_target_pairs={{0,16},{1,17},{2,18},{3,19},{4,20},{5,21},{6,22},{7,23},{8,24},{9,... | collective-permute-start | bytes 196616 | tf_op jit(solution)/shard_map/ppermute | solution.py:416
  20.5 4.7 %collective-permute-done.2.refs_2_.refs_6_ = bf16[128,256]{1,0:T(8,128)(2,1)S(1)} collective-permute-done((bf16[128,256]{1,0:T(8,128)(2,1)S(1)}, bf16[128,256]{1,0:T(8,128)(2,1)S(1)}, u32[]{:S(2)}, u32[]{:S(2)}) %collective-permute-start.2) | collective-permute-done | bytes 65568 | tf_op jit(solution)/shard_map/ppermute | solution.py:416
  29.2 2.8 %collective-permute-done.5.message = bf16[2560,128]{1,0:T(8,128)(2,1)S(1)} collective-permute-done((bf16[2560,128]{1,0:T(8,128)(2,1)}, bf16[2560,128]{1,0:T(8,128)(2,1)S(1)}, u32[]{:S(2)}, u32[]{:S(2)}) %collective-permute-start.5) | collective-permute-done | bytes 655392 | tf_op jit(solution)/shard_map/ppermute | solution.py:416
  32.1 3.7 %collective-permute-start.8 = (bf16[96,512]{1,0:T(8,128)(2,1)S(1)}, bf16[96,512]{1,0:T(8,128)(2,1)S(1)}, u32[]{:S(2)}, u32[]{:S(2)}) collective-permute-start(bf16[96,512]{1,0:T(8,128)(2,1)S(1)} %shard_map.140.refs_0_), channel_id=1, source_target_pairs={{0,24},{1,25},{2,26},{3,27},{4,28},{5,29},{6,30},{7,31},{8,16},{9,... | collective-permute-start | bytes 294920 | tf_op jit(solution)/shard_map/ppermute | solution.py:416
  36.5 3.1 %collective-permute-done.8.refs_3_ = bf16[96,512]{1,0:T(8,128)(2,1)S(1)} collective-permute-done((bf16[96,512]{1,0:T(8,128)(2,1)S(1)}, bf16[96,512]{1,0:T(8,128)(2,1)S(1)}, u32[]{:S(2)}, u32[]{:S(2)}) %collective-permute-start.8) | collective-permute-done | bytes 98336 | tf_op jit(solution)/shard_map/ppermute | solution.py:416
  39.7 5.0 %collective-permute-done.7.refs_2_ = bf16[96,512]{1,0:T(8,128)(2,1)S(1)} collective-permute-done((bf16[96,512]{1,0:T(8,128)(2,1)S(1)}, bf16[96,512]{1,0:T(8,128)(2,1)S(1)}, u32[]{:S(2)}, u32[]{:S(2)}) %collective-permute-start.7) | collective-permute-done | bytes 98336 | tf_op jit(solution)/shard_map/ppermute | solution.py:416
  46.5 2.5 %collective-permute-start.16 = (bf16[2,384,128]{2,1,0:T(8,128)(2,1)S(1)}, bf16[2,384,128]{2,1,0:T(8,128)(2,1)S(1)}, u32[]{:S(2)}, u32[]{:S(2)}) collective-permute-start(bf16[2,384,128]{2,1,0:T(8,128)(2,1)S(1)} %get-tuple-element.145), channel_id=1, source_target_pairs={{0,16},{1,17},{2,18},{3,19},{4,20},{5,21},{6,22},{7,23},{8,24},{9,... | collective-permute-start | bytes 589832 | tf_op jit(solution)/shard_map/ppermute | solution.py:416
  51.2 1.4 %collective-permute-start.14 = (bf16[48,512]{1,0:T(8,128)(2,1)S(1)}, bf16[48,512]{1,0:T(8,128)(2,1)S(1)}, u32[]{:S(2)}, u32[]{:S(2)}) collective-permute-start(bf16[48,512]{1,0:T(8,128)(2,1)S(1)} %get-tuple-element.141), channel_id=1, source_target_pairs={{0,5},{1,4},{2,7},{3,6},{4,1},{5,0},{6,3},{7,2},{8,13},{9,12},{10,... | collective-permute-start | bytes 147464 | tf_op jit(solution)/shard_map/ppermute | solution.py:416
  53.3 1.5 %collective-permute-done.13.refs_2_ = bf16[48,512]{1,0:T(8,128)(2,1)S(1)} collective-permute-done((bf16[48,512]{1,0:T(8,128)(2,1)S(1)}, bf16[48,512]{1,0:T(8,128)(2,1)S(1)}, u32[]{:S(2)}, u32[]{:S(2)}) %collective-permute-start.13) | collective-permute-done | bytes 49184 | tf_op jit(solution)/shard_map/ppermute | solution.py:416
  54.8 1.4 %collective-permute-done.14.refs_3_ = bf16[48,512]{1,0:T(8,128)(2,1)S(1)} collective-permute-done((bf16[48,512]{1,0:T(8,128)(2,1)S(1)}, bf16[48,512]{1,0:T(8,128)(2,1)S(1)}, u32[]{:S(2)}, u32[]{:S(2)}) %collective-permute-start.14) | collective-permute-done | bytes 49184 | tf_op jit(solution)/shard_map/ppermute | solution.py:416
  57.1 1.5 %collective-permute-done.16.refs_2_ = bf16[2,384,128]{2,1,0:T(8,128)(2,1)S(1)} collective-permute-done((bf16[2,384,128]{2,1,0:T(8,128)(2,1)S(1)}, bf16[2,384,128]{2,1,0:T(8,128)(2,1)S(1)}, u32[]{:S(2)}, u32[]{:S(2)}) %collective-permute-start.16) | collective-permute-done | bytes 196640 | tf_op jit(solution)/shard_map/ppermute | solution.py:416
  58.6 2.2 %collective-permute-start.23 = (bf16[2,384,128]{2,1,0:T(8,128)(2,1)S(1)}, bf16[2,384,128]{2,1,0:T(8,128)(2,1)S(1)}, u32[]{:S(2)}, u32[]{:S(2)}) collective-permute-start(bf16[2,384,128]{2,1,0:T(8,128)(2,1)S(1)} %get-tuple-element.159), channel_id=1, source_target_pairs={{0,24},{1,25},{2,26},{3,27},{4,28},{5,29},{6,30},{7,31},{8,16},{9,... | collective-permute-start | bytes 589832 | tf_op jit(solution)/shard_map/ppermute | solution.py:416
  60.9 1.5 %collective-permute-start.19 = (bf16[48,512]{1,0:T(8,128)(2,1)S(1)}, bf16[48,512]{1,0:T(8,128)(2,1)S(1)}, u32[]{:S(2)}, u32[]{:S(2)}) collective-permute-start(bf16[48,512]{1,0:T(8,128)(2,1)S(1)} %shard_map.144.refs_0_.hidden), channel_id=1, source_target_pairs={{0,5},{1,4},{2,7},{3,6},{4,1},{5,0},{6,3},{7,2},{8,13},{9,12},{10,... | collective-permute-start | bytes 147464 | tf_op jit(solution)/shard_map/ppermute | solution.py:416
  64.4 1.8 %collective-permute-done.19.refs_3_ = bf16[48,512]{1,0:T(8,128)(2,1)S(1)} collective-permute-done((bf16[48,512]{1,0:T(8,128)(2,1)S(1)}, bf16[48,512]{1,0:T(8,128)(2,1)S(1)}, u32[]{:S(2)}, u32[]{:S(2)}) %collective-permute-start.19) | collective-permute-done | bytes 49184 | tf_op jit(solution)/shard_map/ppermute | solution.py:416
  67.6 1.5 %shard_map.145 = (f32[208,768]{1,0:T(8,128)S(1)}, bf16[208,768]{1,0:T(8,128)(2,1)S(1)}, f32[112,768]{1,0:T(8,128)S(1)}, f32[96,768]{1,0:T(8,128)S(1)}, bf16[112,...) custom-call(s32[4]{0:T(128)S(1)} %pad_add_fusion.idx, bf16[48,512]{1,0:T(8,128)(2,1)S(1)} %shard_map.144.refs_0_.hidden, ...), custom_call_target="tpu_custom_call" | custom-call | tf_op jit(solution)/shard_map/pallas_call | solution.py:367
  69.2 1.3 %collective-permute-start.21 = (bf16[96,768]{1,0:T(8,128)(2,1)S(1)}, bf16[96,768]{1,0:T(8,128)(2,1)S(1)}, u32[]{:S(2)}, u32[]{:S(2)}) collective-permute-start(bf16[96,768]{1,0:T(8,128)(2,1)S(1)} %get-tuple-element.151), channel_id=1, source_target_pairs={{0,8},{1,9},{2,10},{3,11},{4,12},{5,13},{6,14},{7,15},{8,0},{9,1},... | collective-permute-start | bytes 442376 | tf_op jit(solution)/shard_map/ppermute | solution.py:416
  71.3 4.6 %collective-permute-done.21.got = bf16[96,768]{1,0:T(8,128)(2,1)S(1)} collective-permute-done((bf16[96,768]{1,0:T(8,128)(2,1)S(1)}, bf16[96,768]{1,0:T(8,128)(2,1)S(1)}, u32[]{:S(2)}, u32[]{:S(2)}) %collective-permute-start.21) | collective-permute-done | bytes 147488 | tf_op jit(solution)/shard_map/ppermute | solution.py:416
  75.9 1.3 %collective-permute-start.22 = (bf16[208,768]{1,0:T(8,128)(2,1)S(1)}, bf16[208,768]{1,0:T(8,128)(2,1)S(1)}, u32[]{:S(2)}, u32[]{:S(2)}) collective-permute-start(bf16[208,768]{1,0:T(8,128)(2,1)S(1)} %get-tuple-element.153), channel_id=1, source_target_pairs={{0,8},{1,9},{2,10},{3,11},{4,12},{5,13},{6,14},{7,15},{8,0},{9,1},... | collective-permute-start | bytes 958472 | tf_op jit(solution)/shard_map/ppermute | solution.py:416
  77.2 2.4 %collective-permute-done.24.got = bf16[112,768]{1,0:T(8,128)(2,1)S(1)} collective-permute-done((bf16[112,768]{1,0:T(8,128)(2,1)S(1)}, bf16[112,768]{1,0:T(8,128)(2,1)S(1)}, u32[]{:S(2)}, u32[]{:S(2)}) %collective-permute-start.24) | collective-permute-done | bytes 172064 | tf_op jit(solution)/shard_map/ppermute | solution.py:416
  79.7 1.5 %collective-permute-start.25 = (bf16[112,768]{1,0:T(8,128)(2,1)S(1)}, bf16[112,768]{1,0:T(8,128)(2,1)S(1)}, u32[]{:S(2)}, u32[]{:S(2)}) collective-permute-start(bf16[112,768]{1,0:T(8,128)(2,1)S(1)} %shard_map.146), channel_id=1, source_target_pairs={{0,16},{1,17},{2,18},{3,19},{4,20},{5,21},{6,22},{7,23},{8,24},{9,... | collective-permute-start | bytes 516104 | tf_op jit(solution)/shard_map/ppermute | solution.py:416
  81.2 1.6 %collective-permute-start.26 = (bf16[96,768]{1,0:T(8,128)(2,1)S(1)}, bf16[96,768]{1,0:T(8,128)(2,1)S(1)}, u32[]{:S(2)}, u32[]{:S(2)}) collective-permute-start(bf16[96,768]{1,0:T(8,128)(2,1)S(1)} %shard_map.147), channel_id=1, source_target_pairs={{0,16},{1,17},{2,18},{3,19},{4,20},{5,21},{6,22},{7,23},{8,24},{9,... | collective-permute-start | bytes 442376 | tf_op jit(solution)/shard_map/ppermute | solution.py:416
  82.8 11.8 %collective-permute-done.25.far_head.far_part = bf16[112,768]{1,0:T(8,128)(2,1)S(1)} collective-permute-done((bf16[112,768]{1,0:T(8,128)(2,1)S(1)}, bf16[112,768]{1,0:T(8,128)(2,1)S(1)}, u32[]{:S(2)}, u32[]{:S(2)}) %collective-permute-start.25) | collective-permute-done | bytes 172064 | tf_op jit(solution)/shard_map/ppermute | solution.py:416
  96.8 1.5 %collective-permute-start.30 = (bf16[4,48,512]{2,1,0:T(8,128)(2,1)S(1)}, bf16[4,48,512]{2,1,0:T(8,128)(2,1)S(1)}, u32[]{:S(2)}, u32[]{:S(2)}) collective-permute-start(bf16[4,48,512]{2,1,0:T(8,128)(2,1)S(1)} %get-tuple-element.170), channel_id=1, source_target_pairs={{0,5},{1,4},{2,7},{3,6},{4,1},{5,0},{6,3},{7,2},{8,13},{9,12},{10,... | collective-permute-start | bytes 589832 | tf_op jit(solution)/shard_map/ppermute | solution.py:416
  101.6 2.5 %collective-permute-done.30.refs_3_ = bf16[4,48,512]{2,1,0:T(8,128)(2,1)S(1)} collective-permute-done((bf16[4,48,512]{2,1,0:T(8,128)(2,1)S(1)}, bf16[4,48,512]{2,1,0:T(8,128)(2,1)S(1)}, u32[]{:S(2)}, u32[]{:S(2)}) %collective-permute-start.30) | collective-permute-done | bytes 196640 | tf_op jit(solution)/shard_map/ppermute | solution.py:416
  104.1 2.0 %collective-permute-done.28.refs_1_ = bf16[4,48,512]{2,1,0:T(8,128)(2,1)S(1)} collective-permute-done((bf16[4,48,512]{2,1,0:T(8,128)(2,1)S(1)}, bf16[4,48,512]{2,1,0:T(8,128)(2,1)S(1)}, u32[]{:S(2)}, u32[]{:S(2)}) %collective-permute-start.28) | collective-permute-done | bytes 196640 | tf_op jit(solution)/shard_map/ppermute | solution.py:416
  107.1 1.8 %collective-permute-start.32 = (bf16[64,512]{1,0:T(8,128)(2,1)S(1)}, bf16[64,512]{1,0:T(8,128)(2,1)S(1)}, u32[]{:S(2)}, u32[]{:S(2)}) collective-permute-start(bf16[64,512]{1,0:T(8,128)(2,1)S(1)} %get-tuple-element.173), channel_id=1, source_target_pairs={{0,16},{1,17},{2,18},{3,19},{4,20},{5,21},{6,22},{7,23},{8,24},{9,... | collective-permute-start | bytes 196616 | tf_op jit(solution)/shard_map/ppermute | solution.py:416
  108.9 2.6 %collective-permute-start.33 = (bf16[64,512]{1,0:T(8,128)(2,1)S(1)}, bf16[64,512]{1,0:T(8,128)(2,1)S(1)}, u32[]{:S(2)}, u32[]{:S(2)}) collective-permute-start(bf16[64,512]{1,0:T(8,128)(2,1)S(1)} %get-tuple-element.174), channel_id=1, source_target_pairs={{0,24},{1,25},{2,26},{3,27},{4,28},{5,29},{6,30},{7,31},{8,16},{9,... | collective-permute-start | bytes 196616 | tf_op jit(solution)/shard_map/ppermute | solution.py:416
  112.3 2.6 %collective-permute-done.33.refs_3_ = bf16[64,512]{1,0:T(8,128)(2,1)S(1)} collective-permute-done((bf16[64,512]{1,0:T(8,128)(2,1)S(1)}, bf16[64,512]{1,0:T(8,128)(2,1)S(1)}, u32[]{:S(2)}, u32[]{:S(2)}) %collective-permute-start.33) | collective-permute-done | bytes 65568 | tf_op jit(solution)/shard_map/ppermute | solution.py:416
  (81 shorter events, 30.3 us)
Async XLA Ops:
  1.8 12.0 %all-to-all-start = ((bf16[8,16,1280]{2,1,0:T(8,128)(2,1)}), bf16[8,16,1280]{2,1,0:T(8,128)(2,1)S(1)}, u32[]{:S(2)}, u32[]{:S(2)}) async-start(bf16[8,16,1280]{2,1,0:T(8,128)(2,1)} %shard_map.136), calls=%async_computation | async-start | bytes 655360 | tf_op jit(solution)/shard_map/all_to_all | solution.py:425
  13.9 12.6 %collective-permute-start.4 = (bf16[128,3072]{1,0:T(8,128)(2,1)S(1)}, bf16[128,3072]{1,0:T(8,128)(2,1)S(1)}, u32[]{:S(2)}, u32[]{:S(2)}) collective-permute-start(bf16[128,3072]{1,0:T(8,128)(2,1)S(1)} %get-tuple-element.106.refs_4_), channel_id=1, source_target_pairs={{0,2},{1,3},{2,0},{3,1},{4,6},{5,7},{6,4},{7,5},{8,10},{9,11},{10,... | collective-permute-start | bytes 2359304 | tf_op jit(solution)/shard_map/ppermute | solution.py:416
  14.2 17.8 %collective-permute-start.5 = (bf16[2560,128]{1,0:T(8,128)(2,1)}, bf16[2560,128]{1,0:T(8,128)(2,1)S(1)}, u32[]{:S(2)}, u32[]{:S(2)}) collective-permute-start(bf16[2560,128]{1,0:T(8,128)(2,1)} %copy-done.9), channel_id=1, source_target_pairs={{0,4},{1,5},{2,6},{3,7},{4,0},{5,1},{6,2},{7,3},{8,12},{9,13},{10,... | collective-permute-start | bytes 1966088 | tf_op jit(solution)/shard_map/ppermute | solution.py:416
  16.1 4.5 %collective-permute-start.1 = (bf16[128,256]{1,0:T(8,128)(2,1)S(1)}, bf16[128,256]{1,0:T(8,128)(2,1)S(1)}, u32[]{:S(2)}, u32[]{:S(2)}) collective-permute-start(bf16[128,256]{1,0:T(8,128)(2,1)S(1)} %get-tuple-element.102), channel_id=1, source_target_pairs={{0,8},{1,9},{2,10},{3,11},{4,12},{5,13},{6,14},{7,15},{8,0},{9,1},... | collective-permute-start | bytes 196616 | tf_op jit(solution)/shard_map/ppermute | solution.py:416
  17.7 7.5 %collective-permute-start.2 = (bf16[128,256]{1,0:T(8,128)(2,1)S(1)}, bf16[128,256]{1,0:T(8,128)(2,1)S(1)}, u32[]{:S(2)}, u32[]{:S(2)}) collective-permute-start(bf16[128,256]{1,0:T(8,128)(2,1)S(1)} %get-tuple-element.103), channel_id=1, source_target_pairs={{0,16},{1,17},{2,18},{3,19},{4,20},{5,21},{6,22},{7,23},{8,24},{9,... | collective-permute-start | bytes 196616 | tf_op jit(solution)/shard_map/ppermute | solution.py:416
  20.3 6.2 %collective-permute-start.3 = (bf16[128,256]{1,0:T(8,128)(2,1)S(1)}, bf16[128,256]{1,0:T(8,128)(2,1)S(1)}, u32[]{:S(2)}, u32[]{:S(2)}) collective-permute-start(bf16[128,256]{1,0:T(8,128)(2,1)S(1)} %get-tuple-element.104), channel_id=1, source_target_pairs={{0,24},{1,25},{2,26},{3,27},{4,28},{5,29},{6,30},{7,31},{8,16},{9,... | collective-permute-start | bytes 196616 | tf_op jit(solution)/shard_map/ppermute | solution.py:416
  26.5 22.6 %collective-permute-start.11 = (bf16[128,3072]{1,0:T(8,128)(2,1)}, bf16[128,3072]{1,0:T(8,128)(2,1)S(1)}, u32[]{:S(2)}, u32[]{:S(2)}) collective-permute-start(bf16[128,3072]{1,0:T(8,128)(2,1)} %copy-done.8), channel_id=1, source_target_pairs={{0,4},{1,5},{2,6},{3,7},{4,0},{5,1},{6,2},{7,3},{8,12},{9,13},{10,... | collective-permute-start | bytes 2359304 | tf_op jit(solution)/shard_map/ppermute | solution.py:416
  32.0 12.6 %collective-permute-start.9 = (bf16[512,128]{1,0:T(8,128)(2,1)S(1)}, bf16[512,128]{1,0:T(8,128)(2,1)S(1)}, u32[]{:S(2)}, u32[]{:S(2)}) collective-permute-start(bf16[512,128]{1,0:T(8,128)(2,1)S(1)} %get-tuple-element.119), channel_id=1, source_target_pairs={{0,2},{1,3},{2,0},{3,1},{4,6},{5,7},{6,4},{7,5},{8,10},{9,11},{10,... | collective-permute-start | bytes 393224 | tf_op jit(solution)/shard_map/ppermute | solution.py:416
  32.1 7.6 %collective-permute-start.8 = (bf16[96,512]{1,0:T(8,128)(2,1)S(1)}, bf16[96,512]{1,0:T(8,128)(2,1)S(1)}, u32[]{:S(2)}, u32[]{:S(2)}) collective-permute-start(bf16[96,512]{1,0:T(8,128)(2,1)S(1)} %shard_map.140.refs_0_), channel_id=1, source_target_pairs={{0,24},{1,25},{2,26},{3,27},{4,28},{5,29},{6,30},{7,31},{8,16},{9,... | collective-permute-start | bytes 294920 | tf_op jit(solution)/shard_map/ppermute | solution.py:416
  35.8 8.9 %collective-permute-start.7 = (bf16[96,512]{1,0:T(8,128)(2,1)S(1)}, bf16[96,512]{1,0:T(8,128)(2,1)S(1)}, u32[]{:S(2)}, u32[]{:S(2)}) collective-permute-start(bf16[96,512]{1,0:T(8,128)(2,1)S(1)} %shard_map.140.refs_0_), channel_id=1, source_target_pairs={{0,16},{1,17},{2,18},{3,19},{4,20},{5,21},{6,22},{7,23},{8,24},{9,... | collective-permute-start | bytes 294920 | tf_op jit(solution)/shard_map/ppermute | solution.py:416
  35.8 8.9 %collective-permute-start.6 = (bf16[96,512]{1,0:T(8,128)(2,1)S(1)}, bf16[96,512]{1,0:T(8,128)(2,1)S(1)}, u32[]{:S(2)}, u32[]{:S(2)}) collective-permute-start(bf16[96,512]{1,0:T(8,128)(2,1)S(1)} %shard_map.140.refs_0_), channel_id=1, source_target_pairs={{0,8},{1,9},{2,10},{3,11},{4,12},{5,13},{6,14},{7,15},{8,0},{9,1},... | collective-permute-start | bytes 294920 | tf_op jit(solution)/shard_map/ppermute | solution.py:416
  45.9 11.2 %collective-permute-start.15 = (bf16[2,384,128]{2,1,0:T(8,128)(2,1)S(1)}, bf16[2,384,128]{2,1,0:T(8,128)(2,1)S(1)}, u32[]{:S(2)}, u32[]{:S(2)}) collective-permute-start(bf16[2,384,128]{2,1,0:T(8,128)(2,1)S(1)} %get-tuple-element.144), channel_id=1, source_target_pairs={{0,8},{1,9},{2,10},{3,11},{4,12},{5,13},{6,14},{7,15},{8,0},{9,1},... | collective-permute-start | bytes 589832 | tf_op jit(solution)/shard_map/ppermute | solution.py:416
  46.5 12.1 %collective-permute-start.16 = (bf16[2,384,128]{2,1,0:T(8,128)(2,1)S(1)}, bf16[2,384,128]{2,1,0:T(8,128)(2,1)S(1)}, u32[]{:S(2)}, u32[]{:S(2)}) collective-permute-start(bf16[2,384,128]{2,1,0:T(8,128)(2,1)S(1)} %get-tuple-element.145), channel_id=1, source_target_pairs={{0,16},{1,17},{2,18},{3,19},{4,20},{5,21},{6,22},{7,23},{8,24},{9,... | collective-permute-start | bytes 589832 | tf_op jit(solution)/shard_map/ppermute | solution.py:416
  49.1 4.2 %collective-permute-start.12 = (bf16[48,512]{1,0:T(8,128)(2,1)S(1)}, bf16[48,512]{1,0:T(8,128)(2,1)S(1)}, u32[]{:S(2)}, u32[]{:S(2)}) collective-permute-start(bf16[48,512]{1,0:T(8,128)(2,1)S(1)} %get-tuple-element.139), channel_id=1, source_target_pairs={{0,1},{1,0},{2,3},{3,2},{4,5},{5,4},{6,7},{7,6},{8,9},{9,8},{10,11... | collective-permute-start | bytes 147464 | tf_op jit(solution)/shard_map/ppermute | solution.py:416
  50.3 4.5 %collective-permute-start.13 = (bf16[48,512]{1,0:T(8,128)(2,1)S(1)}, bf16[48,512]{1,0:T(8,128)(2,1)S(1)}, u32[]{:S(2)}, u32[]{:S(2)}) collective-permute-start(bf16[48,512]{1,0:T(8,128)(2,1)S(1)} %get-tuple-element.140), channel_id=1, source_target_pairs={{0,4},{1,5},{2,6},{3,7},{4,0},{5,1},{6,2},{7,3},{8,12},{9,13},{10,... | collective-permute-start | bytes 147464 | tf_op jit(solution)/shard_map/ppermute | solution.py:416
  51.2 5.0 %collective-permute-start.14 = (bf16[48,512]{1,0:T(8,128)(2,1)S(1)}, bf16[48,512]{1,0:T(8,128)(2,1)S(1)}, u32[]{:S(2)}, u32[]{:S(2)}) collective-permute-start(bf16[48,512]{1,0:T(8,128)(2,1)S(1)} %get-tuple-element.141), channel_id=1, source_target_pairs={{0,5},{1,4},{2,7},{3,6},{4,1},{5,0},{6,3},{7,2},{8,13},{9,12},{10,... | collective-permute-start | bytes 147464 | tf_op jit(solution)/shard_map/ppermute | solution.py:416
  58.6 8.9 %collective-permute-start.20 = (bf16[128,3072]{1,0:T(8,128)(2,1)S(1)}, bf16[128,3072]{1,0:T(8,128)(2,1)S(1)}, u32[]{:S(2)}, u32[]{:S(2)}) collective-permute-start(bf16[128,3072]{1,0:T(8,128)(2,1)S(1)} %collective-permute-done.11.refs_6_), channel_id=1, source_target_pairs={{0,2},{1,3},{2,0},{3,1},{4,6},{5,7},{6,4},{7,5},{8,10},{9,11},{10,... | collective-permute-start | bytes 2359304 | tf_op jit(solution)/shard_map/ppermute | solution.py:416
  58.6 10.4 %collective-permute-start.23 = (bf16[2,384,128]{2,1,0:T(8,128)(2,1)S(1)}, bf16[2,384,128]{2,1,0:T(8,128)(2,1)S(1)}, u32[]{:S(2)}, u32[]{:S(2)}) collective-permute-start(bf16[2,384,128]{2,1,0:T(8,128)(2,1)S(1)} %get-tuple-element.159), channel_id=1, source_target_pairs={{0,24},{1,25},{2,26},{3,27},{4,28},{5,29},{6,30},{7,31},{8,16},{9,... | collective-permute-start | bytes 589832 | tf_op jit(solution)/shard_map/ppermute | solution.py:416
  60.9 5.3 %collective-permute-start.19 = (bf16[48,512]{1,0:T(8,128)(2,1)S(1)}, bf16[48,512]{1,0:T(8,128)(2,1)S(1)}, u32[]{:S(2)}, u32[]{:S(2)}) collective-permute-start(bf16[48,512]{1,0:T(8,128)(2,1)S(1)} %shard_map.144.refs_0_.hidden), channel_id=1, source_target_pairs={{0,5},{1,4},{2,7},{3,6},{4,1},{5,0},{6,3},{7,2},{8,13},{9,12},{10,... | collective-permute-start | bytes 147464 | tf_op jit(solution)/shard_map/ppermute | solution.py:416
  62.4 4.1 %collective-permute-start.18 = (bf16[48,512]{1,0:T(8,128)(2,1)S(1)}, bf16[48,512]{1,0:T(8,128)(2,1)S(1)}, u32[]{:S(2)}, u32[]{:S(2)}) collective-permute-start(bf16[48,512]{1,0:T(8,128)(2,1)S(1)} %shard_map.144.refs_0_.hidden), channel_id=1, source_target_pairs={{0,4},{1,5},{2,6},{3,7},{4,0},{5,1},{6,2},{7,3},{8,12},{9,13},{10,... | collective-permute-start | bytes 147464 | tf_op jit(solution)/shard_map/ppermute | solution.py:416
  69.2 25.5 %collective-permute-start.27 = (bf16[4,2,384,128]{3,2,1,0:T(8,128)(2,1)S(1)}, bf16[4,2,384,128]{3,2,1,0:T(8,128)(2,1)S(1)}, u32[]{:S(2)}, u32[]{:S(2)}) collective-permute-start(bf16[4,2,384,128]{3,2,1,0:T(8,128)(2,1)S(1)} %shard_map.148.near), channel_id=1, source_target_pairs={{0,2},{1,3},{2,0},{3,1},{4,6},{5,7},{6,4},{7,5},{8,10},{9,11},{10,... | collective-permute-start | bytes 2359304 | tf_op jit(solution)/shard_map/ppermute | solution.py:416
  69.2 6.7 %collective-permute-start.21 = (bf16[96,768]{1,0:T(8,128)(2,1)S(1)}, bf16[96,768]{1,0:T(8,128)(2,1)S(1)}, u32[]{:S(2)}, u32[]{:S(2)}) collective-permute-start(bf16[96,768]{1,0:T(8,128)(2,1)S(1)} %get-tuple-element.151), channel_id=1, source_target_pairs={{0,8},{1,9},{2,10},{3,11},{4,12},{5,13},{6,14},{7,15},{8,0},{9,1},... | collective-permute-start | bytes 442376 | tf_op jit(solution)/shard_map/ppermute | solution.py:416
  70.6 9.1 %collective-permute-start.24 = (bf16[112,768]{1,0:T(8,128)(2,1)S(1)}, bf16[112,768]{1,0:T(8,128)(2,1)S(1)}, u32[]{:S(2)}, u32[]{:S(2)}) collective-permute-start(bf16[112,768]{1,0:T(8,128)(2,1)S(1)} %get-tuple-element.160), channel_id=1, source_target_pairs={{0,8},{1,9},{2,10},{3,11},{4,12},{5,13},{6,14},{7,15},{8,0},{9,1},... | collective-permute-start | bytes 516104 | tf_op jit(solution)/shard_map/ppermute | solution.py:416
  75.9 18.7 %collective-permute-start.22 = (bf16[208,768]{1,0:T(8,128)(2,1)S(1)}, bf16[208,768]{1,0:T(8,128)(2,1)S(1)}, u32[]{:S(2)}, u32[]{:S(2)}) collective-permute-start(bf16[208,768]{1,0:T(8,128)(2,1)S(1)} %get-tuple-element.153), channel_id=1, source_target_pairs={{0,8},{1,9},{2,10},{3,11},{4,12},{5,13},{6,14},{7,15},{8,0},{9,1},... | collective-permute-start | bytes 958472 | tf_op jit(solution)/shard_map/ppermute | solution.py:416
  79.7 14.9 %collective-permute-start.25 = (bf16[112,768]{1,0:T(8,128)(2,1)S(1)}, bf16[112,768]{1,0:T(8,128)(2,1)S(1)}, u32[]{:S(2)}, u32[]{:S(2)}) collective-permute-start(bf16[112,768]{1,0:T(8,128)(2,1)S(1)} %shard_map.146), channel_id=1, source_target_pairs={{0,16},{1,17},{2,18},{3,19},{4,20},{5,21},{6,22},{7,23},{8,24},{9,... | collective-permute-start | bytes 516104 | tf_op jit(solution)/shard_map/ppermute | solution.py:416
  81.2 17.1 %collective-permute-start.26 = (bf16[96,768]{1,0:T(8,128)(2,1)S(1)}, bf16[96,768]{1,0:T(8,128)(2,1)S(1)}, u32[]{:S(2)}, u32[]{:S(2)}) collective-permute-start(bf16[96,768]{1,0:T(8,128)(2,1)S(1)} %shard_map.147), channel_id=1, source_target_pairs={{0,16},{1,17},{2,18},{3,19},{4,20},{5,21},{6,22},{7,23},{8,24},{9,... | collective-permute-start | bytes 442376 | tf_op jit(solution)/shard_map/ppermute | solution.py:416
  95.8 5.7 %collective-permute-start.29 = (bf16[4,48,512]{2,1,0:T(8,128)(2,1)S(1)}, bf16[4,48,512]{2,1,0:T(8,128)(2,1)S(1)}, u32[]{:S(2)}, u32[]{:S(2)}) collective-permute-start(bf16[4,48,512]{2,1,0:T(8,128)(2,1)S(1)} %get-tuple-element.169), channel_id=1, source_target_pairs={{0,4},{1,5},{2,6},{3,7},{4,0},{5,1},{6,2},{7,3},{8,12},{9,13},{10,... | collective-permute-start | bytes 589832 | tf_op jit(solution)/shard_map/ppermute | solution.py:416
  96.8 7.3 %collective-permute-start.30 = (bf16[4,48,512]{2,1,0:T(8,128)(2,1)S(1)}, bf16[4,48,512]{2,1,0:T(8,128)(2,1)S(1)}, u32[]{:S(2)}, u32[]{:S(2)}) collective-permute-start(bf16[4,48,512]{2,1,0:T(8,128)(2,1)S(1)} %get-tuple-element.170), channel_id=1, source_target_pairs={{0,5},{1,4},{2,7},{3,6},{4,1},{5,0},{6,3},{7,2},{8,13},{9,12},{10,... | collective-permute-start | bytes 589832 | tf_op jit(solution)/shard_map/ppermute | solution.py:416
  99.5 6.6 %collective-permute-start.28 = (bf16[4,48,512]{2,1,0:T(8,128)(2,1)S(1)}, bf16[4,48,512]{2,1,0:T(8,128)(2,1)S(1)}, u32[]{:S(2)}, u32[]{:S(2)}) collective-permute-start(bf16[4,48,512]{2,1,0:T(8,128)(2,1)S(1)} %get-tuple-element.168), channel_id=1, source_target_pairs={{0,1},{1,0},{2,3},{3,2},{4,5},{5,4},{6,7},{7,6},{8,9},{9,8},{10,11... | collective-permute-start | bytes 589832 | tf_op jit(solution)/shard_map/ppermute | solution.py:416
  107.0 4.5 %collective-permute-start.31 = (bf16[64,512]{1,0:T(8,128)(2,1)S(1)}, bf16[64,512]{1,0:T(8,128)(2,1)S(1)}, u32[]{:S(2)}, u32[]{:S(2)}) collective-permute-start(bf16[64,512]{1,0:T(8,128)(2,1)S(1)} %get-tuple-element.172), channel_id=1, source_target_pairs={{0,8},{1,9},{2,10},{3,11},{4,12},{5,13},{6,14},{7,15},{8,0},{9,1},... | collective-permute-start | bytes 196616 | tf_op jit(solution)/shard_map/ppermute | solution.py:416
  107.1 5.2 %collective-permute-start.32 = (bf16[64,512]{1,0:T(8,128)(2,1)S(1)}, bf16[64,512]{1,0:T(8,128)(2,1)S(1)}, u32[]{:S(2)}, u32[]{:S(2)}) collective-permute-start(bf16[64,512]{1,0:T(8,128)(2,1)S(1)} %get-tuple-element.173), channel_id=1, source_target_pairs={{0,16},{1,17},{2,18},{3,19},{4,20},{5,21},{6,22},{7,23},{8,24},{9,... | collective-permute-start | bytes 196616 | tf_op jit(solution)/shard_map/ppermute | solution.py:416
  108.9 6.1 %collective-permute-start.33 = (bf16[64,512]{1,0:T(8,128)(2,1)S(1)}, bf16[64,512]{1,0:T(8,128)(2,1)S(1)}, u32[]{:S(2)}, u32[]{:S(2)}) collective-permute-start(bf16[64,512]{1,0:T(8,128)(2,1)S(1)} %get-tuple-element.174), channel_id=1, source_target_pairs={{0,24},{1,25},{2,26},{3,27},{4,28},{5,29},{6,30},{7,31},{8,16},{9,... | collective-permute-start | bytes 196616 | tf_op jit(solution)/shard_map/ppermute | solution.py:416
  (14 other events, 67.3 us)

commit v9 on v8

--- a/solution.py
+++ b/solution.py
@@ -483,7 +483,8 @@
     )
     message = swap(message, side)
     twin = [swap(gate_up[0], core), None]
-    *messages, gate_up[1], twin[0] = after(*messages, gate_up[1], twin[0])
+    *messages, gate_up[1], twin[0] = after(*messages[::-1], gate_up[1], twin[0])
+    messages = messages[::-1]
     gate_up[1] = swap(gate_up[1], side)
     gated = call(
         functools.partial(attention_kernel, heads, planes),
@@ -582,7 +583,7 @@
     return call(
         functools.partial(last_kernel, planes, tokens),
         like(tokens, features),
-        idx, *across_planes(parts),
+        idx, *after(*across_planes(parts)[::-1])[::-1],
         scratch=[pltpu.VMEM((planes, rows, width), F32)],
     )
 

time: 116 us -> 116 us (level)
  no operation moved by 1% of the time
where the time goes in v9:
time: 116 us
  waiting for transfers between devices  53.9 us (46%)
  starting transfers between devices  43.9 us (38%)
  Pallas kernels  13.9 us (12%)
  local copies, waits for them, and re-layouts  3 us (3%)
    ppermute x34, waiting for transfers between devices, swap(): return lax.ppermute(x, axes, [(i, i ^ mask) for i in range(devices)])  52.8 us
    ppermute x34, starting transfers between devices, swap(): return lax.ppermute(x, axes, [(i, i ^ mask) for i in range(devices)])  38.6 us
    pallas_call x17, Pallas kernels, call(): pl.pallas_call(kernel, out_shape=shapes, in_specs=[SMEM if a.dtype == jnp...  13.9 us
    all_to_all x1, starting transfers between devices, plane_exchange(): lax.all_to_all(x, axes, 0, 0, axis_index_groups=plane_groups, tiled=True)  5.3 us
    unnamed x22, local copies, waits for them, and re-layouts  2.91 us
  transfers between devices with their start and end apart: 35, of which 22 were waited for; matrix products, arithmetic and copies ran while one was open for 0% of the time, Pallas kernels for 9%

profile of v9, /device:TPU:0, one launch (start us, length us, event | category | flops | bytes accessed | tf_op | source)
XLA Modules:
  0.0 115.8 jit_solution(11826658819966744870)
XLA Ops:
  0.0 1.8 %shard_map.136 = bf16[8,16,1280]{2,1,0:T(8,128)(2,1)} custom-call(bf16[12,1024]{1,0:T(8,128)(2,1)} %refs_0_.1, bf16[12,1024]{1,0:T(8,128)(2,1)} %refs_1_.1, bf16[12,4096]{1,0:T(8,128)(2,1)} %refs_2_.1, bf16[12,4096]{1,0:T(8,128)(2,1)} %refs_3_.1), custom_call_target="tpu_custom_call" | custom-call | tf_op jit(solution)/shard_map/pallas_call | solution.py:367
  1.8 5.3 %all-to-all-start = ((bf16[8,16,1280]{2,1,0:T(8,128)(2,1)}), bf16[8,16,1280]{2,1,0:T(8,128)(2,1)S(1)}, u32[]{:S(2)}, u32[]{:S(2)}) async-start(bf16[8,16,1280]{2,1,0:T(8,128)(2,1)} %shard_map.136), calls=%async_computation | async-start | bytes 655360 | tf_op jit(solution)/shard_map/all_to_all | solution.py:425
  8.4 1.3 %shard_map.137 = (bf16[2560,128]{1,0:T(8,128)(2,1)S(1)}, bf16[4,384,128]{2,1,0:T(8,128)(2,1)S(1)}, bf16[512,128]{1,0:T(8,128)(2,1)S(1)}, bf16[512,128]{1,0:T(8,128)(2,1)}) custom-call(s32[4]{0:T(128)S(1)} %pad_add_fusion.idx, bf16[3072,128]{1,0:T(8,128)(2,1)S(1)} %copy-done, bf16[2048,128]{1,0:T(8,128)(2,1)S(1)} %copy-done.3), custom_call_target="tpu_custom_call" | custom-call | tf_op jit(solution)/shard_map/pallas_call | solution.py:367
  16.1 3.7 %collective-permute-start.1 = (bf16[128,256]{1,0:T(8,128)(2,1)S(1)}, bf16[128,256]{1,0:T(8,128)(2,1)S(1)}, u32[]{:S(2)}, u32[]{:S(2)}) collective-permute-start(bf16[128,256]{1,0:T(8,128)(2,1)S(1)} %get-tuple-element.105), channel_id=1, source_target_pairs={{0,24},{1,25},{2,26},{3,27},{4,28},{5,29},{6,30},{7,31},{8,16},{9,... | collective-permute-start | bytes 196616 | tf_op jit(solution)/shard_map/ppermute | solution.py:416
  20.5 2.0 %collective-permute-done.1.refs_3_.refs_7_ = bf16[128,256]{1,0:T(8,128)(2,1)S(1)} collective-permute-done((bf16[128,256]{1,0:T(8,128)(2,1)S(1)}, bf16[128,256]{1,0:T(8,128)(2,1)S(1)}, u32[]{:S(2)}, u32[]{:S(2)}) %collective-permute-start.1) | collective-permute-done | bytes 65568 | tf_op jit(solution)/shard_map/ppermute | solution.py:416
  22.5 3.1 %collective-permute-done.2.refs_2_.refs_6_ = bf16[128,256]{1,0:T(8,128)(2,1)S(1)} collective-permute-done((bf16[128,256]{1,0:T(8,128)(2,1)S(1)}, bf16[128,256]{1,0:T(8,128)(2,1)S(1)}, u32[]{:S(2)}, u32[]{:S(2)}) %collective-permute-start.2) | collective-permute-done | bytes 65568 | tf_op jit(solution)/shard_map/ppermute | solution.py:416
  28.2 3.8 %collective-permute-done.5.message = bf16[2560,128]{1,0:T(8,128)(2,1)S(1)} collective-permute-done((bf16[2560,128]{1,0:T(8,128)(2,1)}, bf16[2560,128]{1,0:T(8,128)(2,1)S(1)}, u32[]{:S(2)}, u32[]{:S(2)}) %collective-permute-start.5) | collective-permute-done | bytes 655392 | tf_op jit(solution)/shard_map/ppermute | solution.py:416
  32.1 3.7 %collective-permute-start.8 = (bf16[96,512]{1,0:T(8,128)(2,1)S(1)}, bf16[96,512]{1,0:T(8,128)(2,1)S(1)}, u32[]{:S(2)}, u32[]{:S(2)}) collective-permute-start(bf16[96,512]{1,0:T(8,128)(2,1)S(1)} %shard_map.140.refs_0_), channel_id=1, source_target_pairs={{0,24},{1,25},{2,26},{3,27},{4,28},{5,29},{6,30},{7,31},{8,16},{9,... | collective-permute-start | bytes 294920 | tf_op jit(solution)/shard_map/ppermute | solution.py:416
  36.5 3.1 %collective-permute-done.8.refs_3_ = bf16[96,512]{1,0:T(8,128)(2,1)S(1)} collective-permute-done((bf16[96,512]{1,0:T(8,128)(2,1)S(1)}, bf16[96,512]{1,0:T(8,128)(2,1)S(1)}, u32[]{:S(2)}, u32[]{:S(2)}) %collective-permute-start.8) | collective-permute-done | bytes 98336 | tf_op jit(solution)/shard_map/ppermute | solution.py:416
  39.7 5.0 %collective-permute-done.7.refs_2_ = bf16[96,512]{1,0:T(8,128)(2,1)S(1)} collective-permute-done((bf16[96,512]{1,0:T(8,128)(2,1)S(1)}, bf16[96,512]{1,0:T(8,128)(2,1)S(1)}, u32[]{:S(2)}, u32[]{:S(2)}) %collective-permute-start.7) | collective-permute-done | bytes 98336 | tf_op jit(solution)/shard_map/ppermute | solution.py:416
  46.5 2.5 %collective-permute-start.16 = (bf16[2,384,128]{2,1,0:T(8,128)(2,1)S(1)}, bf16[2,384,128]{2,1,0:T(8,128)(2,1)S(1)}, u32[]{:S(2)}, u32[]{:S(2)}) collective-permute-start(bf16[2,384,128]{2,1,0:T(8,128)(2,1)S(1)} %get-tuple-element.149), channel_id=1, source_target_pairs={{0,16},{1,17},{2,18},{3,19},{4,20},{5,21},{6,22},{7,23},{8,24},{9,... | collective-permute-start | bytes 589832 | tf_op jit(solution)/shard_map/ppermute | solution.py:416
  51.2 1.4 %collective-permute-start.14 = (bf16[48,512]{1,0:T(8,128)(2,1)S(1)}, bf16[48,512]{1,0:T(8,128)(2,1)S(1)}, u32[]{:S(2)}, u32[]{:S(2)}) collective-permute-start(bf16[48,512]{1,0:T(8,128)(2,1)S(1)} %get-tuple-element.145), channel_id=1, source_target_pairs={{0,5},{1,4},{2,7},{3,6},{4,1},{5,0},{6,3},{7,2},{8,13},{9,12},{10,... | collective-permute-start | bytes 147464 | tf_op jit(solution)/shard_map/ppermute | solution.py:416
  53.3 1.5 %collective-permute-done.13.refs_2_ = bf16[48,512]{1,0:T(8,128)(2,1)S(1)} collective-permute-done((bf16[48,512]{1,0:T(8,128)(2,1)S(1)}, bf16[48,512]{1,0:T(8,128)(2,1)S(1)}, u32[]{:S(2)}, u32[]{:S(2)}) %collective-permute-start.13) | collective-permute-done | bytes 49184 | tf_op jit(solution)/shard_map/ppermute | solution.py:416
  54.8 1.4 %collective-permute-done.14.refs_3_ = bf16[48,512]{1,0:T(8,128)(2,1)S(1)} collective-permute-done((bf16[48,512]{1,0:T(8,128)(2,1)S(1)}, bf16[48,512]{1,0:T(8,128)(2,1)S(1)}, u32[]{:S(2)}, u32[]{:S(2)}) %collective-permute-start.14) | collective-permute-done | bytes 49184 | tf_op jit(solution)/shard_map/ppermute | solution.py:416
  57.1 1.5 %collective-permute-done.16.refs_2_ = bf16[2,384,128]{2,1,0:T(8,128)(2,1)S(1)} collective-permute-done((bf16[2,384,128]{2,1,0:T(8,128)(2,1)S(1)}, bf16[2,384,128]{2,1,0:T(8,128)(2,1)S(1)}, u32[]{:S(2)}, u32[]{:S(2)}) %collective-permute-start.16) | collective-permute-done | bytes 196640 | tf_op jit(solution)/shard_map/ppermute | solution.py:416
  58.6 2.2 %collective-permute-start.23 = (bf16[2,384,128]{2,1,0:T(8,128)(2,1)S(1)}, bf16[2,384,128]{2,1,0:T(8,128)(2,1)S(1)}, u32[]{:S(2)}, u32[]{:S(2)}) collective-permute-start(bf16[2,384,128]{2,1,0:T(8,128)(2,1)S(1)} %get-tuple-element.163), channel_id=1, source_target_pairs={{0,24},{1,25},{2,26},{3,27},{4,28},{5,29},{6,30},{7,31},{8,16},{9,... | collective-permute-start | bytes 589832 | tf_op jit(solution)/shard_map/ppermute | solution.py:416
  60.9 1.5 %collective-permute-start.19 = (bf16[48,512]{1,0:T(8,128)(2,1)S(1)}, bf16[48,512]{1,0:T(8,128)(2,1)S(1)}, u32[]{:S(2)}, u32[]{:S(2)}) collective-permute-start(bf16[48,512]{1,0:T(8,128)(2,1)S(1)} %shard_map.144.refs_0_.hidden), channel_id=1, source_target_pairs={{0,5},{1,4},{2,7},{3,6},{4,1},{5,0},{6,3},{7,2},{8,13},{9,12},{10,... | collective-permute-start | bytes 147464 | tf_op jit(solution)/shard_map/ppermute | solution.py:416
  64.4 1.8 %collective-permute-done.19.refs_3_ = bf16[48,512]{1,0:T(8,128)(2,1)S(1)} collective-permute-done((bf16[48,512]{1,0:T(8,128)(2,1)S(1)}, bf16[48,512]{1,0:T(8,128)(2,1)S(1)}, u32[]{:S(2)}, u32[]{:S(2)}) %collective-permute-start.19) | collective-permute-done | bytes 49184 | tf_op jit(solution)/shard_map/ppermute | solution.py:416
  67.6 1.5 %shard_map.145 = (f32[208,768]{1,0:T(8,128)S(1)}, bf16[208,768]{1,0:T(8,128)(2,1)S(1)}, f32[112,768]{1,0:T(8,128)S(1)}, f32[96,768]{1,0:T(8,128)S(1)}, bf16[112,...) custom-call(s32[4]{0:T(128)S(1)} %pad_add_fusion.idx, bf16[48,512]{1,0:T(8,128)(2,1)S(1)} %shard_map.144.refs_0_.hidden, ...), custom_call_target="tpu_custom_call" | custom-call | tf_op jit(solution)/shard_map/pallas_call | solution.py:367
  69.2 1.3 %collective-permute-start.21 = (bf16[96,768]{1,0:T(8,128)(2,1)S(1)}, bf16[96,768]{1,0:T(8,128)(2,1)S(1)}, u32[]{:S(2)}, u32[]{:S(2)}) collective-permute-start(bf16[96,768]{1,0:T(8,128)(2,1)S(1)} %get-tuple-element.155), channel_id=1, source_target_pairs={{0,8},{1,9},{2,10},{3,11},{4,12},{5,13},{6,14},{7,15},{8,0},{9,1},... | collective-permute-start | bytes 442376 | tf_op jit(solution)/shard_map/ppermute | solution.py:416
  71.3 4.6 %collective-permute-done.21.got = bf16[96,768]{1,0:T(8,128)(2,1)S(1)} collective-permute-done((bf16[96,768]{1,0:T(8,128)(2,1)S(1)}, bf16[96,768]{1,0:T(8,128)(2,1)S(1)}, u32[]{:S(2)}, u32[]{:S(2)}) %collective-permute-start.21) | collective-permute-done | bytes 147488 | tf_op jit(solution)/shard_map/ppermute | solution.py:416
  77.2 2.4 %collective-permute-done.24.got = bf16[112,768]{1,0:T(8,128)(2,1)S(1)} collective-permute-done((bf16[112,768]{1,0:T(8,128)(2,1)S(1)}, bf16[112,768]{1,0:T(8,128)(2,1)S(1)}, u32[]{:S(2)}, u32[]{:S(2)}) %collective-permute-start.24) | collective-permute-done | bytes 172064 | tf_op jit(solution)/shard_map/ppermute | solution.py:416
  79.7 1.5 %collective-permute-start.25 = (bf16[112,768]{1,0:T(8,128)(2,1)S(1)}, bf16[112,768]{1,0:T(8,128)(2,1)S(1)}, u32[]{:S(2)}, u32[]{:S(2)}) collective-permute-start(bf16[112,768]{1,0:T(8,128)(2,1)S(1)} %shard_map.146), channel_id=1, source_target_pairs={{0,16},{1,17},{2,18},{3,19},{4,20},{5,21},{6,22},{7,23},{8,24},{9,... | collective-permute-start | bytes 516104 | tf_op jit(solution)/shard_map/ppermute | solution.py:416
  81.2 1.6 %collective-permute-start.26 = (bf16[96,768]{1,0:T(8,128)(2,1)S(1)}, bf16[96,768]{1,0:T(8,128)(2,1)S(1)}, u32[]{:S(2)}, u32[]{:S(2)}) collective-permute-start(bf16[96,768]{1,0:T(8,128)(2,1)S(1)} %shard_map.147), channel_id=1, source_target_pairs={{0,16},{1,17},{2,18},{3,19},{4,20},{5,21},{6,22},{7,23},{8,24},{9,... | collective-permute-start | bytes 442376 | tf_op jit(solution)/shard_map/ppermute | solution.py:416
  82.8 11.8 %collective-permute-done.25.far_head.far_part = bf16[112,768]{1,0:T(8,128)(2,1)S(1)} collective-permute-done((bf16[112,768]{1,0:T(8,128)(2,1)S(1)}, bf16[112,768]{1,0:T(8,128)(2,1)S(1)}, u32[]{:S(2)}, u32[]{:S(2)}) %collective-permute-start.25) | collective-permute-done | bytes 172064 | tf_op jit(solution)/shard_map/ppermute | solution.py:416
  96.8 1.5 %collective-permute-start.30 = (bf16[4,48,512]{2,1,0:T(8,128)(2,1)S(1)}, bf16[4,48,512]{2,1,0:T(8,128)(2,1)S(1)}, u32[]{:S(2)}, u32[]{:S(2)}) collective-permute-start(bf16[4,48,512]{2,1,0:T(8,128)(2,1)S(1)} %get-tuple-element.174), channel_id=1, source_target_pairs={{0,5},{1,4},{2,7},{3,6},{4,1},{5,0},{6,3},{7,2},{8,13},{9,12},{10,... | collective-permute-start | bytes 589832 | tf_op jit(solution)/shard_map/ppermute | solution.py:416
  101.6 2.5 %collective-permute-done.30.refs_3_ = bf16[4,48,512]{2,1,0:T(8,128)(2,1)S(1)} collective-permute-done((bf16[4,48,512]{2,1,0:T(8,128)(2,1)S(1)}, bf16[4,48,512]{2,1,0:T(8,128)(2,1)S(1)}, u32[]{:S(2)}, u32[]{:S(2)}) %collective-permute-start.30) | collective-permute-done | bytes 196640 | tf_op jit(solution)/shard_map/ppermute | solution.py:416
  104.1 2.0 %collective-permute-done.28.refs_1_ = bf16[4,48,512]{2,1,0:T(8,128)(2,1)S(1)} collective-permute-done((bf16[4,48,512]{2,1,0:T(8,128)(2,1)S(1)}, bf16[4,48,512]{2,1,0:T(8,128)(2,1)S(1)}, u32[]{:S(2)}, u32[]{:S(2)}) %collective-permute-start.28) | collective-permute-done | bytes 196640 | tf_op jit(solution)/shard_map/ppermute | solution.py:416
  107.0 1.3 %collective-permute-start.31 = (bf16[64,512]{1,0:T(8,128)(2,1)S(1)}, bf16[64,512]{1,0:T(8,128)(2,1)S(1)}, u32[]{:S(2)}, u32[]{:S(2)}) collective-permute-start(bf16[64,512]{1,0:T(8,128)(2,1)S(1)} %get-tuple-element.175), channel_id=1, source_target_pairs={{0,24},{1,25},{2,26},{3,27},{4,28},{5,29},{6,30},{7,31},{8,16},{9,... | collective-permute-start | bytes 196616 | tf_op jit(solution)/shard_map/ppermute | solution.py:416
  108.4 3.1 %collective-permute-start.33 = (bf16[64,512]{1,0:T(8,128)(2,1)S(1)}, bf16[64,512]{1,0:T(8,128)(2,1)S(1)}, u32[]{:S(2)}, u32[]{:S(2)}) collective-permute-start(bf16[64,512]{1,0:T(8,128)(2,1)S(1)} %get-tuple-element.177), channel_id=1, source_target_pairs={{0,8},{1,9},{2,10},{3,11},{4,12},{5,13},{6,14},{7,15},{8,0},{9,1},... | collective-permute-start | bytes 196616 | tf_op jit(solution)/shard_map/ppermute | solution.py:416
  111.5 1.7 %collective-permute-done.31.refs_3_ = bf16[64,512]{1,0:T(8,128)(2,1)S(1)} collective-permute-done((bf16[64,512]{1,0:T(8,128)(2,1)S(1)}, bf16[64,512]{1,0:T(8,128)(2,1)S(1)}, u32[]{:S(2)}, u32[]{:S(2)}) %collective-permute-start.31) | collective-permute-done | bytes 65568 | tf_op jit(solution)/shard_map/ppermute | solution.py:416
  113.2 1.4 %collective-permute-done.32.refs_2_ = bf16[64,512]{1,0:T(8,128)(2,1)S(1)} collective-permute-done((bf16[64,512]{1,0:T(8,128)(2,1)S(1)}, bf16[64,512]{1,0:T(8,128)(2,1)S(1)}, u32[]{:S(2)}, u32[]{:S(2)}) %collective-permute-start.32) | collective-permute-done | bytes 65568 | tf_op jit(solution)/shard_map/ppermute | solution.py:416
  (81 shorter events, 29.9 us)
Async XLA Ops:
  1.8 12.0 %all-to-all-start = ((bf16[8,16,1280]{2,1,0:T(8,128)(2,1)}), bf16[8,16,1280]{2,1,0:T(8,128)(2,1)S(1)}, u32[]{:S(2)}, u32[]{:S(2)}) async-start(bf16[8,16,1280]{2,1,0:T(8,128)(2,1)} %shard_map.136), calls=%async_computation | async-start | bytes 655360 | tf_op jit(solution)/shard_map/all_to_all | solution.py:425
  13.9 11.7 %collective-permute-start.4 = (bf16[128,3072]{1,0:T(8,128)(2,1)S(1)}, bf16[128,3072]{1,0:T(8,128)(2,1)S(1)}, u32[]{:S(2)}, u32[]{:S(2)}) collective-permute-start(bf16[128,3072]{1,0:T(8,128)(2,1)S(1)} %get-tuple-element.110.refs_4_), channel_id=1, source_target_pairs={{0,2},{1,3},{2,0},{3,1},{4,6},{5,7},{6,4},{7,5},{8,10},{9,11},{10,... | collective-permute-start | bytes 2359304 | tf_op jit(solution)/shard_map/ppermute | solution.py:416
  14.2 17.8 %collective-permute-start.5 = (bf16[2560,128]{1,0:T(8,128)(2,1)}, bf16[2560,128]{1,0:T(8,128)(2,1)S(1)}, u32[]{:S(2)}, u32[]{:S(2)}) collective-permute-start(bf16[2560,128]{1,0:T(8,128)(2,1)} %copy-done.9), channel_id=1, source_target_pairs={{0,4},{1,5},{2,6},{3,7},{4,0},{5,1},{6,2},{7,3},{8,12},{9,13},{10,... | collective-permute-start | bytes 1966088 | tf_op jit(solution)/shard_map/ppermute | solution.py:416
  16.1 6.4 %collective-permute-start.1 = (bf16[128,256]{1,0:T(8,128)(2,1)S(1)}, bf16[128,256]{1,0:T(8,128)(2,1)S(1)}, u32[]{:S(2)}, u32[]{:S(2)}) collective-permute-start(bf16[128,256]{1,0:T(8,128)(2,1)S(1)} %get-tuple-element.105), channel_id=1, source_target_pairs={{0,24},{1,25},{2,26},{3,27},{4,28},{5,29},{6,30},{7,31},{8,16},{9,... | collective-permute-start | bytes 196616 | tf_op jit(solution)/shard_map/ppermute | solution.py:416
  19.7 5.8 %collective-permute-start.2 = (bf16[128,256]{1,0:T(8,128)(2,1)S(1)}, bf16[128,256]{1,0:T(8,128)(2,1)S(1)}, u32[]{:S(2)}, u32[]{:S(2)}) collective-permute-start(bf16[128,256]{1,0:T(8,128)(2,1)S(1)} %get-tuple-element.106), channel_id=1, source_target_pairs={{0,16},{1,17},{2,18},{3,19},{4,20},{5,21},{6,22},{7,23},{8,24},{9,... | collective-permute-start | bytes 196616 | tf_op jit(solution)/shard_map/ppermute | solution.py:416
  19.8 5.8 %collective-permute-start.3 = (bf16[128,256]{1,0:T(8,128)(2,1)S(1)}, bf16[128,256]{1,0:T(8,128)(2,1)S(1)}, u32[]{:S(2)}, u32[]{:S(2)}) collective-permute-start(bf16[128,256]{1,0:T(8,128)(2,1)S(1)} %get-tuple-element.107), channel_id=1, source_target_pairs={{0,8},{1,9},{2,10},{3,11},{4,12},{5,13},{6,14},{7,15},{8,0},{9,1},... | collective-permute-start | bytes 196616 | tf_op jit(solution)/shard_map/ppermute | solution.py:416
  25.6 23.5 %collective-permute-start.11 = (bf16[128,3072]{1,0:T(8,128)(2,1)}, bf16[128,3072]{1,0:T(8,128)(2,1)S(1)}, u32[]{:S(2)}, u32[]{:S(2)}) collective-permute-start(bf16[128,3072]{1,0:T(8,128)(2,1)} %copy-done.8), channel_id=1, source_target_pairs={{0,4},{1,5},{2,6},{3,7},{4,0},{5,1},{6,2},{7,3},{8,12},{9,13},{10,... | collective-permute-start | bytes 2359304 | tf_op jit(solution)/shard_map/ppermute | solution.py:416
  32.0 12.6 %collective-permute-start.9 = (bf16[512,128]{1,0:T(8,128)(2,1)S(1)}, bf16[512,128]{1,0:T(8,128)(2,1)S(1)}, u32[]{:S(2)}, u32[]{:S(2)}) collective-permute-start(bf16[512,128]{1,0:T(8,128)(2,1)S(1)} %get-tuple-element.123), channel_id=1, source_target_pairs={{0,2},{1,3},{2,0},{3,1},{4,6},{5,7},{6,4},{7,5},{8,10},{9,11},{10,... | collective-permute-start | bytes 393224 | tf_op jit(solution)/shard_map/ppermute | solution.py:416
  32.1 7.6 %collective-permute-start.8 = (bf16[96,512]{1,0:T(8,128)(2,1)S(1)}, bf16[96,512]{1,0:T(8,128)(2,1)S(1)}, u32[]{:S(2)}, u32[]{:S(2)}) collective-permute-start(bf16[96,512]{1,0:T(8,128)(2,1)S(1)} %shard_map.140.refs_0_), channel_id=1, source_target_pairs={{0,24},{1,25},{2,26},{3,27},{4,28},{5,29},{6,30},{7,31},{8,16},{9,... | collective-permute-start | bytes 294920 | tf_op jit(solution)/shard_map/ppermute | solution.py:416
  35.8 8.9 %collective-permute-start.7 = (bf16[96,512]{1,0:T(8,128)(2,1)S(1)}, bf16[96,512]{1,0:T(8,128)(2,1)S(1)}, u32[]{:S(2)}, u32[]{:S(2)}) collective-permute-start(bf16[96,512]{1,0:T(8,128)(2,1)S(1)} %shard_map.140.refs_0_), channel_id=1, source_target_pairs={{0,16},{1,17},{2,18},{3,19},{4,20},{5,21},{6,22},{7,23},{8,24},{9,... | collective-permute-start | bytes 294920 | tf_op jit(solution)/shard_map/ppermute | solution.py:416
  35.8 8.9 %collective-permute-start.6 = (bf16[96,512]{1,0:T(8,128)(2,1)S(1)}, bf16[96,512]{1,0:T(8,128)(2,1)S(1)}, u32[]{:S(2)}, u32[]{:S(2)}) collective-permute-start(bf16[96,512]{1,0:T(8,128)(2,1)S(1)} %shard_map.140.refs_0_), channel_id=1, source_target_pairs={{0,8},{1,9},{2,10},{3,11},{4,12},{5,13},{6,14},{7,15},{8,0},{9,1},... | collective-permute-start | bytes 294920 | tf_op jit(solution)/shard_map/ppermute | solution.py:416
  45.9 11.2 %collective-permute-start.15 = (bf16[2,384,128]{2,1,0:T(8,128)(2,1)S(1)}, bf16[2,384,128]{2,1,0:T(8,128)(2,1)S(1)}, u32[]{:S(2)}, u32[]{:S(2)}) collective-permute-start(bf16[2,384,128]{2,1,0:T(8,128)(2,1)S(1)} %get-tuple-element.148), channel_id=1, source_target_pairs={{0,8},{1,9},{2,10},{3,11},{4,12},{5,13},{6,14},{7,15},{8,0},{9,1},... | collective-permute-start | bytes 589832 | tf_op jit(solution)/shard_map/ppermute | solution.py:416
  46.5 12.1 %collective-permute-start.16 = (bf16[2,384,128]{2,1,0:T(8,128)(2,1)S(1)}, bf16[2,384,128]{2,1,0:T(8,128)(2,1)S(1)}, u32[]{:S(2)}, u32[]{:S(2)}) collective-permute-start(bf16[2,384,128]{2,1,0:T(8,128)(2,1)S(1)} %get-tuple-element.149), channel_id=1, source_target_pairs={{0,16},{1,17},{2,18},{3,19},{4,20},{5,21},{6,22},{7,23},{8,24},{9,... | collective-permute-start | bytes 589832 | tf_op jit(solution)/shard_map/ppermute | solution.py:416
  49.1 4.2 %collective-permute-start.12 = (bf16[48,512]{1,0:T(8,128)(2,1)S(1)}, bf16[48,512]{1,0:T(8,128)(2,1)S(1)}, u32[]{:S(2)}, u32[]{:S(2)}) collective-permute-start(bf16[48,512]{1,0:T(8,128)(2,1)S(1)} %get-tuple-element.143), channel_id=1, source_target_pairs={{0,1},{1,0},{2,3},{3,2},{4,5},{5,4},{6,7},{7,6},{8,9},{9,8},{10,11... | collective-permute-start | bytes 147464 | tf_op jit(solution)/shard_map/ppermute | solution.py:416
  50.3 4.5 %collective-permute-start.13 = (bf16[48,512]{1,0:T(8,128)(2,1)S(1)}, bf16[48,512]{1,0:T(8,128)(2,1)S(1)}, u32[]{:S(2)}, u32[]{:S(2)}) collective-permute-start(bf16[48,512]{1,0:T(8,128)(2,1)S(1)} %get-tuple-element.144), channel_id=1, source_target_pairs={{0,4},{1,5},{2,6},{3,7},{4,0},{5,1},{6,2},{7,3},{8,12},{9,13},{10,... | collective-permute-start | bytes 147464 | tf_op jit(solution)/shard_map/ppermute | solution.py:416
  51.2 5.0 %collective-permute-start.14 = (bf16[48,512]{1,0:T(8,128)(2,1)S(1)}, bf16[48,512]{1,0:T(8,128)(2,1)S(1)}, u32[]{:S(2)}, u32[]{:S(2)}) collective-permute-start(bf16[48,512]{1,0:T(8,128)(2,1)S(1)} %get-tuple-element.145), channel_id=1, source_target_pairs={{0,5},{1,4},{2,7},{3,6},{4,1},{5,0},{6,3},{7,2},{8,13},{9,12},{10,... | collective-permute-start | bytes 147464 | tf_op jit(solution)/shard_map/ppermute | solution.py:416
  58.6 8.9 %collective-permute-start.20 = (bf16[128,3072]{1,0:T(8,128)(2,1)S(1)}, bf16[128,3072]{1,0:T(8,128)(2,1)S(1)}, u32[]{:S(2)}, u32[]{:S(2)}) collective-permute-start(bf16[128,3072]{1,0:T(8,128)(2,1)S(1)} %collective-permute-done.11.refs_6_), channel_id=1, source_target_pairs={{0,2},{1,3},{2,0},{3,1},{4,6},{5,7},{6,4},{7,5},{8,10},{9,11},{10,... | collective-permute-start | bytes 2359304 | tf_op jit(solution)/shard_map/ppermute | solution.py:416
  58.6 10.4 %collective-permute-start.23 = (bf16[2,384,128]{2,1,0:T(8,128)(2,1)S(1)}, bf16[2,384,128]{2,1,0:T(8,128)(2,1)S(1)}, u32[]{:S(2)}, u32[]{:S(2)}) collective-permute-start(bf16[2,384,128]{2,1,0:T(8,128)(2,1)S(1)} %get-tuple-element.163), channel_id=1, source_target_pairs={{0,24},{1,25},{2,26},{3,27},{4,28},{5,29},{6,30},{7,31},{8,16},{9,... | collective-permute-start | bytes 589832 | tf_op jit(solution)/shard_map/ppermute | solution.py:416
  60.9 5.3 %collective-permute-start.19 = (bf16[48,512]{1,0:T(8,128)(2,1)S(1)}, bf16[48,512]{1,0:T(8,128)(2,1)S(1)}, u32[]{:S(2)}, u32[]{:S(2)}) collective-permute-start(bf16[48,512]{1,0:T(8,128)(2,1)S(1)} %shard_map.144.refs_0_.hidden), channel_id=1, source_target_pairs={{0,5},{1,4},{2,7},{3,6},{4,1},{5,0},{6,3},{7,2},{8,13},{9,12},{10,... | collective-permute-start | bytes 147464 | tf_op jit(solution)/shard_map/ppermute | solution.py:416
  62.4 4.1 %collective-permute-start.18 = (bf16[48,512]{1,0:T(8,128)(2,1)S(1)}, bf16[48,512]{1,0:T(8,128)(2,1)S(1)}, u32[]{:S(2)}, u32[]{:S(2)}) collective-permute-start(bf16[48,512]{1,0:T(8,128)(2,1)S(1)} %shard_map.144.refs_0_.hidden), channel_id=1, source_target_pairs={{0,4},{1,5},{2,6},{3,7},{4,0},{5,1},{6,2},{7,3},{8,12},{9,13},{10,... | collective-permute-start | bytes 147464 | tf_op jit(solution)/shard_map/ppermute | solution.py:416
  69.2 25.5 %collective-permute-start.27 = (bf16[4,2,384,128]{3,2,1,0:T(8,128)(2,1)S(1)}, bf16[4,2,384,128]{3,2,1,0:T(8,128)(2,1)S(1)}, u32[]{:S(2)}, u32[]{:S(2)}) collective-permute-start(bf16[4,2,384,128]{3,2,1,0:T(8,128)(2,1)S(1)} %shard_map.148.near), channel_id=1, source_target_pairs={{0,2},{1,3},{2,0},{3,1},{4,6},{5,7},{6,4},{7,5},{8,10},{9,11},{10,... | collective-permute-start | bytes 2359304 | tf_op jit(solution)/shard_map/ppermute | solution.py:416
  69.2 6.7 %collective-permute-start.21 = (bf16[96,768]{1,0:T(8,128)(2,1)S(1)}, bf16[96,768]{1,0:T(8,128)(2,1)S(1)}, u32[]{:S(2)}, u32[]{:S(2)}) collective-permute-start(bf16[96,768]{1,0:T(8,128)(2,1)S(1)} %get-tuple-element.155), channel_id=1, source_target_pairs={{0,8},{1,9},{2,10},{3,11},{4,12},{5,13},{6,14},{7,15},{8,0},{9,1},... | collective-permute-start | bytes 442376 | tf_op jit(solution)/shard_map/ppermute | solution.py:416
  70.6 9.1 %collective-permute-start.24 = (bf16[112,768]{1,0:T(8,128)(2,1)S(1)}, bf16[112,768]{1,0:T(8,128)(2,1)S(1)}, u32[]{:S(2)}, u32[]{:S(2)}) collective-permute-start(bf16[112,768]{1,0:T(8,128)(2,1)S(1)} %get-tuple-element.164), channel_id=1, source_target_pairs={{0,8},{1,9},{2,10},{3,11},{4,12},{5,13},{6,14},{7,15},{8,0},{9,1},... | collective-permute-start | bytes 516104 | tf_op jit(solution)/shard_map/ppermute | solution.py:416
  75.9 18.7 %collective-permute-start.22 = (bf16[208,768]{1,0:T(8,128)(2,1)S(1)}, bf16[208,768]{1,0:T(8,128)(2,1)S(1)}, u32[]{:S(2)}, u32[]{:S(2)}) collective-permute-start(bf16[208,768]{1,0:T(8,128)(2,1)S(1)} %get-tuple-element.157), channel_id=1, source_target_pairs={{0,8},{1,9},{2,10},{3,11},{4,12},{5,13},{6,14},{7,15},{8,0},{9,1},... | collective-permute-start | bytes 958472 | tf_op jit(solution)/shard_map/ppermute | solution.py:416
  79.7 14.9 %collective-permute-start.25 = (bf16[112,768]{1,0:T(8,128)(2,1)S(1)}, bf16[112,768]{1,0:T(8,128)(2,1)S(1)}, u32[]{:S(2)}, u32[]{:S(2)}) collective-permute-start(bf16[112,768]{1,0:T(8,128)(2,1)S(1)} %shard_map.146), channel_id=1, source_target_pairs={{0,16},{1,17},{2,18},{3,19},{4,20},{5,21},{6,22},{7,23},{8,24},{9,... | collective-permute-start | bytes 516104 | tf_op jit(solution)/shard_map/ppermute | solution.py:416
  81.2 17.1 %collective-permute-start.26 = (bf16[96,768]{1,0:T(8,128)(2,1)S(1)}, bf16[96,768]{1,0:T(8,128)(2,1)S(1)}, u32[]{:S(2)}, u32[]{:S(2)}) collective-permute-start(bf16[96,768]{1,0:T(8,128)(2,1)S(1)} %shard_map.147), channel_id=1, source_target_pairs={{0,16},{1,17},{2,18},{3,19},{4,20},{5,21},{6,22},{7,23},{8,24},{9,... | collective-permute-start | bytes 442376 | tf_op jit(solution)/shard_map/ppermute | solution.py:416
  95.8 5.7 %collective-permute-start.29 = (bf16[4,48,512]{2,1,0:T(8,128)(2,1)S(1)}, bf16[4,48,512]{2,1,0:T(8,128)(2,1)S(1)}, u32[]{:S(2)}, u32[]{:S(2)}) collective-permute-start(bf16[4,48,512]{2,1,0:T(8,128)(2,1)S(1)} %get-tuple-element.173), channel_id=1, source_target_pairs={{0,4},{1,5},{2,6},{3,7},{4,0},{5,1},{6,2},{7,3},{8,12},{9,13},{10,... | collective-permute-start | bytes 589832 | tf_op jit(solution)/shard_map/ppermute | solution.py:416
  96.8 7.3 %collective-permute-start.30 = (bf16[4,48,512]{2,1,0:T(8,128)(2,1)S(1)}, bf16[4,48,512]{2,1,0:T(8,128)(2,1)S(1)}, u32[]{:S(2)}, u32[]{:S(2)}) collective-permute-start(bf16[4,48,512]{2,1,0:T(8,128)(2,1)S(1)} %get-tuple-element.174), channel_id=1, source_target_pairs={{0,5},{1,4},{2,7},{3,6},{4,1},{5,0},{6,3},{7,2},{8,13},{9,12},{10,... | collective-permute-start | bytes 589832 | tf_op jit(solution)/shard_map/ppermute | solution.py:416
  99.5 6.6 %collective-permute-start.28 = (bf16[4,48,512]{2,1,0:T(8,128)(2,1)S(1)}, bf16[4,48,512]{2,1,0:T(8,128)(2,1)S(1)}, u32[]{:S(2)}, u32[]{:S(2)}) collective-permute-start(bf16[4,48,512]{2,1,0:T(8,128)(2,1)S(1)} %get-tuple-element.172), channel_id=1, source_target_pairs={{0,1},{1,0},{2,3},{3,2},{4,5},{5,4},{6,7},{7,6},{8,9},{9,8},{10,11... | collective-permute-start | bytes 589832 | tf_op jit(solution)/shard_map/ppermute | solution.py:416
  107.0 6.2 %collective-permute-start.31 = (bf16[64,512]{1,0:T(8,128)(2,1)S(1)}, bf16[64,512]{1,0:T(8,128)(2,1)S(1)}, u32[]{:S(2)}, u32[]{:S(2)}) collective-permute-start(bf16[64,512]{1,0:T(8,128)(2,1)S(1)} %get-tuple-element.175), channel_id=1, source_target_pairs={{0,24},{1,25},{2,26},{3,27},{4,28},{5,29},{6,30},{7,31},{8,16},{9,... | collective-permute-start | bytes 196616 | tf_op jit(solution)/shard_map/ppermute | solution.py:416
  108.3 6.2 %collective-permute-start.32 = (bf16[64,512]{1,0:T(8,128)(2,1)S(1)}, bf16[64,512]{1,0:T(8,128)(2,1)S(1)}, u32[]{:S(2)}, u32[]{:S(2)}) collective-permute-start(bf16[64,512]{1,0:T(8,128)(2,1)S(1)} %get-tuple-element.176), channel_id=1, source_target_pairs={{0,16},{1,17},{2,18},{3,19},{4,20},{5,21},{6,22},{7,23},{8,24},{9,... | collective-permute-start | bytes 196616 | tf_op jit(solution)/shard_map/ppermute | solution.py:416
  108.4 6.2 %collective-permute-start.33 = (bf16[64,512]{1,0:T(8,128)(2,1)S(1)}, bf16[64,512]{1,0:T(8,128)(2,1)S(1)}, u32[]{:S(2)}, u32[]{:S(2)}) collective-permute-start(bf16[64,512]{1,0:T(8,128)(2,1)S(1)} %get-tuple-element.177), channel_id=1, source_target_pairs={{0,8},{1,9},{2,10},{3,11},{4,12},{5,13},{6,14},{7,15},{8,0},{9,1},... | collective-permute-start | bytes 196616 | tf_op jit(solution)/shard_map/ppermute | solution.py:416
  (14 other events, 67.3 us)

commit v10 on v9

--- a/solution.py
+++ b/solution.py
@@ -583,7 +583,7 @@
     return call(
         functools.partial(last_kernel, planes, tokens),
         like(tokens, features),
-        idx, *after(*across_planes(parts)[::-1])[::-1],
+        idx, *across_planes(parts),
         scratch=[pltpu.VMEM((planes, rows, width), F32)],
     )
 

time: 116 us -> 116 us (level)
  no operation moved by 1% of the time
where the time goes in v10:
time: 116 us
  waiting for transfers between devices  54.4 us (47%)
  starting transfers between devices  43.9 us (38%)
  Pallas kernels  13.9 us (12%)
  local copies, waits for them, and re-layouts  3 us (3%)
    ppermute x34, waiting for transfers between devices, swap(): return lax.ppermute(x, axes, [(i, i ^ mask) for i in range(devices)])  53.2 us
    ppermute x34, starting transfers between devices, swap(): return lax.ppermute(x, axes, [(i, i ^ mask) for i in range(devices)])  38.6 us
    pallas_call x17, Pallas kernels, call(): pl.pallas_call(kernel, out_shape=shapes, in_specs=[SMEM if a.dtype == jnp...  13.9 us
    all_to_all x1, starting transfers between devices, plane_exchange(): lax.all_to_all(x, axes, 0, 0, axis_index_groups=plane_groups, tiled=True)  5.3 us
    unnamed x22, local copies, waits for them, and re-layouts  2.91 us
  transfers between devices with their start and end apart: 35, of which 22 were waited for; matrix products, arithmetic and copies ran while one was open for 0% of the time, Pallas kernels for 9%

profile of v10, /device:TPU:0, one launch (start us, length us, event | category | flops | bytes accessed | tf_op | source)
XLA Modules:
  0.0 116.2 jit_solution(12800882031781810108)
XLA Ops:
  0.0 1.8 %shard_map.136 = bf16[8,16,1280]{2,1,0:T(8,128)(2,1)} custom-call(bf16[12,1024]{1,0:T(8,128)(2,1)} %refs_0_.1, bf16[12,1024]{1,0:T(8,128)(2,1)} %refs_1_.1, bf16[12,4096]{1,0:T(8,128)(2,1)} %refs_2_.1, bf16[12,4096]{1,0:T(8,128)(2,1)} %refs_3_.1), custom_call_target="tpu_custom_call" | custom-call | tf_op jit(solution)/shard_map/pallas_call | solution.py:367
  1.8 5.3 %all-to-all-start = ((bf16[8,16,1280]{2,1,0:T(8,128)(2,1)}), bf16[8,16,1280]{2,1,0:T(8,128)(2,1)S(1)}, u32[]{:S(2)}, u32[]{:S(2)}) async-start(bf16[8,16,1280]{2,1,0:T(8,128)(2,1)} %shard_map.136), calls=%async_computation | async-start | bytes 655360 | tf_op jit(solution)/shard_map/all_to_all | solution.py:425
  8.4 1.3 %shard_map.137 = (bf16[2560,128]{1,0:T(8,128)(2,1)S(1)}, bf16[4,384,128]{2,1,0:T(8,128)(2,1)S(1)}, bf16[512,128]{1,0:T(8,128)(2,1)S(1)}, bf16[512,128]{1,0:T(8,128)(2,1)}) custom-call(s32[4]{0:T(128)S(1)} %pad_add_fusion.idx, bf16[3072,128]{1,0:T(8,128)(2,1)S(1)} %copy-done, bf16[2048,128]{1,0:T(8,128)(2,1)S(1)} %copy-done.3), custom_call_target="tpu_custom_call" | custom-call | tf_op jit(solution)/shard_map/pallas_call | solution.py:367
  16.1 3.7 %collective-permute-start.1 = (bf16[128,256]{1,0:T(8,128)(2,1)S(1)}, bf16[128,256]{1,0:T(8,128)(2,1)S(1)}, u32[]{:S(2)}, u32[]{:S(2)}) collective-permute-start(bf16[128,256]{1,0:T(8,128)(2,1)S(1)} %get-tuple-element.101), channel_id=1, source_target_pairs={{0,24},{1,25},{2,26},{3,27},{4,28},{5,29},{6,30},{7,31},{8,16},{9,... | collective-permute-start | bytes 196616 | tf_op jit(solution)/shard_map/ppermute | solution.py:416
  20.5 2.0 %collective-permute-done.1.refs_3_.refs_7_ = bf16[128,256]{1,0:T(8,128)(2,1)S(1)} collective-permute-done((bf16[128,256]{1,0:T(8,128)(2,1)S(1)}, bf16[128,256]{1,0:T(8,128)(2,1)S(1)}, u32[]{:S(2)}, u32[]{:S(2)}) %collective-permute-start.1) | collective-permute-done | bytes 65568 | tf_op jit(solution)/shard_map/ppermute | solution.py:416
  22.5 3.1 %collective-permute-done.2.refs_2_.refs_6_ = bf16[128,256]{1,0:T(8,128)(2,1)S(1)} collective-permute-done((bf16[128,256]{1,0:T(8,128)(2,1)S(1)}, bf16[128,256]{1,0:T(8,128)(2,1)S(1)}, u32[]{:S(2)}, u32[]{:S(2)}) %collective-permute-start.2) | collective-permute-done | bytes 65568 | tf_op jit(solution)/shard_map/ppermute | solution.py:416
  28.2 3.8 %collective-permute-done.5.message = bf16[2560,128]{1,0:T(8,128)(2,1)S(1)} collective-permute-done((bf16[2560,128]{1,0:T(8,128)(2,1)}, bf16[2560,128]{1,0:T(8,128)(2,1)S(1)}, u32[]{:S(2)}, u32[]{:S(2)}) %collective-permute-start.5) | collective-permute-done | bytes 655392 | tf_op jit(solution)/shard_map/ppermute | solution.py:416
  32.1 3.7 %collective-permute-start.8 = (bf16[96,512]{1,0:T(8,128)(2,1)S(1)}, bf16[96,512]{1,0:T(8,128)(2,1)S(1)}, u32[]{:S(2)}, u32[]{:S(2)}) collective-permute-start(bf16[96,512]{1,0:T(8,128)(2,1)S(1)} %shard_map.140.refs_0_), channel_id=1, source_target_pairs={{0,24},{1,25},{2,26},{3,27},{4,28},{5,29},{6,30},{7,31},{8,16},{9,... | collective-permute-start | bytes 294920 | tf_op jit(solution)/shard_map/ppermute | solution.py:416
  36.5 3.1 %collective-permute-done.8.refs_3_ = bf16[96,512]{1,0:T(8,128)(2,1)S(1)} collective-permute-done((bf16[96,512]{1,0:T(8,128)(2,1)S(1)}, bf16[96,512]{1,0:T(8,128)(2,1)S(1)}, u32[]{:S(2)}, u32[]{:S(2)}) %collective-permute-start.8) | collective-permute-done | bytes 98336 | tf_op jit(solution)/shard_map/ppermute | solution.py:416
  39.7 5.0 %collective-permute-done.7.refs_2_ = bf16[96,512]{1,0:T(8,128)(2,1)S(1)} collective-permute-done((bf16[96,512]{1,0:T(8,128)(2,1)S(1)}, bf16[96,512]{1,0:T(8,128)(2,1)S(1)}, u32[]{:S(2)}, u32[]{:S(2)}) %collective-permute-start.7) | collective-permute-done | bytes 98336 | tf_op jit(solution)/shard_map/ppermute | solution.py:416
  46.5 2.5 %collective-permute-start.16 = (bf16[2,384,128]{2,1,0:T(8,128)(2,1)S(1)}, bf16[2,384,128]{2,1,0:T(8,128)(2,1)S(1)}, u32[]{:S(2)}, u32[]{:S(2)}) collective-permute-start(bf16[2,384,128]{2,1,0:T(8,128)(2,1)S(1)} %get-tuple-element.145), channel_id=1, source_target_pairs={{0,16},{1,17},{2,18},{3,19},{4,20},{5,21},{6,22},{7,23},{8,24},{9,... | collective-permute-start | bytes 589832 | tf_op jit(solution)/shard_map/ppermute | solution.py:416
  51.2 1.4 %collective-permute-start.14 = (bf16[48,512]{1,0:T(8,128)(2,1)S(1)}, bf16[48,512]{1,0:T(8,128)(2,1)S(1)}, u32[]{:S(2)}, u32[]{:S(2)}) collective-permute-start(bf16[48,512]{1,0:T(8,128)(2,1)S(1)} %get-tuple-element.141), channel_id=1, source_target_pairs={{0,5},{1,4},{2,7},{3,6},{4,1},{5,0},{6,3},{7,2},{8,13},{9,12},{10,... | collective-permute-start | bytes 147464 | tf_op jit(solution)/shard_map/ppermute | solution.py:416
  53.3 1.5 %collective-permute-done.13.refs_2_ = bf16[48,512]{1,0:T(8,128)(2,1)S(1)} collective-permute-done((bf16[48,512]{1,0:T(8,128)(2,1)S(1)}, bf16[48,512]{1,0:T(8,128)(2,1)S(1)}, u32[]{:S(2)}, u32[]{:S(2)}) %collective-permute-start.13) | collective-permute-done | bytes 49184 | tf_op jit(solution)/shard_map/ppermute | solution.py:416
  54.8 1.4 %collective-permute-done.14.refs_3_ = bf16[48,512]{1,0:T(8,128)(2,1)S(1)} collective-permute-done((bf16[48,512]{1,0:T(8,128)(2,1)S(1)}, bf16[48,512]{1,0:T(8,128)(2,1)S(1)}, u32[]{:S(2)}, u32[]{:S(2)}) %collective-permute-start.14) | collective-permute-done | bytes 49184 | tf_op jit(solution)/shard_map/ppermute | solution.py:416
  57.1 1.5 %collective-permute-done.16.refs_2_ = bf16[2,384,128]{2,1,0:T(8,128)(2,1)S(1)} collective-permute-done((bf16[2,384,128]{2,1,0:T(8,128)(2,1)S(1)}, bf16[2,384,128]{2,1,0:T(8,128)(2,1)S(1)}, u32[]{:S(2)}, u32[]{:S(2)}) %collective-permute-start.16) | collective-permute-done | bytes 196640 | tf_op jit(solution)/shard_map/ppermute | solution.py:416
  58.6 2.2 %collective-permute-start.23 = (bf16[2,384,128]{2,1,0:T(8,128)(2,1)S(1)}, bf16[2,384,128]{2,1,0:T(8,128)(2,1)S(1)}, u32[]{:S(2)}, u32[]{:S(2)}) collective-permute-start(bf16[2,384,128]{2,1,0:T(8,128)(2,1)S(1)} %get-tuple-element.159), channel_id=1, source_target_pairs={{0,24},{1,25},{2,26},{3,27},{4,28},{5,29},{6,30},{7,31},{8,16},{9,... | collective-permute-start | bytes 589832 | tf_op jit(solution)/shard_map/ppermute | solution.py:416
  60.9 1.5 %collective-permute-start.19 = (bf16[48,512]{1,0:T(8,128)(2,1)S(1)}, bf16[48,512]{1,0:T(8,128)(2,1)S(1)}, u32[]{:S(2)}, u32[]{:S(2)}) collective-permute-start(bf16[48,512]{1,0:T(8,128)(2,1)S(1)} %shard_map.144.refs_0_.hidden), channel_id=1, source_target_pairs={{0,5},{1,4},{2,7},{3,6},{4,1},{5,0},{6,3},{7,2},{8,13},{9,12},{10,... | collective-permute-start | bytes 147464 | tf_op jit(solution)/shard_map/ppermute | solution.py:416
  64.4 1.8 %collective-permute-done.19.refs_3_ = bf16[48,512]{1,0:T(8,128)(2,1)S(1)} collective-permute-done((bf16[48,512]{1,0:T(8,128)(2,1)S(1)}, bf16[48,512]{1,0:T(8,128)(2,1)S(1)}, u32[]{:S(2)}, u32[]{:S(2)}) %collective-permute-start.19) | collective-permute-done | bytes 49184 | tf_op jit(solution)/shard_map/ppermute | solution.py:416
  67.6 1.5 %shard_map.145 = (f32[208,768]{1,0:T(8,128)S(1)}, bf16[208,768]{1,0:T(8,128)(2,1)S(1)}, f32[112,768]{1,0:T(8,128)S(1)}, f32[96,768]{1,0:T(8,128)S(1)}, bf16[112,...) custom-call(s32[4]{0:T(128)S(1)} %pad_add_fusion.idx, bf16[48,512]{1,0:T(8,128)(2,1)S(1)} %shard_map.144.refs_0_.hidden, ...), custom_call_target="tpu_custom_call" | custom-call | tf_op jit(solution)/shard_map/pallas_call | solution.py:367
  69.2 1.3 %collective-permute-start.21 = (bf16[96,768]{1,0:T(8,128)(2,1)S(1)}, bf16[96,768]{1,0:T(8,128)(2,1)S(1)}, u32[]{:S(2)}, u32[]{:S(2)}) collective-permute-start(bf16[96,768]{1,0:T(8,128)(2,1)S(1)} %get-tuple-element.151), channel_id=1, source_target_pairs={{0,8},{1,9},{2,10},{3,11},{4,12},{5,13},{6,14},{7,15},{8,0},{9,1},... | collective-permute-start | bytes 442376 | tf_op jit(solution)/shard_map/ppermute | solution.py:416
  71.3 4.6 %collective-permute-done.21.got = bf16[96,768]{1,0:T(8,128)(2,1)S(1)} collective-permute-done((bf16[96,768]{1,0:T(8,128)(2,1)S(1)}, bf16[96,768]{1,0:T(8,128)(2,1)S(1)}, u32[]{:S(2)}, u32[]{:S(2)}) %collective-permute-start.21) | collective-permute-done | bytes 147488 | tf_op jit(solution)/shard_map/ppermute | solution.py:416
  75.9 1.3 %collective-permute-start.22 = (bf16[208,768]{1,0:T(8,128)(2,1)S(1)}, bf16[208,768]{1,0:T(8,128)(2,1)S(1)}, u32[]{:S(2)}, u32[]{:S(2)}) collective-permute-start(bf16[208,768]{1,0:T(8,128)(2,1)S(1)} %get-tuple-element.153), channel_id=1, source_target_pairs={{0,8},{1,9},{2,10},{3,11},{4,12},{5,13},{6,14},{7,15},{8,0},{9,1},... | collective-permute-start | bytes 958472 | tf_op jit(solution)/shard_map/ppermute | solution.py:416
  77.2 2.4 %collective-permute-done.24.got = bf16[112,768]{1,0:T(8,128)(2,1)S(1)} collective-permute-done((bf16[112,768]{1,0:T(8,128)(2,1)S(1)}, bf16[112,768]{1,0:T(8,128)(2,1)S(1)}, u32[]{:S(2)}, u32[]{:S(2)}) %collective-permute-start.24) | collective-permute-done | bytes 172064 | tf_op jit(solution)/shard_map/ppermute | solution.py:416
  79.7 1.5 %collective-permute-start.25 = (bf16[112,768]{1,0:T(8,128)(2,1)S(1)}, bf16[112,768]{1,0:T(8,128)(2,1)S(1)}, u32[]{:S(2)}, u32[]{:S(2)}) collective-permute-start(bf16[112,768]{1,0:T(8,128)(2,1)S(1)} %shard_map.146), channel_id=1, source_target_pairs={{0,16},{1,17},{2,18},{3,19},{4,20},{5,21},{6,22},{7,23},{8,24},{9,... | collective-permute-start | bytes 516104 | tf_op jit(solution)/shard_map/ppermute | solution.py:416
  81.2 1.6 %collective-permute-start.26 = (bf16[96,768]{1,0:T(8,128)(2,1)S(1)}, bf16[96,768]{1,0:T(8,128)(2,1)S(1)}, u32[]{:S(2)}, u32[]{:S(2)}) collective-permute-start(bf16[96,768]{1,0:T(8,128)(2,1)S(1)} %shard_map.147), channel_id=1, source_target_pairs={{0,16},{1,17},{2,18},{3,19},{4,20},{5,21},{6,22},{7,23},{8,24},{9,... | collective-permute-start | bytes 442376 | tf_op jit(solution)/shard_map/ppermute | solution.py:416
  82.8 11.8 %collective-permute-done.25.far_head.far_part = bf16[112,768]{1,0:T(8,128)(2,1)S(1)} collective-permute-done((bf16[112,768]{1,0:T(8,128)(2,1)S(1)}, bf16[112,768]{1,0:T(8,128)(2,1)S(1)}, u32[]{:S(2)}, u32[]{:S(2)}) %collective-permute-start.25) | collective-permute-done | bytes 172064 | tf_op jit(solution)/shard_map/ppermute | solution.py:416
  96.8 1.5 %collective-permute-start.30 = (bf16[4,48,512]{2,1,0:T(8,128)(2,1)S(1)}, bf16[4,48,512]{2,1,0:T(8,128)(2,1)S(1)}, u32[]{:S(2)}, u32[]{:S(2)}) collective-permute-start(bf16[4,48,512]{2,1,0:T(8,128)(2,1)S(1)} %get-tuple-element.170), channel_id=1, source_target_pairs={{0,5},{1,4},{2,7},{3,6},{4,1},{5,0},{6,3},{7,2},{8,13},{9,12},{10,... | collective-permute-start | bytes 589832 | tf_op jit(solution)/shard_map/ppermute | solution.py:416
  101.6 2.5 %collective-permute-done.30.refs_3_ = bf16[4,48,512]{2,1,0:T(8,128)(2,1)S(1)} collective-permute-done((bf16[4,48,512]{2,1,0:T(8,128)(2,1)S(1)}, bf16[4,48,512]{2,1,0:T(8,128)(2,1)S(1)}, u32[]{:S(2)}, u32[]{:S(2)}) %collective-permute-start.30) | collective-permute-done | bytes 196640 | tf_op jit(solution)/shard_map/ppermute | solution.py:416
  104.1 2.0 %collective-permute-done.28.refs_1_ = bf16[4,48,512]{2,1,0:T(8,128)(2,1)S(1)} collective-permute-done((bf16[4,48,512]{2,1,0:T(8,128)(2,1)S(1)}, bf16[4,48,512]{2,1,0:T(8,128)(2,1)S(1)}, u32[]{:S(2)}, u32[]{:S(2)}) %collective-permute-start.28) | collective-permute-done | bytes 196640 | tf_op jit(solution)/shard_map/ppermute | solution.py:416
  107.1 1.8 %collective-permute-start.32 = (bf16[64,512]{1,0:T(8,128)(2,1)S(1)}, bf16[64,512]{1,0:T(8,128)(2,1)S(1)}, u32[]{:S(2)}, u32[]{:S(2)}) collective-permute-start(bf16[64,512]{1,0:T(8,128)(2,1)S(1)} %get-tuple-element.173), channel_id=1, source_target_pairs={{0,16},{1,17},{2,18},{3,19},{4,20},{5,21},{6,22},{7,23},{8,24},{9,... | collective-permute-start | bytes 196616 | tf_op jit(solution)/shard_map/ppermute | solution.py:416
  108.9 2.6 %collective-permute-start.33 = (bf16[64,512]{1,0:T(8,128)(2,1)S(1)}, bf16[64,512]{1,0:T(8,128)(2,1)S(1)}, u32[]{:S(2)}, u32[]{:S(2)}) collective-permute-start(bf16[64,512]{1,0:T(8,128)(2,1)S(1)} %get-tuple-element.174), channel_id=1, source_target_pairs={{0,24},{1,25},{2,26},{3,27},{4,28},{5,29},{6,30},{7,31},{8,16},{9,... | collective-permute-start | bytes 196616 | tf_op jit(solution)/shard_map/ppermute | solution.py:416
  112.3 2.6 %collective-permute-done.33.refs_3_ = bf16[64,512]{1,0:T(8,128)(2,1)S(1)} collective-permute-done((bf16[64,512]{1,0:T(8,128)(2,1)S(1)}, bf16[64,512]{1,0:T(8,128)(2,1)S(1)}, u32[]{:S(2)}, u32[]{:S(2)}) %collective-permute-start.33) | collective-permute-done | bytes 65568 | tf_op jit(solution)/shard_map/ppermute | solution.py:416
  (81 shorter events, 29.5 us)
Async XLA Ops:
  1.8 12.0 %all-to-all-start = ((bf16[8,16,1280]{2,1,0:T(8,128)(2,1)}), bf16[8,16,1280]{2,1,0:T(8,128)(2,1)S(1)}, u32[]{:S(2)}, u32[]{:S(2)}) async-start(bf16[8,16,1280]{2,1,0:T(8,128)(2,1)} %shard_map.136), calls=%async_computation | async-start | bytes 655360 | tf_op jit(solution)/shard_map/all_to_all | solution.py:425
  13.9 11.7 %collective-permute-start.4 = (bf16[128,3072]{1,0:T(8,128)(2,1)S(1)}, bf16[128,3072]{1,0:T(8,128)(2,1)S(1)}, u32[]{:S(2)}, u32[]{:S(2)}) collective-permute-start(bf16[128,3072]{1,0:T(8,128)(2,1)S(1)} %get-tuple-element.106.refs_4_), channel_id=1, source_target_pairs={{0,2},{1,3},{2,0},{3,1},{4,6},{5,7},{6,4},{7,5},{8,10},{9,11},{10,... | collective-permute-start | bytes 2359304 | tf_op jit(solution)/shard_map/ppermute | solution.py:416
  14.2 17.8 %collective-permute-start.5 = (bf16[2560,128]{1,0:T(8,128)(2,1)}, bf16[2560,128]{1,0:T(8,128)(2,1)S(1)}, u32[]{:S(2)}, u32[]{:S(2)}) collective-permute-start(bf16[2560,128]{1,0:T(8,128)(2,1)} %copy-done.9), channel_id=1, source_target_pairs={{0,4},{1,5},{2,6},{3,7},{4,0},{5,1},{6,2},{7,3},{8,12},{9,13},{10,... | collective-permute-start | bytes 1966088 | tf_op jit(solution)/shard_map/ppermute | solution.py:416
  16.1 6.4 %collective-permute-start.1 = (bf16[128,256]{1,0:T(8,128)(2,1)S(1)}, bf16[128,256]{1,0:T(8,128)(2,1)S(1)}, u32[]{:S(2)}, u32[]{:S(2)}) collective-permute-start(bf16[128,256]{1,0:T(8,128)(2,1)S(1)} %get-tuple-element.101), channel_id=1, source_target_pairs={{0,24},{1,25},{2,26},{3,27},{4,28},{5,29},{6,30},{7,31},{8,16},{9,... | collective-permute-start | bytes 196616 | tf_op jit(solution)/shard_map/ppermute | solution.py:416
  19.7 5.8 %collective-permute-start.2 = (bf16[128,256]{1,0:T(8,128)(2,1)S(1)}, bf16[128,256]{1,0:T(8,128)(2,1)S(1)}, u32[]{:S(2)}, u32[]{:S(2)}) collective-permute-start(bf16[128,256]{1,0:T(8,128)(2,1)S(1)} %get-tuple-element.102), channel_id=1, source_target_pairs={{0,16},{1,17},{2,18},{3,19},{4,20},{5,21},{6,22},{7,23},{8,24},{9,... | collective-permute-start | bytes 196616 | tf_op jit(solution)/shard_map/ppermute | solution.py:416
  19.8 5.8 %collective-permute-start.3 = (bf16[128,256]{1,0:T(8,128)(2,1)S(1)}, bf16[128,256]{1,0:T(8,128)(2,1)S(1)}, u32[]{:S(2)}, u32[]{:S(2)}) collective-permute-start(bf16[128,256]{1,0:T(8,128)(2,1)S(1)} %get-tuple-element.103), channel_id=1, source_target_pairs={{0,8},{1,9},{2,10},{3,11},{4,12},{5,13},{6,14},{7,15},{8,0},{9,1},... | collective-permute-start | bytes 196616 | tf_op jit(solution)/shard_map/ppermute | solution.py:416
  25.6 23.5 %collective-permute-start.11 = (bf16[128,3072]{1,0:T(8,128)(2,1)}, bf16[128,3072]{1,0:T(8,128)(2,1)S(1)}, u32[]{:S(2)}, u32[]{:S(2)}) collective-permute-start(bf16[128,3072]{1,0:T(8,128)(2,1)} %copy-done.8), channel_id=1, source_target_pairs={{0,4},{1,5},{2,6},{3,7},{4,0},{5,1},{6,2},{7,3},{8,12},{9,13},{10,... | collective-permute-start | bytes 2359304 | tf_op jit(solution)/shard_map/ppermute | solution.py:416
  32.0 12.6 %collective-permute-start.9 = (bf16[512,128]{1,0:T(8,128)(2,1)S(1)}, bf16[512,128]{1,0:T(8,128)(2,1)S(1)}, u32[]{:S(2)}, u32[]{:S(2)}) collective-permute-start(bf16[512,128]{1,0:T(8,128)(2,1)S(1)} %get-tuple-element.119), channel_id=1, source_target_pairs={{0,2},{1,3},{2,0},{3,1},{4,6},{5,7},{6,4},{7,5},{8,10},{9,11},{10,... | collective-permute-start | bytes 393224 | tf_op jit(solution)/shard_map/ppermute | solution.py:416
  32.1 7.6 %collective-permute-start.8 = (bf16[96,512]{1,0:T(8,128)(2,1)S(1)}, bf16[96,512]{1,0:T(8,128)(2,1)S(1)}, u32[]{:S(2)}, u32[]{:S(2)}) collective-permute-start(bf16[96,512]{1,0:T(8,128)(2,1)S(1)} %shard_map.140.refs_0_), channel_id=1, source_target_pairs={{0,24},{1,25},{2,26},{3,27},{4,28},{5,29},{6,30},{7,31},{8,16},{9,... | collective-permute-start | bytes 294920 | tf_op jit(solution)/shard_map/ppermute | solution.py:416
  35.8 8.9 %collective-permute-start.7 = (bf16[96,512]{1,0:T(8,128)(2,1)S(1)}, bf16[96,512]{1,0:T(8,128)(2,1)S(1)}, u32[]{:S(2)}, u32[]{:S(2)}) collective-permute-start(bf16[96,512]{1,0:T(8,128)(2,1)S(1)} %shard_map.140.refs_0_), channel_id=1, source_target_pairs={{0,16},{1,17},{2,18},{3,19},{4,20},{5,21},{6,22},{7,23},{8,24},{9,... | collective-permute-start | bytes 294920 | tf_op jit(solution)/shard_map/ppermute | solution.py:416
  35.8 8.9 %collective-permute-start.6 = (bf16[96,512]{1,0:T(8,128)(2,1)S(1)}, bf16[96,512]{1,0:T(8,128)(2,1)S(1)}, u32[]{:S(2)}, u32[]{:S(2)}) collective-permute-start(bf16[96,512]{1,0:T(8,128)(2,1)S(1)} %shard_map.140.refs_0_), channel_id=1, source_target_pairs={{0,8},{1,9},{2,10},{3,11},{4,12},{5,13},{6,14},{7,15},{8,0},{9,1},... | collective-permute-start | bytes 294920 | tf_op jit(solution)/shard_map/ppermute | solution.py:416
  45.9 11.2 %collective-permute-start.15 = (bf16[2,384,128]{2,1,0:T(8,128)(2,1)S(1)}, bf16[2,384,128]{2,1,0:T(8,128)(2,1)S(1)}, u32[]{:S(2)}, u32[]{:S(2)}) collective-permute-start(bf16[2,384,128]{2,1,0:T(8,128)(2,1)S(1)} %get-tuple-element.144), channel_id=1, source_target_pairs={{0,8},{1,9},{2,10},{3,11},{4,12},{5,13},{6,14},{7,15},{8,0},{9,1},... | collective-permute-start | bytes 589832 | tf_op jit(solution)/shard_map/ppermute | solution.py:416
  46.5 12.1 %collective-permute-start.16 = (bf16[2,384,128]{2,1,0:T(8,128)(2,1)S(1)}, bf16[2,384,128]{2,1,0:T(8,128)(2,1)S(1)}, u32[]{:S(2)}, u32[]{:S(2)}) collective-permute-start(bf16[2,384,128]{2,1,0:T(8,128)(2,1)S(1)} %get-tuple-element.145), channel_id=1, source_target_pairs={{0,16},{1,17},{2,18},{3,19},{4,20},{5,21},{6,22},{7,23},{8,24},{9,... | collective-permute-start | bytes 589832 | tf_op jit(solution)/shard_map/ppermute | solution.py:416
  49.1 4.2 %collective-permute-start.12 = (bf16[48,512]{1,0:T(8,128)(2,1)S(1)}, bf16[48,512]{1,0:T(8,128)(2,1)S(1)}, u32[]{:S(2)}, u32[]{:S(2)}) collective-permute-start(bf16[48,512]{1,0:T(8,128)(2,1)S(1)} %get-tuple-element.139), channel_id=1, source_target_pairs={{0,1},{1,0},{2,3},{3,2},{4,5},{5,4},{6,7},{7,6},{8,9},{9,8},{10,11... | collective-permute-start | bytes 147464 | tf_op jit(solution)/shard_map/ppermute | solution.py:416
  50.3 4.5 %collective-permute-start.13 = (bf16[48,512]{1,0:T(8,128)(2,1)S(1)}, bf16[48,512]{1,0:T(8,128)(2,1)S(1)}, u32[]{:S(2)}, u32[]{:S(2)}) collective-permute-start(bf16[48,512]{1,0:T(8,128)(2,1)S(1)} %get-tuple-element.140), channel_id=1, source_target_pairs={{0,4},{1,5},{2,6},{3,7},{4,0},{5,1},{6,2},{7,3},{8,12},{9,13},{10,... | collective-permute-start | bytes 147464 | tf_op jit(solution)/shard_map/ppermute | solution.py:416
  51.2 5.0 %collective-permute-start.14 = (bf16[48,512]{1,0:T(8,128)(2,1)S(1)}, bf16[48,512]{1,0:T(8,128)(2,1)S(1)}, u32[]{:S(2)}, u32[]{:S(2)}) collective-permute-start(bf16[48,512]{1,0:T(8,128)(2,1)S(1)} %get-tuple-element.141), channel_id=1, source_target_pairs={{0,5},{1,4},{2,7},{3,6},{4,1},{5,0},{6,3},{7,2},{8,13},{9,12},{10,... | collective-permute-start | bytes 147464 | tf_op jit(solution)/shard_map/ppermute | solution.py:416
  58.6 8.9 %collective-permute-start.20 = (bf16[128,3072]{1,0:T(8,128)(2,1)S(1)}, bf16[128,3072]{1,0:T(8,128)(2,1)S(1)}, u32[]{:S(2)}, u32[]{:S(2)}) collective-permute-start(bf16[128,3072]{1,0:T(8,128)(2,1)S(1)} %collective-permute-done.11.refs_6_), channel_id=1, source_target_pairs={{0,2},{1,3},{2,0},{3,1},{4,6},{5,7},{6,4},{7,5},{8,10},{9,11},{10,... | collective-permute-start | bytes 2359304 | tf_op jit(solution)/shard_map/ppermute | solution.py:416
  58.6 10.4 %collective-permute-start.23 = (bf16[2,384,128]{2,1,0:T(8,128)(2,1)S(1)}, bf16[2,384,128]{2,1,0:T(8,128)(2,1)S(1)}, u32[]{:S(2)}, u32[]{:S(2)}) collective-permute-start(bf16[2,384,128]{2,1,0:T(8,128)(2,1)S(1)} %get-tuple-element.159), channel_id=1, source_target_pairs={{0,24},{1,25},{2,26},{3,27},{4,28},{5,29},{6,30},{7,31},{8,16},{9,... | collective-permute-start | bytes 589832 | tf_op jit(solution)/shard_map/ppermute | solution.py:416
  60.9 5.3 %collective-permute-start.19 = (bf16[48,512]{1,0:T(8,128)(2,1)S(1)}, bf16[48,512]{1,0:T(8,128)(2,1)S(1)}, u32[]{:S(2)}, u32[]{:S(2)}) collective-permute-start(bf16[48,512]{1,0:T(8,128)(2,1)S(1)} %shard_map.144.refs_0_.hidden), channel_id=1, source_target_pairs={{0,5},{1,4},{2,7},{3,6},{4,1},{5,0},{6,3},{7,2},{8,13},{9,12},{10,... | collective-permute-start | bytes 147464 | tf_op jit(solution)/shard_map/ppermute | solution.py:416
  62.4 4.1 %collective-permute-start.18 = (bf16[48,512]{1,0:T(8,128)(2,1)S(1)}, bf16[48,512]{1,0:T(8,128)(2,1)S(1)}, u32[]{:S(2)}, u32[]{:S(2)}) collective-permute-start(bf16[48,512]{1,0:T(8,128)(2,1)S(1)} %shard_map.144.refs_0_.hidden), channel_id=1, source_target_pairs={{0,4},{1,5},{2,6},{3,7},{4,0},{5,1},{6,2},{7,3},{8,12},{9,13},{10,... | collective-permute-start | bytes 147464 | tf_op jit(solution)/shard_map/ppermute | solution.py:416
  69.2 25.5 %collective-permute-start.27 = (bf16[4,2,384,128]{3,2,1,0:T(8,128)(2,1)S(1)}, bf16[4,2,384,128]{3,2,1,0:T(8,128)(2,1)S(1)}, u32[]{:S(2)}, u32[]{:S(2)}) collective-permute-start(bf16[4,2,384,128]{3,2,1,0:T(8,128)(2,1)S(1)} %shard_map.148.near), channel_id=1, source_target_pairs={{0,2},{1,3},{2,0},{3,1},{4,6},{5,7},{6,4},{7,5},{8,10},{9,11},{10,... | collective-permute-start | bytes 2359304 | tf_op jit(solution)/shard_map/ppermute | solution.py:416
  69.2 6.7 %collective-permute-start.21 = (bf16[96,768]{1,0:T(8,128)(2,1)S(1)}, bf16[96,768]{1,0:T(8,128)(2,1)S(1)}, u32[]{:S(2)}, u32[]{:S(2)}) collective-permute-start(bf16[96,768]{1,0:T(8,128)(2,1)S(1)} %get-tuple-element.151), channel_id=1, source_target_pairs={{0,8},{1,9},{2,10},{3,11},{4,12},{5,13},{6,14},{7,15},{8,0},{9,1},... | collective-permute-start | bytes 442376 | tf_op jit(solution)/shard_map/ppermute | solution.py:416
  70.6 9.1 %collective-permute-start.24 = (bf16[112,768]{1,0:T(8,128)(2,1)S(1)}, bf16[112,768]{1,0:T(8,128)(2,1)S(1)}, u32[]{:S(2)}, u32[]{:S(2)}) collective-permute-start(bf16[112,768]{1,0:T(8,128)(2,1)S(1)} %get-tuple-element.160), channel_id=1, source_target_pairs={{0,8},{1,9},{2,10},{3,11},{4,12},{5,13},{6,14},{7,15},{8,0},{9,1},... | collective-permute-start | bytes 516104 | tf_op jit(solution)/shard_map/ppermute | solution.py:416
  75.9 18.7 %collective-permute-start.22 = (bf16[208,768]{1,0:T(8,128)(2,1)S(1)}, bf16[208,768]{1,0:T(8,128)(2,1)S(1)}, u32[]{:S(2)}, u32[]{:S(2)}) collective-permute-start(bf16[208,768]{1,0:T(8,128)(2,1)S(1)} %get-tuple-element.153), channel_id=1, source_target_pairs={{0,8},{1,9},{2,10},{3,11},{4,12},{5,13},{6,14},{7,15},{8,0},{9,1},... | collective-permute-start | bytes 958472 | tf_op jit(solution)/shard_map/ppermute | solution.py:416
  79.7 14.9 %collective-permute-start.25 = (bf16[112,768]{1,0:T(8,128)(2,1)S(1)}, bf16[112,768]{1,0:T(8,128)(2,1)S(1)}, u32[]{:S(2)}, u32[]{:S(2)}) collective-permute-start(bf16[112,768]{1,0:T(8,128)(2,1)S(1)} %shard_map.146), channel_id=1, source_target_pairs={{0,16},{1,17},{2,18},{3,19},{4,20},{5,21},{6,22},{7,23},{8,24},{9,... | collective-permute-start | bytes 516104 | tf_op jit(solution)/shard_map/ppermute | solution.py:416
  81.2 17.1 %collective-permute-start.26 = (bf16[96,768]{1,0:T(8,128)(2,1)S(1)}, bf16[96,768]{1,0:T(8,128)(2,1)S(1)}, u32[]{:S(2)}, u32[]{:S(2)}) collective-permute-start(bf16[96,768]{1,0:T(8,128)(2,1)S(1)} %shard_map.147), channel_id=1, source_target_pairs={{0,16},{1,17},{2,18},{3,19},{4,20},{5,21},{6,22},{7,23},{8,24},{9,... | collective-permute-start | bytes 442376 | tf_op jit(solution)/shard_map/ppermute | solution.py:416
  95.8 5.7 %collective-permute-start.29 = (bf16[4,48,512]{2,1,0:T(8,128)(2,1)S(1)}, bf16[4,48,512]{2,1,0:T(8,128)(2,1)S(1)}, u32[]{:S(2)}, u32[]{:S(2)}) collective-permute-start(bf16[4,48,512]{2,1,0:T(8,128)(2,1)S(1)} %get-tuple-element.169), channel_id=1, source_target_pairs={{0,4},{1,5},{2,6},{3,7},{4,0},{5,1},{6,2},{7,3},{8,12},{9,13},{10,... | collective-permute-start | bytes 589832 | tf_op jit(solution)/shard_map/ppermute | solution.py:416
  96.8 7.3 %collective-permute-start.30 = (bf16[4,48,512]{2,1,0:T(8,128)(2,1)S(1)}, bf16[4,48,512]{2,1,0:T(8,128)(2,1)S(1)}, u32[]{:S(2)}, u32[]{:S(2)}) collective-permute-start(bf16[4,48,512]{2,1,0:T(8,128)(2,1)S(1)} %get-tuple-element.170), channel_id=1, source_target_pairs={{0,5},{1,4},{2,7},{3,6},{4,1},{5,0},{6,3},{7,2},{8,13},{9,12},{10,... | collective-permute-start | bytes 589832 | tf_op jit(solution)/shard_map/ppermute | solution.py:416
  99.5 6.6 %collective-permute-start.28 = (bf16[4,48,512]{2,1,0:T(8,128)(2,1)S(1)}, bf16[4,48,512]{2,1,0:T(8,128)(2,1)S(1)}, u32[]{:S(2)}, u32[]{:S(2)}) collective-permute-start(bf16[4,48,512]{2,1,0:T(8,128)(2,1)S(1)} %get-tuple-element.168), channel_id=1, source_target_pairs={{0,1},{1,0},{2,3},{3,2},{4,5},{5,4},{6,7},{7,6},{8,9},{9,8},{10,11... | collective-permute-start | bytes 589832 | tf_op jit(solution)/shard_map/ppermute | solution.py:416
  107.0 4.5 %collective-permute-start.31 = (bf16[64,512]{1,0:T(8,128)(2,1)S(1)}, bf16[64,512]{1,0:T(8,128)(2,1)S(1)}, u32[]{:S(2)}, u32[]{:S(2)}) collective-permute-start(bf16[64,512]{1,0:T(8,128)(2,1)S(1)} %get-tuple-element.172), channel_id=1, source_target_pairs={{0,8},{1,9},{2,10},{3,11},{4,12},{5,13},{6,14},{7,15},{8,0},{9,1},... | collective-permute-start | bytes 196616 | tf_op jit(solution)/shard_map/ppermute | solution.py:416
  107.1 5.2 %collective-permute-start.32 = (bf16[64,512]{1,0:T(8,128)(2,1)S(1)}, bf16[64,512]{1,0:T(8,128)(2,1)S(1)}, u32[]{:S(2)}, u32[]{:S(2)}) collective-permute-start(bf16[64,512]{1,0:T(8,128)(2,1)S(1)} %get-tuple-element.173), channel_id=1, source_target_pairs={{0,16},{1,17},{2,18},{3,19},{4,20},{5,21},{6,22},{7,23},{8,24},{9,... | collective-permute-start | bytes 196616 | tf_op jit(solution)/shard_map/ppermute | solution.py:416
  108.9 6.1 %collective-permute-start.33 = (bf16[64,512]{1,0:T(8,128)(2,1)S(1)}, bf16[64,512]{1,0:T(8,128)(2,1)S(1)}, u32[]{:S(2)}, u32[]{:S(2)}) collective-permute-start(bf16[64,512]{1,0:T(8,128)(2,1)S(1)} %get-tuple-element.174), channel_id=1, source_target_pairs={{0,24},{1,25},{2,26},{3,27},{4,28},{5,29},{6,30},{7,31},{8,16},{9,... | collective-permute-start | bytes 196616 | tf_op jit(solution)/shard_map/ppermute | solution.py:416
  (14 other events, 67.3 us)
